TPU v7x, 32 devices: a whole 2x2x4 slice. The times are simulated.
32 devices in a mesh: slab: 8 (over z, x), case: 4 (over y, core).
Axes of the slice: x: 2, y: 2, z: 4, core: 2. Of those that a mesh axis runs over, the one named last changes fastest.
Arguments:
- tokens: bfloat16 [4, 16, 8, 8, 512], P('case', 'slab'), may hold values from -6 to 6
- cotangent: bfloat16 [4, 16, 8, 8, 512], P('case', 'slab'), may hold values from -6 to 6
- w_qkv: bfloat16 [512, 1536], replicated, may hold values from -4 to 4
- w_out: bfloat16 [512, 512], replicated, may hold values from -0.25 to 0.25
- w_up: bfloat16 [512, 2048], replicated, may hold values from -0.25 to 0.25
- w_down: bfloat16 [2048, 512], replicated, may hold values from -0.125 to 0.125
- gain_attn: float32 [512], replicated, may hold values from 0.1 to 1.9
- gain_mlp: float32 [512], replicated, may hold values from 0.1 to 1.9
Outputs:
- grad_tokens: bfloat16 [4, 16, 8, 8, 512], P('case', 'slab')
- grad_qkv: float32 [512, 1536], P('slab')
- grad_out: float32 [512, 512], P('slab')
- grad_up: float32 [512, 2048], P('slab')
- grad_down: float32 [2048, 512], P('slab')
- grad_gain_attn: float32 [512], P('slab')
- grad_gain_mlp: float32 [512], P('slab')
All inputs are finite; a program needn't handle non-finite values.
Results may differ from a plain program's by a relative error of at most 0.022.
Values may be sent and summed in bfloat16 or wider, within the bound.
No kernel may reach another device: no remote copies, remote signals or barrier semaphores. Data moves between devices by JAX's collectives and lax.ppermute only.
A program may use at most 128 MiB of HBM per device.

v0:
```python
import math

import jax
import jax.numpy as jnp
from jax import lax
from jax.sharding import PartitionSpec as P

HEADS = 8


epsilon = 1e-06
root_two_pi = math.sqrt(2.0 / math.pi)


def normalize(values, gain):
    inverse = lax.rsqrt(jnp.mean(values * values, axis=-1, keepdims=True) + epsilon)
    normed = values * inverse
    return (normed, inverse, (normed * gain).astype(jnp.bfloat16))


def norm_back(grad_normed, normed, inverse, gain):
    scaled = grad_normed * gain
    return inverse * (scaled - normed * jnp.mean(scaled * normed, axis=-1, keepdims=True))


def gelu_value(inputs):
    inner = root_two_pi * (inputs + 0.044715 * inputs * inputs * inputs)
    return 0.5 * inputs * (1.0 + jnp.tanh(inner))


def gelu_slope(inputs):
    tangent = jnp.tanh(root_two_pi * (inputs + 0.044715 * inputs * inputs * inputs))
    return 0.5 * (1.0 + tangent) + 0.5 * inputs * (1.0 - tangent * tangent) * root_two_pi * (
        1.0 + 3.0 * 0.044715 * inputs * inputs
    )


def line_probs(queries, key_rows):
    scale = queries.shape[-1] ** (-0.5)
    scores = (
        jnp.einsum("blhe,bmhe->bhlm", queries, key_rows, preferred_element_type=jnp.float32) * scale
    )
    top = jnp.max(scores, axis=-1, keepdims=True)
    weights = jnp.exp(scores - top)
    return weights / jnp.sum(weights, axis=-1, keepdims=True)


def attend_lines(queries, key_rows, value_rows):
    probs = line_probs(queries, key_rows).astype(jnp.bfloat16)
    return jnp.einsum("bhlm,bmhe->blhe", probs, value_rows, preferred_element_type=jnp.float32)


def attend_back(queries, key_rows, value_rows, grad_lines):
    scale = queries.shape[-1] ** (-0.5)
    probs = line_probs(queries, key_rows)
    rounded = probs.astype(jnp.bfloat16)
    grad_values = jnp.einsum(
        "bhlm,blhe->bmhe", rounded, grad_lines, preferred_element_type=jnp.float32
    )
    grad_probs = jnp.einsum(
        "blhe,bmhe->bhlm", grad_lines, value_rows, preferred_element_type=jnp.float32
    )
    grad_scores = probs * (grad_probs - jnp.sum(probs * grad_probs, axis=-1, keepdims=True))
    score_b = grad_scores.astype(jnp.bfloat16)
    grad_queries = (
        jnp.einsum("bhlm,bmhe->blhe", score_b, key_rows, preferred_element_type=jnp.float32) * scale
    )
    grad_keys = (
        jnp.einsum("bhlm,blhe->bmhe", score_b, queries, preferred_element_type=jnp.float32) * scale
    )
    return (grad_queries, grad_keys, grad_values)


def lines_x(grid):
    return grid.reshape(grid.shape[0] * grid.shape[1], grid.shape[2], grid.shape[3], grid.shape[4])


def lines_y(grid):
    return jnp.swapaxes(grid, 1, 2).reshape(
        grid.shape[0] * grid.shape[2], grid.shape[1], grid.shape[3], grid.shape[4]
    )


def unlines_y(lines, shape):
    return jnp.swapaxes(lines.reshape(shape[0], shape[2], shape[1], shape[3], shape[4]), 1, 2)


def pencil_lines(block):
    shape = block.shape
    merged = block.reshape(shape[0], shape[1], shape[2] * 2, shape[3] // 2)
    return jnp.transpose(merged, (1, 0, 2, 3))


def pencil_block(lines, shape):
    return jnp.transpose(lines, (1, 0, 2, 3)).reshape(shape)


def body(tokens, cotangent, w_qkv, w_out, w_up, w_down, gain_attn, gain_mlp):
    depth_dev, height, across, width = tokens.shape[1:]
    count = depth_dev * height * across
    head_size = width // HEADS
    shape = (depth_dev, height, across, HEADS, head_size)
    pencil_shape = (depth_dev, height * across, HEADS // 2, 2 * head_size)
    flat = tokens.reshape(count, width).astype(jnp.float32)
    normed_one, inverse_one, hidden_one = normalize(flat, gain_attn)
    projected = jnp.dot(hidden_one, w_qkv, preferred_element_type=jnp.float32).astype(jnp.bfloat16)
    queries = projected[:, :width].reshape(shape)
    key_rows = projected[:, width : 2 * width].reshape(shape)
    value_rows = projected[:, 2 * width :].reshape(shape)
    query_block = projected[:, :width].reshape(pencil_shape)
    key_block = projected[:, width : 2 * width].reshape(pencil_shape)
    value_block = projected[:, 2 * width :].reshape(pencil_shape)
    pieces = (
        lax.all_to_all(query_block, "slab", split_axis=1, concat_axis=0, tiled=True),
        lax.all_to_all(key_block, "slab", split_axis=1, concat_axis=0, tiled=True),
        lax.all_to_all(value_block, "slab", split_axis=1, concat_axis=0, tiled=True),
    )
    line_out = attend_lines(
        pencil_lines(pieces[0]), pencil_lines(pieces[1]), pencil_lines(pieces[2])
    ).astype(jnp.bfloat16)
    out_z = lax.all_to_all(
        pencil_block(line_out, pieces[0].shape), "slab", split_axis=0, concat_axis=1, tiled=True
    )
    out_x = attend_lines(lines_x(queries), lines_x(key_rows), lines_x(value_rows)).reshape(shape)
    out_y = unlines_y(attend_lines(lines_y(queries), lines_y(key_rows), lines_y(value_rows)), shape)
    mixed = (
        (out_x + out_y + out_z.reshape(shape).astype(jnp.float32))
        .reshape(count, width)
        .astype(jnp.bfloat16)
    )
    residual = (flat + jnp.dot(mixed, w_out, preferred_element_type=jnp.float32)).astype(
        jnp.bfloat16
    )
    normed_two, inverse_two, hidden_two = normalize(residual.astype(jnp.float32), gain_mlp)
    upper = jnp.dot(hidden_two, w_up, preferred_element_type=jnp.float32)
    active = gelu_value(upper).astype(jnp.bfloat16)
    factor = 1.0 / math.sqrt(count * lax.axis_size("slab") * lax.axis_size("case"))
    grad_rows = cotangent.reshape(count, width)
    grad_active = jnp.dot(grad_rows, w_down.T, preferred_element_type=jnp.float32)
    total_down = jnp.dot(active.T, grad_rows, preferred_element_type=jnp.float32) * factor
    grad_upper = (grad_active * gelu_slope(upper)).astype(jnp.bfloat16)
    total_up = jnp.dot(hidden_two.T, grad_upper, preferred_element_type=jnp.float32) * factor
    grad_hidden_two = jnp.dot(grad_upper, w_up.T, preferred_element_type=jnp.float32)
    total_gain_two = jnp.sum(grad_hidden_two * normed_two, axis=0) * factor
    grad_residual = grad_rows.astype(jnp.float32) + norm_back(
        grad_hidden_two, normed_two, inverse_two, gain_mlp
    )
    grad_res_b = grad_residual.astype(jnp.bfloat16)
    total_out = jnp.dot(mixed.T, grad_res_b, preferred_element_type=jnp.float32) * factor
    grad_flat = jnp.dot(grad_res_b, w_out.T, preferred_element_type=jnp.float32).astype(
        jnp.bfloat16
    )
    grad_mixed = grad_flat.reshape(shape)
    grad_block = grad_flat.reshape(pencil_shape)
    pieces = (
        lax.all_to_all(query_block, "slab", split_axis=1, concat_axis=0, tiled=True),
        lax.all_to_all(key_block, "slab", split_axis=1, concat_axis=0, tiled=True),
        lax.all_to_all(value_block, "slab", split_axis=1, concat_axis=0, tiled=True),
        lax.all_to_all(grad_block, "slab", split_axis=1, concat_axis=0, tiled=True),
    )
    line_grads = attend_back(
        pencil_lines(pieces[0]),
        pencil_lines(pieces[1]),
        pencil_lines(pieces[2]),
        pencil_lines(pieces[3]),
    )
    sent_back = tuple(
        (pencil_block(piece.astype(jnp.bfloat16), pieces[0].shape) for piece in line_grads)
    )
    back_z = (
        lax.all_to_all(sent_back[0], "slab", split_axis=0, concat_axis=1, tiled=True),
        lax.all_to_all(sent_back[1], "slab", split_axis=0, concat_axis=1, tiled=True),
        lax.all_to_all(sent_back[2], "slab", split_axis=0, concat_axis=1, tiled=True),
    )
    back_x = attend_back(
        lines_x(queries), lines_x(key_rows), lines_x(value_rows), lines_x(grad_mixed)
    )
    back_y = attend_back(
        lines_y(queries), lines_y(key_rows), lines_y(value_rows), lines_y(grad_mixed)
    )
    columns = []
    for which in range(3):
        part_x = back_x[which].reshape(shape)
        part_y = unlines_y(back_y[which], shape)
        columns.append((part_x + part_y).reshape(count, width))
    grad_proj = jnp.concatenate(columns, axis=1).astype(jnp.bfloat16)
    total_qkv = jnp.dot(hidden_one.T, grad_proj, preferred_element_type=jnp.float32)
    grad_hidden_one = jnp.dot(grad_proj, w_qkv.T, preferred_element_type=jnp.float32)
    grad_proj_z = jnp.concatenate(
        [back_z[which].reshape(count, width) for which in range(3)], axis=1
    )
    total_qkv = total_qkv + jnp.dot(hidden_one.T, grad_proj_z, preferred_element_type=jnp.float32)
    grad_hidden_one = grad_hidden_one + jnp.dot(
        grad_proj_z, w_qkv.T, preferred_element_type=jnp.float32
    )
    total_qkv = total_qkv * factor
    total_gain_one = jnp.sum(grad_hidden_one * normed_one, axis=0) * factor
    grad_tokens = (
        grad_residual + norm_back(grad_hidden_one, normed_one, inverse_one, gain_attn)
    ).astype(jnp.bfloat16)
    shares = (
        lax.psum_scatter(total_qkv, "slab", scatter_dimension=0, tiled=True),
        lax.psum_scatter(total_out, "slab", scatter_dimension=0, tiled=True),
        lax.psum_scatter(total_up, "slab", scatter_dimension=0, tiled=True),
        lax.psum_scatter(total_down, "slab", scatter_dimension=0, tiled=True),
        lax.psum_scatter(total_gain_one, "slab", scatter_dimension=0, tiled=True),
        lax.psum_scatter(total_gain_two, "slab", scatter_dimension=0, tiled=True),
    )
    full_qkv, full_out, full_up, full_down, gain_one, gain_two = (
        lax.psum(shares[0].astype(jnp.bfloat16), "case").astype(jnp.float32),
        lax.psum(shares[1].astype(jnp.bfloat16), "case").astype(jnp.float32),
        lax.psum(shares[2].astype(jnp.bfloat16), "case").astype(jnp.float32),
        lax.psum(shares[3].astype(jnp.bfloat16), "case").astype(jnp.float32),
        lax.psum(shares[4].astype(jnp.bfloat16), "case").astype(jnp.float32),
        lax.psum(shares[5].astype(jnp.bfloat16), "case").astype(jnp.float32),
    )
    return (
        grad_tokens.reshape(tokens.shape),
        full_qkv,
        full_out,
        full_up,
        full_down,
        gain_one,
        gain_two,
    )


def solution(mesh):
    placed = (
        P("case", "slab", None, None, None),
        P("case", "slab", None, None, None),
        P(),
        P(),
        P(),
        P(),
        P(),
        P(),
    )
    return jax.shard_map(
        body,
        mesh=mesh,
        in_specs=placed,
        out_specs=(
            P("case", "slab", None, None, None),
            P("slab", None),
            P("slab", None),
            P("slab", None),
            P("slab", None),
            P("slab"),
            P("slab"),
        ),
        check_vma=False,
    )
```

profile of v0, /device:TPU:0, one launch (start us, length us, event | category | flops | bytes accessed | tf_op | source)
XLA Modules:
  0.0 488.7 jit_solution(5212258722518044903)
XLA Ops:
  7.2 1.2 multiply_reduce_fusion.8
  10.1 1.8 convolution_convert_fusion
  12.7 7.3 %all-to-all-start.1 = ((bf16[2,64,4,128]{3,2,0,1:T(4,128)(2,1)}), bf16[2,64,4,128]{3,2,0,1:T(4,128)(2,1)}, u32[]{:S(2)}, u32[]{:S(2)}) async-start(bf16[2,64,4,128]{3,2,0,1:T(4,128)(2,1)} %copy.139), calls=%async_computation.1 | async-start | bytes 262144 | tf_op jit(solution)/shard_map/all_to_all | solution.py:114
  26.5 1.7 copy.143
  28.2 1.6 copy.135
  29.8 2.3 fusion.143
  32.1 6.0 %all-to-all-start.2 = ((bf16[2,64,4,128]{3,2,0,1:T(4,128)(2,1)}), bf16[2,64,4,128]{3,2,0,1:T(4,128)(2,1)S(1)}, u32[]{:S(2)}, u32[]{:S(2)}) async-start(bf16[2,64,4,128]{3,2,0,1:T(4,128)(2,1)} %copy.143), calls=%async_computation.2 | async-start | bytes 262144 | tf_op jit(solution)/shard_map/all_to_all | solution.py:115
  38.1 1.9 fusion.138
  40.0 5.4 %all-to-all-done.2 = bf16[2,64,4,128]{3,2,0,1:T(4,128)(2,1)S(1)} async-done(((bf16[2,64,4,128]{3,2,0,1:T(4,128)(2,1)}), bf16[2,64,4,128]{3,2,0,1:T(4,128)(2,1)S(1)}, u32[]{:S(2)}, u32[]{:S(2)}) %all-to-all-start.2) | async-done | bytes 131104 | tf_op jit(solution)/shard_map/all_to_all | solution.py:115
  45.5 3.4 all-to-all-start
  48.9 2.4 fusion.65
  52.7 3.4 all-to-all-done
  57.1 1.3 fusion.133
  58.4 2.4 fusion.15
  62.7 3.6 all-to-all-start.3
  66.3 2.4 fusion.55
  68.7 4.7 all-to-all-done.3
  73.6 1.4 fusion.28
  82.5 1.9 copy.154
  84.4 2.4 fusion.63
  86.9 1.6 multiply_reduce_fusion.1
  89.8 1.2 convolution_multiply_fusion.8
  90.9 2.5 fusion.44
  93.4 1.6 multiply_reduce_fusion.2
  97.5 1.3 convolution_multiply_fusion.3
  99.5 4.0 all-to-all-start.4
  103.5 2.1 fusion.25
  105.6 1.2 reshape.216
  106.8 2.1 fusion.26
  108.9 1.8 reshape.213
  110.7 1.6 constant_dynamic-update-slice_fusion.2
  112.3 2.1 fusion.24
  115.0 1.2 reshape.219
  118.7 1.7 multiply_reduce_fusion
  122.4 1.8 reshape.222
  124.2 5.9 %all-to-all-start.5 = ((bf16[16,8,4,128]{3,2,1,0:T(4,128)(2,1)}), bf16[16,8,4,128]{3,2,1,0:T(4,128)(2,1)S(1)}, u32[]{:S(2)}, u32[]{:S(2)}) async-start(bf16[16,8,4,128]{3,2,1,0:T(4,128)(2,1)} %reshape.222), calls=%async_computation.5 | async-start | bytes 262144 | tf_op jit(solution)/shard_map/all_to_all | solution.py:171
  130.1 1.3 fusion.13
  132.2 1.8 reshape.224
  134.0 4.1 all-to-all-done.5
  138.8 4.0 all-to-all-start.6
  142.8 2.6 fusion.16
  145.4 1.7 copy.174
  147.1 1.8 reshape.226
  148.9 1.3 all-to-all-done.6
  150.2 4.6 all-to-all-start.7
  155.1 3.3 fusion.145
  160.7 1.6 all-to-all-done.7
  163.8 4.4 fusion.3
  168.3 3.8 convolution_multiply_fusion.1
  173.0 2.7 convolution_multiply_fusion
  177.7 2.2 fusion.144
  180.7 20.6 %all-reduce.2 = (bf16[512]{0:T(512)(128)(2,1)S(1)}, bf16[512]{0:T(512)(128)(2,1)S(1)}) all-reduce(f32[512]{0:T(512)S(1)} %broadcast_multiply_fusion.1, f32[512]{0:T(512)S(1)} %broadcast_multiply_fusion), channel_id=6, replica_groups=mesh['slab'=8,'case'=4] {'slab'}, use_global_device_ids=true, to_apply=%region_22.0.clone | all-reduce | flops 1024 | bytes 6144
  201.4 6.0 %all-reduce.3 = (bf16[64]{0:T(256)(128)(2,1)S(1)}, bf16[64]{0:T(256)(128)(2,1)S(1)}) all-reduce(bf16[64]{0:T(256)(128)(2,1)S(1)} %dynamic-slice.7, bf16[64]{0:T(256)(128)(2,1)S(1)} %dynamic-slice.6), channel_id=1, replica_groups=mesh['slab'=8,'case'=4] {'case'}, use_global_device_ids=true, to_apply=%region_23.0 | all-reduce | flops 128 | bytes 512 | tf_op jit(solution)/shard_map/psum | solution.py:214
  208.5 1.5 convert_element_type.181
  210.0 45.6 %reduce-scatter.5.cloned.1.call-done = f32[64,1536]{1,0:T(8,128)} async-done(((f32[512,1536]{1,0:T(8,128)}), f32[64,1536]{1,0:T(8,128)}) %reduce-scatter.5.cloned.1.call-update) | async-done | bytes 393232 | tf_op jit(solution)/shard_map/reduce_scatter | solution.py:202
  255.6 1.7 convert_element_type.179
  257.3 89.6 %reduce-scatter.9.cloned.1.call-done = f32[64,2048]{1,0:T(8,128)} async-done(((f32[512,2048]{1,0:T(8,128)}), f32[64,2048]{1,0:T(8,128)}) %reduce-scatter.9.cloned.1.call-update) | async-done | bytes 524304 | tf_op jit(solution)/shard_map/reduce_scatter | solution.py:204
  346.9 1.8 convert_element_type.183
  348.7 89.4 %reduce-scatter.11.cloned.1.call-done = f32[256,512]{1,0:T(8,128)} async-done(((f32[2048,512]{1,0:T(8,128)}), f32[256,512]{1,0:T(8,128)}) %reduce-scatter.11.cloned.1.call-update) | async-done | bytes 524304 | tf_op jit(solution)/shard_map/reduce_scatter | solution.py:205
  438.1 1.8 convert_element_type.186
  440.7 35.5 %all-reduce.7.cloned.1.call-done = (bf16[64,1536]{1,0:T(8,128)(2,1)}, bf16[64,512]{1,0:T(8,128)(2,1)}, bf16[64,2048]{1,0:T(8,128)(2,1)}, bf16[256,512]{1,0:T(8,128)(2,1)}) async-done(((bf16[64,1536]{1,0:T(8,128)(2,1)}, bf16[64,512]{1,0:T(8,128)(2,1)}, bf16[64,2048]{1,0:T(8,128)(2,1)}, bf16[256,512]{1,0:T(8,128)(2,1)}), (bf16[64,1536]{1,0:T(8,128)(2,1)}, bf16[64,512]{1,0:T(8,128)(2,1)}, ...) | async-done | bytes 786448 | tf_op jit(solution)/shard_map/psum | solution.py:210
  476.2 1.8 convert_element_type.184
  478.0 1.8 convert_element_type.187
  479.8 1.7 convert_element_type.180
  (188 shorter events, 41.6 us)
Async XLA Ops:
  7.2 68.7 %copy-start = (bf16[512,2048]{1,0:T(8,128)(2,1)S(1)}, bf16[512,2048]{1,0:T(8,128)(2,1)}, u32[]{:S(2)}) copy-start(bf16[512,2048]{1,0:T(8,128)(2,1)} %param.12) | copy-start | bytes 6291460
  9.5 0.7 copy-start.12
  12.7 19.5 %all-to-all-start.1 = ((bf16[2,64,4,128]{3,2,0,1:T(4,128)(2,1)}), bf16[2,64,4,128]{3,2,0,1:T(4,128)(2,1)}, u32[]{:S(2)}, u32[]{:S(2)}) async-start(bf16[2,64,4,128]{3,2,0,1:T(4,128)(2,1)} %copy.139), calls=%async_computation.1 | async-start | bytes 262144 | tf_op jit(solution)/shard_map/all_to_all | solution.py:114
  20.3 45.9 %copy-start.19 = (bf16[16,8,8,64]{3,2,1,0:T(8,128)(2,1)}, bf16[16,8,8,64]{3,2,1,0:T(8,128)(2,1)S(1)}, u32[]{:S(2)}) copy-start(bf16[16,8,8,64]{3,2,1,0:T(8,128)(2,1)S(1)} %reshape_reshape.16) | copy-start | bytes 393220
  23.2 15.0 %copy-start.21 = (bf16[16,8,8,64]{3,2,1,0:T(8,128)(2,1)S(1)}, bf16[16,8,8,64]{3,2,1,0:T(8,128)(2,1)}, u32[]{:S(2)}) copy-start(bf16[16,8,8,64]{3,2,1,0:T(8,128)(2,1)} %reshape_reshape.17) | copy-start | bytes 393220
  26.5 22.3 %copy-start.24 = (bf16[2,8,8,8,64]{4,2,3,1,0:T(8,128)(2,1)S(1)}, bf16[2,8,8,8,64]{4,2,3,1,0:T(8,128)(2,1)}, u32[]{:S(2)}) copy-start(bf16[2,8,8,8,64]{4,2,3,1,0:T(8,128)(2,1)} %copy.130) | copy-start | bytes 393220
  26.5 22.3 %copy-start.26 = (bf16[2,8,8,8,64]{4,2,3,1,0:T(8,128)(2,1)S(1)}, bf16[2,8,8,8,64]{4,2,3,1,0:T(8,128)(2,1)}, u32[]{:S(2)}) copy-start(bf16[2,8,8,8,64]{4,2,3,1,0:T(8,128)(2,1)} %copy.131) | copy-start | bytes 393220
  32.1 19.1 %copy-start.42 = (f32[16,8,8]{2,1,0:T(8,128)}, f32[16,8,8]{2,1,0:T(8,128)S(1)}, u32[]{:S(2)}) copy-start(f32[16,8,8]{2,1,0:T(8,128)S(1)} %get-tuple-element.26) | copy-start | bytes 12292
  32.1 13.3 %all-to-all-start.2 = ((bf16[2,64,4,128]{3,2,0,1:T(4,128)(2,1)}), bf16[2,64,4,128]{3,2,0,1:T(4,128)(2,1)S(1)}, u32[]{:S(2)}, u32[]{:S(2)}) async-start(bf16[2,64,4,128]{3,2,0,1:T(4,128)(2,1)} %copy.143), calls=%async_computation.2 | async-start | bytes 262144 | tf_op jit(solution)/shard_map/all_to_all | solution.py:115
  45.5 10.7 %all-to-all-start = ((bf16[2,64,4,128]{3,2,0,1:T(4,128)(2,1)}), bf16[2,64,4,128]{3,2,0,1:T(4,128)(2,1)S(1)}, u32[]{:S(2)}, u32[]{:S(2)}) async-start(bf16[2,64,4,128]{3,2,0,1:T(4,128)(2,1)} %copy.135), calls=%async_computation | async-start | bytes 262144 | tf_op jit(solution)/shard_map/all_to_all | solution.py:116
  52.4 8.4 %copy-start.16 = (bf16[16,8,8,64]{3,2,1,0:T(8,128)(2,1)}, bf16[16,8,8,64]{3,2,1,0:T(8,128)(2,1)S(1)}, u32[]{:S(2)}) copy-start(bf16[16,8,8,64]{3,2,1,0:T(8,128)(2,1)S(1)} %reshape.205) | copy-start | bytes 393220
  52.7 8.1 %copy-start.17 = (bf16[16,8,8,64]{3,2,1,0:T(8,128)(2,1)}, bf16[16,8,8,64]{3,2,1,0:T(8,128)(2,1)S(1)}, u32[]{:S(2)}) copy-start(bf16[16,8,8,64]{3,2,1,0:T(8,128)(2,1)S(1)} %reshape.207) | copy-start | bytes 393220
  58.4 4.3 copy-start.45
  58.4 7.8 %copy-start.22 = (bf16[16,8,8,64]{3,2,1,0:T(8,128)(2,1)S(1)}, bf16[16,8,8,64]{3,2,1,0:T(8,128)(2,1)}, u32[]{:S(2)}) copy-start(bf16[16,8,8,64]{3,2,1,0:T(8,128)(2,1)} %reshape_reshape.17) | copy-start | bytes 393220
  58.4 7.8 %copy-start.40 = (f32[16,8,8]{2,1,0:T(8,128)S(1)}, f32[16,8,8]{2,1,0:T(8,128)}, u32[]{:S(2)}) copy-start(f32[16,8,8]{2,1,0:T(8,128)} %get-tuple-element.24) | copy-start | bytes 12292
  62.7 10.7 %all-to-all-start.3 = ((bf16[16,8,4,128]{3,2,1,0:T(4,128)(2,1)}), bf16[16,8,4,128]{3,2,1,0:T(4,128)(2,1)S(1)}, u32[]{:S(2)}, u32[]{:S(2)}) async-start(bf16[16,8,4,128]{3,2,1,0:T(4,128)(2,1)} %reshape.208), calls=%async_computation.3 | async-start | bytes 262144 | tf_op jit(solution)/shard_map/all_to_all | solution.py:121
  68.6 6.6 %copy-start.7 = (bf16[512,512]{1,0:T(8,128)(2,1)S(1)}, bf16[512,512]{1,0:T(8,128)(2,1)}, u32[]{:S(2)}) copy-start(bf16[512,512]{1,0:T(8,128)(2,1)} %param.11) | copy-start | bytes 1572868
  68.7 6.6 %copy-start.10 = (bf16[1,2,8,8,512]{4,3,2,1,0:T(8,128)(2,1)S(1)}, bf16[1,2,8,8,512]{4,3,2,1,0:T(8,128)(2,1)}, u32[]{:S(2)}) copy-start(bf16[1,2,8,8,512]{4,3,2,1,0:T(8,128)(2,1)} %param.8) | copy-start | bytes 393220
  73.4 2.5 copy-start.47
  75.2 0.7 copy-start.14
  75.2 1.1 copy-start.38
  75.2 1.7 copy-start.49
  77.9 1.0 copy-start.9
  78.0 1.8 copy-start.8
  79.1 0.7 copy-start.2
  82.5 4.3 copy-start.43
  86.9 1.7 copy-start.33
  86.9 1.8 copy-start.25
  86.9 2.9 copy-start.27
  88.5 2.4 copy-start.41
  93.4 1.7 copy-start.32
  93.4 1.8 copy-start.20
  93.4 2.9 copy-start.23
  95.0 2.4 copy-start.3
  95.0 2.4 copy-start.15
  95.2 3.6 copy-start.29
  99.5 17.4 %all-to-all-start.4 = ((bf16[2,64,4,128]{3,2,0,1:T(4,128)(2,1)}), bf16[2,64,4,128]{3,2,0,1:T(4,128)(2,1)}, u32[]{:S(2)}, u32[]{:S(2)}) async-start(bf16[2,64,4,128]{3,2,0,1:T(4,128)(2,1)} %copy.164), calls=%async_computation.4 | async-start | bytes 262144 | tf_op jit(solution)/shard_map/all_to_all | solution.py:159
  103.5 105.0 %reduce-scatter.7.cloned.1.call-start = ((), (), s32[]{:S(2)}) async-start(), calls=%async_computation.13 | async-start | bytes 1179648 | tf_op jit(solution)/shard_map/reduce_scatter | solution.py:203
  118.7 1.7 copy-start.28
  118.7 1.7 copy-start.46
  118.7 2.6 copy-start.18
  120.6 0.7 copy-start.5
  124.2 13.9 %all-to-all-start.5 = ((bf16[16,8,4,128]{3,2,1,0:T(4,128)(2,1)}), bf16[16,8,4,128]{3,2,1,0:T(4,128)(2,1)S(1)}, u32[]{:S(2)}, u32[]{:S(2)}) async-start(bf16[16,8,4,128]{3,2,1,0:T(4,128)(2,1)} %reshape.222), calls=%async_computation.5 | async-start | bytes 262144 | tf_op jit(solution)/shard_map/all_to_all | solution.py:171
  138.1 0.6 copy-start.30
  138.8 11.4 %all-to-all-start.6 = ((bf16[16,8,4,128]{3,2,1,0:T(4,128)(2,1)}), bf16[16,8,4,128]{3,2,1,0:T(4,128)(2,1)}, u32[]{:S(2)}, u32[]{:S(2)}) async-start(bf16[16,8,4,128]{3,2,1,0:T(4,128)(2,1)} %reshape.224), calls=%async_computation.6 | async-start | bytes 262144 | tf_op jit(solution)/shard_map/all_to_all | solution.py:172
  142.8 12.3 %copy-start.13 = (bf16[128,512]{1,0:T(8,128)(2,1)S(1)}, bf16[128,512]{1,0:T(8,128)(2,1)}, u32[]{:S(2)}) copy-start(bf16[128,512]{1,0:T(8,128)(2,1)} %copy-done.12) | copy-start | bytes 393220
  150.2 12.0 %all-to-all-start.7 = ((bf16[16,8,4,128]{3,2,1,0:T(4,128)(2,1)}), bf16[16,8,4,128]{3,2,1,0:T(4,128)(2,1)}, u32[]{:S(2)}, u32[]{:S(2)}) async-start(bf16[16,8,4,128]{3,2,1,0:T(4,128)(2,1)} %reshape.226), calls=%async_computation.7 | async-start | bytes 262144 | tf_op jit(solution)/shard_map/all_to_all | solution.py:173
  154.8 100.8 %reduce-scatter.5.cloned.1.call-start = ((), (), s32[]{:S(2)}) async-start(), calls=%async_computation.12 | async-start | bytes 3538944 | tf_op jit(solution)/shard_map/reduce_scatter | solution.py:202
  155.1 3.4 copy-start.31
  163.2 0.7 copy-start.36
  168.3 178.6 %reduce-scatter.9.cloned.1.call-start = ((), (), s32[]{:S(2)}) async-start(), calls=%async_computation.14 | async-start | bytes 4718592 | tf_op jit(solution)/shard_map/reduce_scatter | solution.py:204
  172.1 0.9 copy-start.39
  172.2 265.9 %reduce-scatter.11.cloned.1.call-start = ((), (), s32[]{:S(2)}) async-start(), calls=%async_computation.15 | async-start | bytes 4718592 | tf_op jit(solution)/shard_map/reduce_scatter | solution.py:205
  175.8 0.7 copy-start.50
  175.8 1.9 copy-start.6
  175.8 4.1 copy-start.11
  175.8 4.1 copy-start.34
  175.8 4.1 copy-start.35
  175.8 4.1 copy-start.37
  175.8 4.1 copy-start.48
  175.9 300.3 %all-reduce.7.cloned.1.call-start = ((), (), s32[]{:S(2)}) async-start(), calls=%async_computation.16 | async-start | bytes 1572864 | tf_op jit(solution)/shard_map/psum | solution.py:210
  177.7 2.2 copy-start.1
  180.7 259.2 %copy-start.4 = (f32[128,512]{1,0:T(8,128)S(1)}, f32[128,512]{1,0:T(8,128)}, u32[]{:S(2)}) copy-start(f32[128,512]{1,0:T(8,128)} %copy-done.2) | copy-start | bytes 786436
  476.2 5.3 %copy-start.44 = (bf16[64,512]{1,0:T(8,128)(2,1)S(1)}, bf16[64,512]{1,0:T(8,128)(2,1)}, u32[]{:S(2)}) copy-start(bf16[64,512]{1,0:T(8,128)(2,1)} %get-tuple-element.16) | copy-start | bytes 196612
Sparse Core Ops, SparseCore 0:
  112.4 65.4 reduce-scatter.6
  181.9 73.6 reduce-scatter.4
  259.7 87.1 reduce-scatter.8
  350.4 87.6 reduce-scatter.10
  441.3 34.8 all-reduce.6
where the time goes:
time: 491 us; the launch traced here: 489 us
  waiting for transfers between devices  281 us (57%)
  matrix products  54.6 us (11%)
  local copies, waits for them, and re-layouts  47.6 us (10%)
  starting transfers between devices  39 us (8%)
  blocking collectives  26.6 us (5%)
  other arithmetic  24.9 us (5%)
  between operations  15.2 us (3%)
    reduce_scatter x1, waiting for transfers between devices, body(): lax.psum_scatter(total_up, 'slab', scatter_dimension=0, tiled=True)  89.6 us
    reduce_scatter x1, waiting for transfers between devices, body(): lax.psum_scatter(total_down, 'slab', scatter_dimension=0, tiled=True)  89.4 us
    reduce_scatter x1, waiting for transfers between devices, body(): lax.psum_scatter(total_qkv, 'slab', scatter_dimension=0, tiled=True)  45.6 us
    psum x1, waiting for transfers between devices, body(): lax.psum(shares[0].astype(jnp.bfloat16), 'case').astype(jnp.float32)  35.5 us
    unnamed x1, blocking collectives  20.6 us
  transfers between devices with their start and end apart: 13, of which 10 were waited for; matrix products, arithmetic and copies ran while one was open for 16% of the time, Pallas kernels for 0%

commit v1 on v0

v1 whole, which is shorter than its diff:
```python
import functools
import math

import jax
import jax.numpy as jnp
from jax import lax
from jax.experimental import pallas as pl
from jax.experimental.pallas import tpu as pltpu
from jax.sharding import PartitionSpec as P

HEADS = 8
LANES = 128
EPSILON = 1e-06
ROOT_TWO_PI = math.sqrt(2.0 / math.pi)
F32 = jnp.float32
BF16 = jnp.bfloat16
BOTH = ("slab", "case")
VMEM_BYTES = 24 * 1024 * 1024


def dot(a, b):
    return lax.dot_general(a, b, (((1,), (0,)), ((), ())), preferred_element_type=F32)


def dot_nt(a, b):
    return lax.dot_general(a, b, (((1,), (1,)), ((), ())), preferred_element_type=F32)


def dot_tn(a, b):
    return lax.dot_general(a, b, (((0,), (0,)), ((), ())), preferred_element_type=F32)


def norm_stats(values):
    inverse = lax.rsqrt(jnp.mean(values * values, axis=-1, keepdims=True) + EPSILON)
    return values * inverse, inverse


def norm_back(scaled, normed, inverse):
    return inverse * (scaled - normed * jnp.mean(scaled * normed, axis=-1, keepdims=True))


def call(kernel, outs, *args, after=(), scratch=(), near=None, flops=10**7):
    count = len(args)
    near = [True] * count if near is None else near

    def run(*refs):
        kernel(*refs[:count], *refs[count + len(after) :])

    vmem, far = pl.BlockSpec(memory_space=pltpu.VMEM), pl.BlockSpec(memory_space=pltpu.HBM)
    return pl.pallas_call(
        run,
        out_shape=outs,
        in_specs=[vmem if one else far for one in near] + [pl.BlockSpec(memory_space=pl.ANY)] * len(after),
        out_specs=[vmem] * len(outs),
        scratch_shapes=list(scratch),
        cost_estimate=pl.CostEstimate(flops=flops, transcendentals=0, bytes_accessed=10**4),
        compiler_params=pltpu.CompilerParams(vmem_limit_bytes=VMEM_BYTES),
    )(
        *[
            arg if one else pltpu.with_memory_space_constraint(arg, pltpu.HBM)
            for arg, one in zip(args, near)
        ],
        *after,
    )


def shape_of(shape, dtype):
    return jax.ShapeDtypeStruct(shape, dtype)


def line_masks(sizes, kind):
    depth, per, across, count = sizes
    rows = lax.broadcasted_iota(jnp.int32, (2 * count, count), 0) & (count - 1)
    cols = lax.broadcasted_iota(jnp.int32, (2 * count, count), 1)

    def parts(t):
        chunk = t // (depth * per)
        plane = (t // per) & (depth - 1)
        spot = chunk * per + (t & (per - 1))
        return plane, spot // across, spot & (across - 1), t & (per - 1)

    a, b = parts(rows), parts(cols)
    if kind == "z":
        return [a[3] == b[3]]
    same = a[0] == b[0]
    return [same & (a[1] == b[1]), same & (a[2] == b[2])]


def softmax_in(scores, mask):
    held = jnp.where(mask, scores, -1e30)
    weights = jnp.exp(held - jnp.max(held, axis=-1, keepdims=True))
    return weights / jnp.sum(weights, axis=-1, keepdims=True)


def pair_parts(proj, pair, width):
    at = pair * LANES
    return [proj[:, which * width + at : which * width + at + LANES] for which in range(3)]


def halves():
    lane = lax.broadcasted_iota(jnp.int32, (1, LANES), 1)
    low = (lane < LANES // 2).astype(F32)
    return low.astype(BF16), (1.0 - low).astype(BF16)


def stack(block, low, high):
    return jnp.concatenate([block * low, block * high], axis=0)


def side(block):
    count = block.shape[0] // 2
    return jnp.concatenate([block[:count], block[count:]], axis=1)


def attend(proj, masks, width):
    low, high = halves()
    scale = (width // HEADS) ** (-0.5)
    outs = []
    for pair in range(HEADS // 2):
        q2, k2, v2 = pair_parts(proj, pair, width)
        scores = dot_nt(stack(q2, low, high), k2) * scale
        probs = sum(softmax_in(scores, mask).astype(BF16).astype(F32) for mask in masks)
        outs.append(dot(side(probs.astype(BF16)), stack(v2, low, high)))
    return jnp.concatenate(outs, axis=1)


def attend_back(proj, grad, masks, width, out_ref, at):
    low, high = halves()
    scale = (width // HEADS) ** (-0.5)
    for pair in range(HEADS // 2):
        q2, k2, v2 = pair_parts(proj, pair, width)
        g2 = grad[:, pair * LANES : (pair + 1) * LANES]
        qs, gs = stack(q2, low, high), stack(g2, low, high)
        scores = dot_nt(qs, k2) * scale
        grad_probs = dot_nt(gs, v2)
        probs = jnp.zeros_like(scores)
        grad_scores = jnp.zeros_like(scores)
        for mask in masks:
            one = softmax_in(scores, mask)
            probs += one.astype(BF16).astype(F32)
            grad_scores += one * (grad_probs - jnp.sum(one * grad_probs, axis=-1, keepdims=True))
        probs, grad_scores = probs.astype(BF16), grad_scores.astype(BF16)
        found = (
            dot(side(grad_scores), stack(k2, low, high)) * scale,
            dot_tn(grad_scores, qs) * scale,
            dot_tn(probs, gs),
        )
        for which in range(3):
            start = at + which * width + pair * LANES
            out_ref[0 : q2.shape[0], start : start + LANES] = found[which].astype(BF16)


def chunk_order(sizes, parts):
    depth, per, _, count = sizes
    rows = lax.broadcasted_iota(jnp.int32, (count, count), 0)
    cols = lax.broadcasted_iota(jnp.int32, (count, count), 1)
    chunk = rows // (depth * per)
    if parts > 1:
        chunk = chunk ^ lax.axis_index("slab")
    plane = (rows // per) & (depth - 1)
    return plane * (count // depth) + chunk * per + (rows & (per - 1)) == cols


def put_parts(refs, at, value):
    rows = refs[0].shape[0]
    for j, ref in enumerate(refs):
        ref[:, at : at + value.shape[1]] = value[j * rows : (j + 1) * rows]


def joined(refs, start, stop):
    return jnp.concatenate([ref[:, start:stop] for ref in refs], axis=0)


def plane_kernel(sizes, x_ref, cot_ref, gain_ref, w_ref, *refs):
    parts, hold_x = refs[:-7], refs[-7]
    x_in, cot_in, gain_in, w_in, proj, sems = refs[-6:]
    copies = [
        pltpu.make_async_copy(src, dst, sems.at[i])
        for i, (src, dst) in enumerate(
            ((x_ref, x_in), (gain_ref, gain_in), (w_ref, w_in), (cot_ref, cot_in))
        )
    ]
    for copy in copies:
        copy.start()
    width = w_in.shape[0]
    order = chunk_order(sizes, len(parts)).astype(F32).astype(BF16)
    masks = line_masks(sizes, "xy")
    copies[0].wait()
    x = dot(order, x_in[...])
    hold_x[...] = x.astype(BF16)
    put_parts(parts, 0, hold_x[...])
    copies[1].wait()
    normed, _ = norm_stats(x)
    hidden = (normed * gain_in[...]).astype(BF16)
    copies[2].wait()
    proj[...] = dot(hidden, w_in[...]).astype(BF16)
    put_parts(parts, 2 * width, attend(proj[...], masks, width).astype(BF16))
    copies[3].wait()
    put_parts(parts, width, dot(order, cot_in[...]).astype(BF16))


def prepare_kernel(slabs, w_up_ref, w_down_ref, up_ref, down_ref):
    x = lax.axis_index("slab") & 1
    quarter = lax.axis_index("case")
    units = w_up_ref.shape[1]
    fine = units // slabs // 4
    rows = lax.broadcasted_iota(jnp.int32, (8 * LANES, LANES), 0)
    cols = lax.broadcasted_iota(jnp.int32, (8 * LANES, LANES), 1)
    wanted = ((cols // fine * 2 + x) * 4 + quarter) * fine + (cols & (fine - 1))
    pick = (rows == wanted).astype(F32).astype(BF16)
    for group in range(up_ref.shape[1] // LANES):
        up_ref[:, group * LANES : (group + 1) * LANES] = dot(
            w_up_ref[:, group * 8 * LANES : (group + 1) * 8 * LANES], pick
        ).astype(BF16)
    for z in range(slabs // 2):
        start = pl.multiple_of(((z * 2 + x) * 4 + quarter) * fine, 8)
        down_ref[z * fine : (z + 1) * fine, :] = w_down_ref[pl.ds(start, fine), :]


def lines_kernel(sizes, parts, *refs):
    got = refs[:parts]
    gain_one_ref, gain_two_ref, w_ref, w_out_ref = refs[parts : parts + 4]
    shared_ref, proj_ref, mixed_ref, residual_ref, hold_x = refs[parts + 4 :]
    width = w_ref.shape[0]
    hold_x[...] = joined(got, 0, width)
    x = hold_x[...].astype(F32)
    normed, _ = norm_stats(x)
    proj_ref[...] = dot((normed * gain_one_ref[...]).astype(BF16), w_ref[...]).astype(BF16)
    out_z = attend(proj_ref[...], line_masks(sizes, "z"), width).astype(BF16)
    mixed = (joined(got, 2 * width, 3 * width).astype(F32) + out_z.astype(F32)).astype(BF16)
    residual = (x + dot(mixed, w_out_ref[...])).astype(BF16)
    normed_two, _ = norm_stats(residual.astype(F32))
    shared_ref[:, :width] = (normed_two * gain_two_ref[...]).astype(BF16)
    shared_ref[:, width:] = joined(got, width, 2 * width)
    mixed_ref[...] = mixed
    residual_ref[...] = residual


def gelu_parts(upper):
    square = upper * upper
    tangent = jnp.tanh(ROOT_TWO_PI * (upper + 0.044715 * upper * square))
    half = 0.5 * (1.0 + tangent)
    slope = half + 0.5 * upper * (1.0 - tangent * tangent) * ROOT_TWO_PI * (
        1.0 + 3.0 * 0.044715 * square
    )
    return (upper * half).astype(BF16), slope


def mlp_kernel(
    shared_ref, residual_ref, gain_ref, w_out_ref, w_up_ref, w_down_ref, grad_ref, gres_ref
):
    width, units = w_up_ref.shape
    hidden, cot = shared_ref[:, :width], shared_ref[:, width:]
    normed, inverse = norm_stats(residual_ref[...].astype(F32))
    step = min(512, units)
    grad_hidden = jnp.zeros(normed.shape, F32)
    for at in range(0, units, step):
        _, slope = gelu_parts(dot(hidden, w_up_ref[:, at : at + step]))
        grad_upper = (dot_nt(cot, w_down_ref[at : at + step, :]) * slope).astype(BF16)
        grad_hidden += dot_nt(grad_upper, w_up_ref[:, at : at + step])
    grad_residual = cot.astype(F32) + norm_back(grad_hidden * gain_ref[...], normed, inverse)
    gres_ref[...] = grad_residual
    grad_ref[...] = dot_nt(grad_residual.astype(BF16), w_out_ref[...]).astype(BF16)


def lines_back_kernel(sizes, proj_ref, grad_ref, gres_ref, mixed_ref, x_ref, gain_ref, w_ref, *refs):
    backs, pack_ref = refs[:-1], refs[-1]
    width = w_ref.shape[0]
    put_parts(backs, 0, grad_ref[...])
    pack_ref[:, 4 * width : 5 * width] = mixed_ref[...]
    pack_ref[:, 5 * width :] = gres_ref[...].astype(BF16)
    attend_back(proj_ref[...], grad_ref[...], line_masks(sizes, "z"), width, pack_ref, width)
    normed, inverse = norm_stats(x_ref[...].astype(F32))
    pack_ref[:, :width] = (normed * gain_ref[...]).astype(BF16)
    grad_hidden = dot_nt(pack_ref[:, width : 4 * width], w_ref[...])
    back = norm_back(grad_hidden * gain_ref[...], normed, inverse)
    put_parts(backs, width, (gres_ref[...] + back).astype(BF16))


def join_kernel(*refs):
    put = refs[-1]
    rows = refs[0].shape[0]
    for j, ref in enumerate(refs[:-1]):
        put[j * rows : (j + 1) * rows, :] = ref[...]


def plane_grads_kernel(sizes, parts, *refs):
    backs = refs[:parts]
    x_ref, gain_ref, w_ref, pack_ref, proj = refs[parts:]
    width = w_ref.shape[0]
    normed, _ = norm_stats(x_ref[...].astype(F32))
    pack_ref[:, :width] = (normed * gain_ref[...]).astype(BF16)
    proj[...] = dot(pack_ref[:, :width], w_ref[...]).astype(BF16)
    grad = joined(backs, 0, width)
    attend_back(proj[...], grad, line_masks(sizes, "xy"), width, pack_ref, width)


def plane_tokens_kernel(sizes, parts, *refs):
    backs = refs[:parts]
    pack_ref, x_ref, gain_ref, w_ref, grad_ref = refs[parts:]
    width = w_ref.shape[0]
    normed, inverse = norm_stats(x_ref[...].astype(F32))
    grad_hidden = dot_nt(pack_ref[:, width:], w_ref[...])
    back = norm_back(grad_hidden * gain_ref[...], normed, inverse)
    part = joined(backs, width, 2 * width).astype(F32)
    order = chunk_order(sizes, parts).astype(F32).astype(BF16)
    grad_ref[...] = dot_tn(order, (back + part).astype(BF16)).astype(BF16)


def place():
    slab, case = lax.axis_index("slab"), lax.axis_index("case")
    return slab & 1, case >> 1, case & 1, slab >> 1


def store_units(scratch, rows, units, x, flip, outs, at):
    blocks = outs[0].shape[0]
    for z in range(blocks):
        start = pl.multiple_of((z * 2 + (x ^ flip)) * rows, 8)
        block = scratch[pl.ds(start, rows), 0 : units * LANES].astype(BF16)
        for unit in range(units):
            outs[flip][z, at + unit * rows : at + (unit + 1) * rows, :] = block[
                :, unit * LANES : (unit + 1) * LANES
            ]


def grads_mlp_kernel(factor, shift, here_ref, there_ref, w_up_ref, w_down_ref, *refs):
    outs, down, up = refs[:-2], refs[-2], refs[-1]
    width, units = w_up_ref.shape
    slab = lax.axis_index("slab")
    digit = (slab >> shift) & (len(outs) - 1)
    hidden = jnp.concatenate([ref[:, :width] for ref in (here_ref, there_ref)], axis=0)
    cot = jnp.concatenate([ref[:, width:] for ref in (here_ref, there_ref)], axis=0)
    active, slope = gelu_parts(dot(hidden, w_up_ref[...]))
    grad_upper = (dot_nt(cot, w_down_ref[...]) * slope).astype(BF16)
    down[...] = dot_tn(active, cot) * factor
    up[...] = dot_tn(hidden, grad_upper) * factor
    rest, rows = outs[0].shape[:2]
    for j, out in enumerate(outs):
        for k in range(rest):
            z = (digit ^ j) * rest + k
            at = pl.ds(pl.multiple_of(z * rows, 8), rows)
            out[k, :, :width] = down[at, :].astype(BF16)
            for flip in range(2):
                at = pl.ds(pl.multiple_of((z * 2 + ((slab & 1) ^ flip)) * rows, 8), rows)
                out[k, :, width + flip * units : width + (flip + 1) * units] = up[at, :].astype(BF16)


def total_kernel(keep, *refs):
    ins, (mine_ref, other_ref) = refs[:-2], refs[-2:]
    total = sum(ref[0].astype(F32) for ref in ins).astype(BF16)
    mine_ref[...] = total[:, :keep]
    other_ref[...] = total[:, keep:]


def beside_kernel(a_ref, b_ref, out_ref):
    out_ref[...] = jnp.concatenate([a_ref[...], b_ref[...]], axis=1)


def grads_qkv_kernel(factor, width, slabs, za_ref, zb_ref, pa_ref, pb_ref, *refs):
    outs, scratch = refs[:4], refs[4]
    x, y, core, _ = place()
    size, narrow = 3 * width // 4, width // 4
    rows = width // slabs
    hidden = jnp.concatenate([r[:, :width] for r in (za_ref, zb_ref, pa_ref, pb_ref)], axis=0)
    mixed = jnp.concatenate([r[:, 4 * width : 5 * width] for r in (za_ref, zb_ref)], axis=0)
    for flip_y in range(2):
        quarter = (y ^ flip_y) * 2 + core
        at = pl.multiple_of(width + quarter * size, LANES)
        cols = jnp.concatenate(
            [r[:, pl.ds(at, size)] for r in (za_ref, zb_ref, pa_ref, pb_ref)], axis=0
        )
        scratch[:, :size] = dot_tn(hidden, cols) * factor
        at = pl.multiple_of(5 * width + quarter * narrow, LANES)
        cols = jnp.concatenate([r[:, pl.ds(at, narrow)] for r in (za_ref, zb_ref)], axis=0)
        scratch[:, size:] = dot_tn(mixed, cols) * factor
        for flip in range(2):
            store_units(scratch, rows, width // LANES, x, flip, outs[2 * flip_y : 2 * flip_y + 2], 0)


def fold_kernel(shift, radix, count, *refs):
    ins, outs = refs[:count], refs[count:]
    digit = (lax.axis_index("slab") >> shift) & (radix - 1)
    rest = ins[0].shape[0] // radix
    for j in range(radix):
        for k in range(rest):
            at = (digit ^ j) * rest + k
            total = ins[0][at].astype(F32)
            for ref in ins[1:]:
                total += ref[at].astype(F32)
            outs[j][k] = total.astype(BF16)


def fold(shift, radix, pieces, after=()):
    first = pieces[0].shape
    outs = [shape_of((first[0] // radix,) + first[1:], BF16)] * radix
    kernel = functools.partial(fold_kernel, shift, radix, len(pieces))
    return call(kernel, outs, *pieces, after=after)


def swap_pairs(slabs, cases, flip_slab, flip_case):
    return [
        (s * cases + c, (s ^ flip_slab) * cases + (c ^ flip_case))
        for s in range(slabs)
        for c in range(cases)
    ]


def gain_sums(grad, w_rows, gain_ref):
    rows, width = grad.shape[0], gain_ref.shape[1]
    spot = lax.axis_index("slab") * rows + lax.broadcasted_iota(jnp.int32, (rows, width), 0)
    lanes = lax.broadcasted_iota(jnp.int32, (rows, width), 1)
    gain = jnp.sum(jnp.where(lanes == spot, gain_ref[...], 0.0), axis=1, keepdims=True)
    total = jnp.sum(grad * w_rows.astype(F32), axis=1, keepdims=True) / gain
    return jnp.transpose(jnp.broadcast_to(total, (rows, LANES)))[0:1, :]


def place_mlp_kernel(slabs, width, units, *refs):
    pieces, (gain_ref, w_up_ref, w_ref) = refs[:4], refs[4:7]
    up, down, two, w_rows, held, up_rows, sems = refs[7:]
    rows = width // slabs
    here = pl.ds(pl.multiple_of(lax.axis_index("slab") * rows, 8), rows)
    copies = [
        pltpu.make_async_copy(w_up_ref.at[here], up_rows, sems.at[0]),
        pltpu.make_async_copy(w_ref.at[here], w_rows, sems.at[1]),
    ]
    for copy in copies:
        copy.start()
    case, x = lax.axis_index("case"), lax.axis_index("slab") & 1
    eighth, fine = units // 8, units // 4 // slabs
    for j in range(4):
        piece = pieces[j][...].astype(F32)
        held[case ^ j, :, :width] = piece[:, :width]
        for flip in range(2):
            at = pl.multiple_of(width + (x ^ flip) * eighth, LANES)
            held[case ^ j, :, pl.ds(at, eighth)] = piece[
                :, width + flip * eighth : width + (flip + 1) * eighth
            ]
    for quarter in range(4):
        down[quarter * rows : (quarter + 1) * rows, :] = held[quarter, :, :width]
    for block in range(slabs):
        up[:, block * 4 * fine : (block + 1) * 4 * fine] = jnp.concatenate(
            [
                held[quarter, :, pl.ds(width + block % 2 * eighth + block // 2 * fine, fine)]
                for quarter in range(4)
            ],
            axis=1,
        )
    for copy in copies:
        copy.wait()
    two[...] = gain_sums(up[...], up_rows[...], gain_ref)


def place_qkv_kernel(slabs, width, *refs):
    pieces, (gain_ref, w_rows), (qkv, out, one) = refs[:4], refs[4:6], refs[6:]
    case = lax.axis_index("case")
    rows = width // slabs
    size = 3 * width // 4
    for j in range(4):
        quarter = case ^ j
        for unit in range(width // LANES):
            piece = pieces[j][0, unit * rows : (unit + 1) * rows, :].astype(F32)
            if unit < size // LANES:
                start = pl.multiple_of(quarter * size + unit * LANES, LANES)
                qkv[:, pl.ds(start, LANES)] = piece
            else:
                start = pl.multiple_of(quarter * (width // 4) + unit * LANES - size, LANES)
                out[:, pl.ds(start, LANES)] = piece
    one[...] = gain_sums(qkv[...], w_rows[...], gain_ref)


def body(tokens, cotangent, w_qkv, w_out, w_up, w_down, gain_attn, gain_mlp):
    slabs, cases = lax.axis_size("slab"), lax.axis_size("case")
    depth, height, across, width = tokens.shape[1:]
    units = w_up.shape[1]
    lines = height * across
    per = lines // slabs
    count = depth * lines
    sizes = (depth, per, across, count)
    factor = 1.0 / math.sqrt(count * slabs * cases)
    gain_one, gain_two = gain_attn.reshape(1, width), gain_mlp.reshape(1, width)
    spans = slabs // 2
    rows = width // slabs
    parts = slabs if depth * per % 16 == 0 else 1

    def permute(array, flip_slab, flip_case):
        return lax.ppermute(array, BOTH, swap_pairs(slabs, cases, flip_slab, flip_case))

    def exchange(blocks):
        if parts == 1:
            return [lax.all_to_all(blocks[0], "slab", split_axis=0, concat_axis=0, tiled=True)]
        got = {j: permute(blocks[j], j, 0) for j in range(parts - 1, 0, -1)}
        return [blocks[0]] + [got[j] for j in range(1, parts)]

    proj_bf = shape_of((count, 3 * width), BF16)
    rows_bf = shape_of((count, width), BF16)
    *mine, hold_x = call(
        functools.partial(plane_kernel, sizes),
        [shape_of((count // parts, 3 * width), BF16)] * parts + [rows_bf],
        tokens.reshape(count, width),
        cotangent.reshape(count, width),
        gain_one,
        w_qkv,
        near=[False] * 4,
        scratch=[
            pltpu.VMEM((count, width), BF16),
            pltpu.VMEM((count, width), BF16),
            pltpu.VMEM((1, width), F32),
            pltpu.VMEM((width, 3 * width), BF16),
            pltpu.VMEM((count, 3 * width), BF16),
            pltpu.SemaphoreType.DMA((4,)),
        ],
    )
    w_up_mine, w_down_mine = call(
        functools.partial(prepare_kernel, slabs),
        [shape_of((width, units // 8), BF16), shape_of((units // 8, width), BF16)],
        w_up,
        w_down,
    )
    got = exchange(mine)
    shared, proj_z, mixed, residual, hold_z = call(
        functools.partial(lines_kernel, sizes, parts),
        [shape_of((count, 2 * width), BF16), proj_bf, rows_bf, rows_bf, rows_bf],
        *got,
        gain_one,
        gain_two,
        w_qkv,
        w_out,
        after=[w_up_mine],
    )
    around = [shared, permute(shared, 0, 2), permute(shared, 1, 0), permute(shared, 1, 2)]
    grad_mixed, grad_residual = call(
        mlp_kernel,
        [rows_bf, shape_of((count, width), F32)],
        shared,
        residual,
        gain_two,
        w_out,
        w_up,
        w_down,
    )
    *backs, pack_z = call(
        functools.partial(lines_back_kernel, sizes),
        [shape_of((count // parts, 2 * width), BF16)] * parts + [shape_of((count, 6 * width), BF16)],
        proj_z,
        grad_mixed,
        grad_residual,
        mixed,
        hold_z,
        gain_one,
        w_qkv,
    )
    backs = exchange(backs)
    (around,) = call(
        join_kernel, [shape_of((4 * count, 2 * width), BF16)], *around, after=backs[1:]
    )
    around_core = permute(around, 0, 1)
    radix = min(4, spans)
    shift = (slabs // radix).bit_length() - 1
    big = call(
        functools.partial(grads_mlp_kernel, factor, shift),
        [shape_of((spans // radix, rows, 2 * width), BF16)] * radix,
        around,
        around_core,
        w_up_mine,
        w_down_mine,
        scratch=[pltpu.VMEM((units // 8, width), F32), pltpu.VMEM((width, units // 8), F32)],
    )
    pack_z_core = permute(pack_z, 0, 1)
    def reduce_z(split):
        left = spans
        while True:
            radix = len(split)
            left //= radix
            shift = (left * 2).bit_length() - 1
            pieces = [split[0]] + [permute(split[j], j << shift, 0) for j in range(1, radix)]
            if left == 1:
                return pieces
            radix = min(4, left)
            split = fold((left // radix * 2).bit_length() - 1, radix, pieces)

    def gather(last):
        return [last] + [permute(last, 0, j) for j in range(1, 4)]

    early = big[0]
    big = reduce_z(big)
    (pack_p,) = call(
        functools.partial(plane_grads_kernel, sizes, parts),
        [shape_of((count, 4 * width), BF16)],
        *backs,
        hold_x,
        gain_one,
        w_qkv,
        scratch=[pltpu.VMEM((count, 3 * width), BF16)],
    )
    small = call(
        functools.partial(grads_qkv_kernel, factor, width, slabs),
        [shape_of((spans, rows * (width // LANES), LANES), BF16)] * 4,
        pack_z,
        pack_z_core,
        pack_p,
        permute(pack_p, 0, 1),
        after=[early],
        scratch=[pltpu.VMEM((width, width), F32)],
    )
    ready = small[0]
    small = [small[0], permute(small[1], 1, 0), permute(small[2], 0, 2), permute(small[3], 1, 2)]
    (grad_tokens,) = call(
        functools.partial(plane_tokens_kernel, sizes, parts),
        [rows_bf],
        *backs,
        pack_p,
        hold_x,
        gain_one,
        w_qkv,
        after=[ready],
    )

    small = reduce_z(fold(shift, radix, small))
    keep = width + units // 8
    mine_big, other_big = call(
        functools.partial(total_kernel, keep),
        [shape_of((rows, keep), BF16), shape_of((rows, units // 8), BF16)],
        *big,
        after=[small[0]],
    )
    (last,) = call(
        beside_kernel, [shape_of((rows, 2 * width), BF16)], mine_big, permute(other_big, 1, 0)
    )
    big = gather(last)
    full_up, full_down, full_two, w_rows = call(
        functools.partial(place_mlp_kernel, slabs, width, units),
        [
            shape_of((rows, units), F32),
            shape_of((units // slabs, width), F32),
            shape_of((1, rows), F32),
            shape_of((rows, 3 * width), BF16),
        ],
        *big,
        gain_two,
        w_up,
        w_qkv,
        near=[True] * 5 + [False] * 2,
        scratch=[
            pltpu.VMEM((4, rows, 2 * width), F32),
            pltpu.VMEM((rows, units), BF16),
            pltpu.SemaphoreType.DMA((2,)),
        ],
    )
    small = gather(fold(0, 1, small)[0])
    full_qkv, full_out, full_one = call(
        functools.partial(place_qkv_kernel, slabs, width),
        [shape_of((rows, 3 * width), F32), shape_of((rows, width), F32), shape_of((1, rows), F32)],
        *small,
        gain_one,
        w_rows,
    )
    return (
        grad_tokens.reshape(tokens.shape),
        full_qkv,
        full_out,
        full_up,
        full_down,
        full_one.reshape(rows),
        full_two.reshape(rows),
    )


def solution(mesh):
    grid = P("case", "slab", None, None, None)
    return jax.shard_map(
        body,
        mesh=mesh,
        in_specs=(grid, grid, P(), P(), P(), P(), P(), P()),
        out_specs=(
            grid,
            P("slab", None),
            P("slab", None),
            P("slab", None),
            P("slab", None),
            P("slab"),
            P("slab"),
        ),
        check_vma=False,
    )
```

time: 491 us -> 95.6 us (0.19)
  waiting for transfers between devices: 281 us -> 27.2 us
  matrix products: 54.6 us -> 0 us
  local copies, waits for them, and re-layouts: 47.6 us -> 3.32 us
  blocking collectives: 26.6 us -> 0 us
  other arithmetic: 24.9 us -> 0 us
  Pallas kernels: 0 us -> 20.3 us
  between operations: 15.2 us -> 0.87 us
    reduce_scatter x4 -> x0, waiting for transfers between devices: 225 us -> none  [the longest x1 89.6 us: body(): lax.psum_scatter(total_up, 'slab', scatter_dimension=0, tiled=True)]
    dot_general x28 -> x0, matrix products: 49 us -> none  [the longest x3 7.47 us: attend_back(): jnp.einsum('bhlm,blhe->bmhe', rounded, grad_lines, preferred_element_type...]
    ppermute x0 -> x36, starting transfers between devices: none -> 43.6 us  [permute(): lax.ppermute(array, BOTH, swap_pairs(slabs, cases, flip_slab, flip_case))]
    all_to_all x8 -> x0, starting transfers between devices: 38.6 us -> none  [the longest x1 7.26 us: body(): lax.all_to_all(query_block, 'slab', split_axis=1, concat_axis=0, tiled=True)]
    psum x1 -> x0, waiting for transfers between devices: 35.5 us -> none  [body(): lax.psum(shares[0].astype(jnp.bfloat16), 'case').astype(jnp.float32)]
    ppermute x0 -> x36, waiting for transfers between devices: none -> 27.2 us  [permute(): lax.ppermute(array, BOTH, swap_pairs(slabs, cases, flip_slab, flip_case))]
    all_to_all x8 -> x0, waiting for transfers between devices: 20.6 us -> none  [the longest x1 5.44 us: body(): lax.all_to_all(key_block, 'slab', split_axis=1, concat_axis=0, tiled=True)]
    unnamed x1 -> x0, blocking collectives: 20.6 us -> none
  transfers between devices with their start and end apart: 13 -> 36, of which waited for: 10 -> 16; matrix products, arithmetic and copies ran while one was open for 16% -> 0% of each run, Pallas kernels for 0% -> 15%
where the time goes in v1:
time: 95.6 us; the launch traced here: 95.4 us
  starting transfers between devices  43.6 us (46%)
  waiting for transfers between devices  27.2 us (28%)
  Pallas kernels  20.3 us (21%)
  local copies, waits for them, and re-layouts  3.32 us (3%)
    ppermute x36, starting transfers between devices, permute(): lax.ppermute(array, BOTH, swap_pairs(slabs, cases, flip_slab, flip_case))  43.6 us
    ppermute x36, waiting for transfers between devices, permute(): lax.ppermute(array, BOTH, swap_pairs(slabs, cases, flip_slab, flip_case))  27.2 us
    pallas_call x16, Pallas kernels, call(): pl.pallas_call(run, out_shape=outs, in_specs=[vmem if one else far for on...  20.3 us
    unnamed x16, local copies, waits for them, and re-layouts  3.32 us
  transfers between devices with their start and end apart: 36, of which 16 were waited for; matrix products, arithmetic and copies ran while one was open for 0% of the time, Pallas kernels for 15%

profile of v1, /device:TPU:0, one launch (start us, length us, event | category | flops | bytes accessed | tf_op | source)
XLA Modules:
  0.0 95.4 jit_solution(17828195400438185798)
XLA Ops:
  0.6 2.9 %shard_map.135 = (bf16[16,1536]{1,0:T(8,128)(2,1)S(1)}, bf16[16,1536]{1,0:T(8,128)(2,1)S(1)}, bf16[16,1536]{1,0:T(8,128)(2,1)S(1)}, bf16[16,1536]{1,0:T(8,128)(2...) custom-call(bf16[128,512]{1,0:T(8,128)(2,1)} %bitcast.16, ...), custom_call_target="tpu_custom_call" | custom-call | flops 10000000 | bytes 10000 | tf_op jit(solution)/shard_map/pallas_call | solution.py:50
  3.5 3.0 %collective-permute-start = (bf16[16,1536]{1,0:T(8,128)(2,1)S(1)}, bf16[16,1536]{1,0:T(8,128)(2,1)S(1)}, u32[]{:S(2)}, u32[]{:S(2)}) collective-permute-start(bf16[16,1536]{1,0:T(8,128)(2,1)S(1)} %get-tuple-element.56), channel_id=1, source_target_pairs={{0,4},{1,5},{2,6},{3,7},{4,0},{5,1},{6,2},{7,3},{8,12},{9,13},{10,... | collective-permute-start | bytes 147464 | tf_op jit(solution)/shard_map/ppermute | solution.py:486
  6.5 1.6 %collective-permute-start.1 = (bf16[16,1536]{1,0:T(8,128)(2,1)S(1)}, bf16[16,1536]{1,0:T(8,128)(2,1)S(1)}, u32[]{:S(2)}, u32[]{:S(2)}) collective-permute-start(bf16[16,1536]{1,0:T(8,128)(2,1)S(1)} %get-tuple-element.57), channel_id=1, source_target_pairs={{0,8},{1,9},{2,10},{3,11},{4,12},{5,13},{6,14},{7,15},{8,0},{9,1},... | collective-permute-start | bytes 147464 | tf_op jit(solution)/shard_map/ppermute | solution.py:486
  8.1 3.0 %collective-permute-start.3 = (bf16[16,1536]{1,0:T(8,128)(2,1)S(1)}, bf16[16,1536]{1,0:T(8,128)(2,1)S(1)}, u32[]{:S(2)}, u32[]{:S(2)}) collective-permute-start(bf16[16,1536]{1,0:T(8,128)(2,1)S(1)} %get-tuple-element.59), channel_id=1, source_target_pairs={{0,16},{1,17},{2,18},{3,19},{4,20},{5,21},{6,22},{7,23},{8,24},{9,... | collective-permute-start | bytes 147464 | tf_op jit(solution)/shard_map/ppermute | solution.py:486
  11.1 1.3 %collective-permute-start.4 = (bf16[16,1536]{1,0:T(8,128)(2,1)S(1)}, bf16[16,1536]{1,0:T(8,128)(2,1)S(1)}, u32[]{:S(2)}, u32[]{:S(2)}) collective-permute-start(bf16[16,1536]{1,0:T(8,128)(2,1)S(1)} %get-tuple-element.60), channel_id=1, source_target_pairs={{0,20},{1,21},{2,22},{3,23},{4,16},{5,17},{6,18},{7,19},{8,28},{9,... | collective-permute-start | bytes 147464 | tf_op jit(solution)/shard_map/ppermute | solution.py:486
  12.4 3.6 %collective-permute-start.5 = (bf16[16,1536]{1,0:T(8,128)(2,1)S(1)}, bf16[16,1536]{1,0:T(8,128)(2,1)S(1)}, u32[]{:S(2)}, u32[]{:S(2)}) collective-permute-start(bf16[16,1536]{1,0:T(8,128)(2,1)S(1)} %get-tuple-element.61), channel_id=1, source_target_pairs={{0,24},{1,25},{2,26},{3,27},{4,28},{5,29},{6,30},{7,31},{8,16},{9,... | collective-permute-start | bytes 147464 | tf_op jit(solution)/shard_map/ppermute | solution.py:486
  16.1 1.7 %copy-done.1 = bf16[512,2048]{1,0:T(8,128)(2,1)S(1)} copy-done((bf16[512,2048]{1,0:T(8,128)(2,1)S(1)}, bf16[512,2048]{1,0:T(8,128)(2,1)}, u32[]{:S(2)}) %copy-start.1) | copy-done | bytes 2097176
  17.8 1.6 %copy-done.3 = bf16[2048,512]{1,0:T(8,128)(2,1)S(1)} copy-done((bf16[2048,512]{1,0:T(8,128)(2,1)S(1)}, bf16[2048,512]{1,0:T(8,128)(2,1)}, u32[]{:S(2)}) %copy-start.3) | copy-done | bytes 2097176
  19.4 0.7 shard_map.136
  20.2 2.6 %collective-permute-done.6.refs_7_ = bf16[16,1536]{1,0:T(8,128)(2,1)S(1)} collective-permute-done((bf16[16,1536]{1,0:T(8,128)(2,1)S(1)}, bf16[16,1536]{1,0:T(8,128)(2,1)S(1)}, u32[]{:S(2)}, u32[]{:S(2)}) %collective-permute-start.6) | collective-permute-done | bytes 49184 | tf_op jit(solution)/shard_map/ppermute | solution.py:486
  22.8 1.3 %shard_map.137 = (bf16[128,1024]{1,0:T(8,128)(2,1)S(1)}, bf16[128,1536]{1,0:T(8,128)(2,1)S(1)}, bf16[128,512]{1,0:T(8,128)(2,1)S(1)}, bf16[128,512]{1,0:T(8,128)(2,1)S(1)}, bf16[128,512]{1,0:T(8,128)(2,1)S(1)}) custom-call(bf16[16,1536]{1,0:T(8,128)(2,1)S(1)} %get-tuple-element.55.refs_0_, bf16[16,1536]{1,0:T(8,128)(2,1)S(1)} %collective-permute-done.refs_1_, ...), custom_call_target="tpu_custom_call" | custom-call | flops 10000000 | bytes 10000 | tf_op jit(solution)/shard_map/pallas_call | solution.py:50
  24.1 1.6 %collective-permute-start.16 = (bf16[128,1024]{1,0:T(8,128)(2,1)S(1)}, bf16[128,1024]{1,0:T(8,128)(2,1)S(1)}, u32[]{:S(2)}, u32[]{:S(2)}) collective-permute-start(bf16[128,1024]{1,0:T(8,128)(2,1)S(1)} %get-tuple-element.65.refs_0_), channel_id=1, source_target_pairs={{0,2},{1,3},{2,0},{3,1},{4,6},{5,7},{6,4},{7,5},{8,10},{9,11},{10,... | collective-permute-start | bytes 786440 | tf_op jit(solution)/shard_map/ppermute | solution.py:486
  25.7 0.5 collective-permute-start.17
  26.2 1.4 %collective-permute-start.18 = (bf16[128,1024]{1,0:T(8,128)(2,1)S(1)}, bf16[128,1024]{1,0:T(8,128)(2,1)S(1)}, u32[]{:S(2)}, u32[]{:S(2)}) collective-permute-start(bf16[128,1024]{1,0:T(8,128)(2,1)S(1)} %get-tuple-element.65.refs_0_), channel_id=1, source_target_pairs={{0,6},{1,7},{2,4},{3,5},{4,2},{5,3},{6,0},{7,1},{8,14},{9,15},{10,... | collective-permute-start | bytes 786440 | tf_op jit(solution)/shard_map/ppermute | solution.py:486
  27.7 2.4 %shard_map.138 = (bf16[128,512]{1,0:T(8,128)(2,1)S(1)}, f32[128,512]{1,0:T(8,128)S(1)}) custom-call(bf16[128,1024]{1,0:T(8,128)(2,1)S(1)} %get-tuple-element.65.refs_0_, bf16[128,512]{1,0:T(8,128)(2,1)S(1)} %get-tuple-element.66.refs_1_, f32[1,512]{1,0:T(1,128)S(1)} %bitcast.14, bf16[512,512]{1,0:T(8,128)(2,1)S(1)} %copy-done.5, ...), custom_call_target="tpu_custom_call" | custom-call | flops 10000000 | bytes 10000 | tf_op jit(solution)/shard_map/pallas_call | solution.py:50
  30.0 2.7 %shard_map.139 = (bf16[16,1024]{1,0:T(8,128)(2,1)S(1)}, bf16[16,1024]{1,0:T(8,128)(2,1)S(1)}, bf16[16,1024]{1,0:T(8,128)(2,1)S(1)}, bf16[16,1024]{1,0:T(8,128)(2...) custom-call(bf16[128,1536]{1,0:T(8,128)(2,1)S(1)} %get-tuple-element, ...), custom_call_target="tpu_custom_call" | custom-call | flops 10000000 | bytes 10000 | tf_op jit(solution)/shard_map/pallas_call | solution.py:50
  32.7 0.2 collective-permute-start.10
  32.9 2.7 %collective-permute-start.11 = (bf16[16,1024]{1,0:T(8,128)(2,1)S(1)}, bf16[16,1024]{1,0:T(8,128)(2,1)S(1)}, u32[]{:S(2)}, u32[]{:S(2)}) collective-permute-start(bf16[16,1024]{1,0:T(8,128)(2,1)S(1)} %get-tuple-element.76), channel_id=1, source_target_pairs={{0,20},{1,21},{2,22},{3,23},{4,16},{5,17},{6,18},{7,19},{8,28},{9,... | collective-permute-start | bytes 98312 | tf_op jit(solution)/shard_map/ppermute | solution.py:486
  35.7 2.1 %collective-permute-done.10.refs_4_.refs_7_ = bf16[16,1024]{1,0:T(8,128)(2,1)S(1)} collective-permute-done((bf16[16,1024]{1,0:T(8,128)(2,1)S(1)}, bf16[16,1024]{1,0:T(8,128)(2,1)S(1)}, u32[]{:S(2)}, u32[]{:S(2)}) %collective-permute-start.10) | collective-permute-done | bytes 32800 | tf_op jit(solution)/shard_map/ppermute | solution.py:486
  37.8 1.2 %collective-permute-start.12 = (bf16[16,1024]{1,0:T(8,128)(2,1)S(1)}, bf16[16,1024]{1,0:T(8,128)(2,1)S(1)}, u32[]{:S(2)}, u32[]{:S(2)}) collective-permute-start(bf16[16,1024]{1,0:T(8,128)(2,1)S(1)} %get-tuple-element.77), channel_id=1, source_target_pairs={{0,24},{1,25},{2,26},{3,27},{4,28},{5,29},{6,30},{7,31},{8,16},{9,... | collective-permute-start | bytes 98312 | tf_op jit(solution)/shard_map/ppermute | solution.py:486
  39.0 2.6 %collective-permute-start.13 = (bf16[16,1024]{1,0:T(8,128)(2,1)S(1)}, bf16[16,1024]{1,0:T(8,128)(2,1)S(1)}, u32[]{:S(2)}, u32[]{:S(2)}) collective-permute-start(bf16[16,1024]{1,0:T(8,128)(2,1)S(1)} %get-tuple-element.78), channel_id=1, source_target_pairs={{0,28},{1,29},{2,30},{3,31},{4,24},{5,25},{6,26},{7,27},{8,20},{9,... | collective-permute-start | bytes 98312 | tf_op jit(solution)/shard_map/ppermute | solution.py:486
  41.7 2.0 %collective-permute-done.12.refs_6_.refs_9_ = bf16[16,1024]{1,0:T(8,128)(2,1)S(1)} collective-permute-done((bf16[16,1024]{1,0:T(8,128)(2,1)S(1)}, bf16[16,1024]{1,0:T(8,128)(2,1)S(1)}, u32[]{:S(2)}, u32[]{:S(2)}) %collective-permute-start.12) | collective-permute-done | bytes 32800 | tf_op jit(solution)/shard_map/ppermute | solution.py:486
  43.6 0.7 collective-permute-start.7
  44.3 1.3 %collective-permute-done.13.refs_7_.refs_10_ = bf16[16,1024]{1,0:T(8,128)(2,1)S(1)} collective-permute-done((bf16[16,1024]{1,0:T(8,128)(2,1)S(1)}, bf16[16,1024]{1,0:T(8,128)(2,1)S(1)}, u32[]{:S(2)}, u32[]{:S(2)}) %collective-permute-start.13) | collective-permute-done | bytes 32800 | tf_op jit(solution)/shard_map/ppermute | solution.py:486
  45.6 1.9 %collective-permute-done.7.refs_1_.refs_4_ = bf16[16,1024]{1,0:T(8,128)(2,1)S(1)} collective-permute-done((bf16[16,1024]{1,0:T(8,128)(2,1)S(1)}, bf16[16,1024]{1,0:T(8,128)(2,1)S(1)}, u32[]{:S(2)}, u32[]{:S(2)}) %collective-permute-start.7) | collective-permute-done | bytes 32800 | tf_op jit(solution)/shard_map/ppermute | solution.py:486
  47.5 0.9 collective-permute-start.9
  48.4 1.2 %collective-permute-done.8.refs_2_.refs_5_ = bf16[16,1024]{1,0:T(8,128)(2,1)S(1)} collective-permute-done((bf16[16,1024]{1,0:T(8,128)(2,1)S(1)}, bf16[16,1024]{1,0:T(8,128)(2,1)S(1)}, u32[]{:S(2)}, u32[]{:S(2)}) %collective-permute-start.8) | collective-permute-done | bytes 32800 | tf_op jit(solution)/shard_map/ppermute | solution.py:486
  49.5 2.8 %collective-permute-done.9.refs_3_.refs_6_ = bf16[16,1024]{1,0:T(8,128)(2,1)S(1)} collective-permute-done((bf16[16,1024]{1,0:T(8,128)(2,1)S(1)}, bf16[16,1024]{1,0:T(8,128)(2,1)S(1)}, u32[]{:S(2)}, u32[]{:S(2)}) %collective-permute-start.9) | collective-permute-done | bytes 32800 | tf_op jit(solution)/shard_map/ppermute | solution.py:486
  52.4 0.1 shard_map.141.refs_0_
  52.4 0.1 collective-permute-start.19
  52.5 0.5 collective-permute-start.14
  53.0 2.6 %shard_map.140.refs_2_.refs_8_ = bf16[128,2048]{1,0:T(8,128)(2,1)S(1)} custom-call(bf16[16,1024]{1,0:T(8,128)(2,1)S(1)} %get-tuple-element.71.refs_0_, bf16[16,1024]{1,0:T(8,128)(2,1)S(1)} %collective-permute-done.7.refs_1_.refs_4_, bf16[16,1024]{1,0:T(8,128)(2,1)S(1)} %collective-permute-done.8.refs_2_.refs_5_, ...), custom_call_target="tpu_custom_call" | custom-call | flops 10000000 | bytes 10000 | tf_op jit(solution)/shard_map/pallas_call | solution.py:50
  55.6 0.1 collective-permute-start.15
  55.8 1.7 %shard_map.142 = (bf16[1,64,1024]{2,1,0:T(8,128)(2,1)S(1)}, bf16[1,64,1024]{2,1,0:T(8,128)(2,1)S(1)}, bf16[1,64,1024]{2,1,0:T(8,128)(2,1)S(1)}, bf16[1,64,1024]{2,1,0:T(8,128)(2,1)S(1)}) custom-call(bf16[512,1024]{1,0:T(8,128)(2,1)S(1)} %shard_map.141.refs_0_, bf16[512,1024]{1,0:T(8,128)(2,1)S(1)} %collective-permute-done.19.refs_1_, ...), custom_call_target="tpu_custom_call" | custom-call | flops 10000000 | bytes 10000 | tf_op jit(solution)/shard_map/pallas_call | solution.py:50
  57.5 0.1 collective-permute-done.15.refs_3_
  57.6 1.2 %shard_map.143 = (bf16[4,256,128]{2,1,0:T(8,128)(2,1)S(1)}, bf16[4,256,128]{2,1,0:T(8,128)(2,1)S(1)}, bf16[4,256,128]{2,1,0:T(8,128)(2,1)S(1)}, bf16[4,256,128]{2,1,0:T(8,128)(2,1)S(1)}) custom-call(bf16[128,3072]{1,0:T(8,128)(2,1)S(1)} %get-tuple-element.80.refs_0_, bf16[128,3072]{1,0:T(8,128)(2,1)S(1)} %collective-permute-done.14.refs_1_, ...), custom_call_target="tpu_custom_call" | custom-call | flops 10000000 | bytes 10000 | tf_op jit(solution)/shard_map/pallas_call | solution.py:50
  58.9 0.9 collective-permute-start.20
  59.7 1.5 %collective-permute-start.21 = (bf16[4,256,128]{2,1,0:T(8,128)(2,1)S(1)}, bf16[4,256,128]{2,1,0:T(8,128)(2,1)S(1)}, u32[]{:S(2)}, u32[]{:S(2)}) collective-permute-start(bf16[4,256,128]{2,1,0:T(8,128)(2,1)S(1)} %get-tuple-element.85), channel_id=1, source_target_pairs={{0,2},{1,3},{2,0},{3,1},{4,6},{5,7},{6,4},{7,5},{8,10},{9,11},{10,... | collective-permute-start | bytes 786440 | tf_op jit(solution)/shard_map/ppermute | solution.py:486
  61.2 1.2 %collective-permute-start.22 = (bf16[4,256,128]{2,1,0:T(8,128)(2,1)S(1)}, bf16[4,256,128]{2,1,0:T(8,128)(2,1)S(1)}, u32[]{:S(2)}, u32[]{:S(2)}) collective-permute-start(bf16[4,256,128]{2,1,0:T(8,128)(2,1)S(1)} %get-tuple-element.86), channel_id=1, source_target_pairs={{0,6},{1,7},{2,4},{3,5},{4,2},{5,3},{6,0},{7,1},{8,14},{9,15},{10,... | collective-permute-start | bytes 786440 | tf_op jit(solution)/shard_map/ppermute | solution.py:486
  62.4 0.1 collective-permute-start.29
  62.6 1.7 %collective-permute-start.30 = (bf16[1,64,1024]{2,1,0:T(8,128)(2,1)S(1)}, bf16[1,64,1024]{2,1,0:T(8,128)(2,1)S(1)}, u32[]{:S(2)}, u32[]{:S(2)}) collective-permute-start(bf16[1,64,1024]{2,1,0:T(8,128)(2,1)S(1)} %get-tuple-element.92), channel_id=1, source_target_pairs={{0,16},{1,17},{2,18},{3,19},{4,20},{5,21},{6,22},{7,23},{8,24},{9,... | collective-permute-start | bytes 393224 | tf_op jit(solution)/shard_map/ppermute | solution.py:486
  64.2 3.8 %collective-permute-done.20.refs_1_ = bf16[4,256,128]{2,1,0:T(8,128)(2,1)S(1)} collective-permute-done((bf16[4,256,128]{2,1,0:T(8,128)(2,1)S(1)}, bf16[4,256,128]{2,1,0:T(8,128)(2,1)S(1)}, u32[]{:S(2)}, u32[]{:S(2)}) %collective-permute-start.20) | collective-permute-done | bytes 262176 | tf_op jit(solution)/shard_map/ppermute | solution.py:486
  68.1 1.2 %collective-permute-start.31 = (bf16[1,64,1024]{2,1,0:T(8,128)(2,1)S(1)}, bf16[1,64,1024]{2,1,0:T(8,128)(2,1)S(1)}, u32[]{:S(2)}, u32[]{:S(2)}) collective-permute-start(bf16[1,64,1024]{2,1,0:T(8,128)(2,1)S(1)} %get-tuple-element.93), channel_id=1, source_target_pairs={{0,24},{1,25},{2,26},{3,27},{4,28},{5,29},{6,30},{7,31},{8,16},{9,... | collective-permute-start | bytes 393224 | tf_op jit(solution)/shard_map/ppermute | solution.py:486
  69.3 3.4 %collective-permute-done.21.refs_2_ = bf16[4,256,128]{2,1,0:T(8,128)(2,1)S(1)} collective-permute-done((bf16[4,256,128]{2,1,0:T(8,128)(2,1)S(1)}, bf16[4,256,128]{2,1,0:T(8,128)(2,1)S(1)}, u32[]{:S(2)}, u32[]{:S(2)}) %collective-permute-start.21) | collective-permute-done | bytes 262176 | tf_op jit(solution)/shard_map/ppermute | solution.py:486
  72.7 1.4 %collective-permute-done.22.refs_3_ = bf16[4,256,128]{2,1,0:T(8,128)(2,1)S(1)} collective-permute-done((bf16[4,256,128]{2,1,0:T(8,128)(2,1)S(1)}, bf16[4,256,128]{2,1,0:T(8,128)(2,1)S(1)}, u32[]{:S(2)}, u32[]{:S(2)}) %collective-permute-start.22) | collective-permute-done | bytes 262176 | tf_op jit(solution)/shard_map/ppermute | solution.py:486
  74.1 0.1 shard_map.145
  74.2 0.7 collective-permute-done.31.refs_3_
  75.0 0.1 shard_map.147
  75.0 0.8 collective-permute-start.32
  75.9 2.7 %collective-permute-start.23 = (bf16[1,256,128]{2,1,0:T(8,128)(2,1)S(1)}, bf16[1,256,128]{2,1,0:T(8,128)(2,1)S(1)}, u32[]{:S(2)}, u32[]{:S(2)}) collective-permute-start(bf16[1,256,128]{2,1,0:T(8,128)(2,1)S(1)} %get-tuple-element.88), channel_id=1, source_target_pairs={{0,8},{1,9},{2,10},{3,11},{4,12},{5,13},{6,14},{7,15},{8,0},{9,1},... | collective-permute-start | bytes 196616 | tf_op jit(solution)/shard_map/ppermute | solution.py:486
  78.6 0.4 collective-permute-done.32.refs_1_
  79.0 0.1 collective-permute-start.33
  79.1 3.4 %collective-permute-start.24 = (bf16[1,256,128]{2,1,0:T(8,128)(2,1)S(1)}, bf16[1,256,128]{2,1,0:T(8,128)(2,1)S(1)}, u32[]{:S(2)}, u32[]{:S(2)}) collective-permute-start(bf16[1,256,128]{2,1,0:T(8,128)(2,1)S(1)} %get-tuple-element.89), channel_id=1, source_target_pairs={{0,16},{1,17},{2,18},{3,19},{4,20},{5,21},{6,22},{7,23},{8,24},{9,... | collective-permute-start | bytes 196616 | tf_op jit(solution)/shard_map/ppermute | solution.py:486
  82.5 1.4 %collective-permute-start.25 = (bf16[1,256,128]{2,1,0:T(8,128)(2,1)S(1)}, bf16[1,256,128]{2,1,0:T(8,128)(2,1)S(1)}, u32[]{:S(2)}, u32[]{:S(2)}) collective-permute-start(bf16[1,256,128]{2,1,0:T(8,128)(2,1)S(1)} %get-tuple-element.90), channel_id=1, source_target_pairs={{0,24},{1,25},{2,26},{3,27},{4,28},{5,29},{6,30},{7,31},{8,16},{9,... | collective-permute-start | bytes 196616 | tf_op jit(solution)/shard_map/ppermute | solution.py:486
  83.9 1.5 %collective-permute-start.34 = (bf16[64,1024]{1,0:T(8,128)(2,1)S(1)}, bf16[64,1024]{1,0:T(8,128)(2,1)S(1)}, u32[]{:S(2)}, u32[]{:S(2)}) collective-permute-start(bf16[64,1024]{1,0:T(8,128)(2,1)S(1)} %shard_map.148.refs_0_), channel_id=1, source_target_pairs={{0,2},{1,3},{2,0},{3,1},{4,6},{5,7},{6,4},{7,5},{8,10},{9,11},{10,... | collective-permute-start | bytes 393224 | tf_op jit(solution)/shard_map/ppermute | solution.py:486
  85.4 1.4 %collective-permute-done.24.refs_2_ = bf16[1,256,128]{2,1,0:T(8,128)(2,1)S(1)} collective-permute-done((bf16[1,256,128]{2,1,0:T(8,128)(2,1)S(1)}, bf16[1,256,128]{2,1,0:T(8,128)(2,1)S(1)}, u32[]{:S(2)}, u32[]{:S(2)}) %collective-permute-start.24) | collective-permute-done | bytes 65568 | tf_op jit(solution)/shard_map/ppermute | solution.py:486
  86.8 1.8 %collective-permute-done.25.refs_3_ = bf16[1,256,128]{2,1,0:T(8,128)(2,1)S(1)} collective-permute-done((bf16[1,256,128]{2,1,0:T(8,128)(2,1)S(1)}, bf16[1,256,128]{2,1,0:T(8,128)(2,1)S(1)}, u32[]{:S(2)}, u32[]{:S(2)}) %collective-permute-start.25) | collective-permute-done | bytes 65568 | tf_op jit(solution)/shard_map/ppermute | solution.py:486
  88.6 0.1 collective-permute-start.26
  88.7 1.6 %collective-permute-start.27 = (bf16[1,256,128]{2,1,0:T(8,128)(2,1)S(1)}, bf16[1,256,128]{2,1,0:T(8,128)(2,1)S(1)}, u32[]{:S(2)}, u32[]{:S(2)}) collective-permute-start(bf16[1,256,128]{2,1,0:T(8,128)(2,1)S(1)} %shard_map.146.refs_0_), channel_id=1, source_target_pairs={{0,2},{1,3},{2,0},{3,1},{4,6},{5,7},{6,4},{7,5},{8,10},{9,11},{10,... | collective-permute-start | bytes 196616 | tf_op jit(solution)/shard_map/ppermute | solution.py:486
  90.3 0.3 collective-permute-start.28
  90.6 1.6 %shard_map.144 = bf16[128,512]{1,0:T(8,128)(2,1)} custom-call(bf16[16,1024]{1,0:T(8,128)(2,1)S(1)} %get-tuple-element.71.refs_0_, bf16[16,1024]{1,0:T(8,128)(2,1)S(1)} %collective-permute-done.7.refs_1_.refs_4_, bf16[16,1024]{1,0:T(8,128)(2,1)S(1)} %collective-permute-done.8.refs_2_.refs_5_, bf16[16,1024]{1,0:T(8,128)(2,1)S(1)} %collective-permute-done.9.refs_3_.refs_6_, ...), custom_call_target="tpu_custom_call" | custom-call | flops 10000000 | bytes 10000 | tf_op jit(solution)/shard_map/pallas_call | solution.py:50
  92.1 2.1 %shard_map.149 = (f32[64,2048]{1,0:T(8,128)}, f32[256,512]{1,0:T(8,128)}, f32[1,64]{1,0:T(1,128)}, bf16[64,1536]{1,0:T(8,128)(2,1)S(1)}) custom-call(bf16[64,1024]{1,0:T(8,128)(2,1)S(1)} %shard_map.148.refs_0_, bf16[64,1024]{1,0:T(8,128)(2,1)S(1)} %collective-permute-done.33.refs_1_, bf16[64,1024]{1,0:T(8,128)(2,1)S(1)} %collective-permute-done.34.refs_2_, ...), custom_call_target="tpu_custom_call" | custom-call | flops 10000000 | bytes 10000 | tf_op jit(solution)/shard_map/pallas_call | solution.py:50
  94.2 0.3 collective-permute-done.28.refs_3_
  94.5 0.8 shard_map.150
  (40 shorter events, 0.2 us)
Async XLA Ops:
  3.5 8.9 %collective-permute-start = (bf16[16,1536]{1,0:T(8,128)(2,1)S(1)}, bf16[16,1536]{1,0:T(8,128)(2,1)S(1)}, u32[]{:S(2)}, u32[]{:S(2)}) collective-permute-start(bf16[16,1536]{1,0:T(8,128)(2,1)S(1)} %get-tuple-element.56), channel_id=1, source_target_pairs={{0,4},{1,5},{2,6},{3,7},{4,0},{5,1},{6,2},{7,3},{8,12},{9,13},{10,... | collective-permute-start | bytes 147464 | tf_op jit(solution)/shard_map/ppermute | solution.py:486
  6.5 9.5 %collective-permute-start.1 = (bf16[16,1536]{1,0:T(8,128)(2,1)S(1)}, bf16[16,1536]{1,0:T(8,128)(2,1)S(1)}, u32[]{:S(2)}, u32[]{:S(2)}) collective-permute-start(bf16[16,1536]{1,0:T(8,128)(2,1)S(1)} %get-tuple-element.57), channel_id=1, source_target_pairs={{0,8},{1,9},{2,10},{3,11},{4,12},{5,13},{6,14},{7,15},{8,0},{9,1},... | collective-permute-start | bytes 147464 | tf_op jit(solution)/shard_map/ppermute | solution.py:486
  8.1 12.0 %collective-permute-start.2 = (bf16[16,1536]{1,0:T(8,128)(2,1)S(1)}, bf16[16,1536]{1,0:T(8,128)(2,1)S(1)}, u32[]{:S(2)}, u32[]{:S(2)}) collective-permute-start(bf16[16,1536]{1,0:T(8,128)(2,1)S(1)} %get-tuple-element.58), channel_id=1, source_target_pairs={{0,12},{1,13},{2,14},{3,15},{4,8},{5,9},{6,10},{7,11},{8,4},{9,5},... | collective-permute-start | bytes 147464 | tf_op jit(solution)/shard_map/ppermute | solution.py:486
  8.1 12.0 %collective-permute-start.3 = (bf16[16,1536]{1,0:T(8,128)(2,1)S(1)}, bf16[16,1536]{1,0:T(8,128)(2,1)S(1)}, u32[]{:S(2)}, u32[]{:S(2)}) collective-permute-start(bf16[16,1536]{1,0:T(8,128)(2,1)S(1)} %get-tuple-element.59), channel_id=1, source_target_pairs={{0,16},{1,17},{2,18},{3,19},{4,20},{5,21},{6,22},{7,23},{8,24},{9,... | collective-permute-start | bytes 147464 | tf_op jit(solution)/shard_map/ppermute | solution.py:486
  11.1 9.0 %collective-permute-start.4 = (bf16[16,1536]{1,0:T(8,128)(2,1)S(1)}, bf16[16,1536]{1,0:T(8,128)(2,1)S(1)}, u32[]{:S(2)}, u32[]{:S(2)}) collective-permute-start(bf16[16,1536]{1,0:T(8,128)(2,1)S(1)} %get-tuple-element.60), channel_id=1, source_target_pairs={{0,20},{1,21},{2,22},{3,23},{4,16},{5,17},{6,18},{7,19},{8,28},{9,... | collective-permute-start | bytes 147464 | tf_op jit(solution)/shard_map/ppermute | solution.py:486
  12.4 7.8 %collective-permute-start.5 = (bf16[16,1536]{1,0:T(8,128)(2,1)S(1)}, bf16[16,1536]{1,0:T(8,128)(2,1)S(1)}, u32[]{:S(2)}, u32[]{:S(2)}) collective-permute-start(bf16[16,1536]{1,0:T(8,128)(2,1)S(1)} %get-tuple-element.61), channel_id=1, source_target_pairs={{0,24},{1,25},{2,26},{3,27},{4,28},{5,29},{6,30},{7,31},{8,16},{9,... | collective-permute-start | bytes 147464 | tf_op jit(solution)/shard_map/ppermute | solution.py:486
  16.0 6.8 %copy-start = (bf16[512,1536]{1,0:T(8,128)(2,1)S(1)}, bf16[512,1536]{1,0:T(8,128)(2,1)}, u32[]{:S(2)}) copy-start(bf16[512,1536]{1,0:T(8,128)(2,1)} %refs_6_.3) | copy-start | bytes 4718596
  16.0 6.8 %collective-permute-start.6 = (bf16[16,1536]{1,0:T(8,128)(2,1)S(1)}, bf16[16,1536]{1,0:T(8,128)(2,1)S(1)}, u32[]{:S(2)}, u32[]{:S(2)}) collective-permute-start(bf16[16,1536]{1,0:T(8,128)(2,1)S(1)} %get-tuple-element.62), channel_id=1, source_target_pairs={{0,28},{1,29},{2,30},{3,31},{4,24},{5,25},{6,26},{7,27},{8,20},{9,... | collective-permute-start | bytes 147464 | tf_op jit(solution)/shard_map/ppermute | solution.py:486
  16.1 1.7 %copy-start.1 = (bf16[512,2048]{1,0:T(8,128)(2,1)S(1)}, bf16[512,2048]{1,0:T(8,128)(2,1)}, u32[]{:S(2)}) copy-start(bf16[512,2048]{1,0:T(8,128)(2,1)} %refs_5_.3) | copy-start | bytes 6291460
  17.8 1.6 %copy-start.3 = (bf16[2048,512]{1,0:T(8,128)(2,1)S(1)}, bf16[2048,512]{1,0:T(8,128)(2,1)}, u32[]{:S(2)}) copy-start(bf16[2048,512]{1,0:T(8,128)(2,1)} %refs_5_.2) | copy-start | bytes 6291460
  19.4 3.5 %copy-start.5 = (bf16[512,512]{1,0:T(8,128)(2,1)S(1)}, bf16[512,512]{1,0:T(8,128)(2,1)}, u32[]{:S(2)}) copy-start(bf16[512,512]{1,0:T(8,128)(2,1)} %refs_3_.3) | copy-start | bytes 1572868
  19.4 3.5 %copy-start.6 = (f32[512]{0:T(512)S(1)}, f32[512]{0:T(512)}, u32[]{:S(2)}) copy-start(f32[512]{0:T(512)} %param.14) | copy-start | bytes 6148
  19.4 3.5 %copy-start.7 = (f32[512]{0:T(512)S(1)}, f32[512]{0:T(512)}, u32[]{:S(2)}) copy-start(f32[512]{0:T(512)} %param.15) | copy-start | bytes 6148
  19.4 8.3 %copy-start.4 = (bf16[2048,512]{1,0:T(8,128)(2,1)S(1)}, bf16[2048,512]{1,0:T(8,128)(2,1)}, u32[]{:S(2)}) copy-start(bf16[2048,512]{1,0:T(8,128)(2,1)} %refs_5_.2) | copy-start | bytes 6291460
  20.1 7.6 %copy-start.2 = (bf16[512,2048]{1,0:T(8,128)(2,1)S(1)}, bf16[512,2048]{1,0:T(8,128)(2,1)}, u32[]{:S(2)}) copy-start(bf16[512,2048]{1,0:T(8,128)(2,1)} %refs_5_.3) | copy-start | bytes 6291460
  24.1 28.2 %collective-permute-start.16 = (bf16[128,1024]{1,0:T(8,128)(2,1)S(1)}, bf16[128,1024]{1,0:T(8,128)(2,1)S(1)}, u32[]{:S(2)}, u32[]{:S(2)}) collective-permute-start(bf16[128,1024]{1,0:T(8,128)(2,1)S(1)} %get-tuple-element.65.refs_0_), channel_id=1, source_target_pairs={{0,2},{1,3},{2,0},{3,1},{4,6},{5,7},{6,4},{7,5},{8,10},{9,11},{10,... | collective-permute-start | bytes 786440 | tf_op jit(solution)/shard_map/ppermute | solution.py:486
  25.7 26.7 %collective-permute-start.17 = (bf16[128,1024]{1,0:T(8,128)(2,1)S(1)}, bf16[128,1024]{1,0:T(8,128)(2,1)S(1)}, u32[]{:S(2)}, u32[]{:S(2)}) collective-permute-start(bf16[128,1024]{1,0:T(8,128)(2,1)S(1)} %get-tuple-element.65.refs_0_), channel_id=1, source_target_pairs={{0,4},{1,5},{2,6},{3,7},{4,0},{5,1},{6,2},{7,3},{8,12},{9,13},{10,... | collective-permute-start | bytes 786440 | tf_op jit(solution)/shard_map/ppermute | solution.py:486
  26.2 26.1 %collective-permute-start.18 = (bf16[128,1024]{1,0:T(8,128)(2,1)S(1)}, bf16[128,1024]{1,0:T(8,128)(2,1)S(1)}, u32[]{:S(2)}, u32[]{:S(2)}) collective-permute-start(bf16[128,1024]{1,0:T(8,128)(2,1)S(1)} %get-tuple-element.65.refs_0_), channel_id=1, source_target_pairs={{0,6},{1,7},{2,4},{3,5},{4,2},{5,3},{6,0},{7,1},{8,14},{9,15},{10,... | collective-permute-start | bytes 786440 | tf_op jit(solution)/shard_map/ppermute | solution.py:486
  32.7 5.1 %collective-permute-start.10 = (bf16[16,1024]{1,0:T(8,128)(2,1)S(1)}, bf16[16,1024]{1,0:T(8,128)(2,1)S(1)}, u32[]{:S(2)}, u32[]{:S(2)}) collective-permute-start(bf16[16,1024]{1,0:T(8,128)(2,1)S(1)} %get-tuple-element.75), channel_id=1, source_target_pairs={{0,16},{1,17},{2,18},{3,19},{4,20},{5,21},{6,22},{7,23},{8,24},{9,... | collective-permute-start | bytes 98312 | tf_op jit(solution)/shard_map/ppermute | solution.py:486
  32.9 6.1 %collective-permute-start.11 = (bf16[16,1024]{1,0:T(8,128)(2,1)S(1)}, bf16[16,1024]{1,0:T(8,128)(2,1)S(1)}, u32[]{:S(2)}, u32[]{:S(2)}) collective-permute-start(bf16[16,1024]{1,0:T(8,128)(2,1)S(1)} %get-tuple-element.76), channel_id=1, source_target_pairs={{0,20},{1,21},{2,22},{3,23},{4,16},{5,17},{6,18},{7,19},{8,28},{9,... | collective-permute-start | bytes 98312 | tf_op jit(solution)/shard_map/ppermute | solution.py:486
  37.8 5.8 %collective-permute-start.12 = (bf16[16,1024]{1,0:T(8,128)(2,1)S(1)}, bf16[16,1024]{1,0:T(8,128)(2,1)S(1)}, u32[]{:S(2)}, u32[]{:S(2)}) collective-permute-start(bf16[16,1024]{1,0:T(8,128)(2,1)S(1)} %get-tuple-element.77), channel_id=1, source_target_pairs={{0,24},{1,25},{2,26},{3,27},{4,28},{5,29},{6,30},{7,31},{8,16},{9,... | collective-permute-start | bytes 98312 | tf_op jit(solution)/shard_map/ppermute | solution.py:486
  39.0 6.6 %collective-permute-start.13 = (bf16[16,1024]{1,0:T(8,128)(2,1)S(1)}, bf16[16,1024]{1,0:T(8,128)(2,1)S(1)}, u32[]{:S(2)}, u32[]{:S(2)}) collective-permute-start(bf16[16,1024]{1,0:T(8,128)(2,1)S(1)} %get-tuple-element.78), channel_id=1, source_target_pairs={{0,28},{1,29},{2,30},{3,31},{4,24},{5,25},{6,26},{7,27},{8,20},{9,... | collective-permute-start | bytes 98312 | tf_op jit(solution)/shard_map/ppermute | solution.py:486
  43.6 3.9 %collective-permute-start.7 = (bf16[16,1024]{1,0:T(8,128)(2,1)S(1)}, bf16[16,1024]{1,0:T(8,128)(2,1)S(1)}, u32[]{:S(2)}, u32[]{:S(2)}) collective-permute-start(bf16[16,1024]{1,0:T(8,128)(2,1)S(1)} %get-tuple-element.72), channel_id=1, source_target_pairs={{0,4},{1,5},{2,6},{3,7},{4,0},{5,1},{6,2},{7,3},{8,12},{9,13},{10,... | collective-permute-start | bytes 98312 | tf_op jit(solution)/shard_map/ppermute | solution.py:486
  45.6 3.9 %collective-permute-start.8 = (bf16[16,1024]{1,0:T(8,128)(2,1)S(1)}, bf16[16,1024]{1,0:T(8,128)(2,1)S(1)}, u32[]{:S(2)}, u32[]{:S(2)}) collective-permute-start(bf16[16,1024]{1,0:T(8,128)(2,1)S(1)} %get-tuple-element.73), channel_id=1, source_target_pairs={{0,8},{1,9},{2,10},{3,11},{4,12},{5,13},{6,14},{7,15},{8,0},{9,1},... | collective-permute-start | bytes 98312 | tf_op jit(solution)/shard_map/ppermute | solution.py:486
  47.5 4.8 %collective-permute-start.9 = (bf16[16,1024]{1,0:T(8,128)(2,1)S(1)}, bf16[16,1024]{1,0:T(8,128)(2,1)S(1)}, u32[]{:S(2)}, u32[]{:S(2)}) collective-permute-start(bf16[16,1024]{1,0:T(8,128)(2,1)S(1)} %get-tuple-element.74), channel_id=1, source_target_pairs={{0,12},{1,13},{2,14},{3,15},{4,8},{5,9},{6,10},{7,11},{8,4},{9,5},... | collective-permute-start | bytes 98312 | tf_op jit(solution)/shard_map/ppermute | solution.py:486
  52.4 3.4 %collective-permute-start.19 = (bf16[512,1024]{1,0:T(8,128)(2,1)S(1)}, bf16[512,1024]{1,0:T(8,128)(2,1)S(1)}, u32[]{:S(2)}, u32[]{:S(2)}) collective-permute-start(bf16[512,1024]{1,0:T(8,128)(2,1)S(1)} %shard_map.141.refs_0_), channel_id=1, source_target_pairs={{0,1},{1,0},{2,3},{3,2},{4,5},{5,4},{6,7},{7,6},{8,9},{9,8},{10,11... | collective-permute-start | bytes 3145736 | tf_op jit(solution)/shard_map/ppermute | solution.py:486
  52.5 5.1 %collective-permute-start.14 = (bf16[128,3072]{1,0:T(8,128)(2,1)S(1)}, bf16[128,3072]{1,0:T(8,128)(2,1)S(1)}, u32[]{:S(2)}, u32[]{:S(2)}) collective-permute-start(bf16[128,3072]{1,0:T(8,128)(2,1)S(1)} %get-tuple-element.80.refs_0_), channel_id=1, source_target_pairs={{0,1},{1,0},{2,3},{3,2},{4,5},{5,4},{6,7},{7,6},{8,9},{9,8},{10,11... | collective-permute-start | bytes 2359304 | tf_op jit(solution)/shard_map/ppermute | solution.py:486
  55.6 2.0 %collective-permute-start.15 = (bf16[128,2048]{1,0:T(8,128)(2,1)S(1)}, bf16[128,2048]{1,0:T(8,128)(2,1)S(1)}, u32[]{:S(2)}, u32[]{:S(2)}) collective-permute-start(bf16[128,2048]{1,0:T(8,128)(2,1)S(1)} %shard_map.140.refs_2_.refs_8_), channel_id=1, source_target_pairs={{0,1},{1,0},{2,3},{3,2},{4,5},{5,4},{6,7},{7,6},{8,9},{9,8},{10,11... | collective-permute-start | bytes 1572872 | tf_op jit(solution)/shard_map/ppermute | solution.py:486
  58.9 9.2 %collective-permute-start.20 = (bf16[4,256,128]{2,1,0:T(8,128)(2,1)S(1)}, bf16[4,256,128]{2,1,0:T(8,128)(2,1)S(1)}, u32[]{:S(2)}, u32[]{:S(2)}) collective-permute-start(bf16[4,256,128]{2,1,0:T(8,128)(2,1)S(1)} %get-tuple-element.84), channel_id=1, source_target_pairs={{0,4},{1,5},{2,6},{3,7},{4,0},{5,1},{6,2},{7,3},{8,12},{9,13},{10,... | collective-permute-start | bytes 786440 | tf_op jit(solution)/shard_map/ppermute | solution.py:486
  59.7 12.9 %collective-permute-start.21 = (bf16[4,256,128]{2,1,0:T(8,128)(2,1)S(1)}, bf16[4,256,128]{2,1,0:T(8,128)(2,1)S(1)}, u32[]{:S(2)}, u32[]{:S(2)}) collective-permute-start(bf16[4,256,128]{2,1,0:T(8,128)(2,1)S(1)} %get-tuple-element.85), channel_id=1, source_target_pairs={{0,2},{1,3},{2,0},{3,1},{4,6},{5,7},{6,4},{7,5},{8,10},{9,11},{10,... | collective-permute-start | bytes 786440 | tf_op jit(solution)/shard_map/ppermute | solution.py:486
  61.2 12.8 %collective-permute-start.22 = (bf16[4,256,128]{2,1,0:T(8,128)(2,1)S(1)}, bf16[4,256,128]{2,1,0:T(8,128)(2,1)S(1)}, u32[]{:S(2)}, u32[]{:S(2)}) collective-permute-start(bf16[4,256,128]{2,1,0:T(8,128)(2,1)S(1)} %get-tuple-element.86), channel_id=1, source_target_pairs={{0,6},{1,7},{2,4},{3,5},{4,2},{5,3},{6,0},{7,1},{8,14},{9,15},{10,... | collective-permute-start | bytes 786440 | tf_op jit(solution)/shard_map/ppermute | solution.py:486
  62.4 11.8 %collective-permute-start.29 = (bf16[1,64,1024]{2,1,0:T(8,128)(2,1)S(1)}, bf16[1,64,1024]{2,1,0:T(8,128)(2,1)S(1)}, u32[]{:S(2)}, u32[]{:S(2)}) collective-permute-start(bf16[1,64,1024]{2,1,0:T(8,128)(2,1)S(1)} %get-tuple-element.91), channel_id=1, source_target_pairs={{0,8},{1,9},{2,10},{3,11},{4,12},{5,13},{6,14},{7,15},{8,0},{9,1},... | collective-permute-start | bytes 393224 | tf_op jit(solution)/shard_map/ppermute | solution.py:486
  62.6 11.7 %collective-permute-start.30 = (bf16[1,64,1024]{2,1,0:T(8,128)(2,1)S(1)}, bf16[1,64,1024]{2,1,0:T(8,128)(2,1)S(1)}, u32[]{:S(2)}, u32[]{:S(2)}) collective-permute-start(bf16[1,64,1024]{2,1,0:T(8,128)(2,1)S(1)} %get-tuple-element.92), channel_id=1, source_target_pairs={{0,16},{1,17},{2,18},{3,19},{4,20},{5,21},{6,22},{7,23},{8,24},{9,... | collective-permute-start | bytes 393224 | tf_op jit(solution)/shard_map/ppermute | solution.py:486
  68.1 6.9 %collective-permute-start.31 = (bf16[1,64,1024]{2,1,0:T(8,128)(2,1)S(1)}, bf16[1,64,1024]{2,1,0:T(8,128)(2,1)S(1)}, u32[]{:S(2)}, u32[]{:S(2)}) collective-permute-start(bf16[1,64,1024]{2,1,0:T(8,128)(2,1)S(1)} %get-tuple-element.93), channel_id=1, source_target_pairs={{0,24},{1,25},{2,26},{3,27},{4,28},{5,29},{6,30},{7,31},{8,16},{9,... | collective-permute-start | bytes 393224 | tf_op jit(solution)/shard_map/ppermute | solution.py:486
  75.0 4.0 %collective-permute-start.32 = (bf16[64,256]{1,0:T(8,128)(2,1)S(1)}, bf16[64,256]{1,0:T(8,128)(2,1)S(1)}, u32[]{:S(2)}, u32[]{:S(2)}) collective-permute-start(bf16[64,256]{1,0:T(8,128)(2,1)S(1)} %get-tuple-element.95), channel_id=1, source_target_pairs={{0,4},{1,5},{2,6},{3,7},{4,0},{5,1},{6,2},{7,3},{8,12},{9,13},{10,... | collective-permute-start | bytes 98312 | tf_op jit(solution)/shard_map/ppermute | solution.py:486
  75.9 9.5 %collective-permute-start.23 = (bf16[1,256,128]{2,1,0:T(8,128)(2,1)S(1)}, bf16[1,256,128]{2,1,0:T(8,128)(2,1)S(1)}, u32[]{:S(2)}, u32[]{:S(2)}) collective-permute-start(bf16[1,256,128]{2,1,0:T(8,128)(2,1)S(1)} %get-tuple-element.88), channel_id=1, source_target_pairs={{0,8},{1,9},{2,10},{3,11},{4,12},{5,13},{6,14},{7,15},{8,0},{9,1},... | collective-permute-start | bytes 196616 | tf_op jit(solution)/shard_map/ppermute | solution.py:486
  79.0 11.3 %collective-permute-start.33 = (bf16[64,1024]{1,0:T(8,128)(2,1)S(1)}, bf16[64,1024]{1,0:T(8,128)(2,1)S(1)}, u32[]{:S(2)}, u32[]{:S(2)}) collective-permute-start(bf16[64,1024]{1,0:T(8,128)(2,1)S(1)} %shard_map.148.refs_0_), channel_id=1, source_target_pairs={{0,1},{1,0},{2,3},{3,2},{4,5},{5,4},{6,7},{7,6},{8,9},{9,8},{10,11... | collective-permute-start | bytes 393224 | tf_op jit(solution)/shard_map/ppermute | solution.py:486
  79.1 7.7 %collective-permute-start.24 = (bf16[1,256,128]{2,1,0:T(8,128)(2,1)S(1)}, bf16[1,256,128]{2,1,0:T(8,128)(2,1)S(1)}, u32[]{:S(2)}, u32[]{:S(2)}) collective-permute-start(bf16[1,256,128]{2,1,0:T(8,128)(2,1)S(1)} %get-tuple-element.89), channel_id=1, source_target_pairs={{0,16},{1,17},{2,18},{3,19},{4,20},{5,21},{6,22},{7,23},{8,24},{9,... | collective-permute-start | bytes 196616 | tf_op jit(solution)/shard_map/ppermute | solution.py:486
  82.5 6.1 %collective-permute-start.25 = (bf16[1,256,128]{2,1,0:T(8,128)(2,1)S(1)}, bf16[1,256,128]{2,1,0:T(8,128)(2,1)S(1)}, u32[]{:S(2)}, u32[]{:S(2)}) collective-permute-start(bf16[1,256,128]{2,1,0:T(8,128)(2,1)S(1)} %get-tuple-element.90), channel_id=1, source_target_pairs={{0,24},{1,25},{2,26},{3,27},{4,28},{5,29},{6,30},{7,31},{8,16},{9,... | collective-permute-start | bytes 196616 | tf_op jit(solution)/shard_map/ppermute | solution.py:486
  83.9 8.3 %collective-permute-start.34 = (bf16[64,1024]{1,0:T(8,128)(2,1)S(1)}, bf16[64,1024]{1,0:T(8,128)(2,1)S(1)}, u32[]{:S(2)}, u32[]{:S(2)}) collective-permute-start(bf16[64,1024]{1,0:T(8,128)(2,1)S(1)} %shard_map.148.refs_0_), channel_id=1, source_target_pairs={{0,2},{1,3},{2,0},{3,1},{4,6},{5,7},{6,4},{7,5},{8,10},{9,11},{10,... | collective-permute-start | bytes 393224 | tf_op jit(solution)/shard_map/ppermute | solution.py:486
  85.4 6.8 %collective-permute-start.35 = (bf16[64,1024]{1,0:T(8,128)(2,1)S(1)}, bf16[64,1024]{1,0:T(8,128)(2,1)S(1)}, u32[]{:S(2)}, u32[]{:S(2)}) collective-permute-start(bf16[64,1024]{1,0:T(8,128)(2,1)S(1)} %shard_map.148.refs_0_), channel_id=1, source_target_pairs={{0,3},{1,2},{2,1},{3,0},{4,7},{5,6},{6,5},{7,4},{8,11},{9,10},{10,... | collective-permute-start | bytes 393224 | tf_op jit(solution)/shard_map/ppermute | solution.py:486
  88.6 5.6 %collective-permute-start.26 = (bf16[1,256,128]{2,1,0:T(8,128)(2,1)S(1)}, bf16[1,256,128]{2,1,0:T(8,128)(2,1)S(1)}, u32[]{:S(2)}, u32[]{:S(2)}) collective-permute-start(bf16[1,256,128]{2,1,0:T(8,128)(2,1)S(1)} %shard_map.146.refs_0_), channel_id=1, source_target_pairs={{0,1},{1,0},{2,3},{3,2},{4,5},{5,4},{6,7},{7,6},{8,9},{9,8},{10,11... | collective-permute-start | bytes 196616 | tf_op jit(solution)/shard_map/ppermute | solution.py:486
  88.7 5.5 %collective-permute-start.27 = (bf16[1,256,128]{2,1,0:T(8,128)(2,1)S(1)}, bf16[1,256,128]{2,1,0:T(8,128)(2,1)S(1)}, u32[]{:S(2)}, u32[]{:S(2)}) collective-permute-start(bf16[1,256,128]{2,1,0:T(8,128)(2,1)S(1)} %shard_map.146.refs_0_), channel_id=1, source_target_pairs={{0,2},{1,3},{2,0},{3,1},{4,6},{5,7},{6,4},{7,5},{8,10},{9,11},{10,... | collective-permute-start | bytes 196616 | tf_op jit(solution)/shard_map/ppermute | solution.py:486
  90.3 4.2 %collective-permute-start.28 = (bf16[1,256,128]{2,1,0:T(8,128)(2,1)S(1)}, bf16[1,256,128]{2,1,0:T(8,128)(2,1)S(1)}, u32[]{:S(2)}, u32[]{:S(2)}) collective-permute-start(bf16[1,256,128]{2,1,0:T(8,128)(2,1)S(1)} %shard_map.146.refs_0_), channel_id=1, source_target_pairs={{0,3},{1,2},{2,1},{3,0},{4,7},{5,6},{6,5},{7,4},{8,11},{9,10},{10,... | collective-permute-start | bytes 196616 | tf_op jit(solution)/shard_map/ppermute | solution.py:486

commit v2 on v1

--- a/solution.py
+++ b/solution.py
@@ -15,7 +15,7 @@
 F32 = jnp.float32
 BF16 = jnp.bfloat16
 BOTH = ("slab", "case")
-VMEM_BYTES = 24 * 1024 * 1024
+VMEM_BYTES = 16 * 1024 * 1024
 
 
 def dot(a, b):
@@ -200,21 +200,21 @@
 
 
 def prepare_kernel(slabs, w_up_ref, w_down_ref, up_ref, down_ref):
-    x = lax.axis_index("slab") & 1
     quarter = lax.axis_index("case")
     units = w_up_ref.shape[1]
     fine = units // slabs // 4
-    rows = lax.broadcasted_iota(jnp.int32, (8 * LANES, LANES), 0)
-    cols = lax.broadcasted_iota(jnp.int32, (8 * LANES, LANES), 1)
-    wanted = ((cols // fine * 2 + x) * 4 + quarter) * fine + (cols & (fine - 1))
+    pack = LANES // fine
+    rows = lax.broadcasted_iota(jnp.int32, (4 * LANES, LANES), 0)
+    cols = lax.broadcasted_iota(jnp.int32, (4 * LANES, LANES), 1)
+    wanted = (cols // fine) * (4 * fine) + quarter * fine + (cols & (fine - 1))
     pick = (rows == wanted).astype(F32).astype(BF16)
-    for group in range(up_ref.shape[1] // LANES):
+    for group in range(slabs // pack):
         up_ref[:, group * LANES : (group + 1) * LANES] = dot(
-            w_up_ref[:, group * 8 * LANES : (group + 1) * 8 * LANES], pick
+            w_up_ref[:, group * 4 * LANES : (group + 1) * 4 * LANES], pick
         ).astype(BF16)
-    for z in range(slabs // 2):
-        start = pl.multiple_of(((z * 2 + x) * 4 + quarter) * fine, 8)
-        down_ref[z * fine : (z + 1) * fine, :] = w_down_ref[pl.ds(start, fine), :]
+    for block in range(slabs):
+        start = pl.multiple_of((block * 4 + quarter) * fine, 8)
+        down_ref[block * fine : (block + 1) * fine, :] = w_down_ref[pl.ds(start, fine), :]
 
 
 def lines_kernel(sizes, parts, *refs):
@@ -263,10 +263,10 @@
     grad_ref[...] = dot_nt(grad_residual.astype(BF16), w_out_ref[...]).astype(BF16)
 
 
-def lines_back_kernel(sizes, proj_ref, grad_ref, gres_ref, mixed_ref, x_ref, gain_ref, w_ref, *refs):
-    backs, pack_ref = refs[:-1], refs[-1]
+def lines_back_kernel(
+    sizes, parts, proj_ref, grad_ref, gres_ref, mixed_ref, x_ref, gain_ref, w_ref, back_ref, pack_ref
+):
     width = w_ref.shape[0]
-    put_parts(backs, 0, grad_ref[...])
     pack_ref[:, 4 * width : 5 * width] = mixed_ref[...]
     pack_ref[:, 5 * width :] = gres_ref[...].astype(BF16)
     attend_back(proj_ref[...], grad_ref[...], line_masks(sizes, "z"), width, pack_ref, width)
@@ -274,35 +274,50 @@
     pack_ref[:, :width] = (normed * gain_ref[...]).astype(BF16)
     grad_hidden = dot_nt(pack_ref[:, width : 4 * width], w_ref[...])
     back = norm_back(grad_hidden * gain_ref[...], normed, inverse)
-    put_parts(backs, width, (gres_ref[...] + back).astype(BF16))
-
-
-def join_kernel(*refs):
-    put = refs[-1]
-    rows = refs[0].shape[0]
-    for j, ref in enumerate(refs[:-1]):
-        put[j * rows : (j + 1) * rows, :] = ref[...]
+    part = (gres_ref[...] + back).astype(BF16)
+    for j, (spot, size) in enumerate(blocks_of(part.shape[0], parts)):
+        back_ref[pl.ds(spot, size), :width] = grad_ref[j * size : (j + 1) * size, :]
+        back_ref[pl.ds(spot, size), width:] = part[j * size : (j + 1) * size]
+
+
+def blocks_of(count, parts):
+    size = count // parts
+    if parts == 1:
+        return [(0, size)]
+    me = lax.axis_index("slab")
+    return [(pl.multiple_of((me ^ j) * size, 16), size) for j in range(parts)]
+
+
+def partner_order(ref, parts, start, stop):
+    return jnp.concatenate(
+        [ref[pl.ds(spot, size), start:stop] for spot, size in blocks_of(ref.shape[0], parts)], axis=0
+    )
+
+
+def join_kernel(a_ref, b_ref, back_ref, out_ref, passed_ref):
+    rows = a_ref.shape[0]
+    out_ref[:rows, :] = a_ref[...]
+    out_ref[rows:, :] = b_ref[...]
+    passed_ref[...] = back_ref[...]
 
 
 def plane_grads_kernel(sizes, parts, *refs):
-    backs = refs[:parts]
-    x_ref, gain_ref, w_ref, pack_ref, proj = refs[parts:]
+    back_ref, x_ref, gain_ref, w_ref, pack_ref, proj = refs
     width = w_ref.shape[0]
     normed, _ = norm_stats(x_ref[...].astype(F32))
     pack_ref[:, :width] = (normed * gain_ref[...]).astype(BF16)
     proj[...] = dot(pack_ref[:, :width], w_ref[...]).astype(BF16)
-    grad = joined(backs, 0, width)
+    grad = partner_order(back_ref, parts, 0, width)
     attend_back(proj[...], grad, line_masks(sizes, "xy"), width, pack_ref, width)
 
 
 def plane_tokens_kernel(sizes, parts, *refs):
-    backs = refs[:parts]
-    pack_ref, x_ref, gain_ref, w_ref, grad_ref = refs[parts:]
+    back_ref, pack_ref, x_ref, gain_ref, w_ref, grad_ref = refs
     width = w_ref.shape[0]
     normed, inverse = norm_stats(x_ref[...].astype(F32))
     grad_hidden = dot_nt(pack_ref[:, width:], w_ref[...])
     back = norm_back(grad_hidden * gain_ref[...], normed, inverse)
-    part = joined(backs, width, 2 * width).astype(F32)
+    part = partner_order(back_ref, parts, width, 2 * width).astype(F32)
     order = chunk_order(sizes, parts).astype(F32).astype(BF16)
     grad_ref[...] = dot_tn(order, (back + part).astype(BF16)).astype(BF16)
 
@@ -323,37 +338,21 @@
             ]
 
 
-def grads_mlp_kernel(factor, shift, here_ref, there_ref, w_up_ref, w_down_ref, *refs):
-    outs, down, up = refs[:-2], refs[-2], refs[-1]
+def grads_mlp_kernel(factor, here_ref, there_ref, w_up_ref, w_down_ref, keep_ref, send_ref, down, up):
     width, units = w_up_ref.shape
-    slab = lax.axis_index("slab")
-    digit = (slab >> shift) & (len(outs) - 1)
+    x, _, _, _ = place()
     hidden = jnp.concatenate([ref[:, :width] for ref in (here_ref, there_ref)], axis=0)
     cot = jnp.concatenate([ref[:, width:] for ref in (here_ref, there_ref)], axis=0)
     active, slope = gelu_parts(dot(hidden, w_up_ref[...]))
     grad_upper = (dot_nt(cot, w_down_ref[...]) * slope).astype(BF16)
     down[...] = dot_tn(active, cot) * factor
     up[...] = dot_tn(hidden, grad_upper) * factor
-    rest, rows = outs[0].shape[:2]
-    for j, out in enumerate(outs):
-        for k in range(rest):
-            z = (digit ^ j) * rest + k
-            at = pl.ds(pl.multiple_of(z * rows, 8), rows)
-            out[k, :, :width] = down[at, :].astype(BF16)
-            for flip in range(2):
-                at = pl.ds(pl.multiple_of((z * 2 + ((slab & 1) ^ flip)) * rows, 8), rows)
-                out[k, :, width + flip * units : width + (flip + 1) * units] = up[at, :].astype(BF16)
-
-
-def total_kernel(keep, *refs):
-    ins, (mine_ref, other_ref) = refs[:-2], refs[-2:]
-    total = sum(ref[0].astype(F32) for ref in ins).astype(BF16)
-    mine_ref[...] = total[:, :keep]
-    other_ref[...] = total[:, keep:]
-
-
-def beside_kernel(a_ref, b_ref, out_ref):
-    out_ref[...] = jnp.concatenate([a_ref[...], b_ref[...]], axis=1)
+    spans, rows = keep_ref.shape[:2]
+    for flip, out in ((0, keep_ref), (1, send_ref)):
+        for z in range(spans):
+            at = pl.ds(pl.multiple_of((z * 2 + (x ^ flip)) * rows, 8), rows)
+            out[z, :, :width] = down[at, :].astype(BF16)
+            out[z, :, width:] = up[at, :].astype(BF16)
 
 
 def grads_qkv_kernel(factor, width, slabs, za_ref, zb_ref, pa_ref, pb_ref, *refs):
@@ -425,24 +424,15 @@
     ]
     for copy in copies:
         copy.start()
-    case, x = lax.axis_index("case"), lax.axis_index("slab") & 1
-    eighth, fine = units // 8, units // 4 // slabs
+    case = lax.axis_index("case")
     for j in range(4):
-        piece = pieces[j][...].astype(F32)
-        held[case ^ j, :, :width] = piece[:, :width]
-        for flip in range(2):
-            at = pl.multiple_of(width + (x ^ flip) * eighth, LANES)
-            held[case ^ j, :, pl.ds(at, eighth)] = piece[
-                :, width + flip * eighth : width + (flip + 1) * eighth
-            ]
+        held[case ^ j] = pieces[j][0].astype(F32)
+    fine = units // 4 // slabs
     for quarter in range(4):
         down[quarter * rows : (quarter + 1) * rows, :] = held[quarter, :, :width]
     for block in range(slabs):
         up[:, block * 4 * fine : (block + 1) * 4 * fine] = jnp.concatenate(
-            [
-                held[quarter, :, pl.ds(width + block % 2 * eighth + block // 2 * fine, fine)]
-                for quarter in range(4)
-            ],
+            [held[quarter, :, width + block * fine : width + (block + 1) * fine] for quarter in range(4)],
             axis=1,
         )
     for copy in copies:
@@ -512,7 +502,7 @@
     )
     w_up_mine, w_down_mine = call(
         functools.partial(prepare_kernel, slabs),
-        [shape_of((width, units // 8), BF16), shape_of((units // 8, width), BF16)],
+        [shape_of((width, units // 4), BF16), shape_of((units // 4, width), BF16)],
         w_up,
         w_down,
     )
@@ -527,7 +517,7 @@
         w_out,
         after=[w_up_mine],
     )
-    around = [shared, permute(shared, 0, 2), permute(shared, 1, 0), permute(shared, 1, 2)]
+    shared_y = permute(shared, 0, 2)
     grad_mixed, grad_residual = call(
         mlp_kernel,
         [rows_bf, shape_of((count, width), F32)],
@@ -538,9 +528,9 @@
         w_up,
         w_down,
     )
-    *backs, pack_z = call(
-        functools.partial(lines_back_kernel, sizes),
-        [shape_of((count // parts, 2 * width), BF16)] * parts + [shape_of((count, 6 * width), BF16)],
+    back, pack_z = call(
+        functools.partial(lines_back_kernel, sizes, parts),
+        [shape_of((count, 2 * width), BF16), shape_of((count, 6 * width), BF16)],
         proj_z,
         grad_mixed,
         grad_residual,
@@ -549,44 +539,28 @@
         gain_one,
         w_qkv,
     )
-    backs = exchange(backs)
-    (around,) = call(
-        join_kernel, [shape_of((4 * count, 2 * width), BF16)], *around, after=backs[1:]
-    )
-    around_core = permute(around, 0, 1)
-    radix = min(4, spans)
-    shift = (slabs // radix).bit_length() - 1
-    big = call(
-        functools.partial(grads_mlp_kernel, factor, shift),
-        [shape_of((spans // radix, rows, 2 * width), BF16)] * radix,
+    around, back = call(
+        join_kernel,
+        [shape_of((2 * count, 2 * width), BF16), shape_of((count, 2 * width), BF16)],
+        shared,
+        shared_y,
+        back,
+    )
+    back = lax.all_to_all(back, "slab", split_axis=0, concat_axis=0, tiled=True)
+    pack_z_core = permute(pack_z, 0, 1)
+    big_keep, big_send = call(
+        functools.partial(grads_mlp_kernel, factor),
+        [shape_of((spans, rows, 2 * width), BF16)] * 2,
         around,
-        around_core,
+        permute(around, 0, 1),
         w_up_mine,
         w_down_mine,
-        scratch=[pltpu.VMEM((units // 8, width), F32), pltpu.VMEM((width, units // 8), F32)],
-    )
-    pack_z_core = permute(pack_z, 0, 1)
-    def reduce_z(split):
-        left = spans
-        while True:
-            radix = len(split)
-            left //= radix
-            shift = (left * 2).bit_length() - 1
-            pieces = [split[0]] + [permute(split[j], j << shift, 0) for j in range(1, radix)]
-            if left == 1:
-                return pieces
-            radix = min(4, left)
-            split = fold((left // radix * 2).bit_length() - 1, radix, pieces)
-
-    def gather(last):
-        return [last] + [permute(last, 0, j) for j in range(1, 4)]
-
-    early = big[0]
-    big = reduce_z(big)
+        scratch=[pltpu.VMEM((units // 4, width), F32), pltpu.VMEM((width, units // 4), F32)],
+    )
     (pack_p,) = call(
         functools.partial(plane_grads_kernel, sizes, parts),
         [shape_of((count, 4 * width), BF16)],
-        *backs,
+        back,
         hold_x,
         gain_one,
         w_qkv,
@@ -599,7 +573,7 @@
         pack_z_core,
         pack_p,
         permute(pack_p, 0, 1),
-        after=[early],
+        after=[big_keep],
         scratch=[pltpu.VMEM((width, width), F32)],
     )
     ready = small[0]
@@ -607,7 +581,7 @@
     (grad_tokens,) = call(
         functools.partial(plane_tokens_kernel, sizes, parts),
         [rows_bf],
-        *backs,
+        back,
         pack_p,
         hold_x,
         gain_one,
@@ -615,18 +589,23 @@
         after=[ready],
     )
 
-    small = reduce_z(fold(shift, radix, small))
-    keep = width + units // 8
-    mine_big, other_big = call(
-        functools.partial(total_kernel, keep),
-        [shape_of((rows, keep), BF16), shape_of((rows, units // 8), BF16)],
-        *big,
-        after=[small[0]],
-    )
-    (last,) = call(
-        beside_kernel, [shape_of((rows, 2 * width), BF16)], mine_big, permute(other_big, 1, 0)
-    )
-    big = gather(last)
+    def reduce_z(pieces, after=()):
+        left = spans
+        while left > 1:
+            radix = min(4, left)
+            left //= radix
+            shift = (left * 2).bit_length() - 1
+            split = fold(shift, radix, pieces, after)
+            pieces = [split[0]] + [permute(split[j], j << shift, 0) for j in range(1, radix)]
+        return pieces
+
+    def gather(pieces, after=()):
+        (last,) = fold(0, 1, pieces, after)
+        return [last] + [permute(last, 0, j) for j in range(1, 4)]
+
+    big = reduce_z([big_keep, permute(big_send, 1, 0)], [ready])
+    small = reduce_z(small)
+    big = gather(big, [small[0]])
     full_up, full_down, full_two, w_rows = call(
         functools.partial(place_mlp_kernel, slabs, width, units),
         [
@@ -646,7 +625,7 @@
             pltpu.SemaphoreType.DMA((2,)),
         ],
     )
-    small = gather(fold(0, 1, small)[0])
+    small = gather(small)
     full_qkv, full_out, full_one = call(
         functools.partial(place_qkv_kernel, slabs, width),
         [shape_of((rows, 3 * width), F32), shape_of((rows, width), F32), shape_of((1, rows), F32)],

time: 95.6 us -> 93.8 us (0.981)
  starting transfers between devices: 43.6 us -> 32.1 us
  waiting for transfers between devices: 27.2 us -> 33.2 us
  Pallas kernels: 20.3 us -> 23 us
    ppermute x36 -> x27, starting transfers between devices: 43.6 us -> 28.5 us  [permute(): lax.ppermute(array, BOTH, swap_pairs(slabs, cases, flip_slab, flip_case))]
    all_to_all x0 -> x1, waiting for transfers between devices: none -> 7.47 us  [body(): back = lax.all_to_all(back, 'slab', split_axis=0, concat_axis=0, tiled=True)]
    all_to_all x0 -> x1, starting transfers between devices: none -> 3.59 us  [body(): back = lax.all_to_all(back, 'slab', split_axis=0, concat_axis=0, tiled=True)]
    pallas_call x16, Pallas kernels: 20.3 us -> 23 us  [call(): pl.pallas_call(run, out_shape=outs, in_specs=[vmem if one else far for on...]
    ppermute x36 -> x27, waiting for transfers between devices: 27.2 us -> 25.8 us  [permute(): lax.ppermute(array, BOTH, swap_pairs(slabs, cases, flip_slab, flip_case))]
    unnamed x16 -> x24, local copies, waits for them, and re-layouts: 3.32 us -> 4.12 us
  transfers between devices with their start and end apart: 36 -> 28, of which waited for: 16 -> 8; matrix products, arithmetic and copies ran while one was open for 0% -> 0% of each run, Pallas kernels for 15% -> 18%
where the time goes in v2:
time: 93.8 us; the launch traced here: 93.4 us
  waiting for transfers between devices  33.2 us (35%)
  starting transfers between devices  32.1 us (34%)
  Pallas kernels  23 us (25%)
  local copies, waits for them, and re-layouts  4.12 us (4%)
    ppermute x27, starting transfers between devices, permute(): lax.ppermute(array, BOTH, swap_pairs(slabs, cases, flip_slab, flip_case))  28.5 us
    ppermute x27, waiting for transfers between devices, permute(): lax.ppermute(array, BOTH, swap_pairs(slabs, cases, flip_slab, flip_case))  25.8 us
    pallas_call x16, Pallas kernels, call(): pl.pallas_call(run, out_shape=outs, in_specs=[vmem if one else far for on...  23 us
    all_to_all x1, waiting for transfers between devices, body(): back = lax.all_to_all(back, 'slab', split_axis=0, concat_axis=0, tiled=True)  7.47 us
    unnamed x24, local copies, waits for them, and re-layouts  4.12 us
    all_to_all x1, starting transfers between devices, body(): back = lax.all_to_all(back, 'slab', split_axis=0, concat_axis=0, tiled=True)  3.59 us
  transfers between devices with their start and end apart: 28, of which 8 were waited for; matrix products, arithmetic and copies ran while one was open for 0% of the time, Pallas kernels for 18%

profile of v2, /device:TPU:0, one launch (start us, length us, event | category | flops | bytes accessed | tf_op | source)
XLA Modules:
  0.0 93.4 jit_solution(3913058682671591244)
XLA Ops:
  0.6 2.9 %shard_map.135 = (bf16[16,1536]{1,0:T(8,128)(2,1)S(1)}, bf16[16,1536]{1,0:T(8,128)(2,1)S(1)}, bf16[16,1536]{1,0:T(8,128)(2,1)S(1)}, bf16[16,1536]{1,0:T(8,128)(2...) custom-call(bf16[128,512]{1,0:T(8,128)(2,1)} %bitcast.20, ...), custom_call_target="tpu_custom_call" | custom-call | flops 10000000 | bytes 10000 | tf_op jit(solution)/shard_map/pallas_call | solution.py:50
  3.5 3.0 %collective-permute-start = (bf16[16,1536]{1,0:T(8,128)(2,1)S(1)}, bf16[16,1536]{1,0:T(8,128)(2,1)S(1)}, u32[]{:S(2)}, u32[]{:S(2)}) collective-permute-start(bf16[16,1536]{1,0:T(8,128)(2,1)S(1)} %get-tuple-element.51), channel_id=1, source_target_pairs={{0,4},{1,5},{2,6},{3,7},{4,0},{5,1},{6,2},{7,3},{8,12},{9,13},{10,... | collective-permute-start | bytes 147464 | tf_op jit(solution)/shard_map/ppermute | solution.py:476
  6.5 1.6 %collective-permute-start.1 = (bf16[16,1536]{1,0:T(8,128)(2,1)S(1)}, bf16[16,1536]{1,0:T(8,128)(2,1)S(1)}, u32[]{:S(2)}, u32[]{:S(2)}) collective-permute-start(bf16[16,1536]{1,0:T(8,128)(2,1)S(1)} %get-tuple-element.52), channel_id=1, source_target_pairs={{0,8},{1,9},{2,10},{3,11},{4,12},{5,13},{6,14},{7,15},{8,0},{9,1},... | collective-permute-start | bytes 147464 | tf_op jit(solution)/shard_map/ppermute | solution.py:476
  8.1 0.0 collective-permute-start.2
  8.1 3.0 %collective-permute-start.3 = (bf16[16,1536]{1,0:T(8,128)(2,1)S(1)}, bf16[16,1536]{1,0:T(8,128)(2,1)S(1)}, u32[]{:S(2)}, u32[]{:S(2)}) collective-permute-start(bf16[16,1536]{1,0:T(8,128)(2,1)S(1)} %get-tuple-element.54), channel_id=1, source_target_pairs={{0,16},{1,17},{2,18},{3,19},{4,20},{5,21},{6,22},{7,23},{8,24},{9,... | collective-permute-start | bytes 147464 | tf_op jit(solution)/shard_map/ppermute | solution.py:476
  11.1 1.3 %collective-permute-start.4 = (bf16[16,1536]{1,0:T(8,128)(2,1)S(1)}, bf16[16,1536]{1,0:T(8,128)(2,1)S(1)}, u32[]{:S(2)}, u32[]{:S(2)}) collective-permute-start(bf16[16,1536]{1,0:T(8,128)(2,1)S(1)} %get-tuple-element.55), channel_id=1, source_target_pairs={{0,20},{1,21},{2,22},{3,23},{4,16},{5,17},{6,18},{7,19},{8,28},{9,... | collective-permute-start | bytes 147464 | tf_op jit(solution)/shard_map/ppermute | solution.py:476
  12.4 3.6 %collective-permute-start.5 = (bf16[16,1536]{1,0:T(8,128)(2,1)S(1)}, bf16[16,1536]{1,0:T(8,128)(2,1)S(1)}, u32[]{:S(2)}, u32[]{:S(2)}) collective-permute-start(bf16[16,1536]{1,0:T(8,128)(2,1)S(1)} %get-tuple-element.56), channel_id=1, source_target_pairs={{0,24},{1,25},{2,26},{3,27},{4,28},{5,29},{6,30},{7,31},{8,16},{9,... | collective-permute-start | bytes 147464 | tf_op jit(solution)/shard_map/ppermute | solution.py:476
  16.0 0.0 collective-permute-start.6
  16.1 1.7 %copy-done.1 = bf16[512,2048]{1,0:T(8,128)(2,1)S(1)} copy-done((bf16[512,2048]{1,0:T(8,128)(2,1)S(1)}, bf16[512,2048]{1,0:T(8,128)(2,1)}, u32[]{:S(2)}) %copy-start.1) | copy-done | bytes 2097176
  17.8 1.6 %copy-done.3 = bf16[2048,512]{1,0:T(8,128)(2,1)S(1)} copy-done((bf16[2048,512]{1,0:T(8,128)(2,1)S(1)}, bf16[2048,512]{1,0:T(8,128)(2,1)}, u32[]{:S(2)}) %copy-start.3) | copy-done | bytes 2097176
  19.4 0.7 shard_map.136
  20.1 0.0 copy-start.6
  20.1 0.0 copy-start.2
  20.1 0.0 collective-permute-done.2.refs_3_
  20.2 0.0 collective-permute-done.4.refs_5_
  20.2 0.0 collective-permute-done.5.refs_6_
  20.2 2.6 %collective-permute-done.6.refs_7_ = bf16[16,1536]{1,0:T(8,128)(2,1)S(1)} collective-permute-done((bf16[16,1536]{1,0:T(8,128)(2,1)S(1)}, bf16[16,1536]{1,0:T(8,128)(2,1)S(1)}, u32[]{:S(2)}, u32[]{:S(2)}) %collective-permute-start.6) | collective-permute-done | bytes 49184 | tf_op jit(solution)/shard_map/ppermute | solution.py:476
  22.8 1.3 %shard_map.137 = (bf16[128,1024]{1,0:T(8,128)(2,1)S(1)}, bf16[128,1536]{1,0:T(8,128)(2,1)S(1)}, bf16[128,512]{1,0:T(8,128)(2,1)S(1)}, bf16[128,512]{1,0:T(8,128)(2,1)S(1)}, bf16[128,512]{1,0:T(8,128)(2,1)S(1)}) custom-call(bf16[16,1536]{1,0:T(8,128)(2,1)S(1)} %get-tuple-element.50.refs_0_, bf16[16,1536]{1,0:T(8,128)(2,1)S(1)} %collective-permute-done.refs_1_, ...), custom_call_target="tpu_custom_call" | custom-call | flops 10000000 | bytes 10000 | tf_op jit(solution)/shard_map/pallas_call | solution.py:50
  24.1 1.6 %collective-permute-start.7 = (bf16[128,1024]{1,0:T(8,128)(2,1)S(1)}, bf16[128,1024]{1,0:T(8,128)(2,1)S(1)}, u32[]{:S(2)}, u32[]{:S(2)}) collective-permute-start(bf16[128,1024]{1,0:T(8,128)(2,1)S(1)} %get-tuple-element.59.refs_0_), channel_id=1, source_target_pairs={{0,2},{1,3},{2,0},{3,1},{4,6},{5,7},{6,4},{7,5},{8,10},{9,11},{10,... | collective-permute-start | bytes 786440 | tf_op jit(solution)/shard_map/ppermute | solution.py:476
  25.7 2.4 %shard_map.138 = (bf16[128,512]{1,0:T(8,128)(2,1)S(1)}, f32[128,512]{1,0:T(8,128)S(1)}) custom-call(bf16[128,1024]{1,0:T(8,128)(2,1)S(1)} %get-tuple-element.59.refs_0_, bf16[128,512]{1,0:T(8,128)(2,1)S(1)} %get-tuple-element.61.refs_1_, f32[1,512]{1,0:T(1,128)S(1)} %bitcast.18, bf16[512,512]{1,0:T(8,128)(2,1)S(1)} %copy-done.5, ...), custom_call_target="tpu_custom_call" | custom-call | flops 10000000 | bytes 10000 | tf_op jit(solution)/shard_map/pallas_call | solution.py:50
  28.0 2.6 %shard_map.139 = (bf16[128,1024]{1,0:T(8,128)(2,1)S(1)}, bf16[128,3072]{1,0:T(8,128)(2,1)S(1)}) custom-call(bf16[128,1536]{1,0:T(8,128)(2,1)S(1)} %get-tuple-element.60.refs_0_, bf16[128,512]{1,0:T(8,128)(2,1)S(1)} %get-tuple-element.62.refs_1_, f32[128,512]{1,0:T(8,128)S(1)} %get-tuple-element.63.refs_2_, bf16[128,512]{1,0:T(8,128)(2,1)S(1)} %get-tuple-element.64.refs_3_, ...), custom_call_target="tpu_custom_call" | custom-call | flops 10000000 | bytes 10000 | tf_op jit(solution)/shard_map/pallas_call | solution.py:50
  30.7 0.0 collective-permute-done.7.refs_1_
  30.7 0.8 shard_map.140
  31.5 0.8 copy-done.8
  32.3 3.6 %all-to-all-start = ((bf16[8,16,1024]{2,1,0:T(8,128)(2,1)}), bf16[8,16,1024]{2,1,0:T(8,128)(2,1)S(1)}, u32[]{:S(2)}, u32[]{:S(2)}) async-start(bf16[8,16,1024]{2,1,0:T(8,128)(2,1)} %bitcast.4), calls=%async_computation | async-start | bytes 524288 | tf_op jit(solution)/shard_map/all_to_all | solution.py:549
  35.9 0.1 collective-permute-start.10
  35.9 0.5 collective-permute-start.8
  36.4 7.5 %all-to-all-done = bf16[8,16,1024]{2,1,0:T(8,128)(2,1)S(1)} async-done(((bf16[8,16,1024]{2,1,0:T(8,128)(2,1)}), bf16[8,16,1024]{2,1,0:T(8,128)(2,1)S(1)}, u32[]{:S(2)}, u32[]{:S(2)}) %all-to-all-start) | async-done | bytes 262176 | tf_op jit(solution)/shard_map/all_to_all | solution.py:549
  43.9 2.6 %shard_map.141.refs_2_.refs_1_ = bf16[128,2048]{1,0:T(8,128)(2,1)S(1)} custom-call(bf16[128,1024]{1,0:T(8,128)(2,1)S(1)} %bitcast.9, bf16[128,512]{1,0:T(8,128)(2,1)S(1)} %get-tuple-element.68.refs_1_.refs_2_, f32[1,512]{1,0:T(1,128)S(1)} %bitcast.14, bf16[512,1536]{1,0:T(8,128)(2,1)S(1)} %copy-done), custom_call_target="tpu_custom_call" | custom-call | flops 10000000 | bytes 10000 | tf_op jit(solution)/shard_map/pallas_call | solution.py:50
  46.6 0.1 collective-permute-start.9
  46.6 0.0 collective-permute-done.10.refs_1_
  46.7 2.7 %shard_map.142 = (bf16[4,64,1024]{2,1,0:T(8,128)(2,1)S(1)}, bf16[4,64,1024]{2,1,0:T(8,128)(2,1)S(1)}) custom-call(bf16[256,1024]{1,0:T(8,128)(2,1)S(1)} %copy-done.9, bf16[256,1024]{1,0:T(8,128)(2,1)} %collective-permute-done.10.refs_1_, bf16[512,512]{1,0:T(8,128)(2,1)S(1)} %get-tuple-element.58.refs_12_.refs_2_, bf16[512,512]{1,0:T(8,128)(2,1)S(1)} %copy-done.7), custom_call_target="tpu_custom_call" | custom-call | flops 10000000 | bytes 10000 | tf_op jit(solution)/shard_map/pallas_call | solution.py:50
  49.4 0.2 collective-permute-start.20
  49.5 2.2 %shard_map.143 = (bf16[4,256,128]{2,1,0:T(8,128)(2,1)S(1)}, bf16[4,256,128]{2,1,0:T(8,128)(2,1)S(1)}, bf16[4,256,128]{2,1,0:T(8,128)(2,1)S(1)}, bf16[4,256,128]{2,1,0:T(8,128)(2,1)S(1)}) custom-call(bf16[128,3072]{1,0:T(8,128)(2,1)S(1)} %get-tuple-element.69.refs_0_, bf16[128,3072]{1,0:T(8,128)(2,1)} %collective-permute-done.8.refs_1_, ...), custom_call_target="tpu_custom_call" | custom-call | flops 10000000 | bytes 10000 | tf_op jit(solution)/shard_map/pallas_call | solution.py:50
  51.7 2.0 %collective-permute-start.11 = (bf16[4,256,128]{2,1,0:T(8,128)(2,1)S(1)}, bf16[4,256,128]{2,1,0:T(8,128)(2,1)S(1)}, u32[]{:S(2)}, u32[]{:S(2)}) collective-permute-start(bf16[4,256,128]{2,1,0:T(8,128)(2,1)S(1)} %get-tuple-element.74), channel_id=1, source_target_pairs={{0,4},{1,5},{2,6},{3,7},{4,0},{5,1},{6,2},{7,3},{8,12},{9,13},{10,... | collective-permute-start | bytes 786440 | tf_op jit(solution)/shard_map/ppermute | solution.py:476
  53.8 1.3 %collective-permute-start.12 = (bf16[4,256,128]{2,1,0:T(8,128)(2,1)S(1)}, bf16[4,256,128]{2,1,0:T(8,128)(2,1)S(1)}, u32[]{:S(2)}, u32[]{:S(2)}) collective-permute-start(bf16[4,256,128]{2,1,0:T(8,128)(2,1)S(1)} %get-tuple-element.75), channel_id=1, source_target_pairs={{0,2},{1,3},{2,0},{3,1},{4,6},{5,7},{6,4},{7,5},{8,10},{9,11},{10,... | collective-permute-start | bytes 786440 | tf_op jit(solution)/shard_map/ppermute | solution.py:476
  55.1 0.2 collective-permute-start.13
  55.3 8.9 %collective-permute-done.20.refs_1_ = bf16[4,64,1024]{2,1,0:T(8,128)(2,1)S(1)} collective-permute-done((bf16[4,64,1024]{2,1,0:T(8,128)(2,1)S(1)}, bf16[4,64,1024]{2,1,0:T(8,128)(2,1)S(1)}, u32[]{:S(2)}, u32[]{:S(2)}) %collective-permute-start.20) | collective-permute-done | bytes 524320 | tf_op jit(solution)/shard_map/ppermute | solution.py:476
  64.2 0.1 shard_map.147
  64.3 0.1 collective-permute-start.21
  64.4 1.1 %collective-permute-start.22 = (bf16[1,64,1024]{2,1,0:T(8,128)(2,1)S(1)}, bf16[1,64,1024]{2,1,0:T(8,128)(2,1)S(1)}, u32[]{:S(2)}, u32[]{:S(2)}) collective-permute-start(bf16[1,64,1024]{2,1,0:T(8,128)(2,1)S(1)} %get-tuple-element.84), channel_id=1, source_target_pairs={{0,16},{1,17},{2,18},{3,19},{4,20},{5,21},{6,22},{7,23},{8,24},{9,... | collective-permute-start | bytes 393224 | tf_op jit(solution)/shard_map/ppermute | solution.py:476
  65.5 4.3 %collective-permute-done.11.refs_1_ = bf16[4,256,128]{2,1,0:T(8,128)(2,1)S(1)} collective-permute-done((bf16[4,256,128]{2,1,0:T(8,128)(2,1)S(1)}, bf16[4,256,128]{2,1,0:T(8,128)(2,1)S(1)}, u32[]{:S(2)}, u32[]{:S(2)}) %collective-permute-start.11) | collective-permute-done | bytes 262176 | tf_op jit(solution)/shard_map/ppermute | solution.py:476
  69.8 0.6 collective-permute-start.23
  70.4 0.0 collective-permute-done.12.refs_2_
  70.4 5.4 %collective-permute-done.13.refs_3_ = bf16[4,256,128]{2,1,0:T(8,128)(2,1)S(1)} collective-permute-done((bf16[4,256,128]{2,1,0:T(8,128)(2,1)S(1)}, bf16[4,256,128]{2,1,0:T(8,128)(2,1)S(1)}, u32[]{:S(2)}, u32[]{:S(2)}) %collective-permute-start.13) | collective-permute-done | bytes 262176 | tf_op jit(solution)/shard_map/ppermute | solution.py:476
  75.7 0.1 shard_map.145
  75.9 0.1 collective-permute-start.14
  76.0 0.0 collective-permute-done.21.refs_1_
  76.0 0.6 collective-permute-done.23.refs_3_
  76.6 0.1 shard_map.148.refs_0_
  76.7 0.1 collective-permute-start.24
  76.8 1.4 %collective-permute-start.25 = (bf16[1,64,1024]{2,1,0:T(8,128)(2,1)S(1)}, bf16[1,64,1024]{2,1,0:T(8,128)(2,1)S(1)}, u32[]{:S(2)}, u32[]{:S(2)}) collective-permute-start(bf16[1,64,1024]{2,1,0:T(8,128)(2,1)S(1)} %shard_map.148.refs_0_), channel_id=1, source_target_pairs={{0,2},{1,3},{2,0},{3,1},{4,6},{5,7},{6,4},{7,5},{8,10},{9,11},{10,... | collective-permute-start | bytes 393224 | tf_op jit(solution)/shard_map/ppermute | solution.py:476
  78.2 2.6 %collective-permute-start.15 = (bf16[1,256,128]{2,1,0:T(8,128)(2,1)S(1)}, bf16[1,256,128]{2,1,0:T(8,128)(2,1)S(1)}, u32[]{:S(2)}, u32[]{:S(2)}) collective-permute-start(bf16[1,256,128]{2,1,0:T(8,128)(2,1)S(1)} %get-tuple-element.79), channel_id=1, source_target_pairs={{0,16},{1,17},{2,18},{3,19},{4,20},{5,21},{6,22},{7,23},{8,24},{9,... | collective-permute-start | bytes 196616 | tf_op jit(solution)/shard_map/ppermute | solution.py:476
  80.7 2.2 %collective-permute-start.16 = (bf16[1,256,128]{2,1,0:T(8,128)(2,1)S(1)}, bf16[1,256,128]{2,1,0:T(8,128)(2,1)S(1)}, u32[]{:S(2)}, u32[]{:S(2)}) collective-permute-start(bf16[1,256,128]{2,1,0:T(8,128)(2,1)S(1)} %get-tuple-element.80), channel_id=1, source_target_pairs={{0,24},{1,25},{2,26},{3,27},{4,28},{5,29},{6,30},{7,31},{8,16},{9,... | collective-permute-start | bytes 196616 | tf_op jit(solution)/shard_map/ppermute | solution.py:476
  82.9 0.0 collective-permute-done.14.refs_1_
  83.0 3.0 %collective-permute-done.15.refs_2_ = bf16[1,256,128]{2,1,0:T(8,128)(2,1)S(1)} collective-permute-done((bf16[1,256,128]{2,1,0:T(8,128)(2,1)S(1)}, bf16[1,256,128]{2,1,0:T(8,128)(2,1)S(1)}, u32[]{:S(2)}, u32[]{:S(2)}) %collective-permute-start.15) | collective-permute-done | bytes 65568 | tf_op jit(solution)/shard_map/ppermute | solution.py:476
  86.0 0.9 collective-permute-done.16.refs_3_
  86.9 0.1 collective-permute-start.17
  87.0 0.8 collective-permute-start.18
  87.8 1.1 %collective-permute-start.19 = (bf16[1,256,128]{2,1,0:T(8,128)(2,1)S(1)}, bf16[1,256,128]{2,1,0:T(8,128)(2,1)S(1)}, u32[]{:S(2)}, u32[]{:S(2)}) collective-permute-start(bf16[1,256,128]{2,1,0:T(8,128)(2,1)S(1)} %shard_map.146.refs_0_), channel_id=1, source_target_pairs={{0,3},{1,2},{2,1},{3,0},{4,7},{5,6},{6,5},{7,4},{8,11},{9,10},{10,... | collective-permute-start | bytes 196616 | tf_op jit(solution)/shard_map/ppermute | solution.py:476
  88.9 1.6 %shard_map.144 = bf16[128,512]{1,0:T(8,128)(2,1)} custom-call(bf16[128,1024]{1,0:T(8,128)(2,1)S(1)} %bitcast.10, bf16[128,2048]{1,0:T(8,128)(2,1)S(1)} %shard_map.141.refs_2_.refs_1_, bf16[128,512]{1,0:T(8,128)(2,1)S(1)} %get-tuple-element.68.refs_1_.refs_2_, f32[1,512]{1,0:T(1,128)S(1)} %bitcast.15, bf16[512,1536]{1,0:T(8,128)(2,1)S(1)} %copy-done, ...), custom_call_target="tpu_custom_call" | custom-call | flops 10000000 | bytes 10000 | tf_op jit(solution)/shard_map/pallas_call | solution.py:50
  90.4 0.0 collective-permute-done.25.refs_2_
  90.4 2.1 %shard_map.149 = (f32[64,2048]{1,0:T(8,128)}, f32[256,512]{1,0:T(8,128)}, f32[1,64]{1,0:T(1,128)}, bf16[64,1536]{1,0:T(8,128)(2,1)S(1)}) custom-call(bf16[1,64,1024]{2,1,0:T(8,128)(2,1)S(1)} %shard_map.148.refs_0_, bf16[1,64,1024]{2,1,0:T(8,128)(2,1)S(1)} %collective-permute-done.24.refs_1_, bf16[1,64,1024]{2,1,0:T(8,128)(2,1)S(1)} %collective-permute-done.25.refs_2_, ...), custom_call_target="tpu_custom_call" | custom-call | flops 10000000 | bytes 10000 | tf_op jit(solution)/shard_map/pallas_call | solution.py:50
  92.5 0.8 shard_map.150
  (32 shorter events, 0.1 us)
Async XLA Ops:
  3.5 8.9 %collective-permute-start = (bf16[16,1536]{1,0:T(8,128)(2,1)S(1)}, bf16[16,1536]{1,0:T(8,128)(2,1)S(1)}, u32[]{:S(2)}, u32[]{:S(2)}) collective-permute-start(bf16[16,1536]{1,0:T(8,128)(2,1)S(1)} %get-tuple-element.51), channel_id=1, source_target_pairs={{0,4},{1,5},{2,6},{3,7},{4,0},{5,1},{6,2},{7,3},{8,12},{9,13},{10,... | collective-permute-start | bytes 147464 | tf_op jit(solution)/shard_map/ppermute | solution.py:476
  6.5 9.5 %collective-permute-start.1 = (bf16[16,1536]{1,0:T(8,128)(2,1)S(1)}, bf16[16,1536]{1,0:T(8,128)(2,1)S(1)}, u32[]{:S(2)}, u32[]{:S(2)}) collective-permute-start(bf16[16,1536]{1,0:T(8,128)(2,1)S(1)} %get-tuple-element.52), channel_id=1, source_target_pairs={{0,8},{1,9},{2,10},{3,11},{4,12},{5,13},{6,14},{7,15},{8,0},{9,1},... | collective-permute-start | bytes 147464 | tf_op jit(solution)/shard_map/ppermute | solution.py:476
  8.1 12.0 %collective-permute-start.2 = (bf16[16,1536]{1,0:T(8,128)(2,1)S(1)}, bf16[16,1536]{1,0:T(8,128)(2,1)S(1)}, u32[]{:S(2)}, u32[]{:S(2)}) collective-permute-start(bf16[16,1536]{1,0:T(8,128)(2,1)S(1)} %get-tuple-element.53), channel_id=1, source_target_pairs={{0,12},{1,13},{2,14},{3,15},{4,8},{5,9},{6,10},{7,11},{8,4},{9,5},... | collective-permute-start | bytes 147464 | tf_op jit(solution)/shard_map/ppermute | solution.py:476
  8.1 12.0 %collective-permute-start.3 = (bf16[16,1536]{1,0:T(8,128)(2,1)S(1)}, bf16[16,1536]{1,0:T(8,128)(2,1)S(1)}, u32[]{:S(2)}, u32[]{:S(2)}) collective-permute-start(bf16[16,1536]{1,0:T(8,128)(2,1)S(1)} %get-tuple-element.54), channel_id=1, source_target_pairs={{0,16},{1,17},{2,18},{3,19},{4,20},{5,21},{6,22},{7,23},{8,24},{9,... | collective-permute-start | bytes 147464 | tf_op jit(solution)/shard_map/ppermute | solution.py:476
  11.1 9.0 %collective-permute-start.4 = (bf16[16,1536]{1,0:T(8,128)(2,1)S(1)}, bf16[16,1536]{1,0:T(8,128)(2,1)S(1)}, u32[]{:S(2)}, u32[]{:S(2)}) collective-permute-start(bf16[16,1536]{1,0:T(8,128)(2,1)S(1)} %get-tuple-element.55), channel_id=1, source_target_pairs={{0,20},{1,21},{2,22},{3,23},{4,16},{5,17},{6,18},{7,19},{8,28},{9,... | collective-permute-start | bytes 147464 | tf_op jit(solution)/shard_map/ppermute | solution.py:476
  12.4 7.8 %collective-permute-start.5 = (bf16[16,1536]{1,0:T(8,128)(2,1)S(1)}, bf16[16,1536]{1,0:T(8,128)(2,1)S(1)}, u32[]{:S(2)}, u32[]{:S(2)}) collective-permute-start(bf16[16,1536]{1,0:T(8,128)(2,1)S(1)} %get-tuple-element.56), channel_id=1, source_target_pairs={{0,24},{1,25},{2,26},{3,27},{4,28},{5,29},{6,30},{7,31},{8,16},{9,... | collective-permute-start | bytes 147464 | tf_op jit(solution)/shard_map/ppermute | solution.py:476
  16.0 6.8 %copy-start = (bf16[512,1536]{1,0:T(8,128)(2,1)S(1)}, bf16[512,1536]{1,0:T(8,128)(2,1)}, u32[]{:S(2)}) copy-start(bf16[512,1536]{1,0:T(8,128)(2,1)} %refs_6_.3) | copy-start | bytes 4718596
  16.0 6.8 %collective-permute-start.6 = (bf16[16,1536]{1,0:T(8,128)(2,1)S(1)}, bf16[16,1536]{1,0:T(8,128)(2,1)S(1)}, u32[]{:S(2)}, u32[]{:S(2)}) collective-permute-start(bf16[16,1536]{1,0:T(8,128)(2,1)S(1)} %get-tuple-element.57), channel_id=1, source_target_pairs={{0,28},{1,29},{2,30},{3,31},{4,24},{5,25},{6,26},{7,27},{8,20},{9,... | collective-permute-start | bytes 147464 | tf_op jit(solution)/shard_map/ppermute | solution.py:476
  16.1 1.7 %copy-start.1 = (bf16[512,2048]{1,0:T(8,128)(2,1)S(1)}, bf16[512,2048]{1,0:T(8,128)(2,1)}, u32[]{:S(2)}) copy-start(bf16[512,2048]{1,0:T(8,128)(2,1)} %refs_5_.3) | copy-start | bytes 6291460
  17.8 1.6 %copy-start.3 = (bf16[2048,512]{1,0:T(8,128)(2,1)S(1)}, bf16[2048,512]{1,0:T(8,128)(2,1)}, u32[]{:S(2)}) copy-start(bf16[2048,512]{1,0:T(8,128)(2,1)} %refs_5_.2) | copy-start | bytes 6291460
  19.4 3.5 %copy-start.5 = (bf16[512,512]{1,0:T(8,128)(2,1)S(1)}, bf16[512,512]{1,0:T(8,128)(2,1)}, u32[]{:S(2)}) copy-start(bf16[512,512]{1,0:T(8,128)(2,1)} %refs_3_.4) | copy-start | bytes 1572868
  19.4 3.5 %copy-start.10 = (f32[512]{0:T(512)S(1)}, f32[512]{0:T(512)}, u32[]{:S(2)}) copy-start(f32[512]{0:T(512)} %param.14) | copy-start | bytes 6148
  19.4 3.5 %copy-start.11 = (f32[512]{0:T(512)S(1)}, f32[512]{0:T(512)}, u32[]{:S(2)}) copy-start(f32[512]{0:T(512)} %param.15) | copy-start | bytes 6148
  19.4 6.3 %copy-start.4 = (bf16[2048,512]{1,0:T(8,128)(2,1)S(1)}, bf16[2048,512]{1,0:T(8,128)(2,1)}, u32[]{:S(2)}) copy-start(bf16[2048,512]{1,0:T(8,128)(2,1)} %refs_5_.2) | copy-start | bytes 6291460
  20.1 7.9 %copy-start.6 = (bf16[512,512]{1,0:T(8,128)(2,1)}, bf16[512,512]{1,0:T(8,128)(2,1)S(1)}, u32[]{:S(2)}) copy-start(bf16[512,512]{1,0:T(8,128)(2,1)S(1)} %get-tuple-element.71.refs_3_) | copy-start | bytes 1572868
  20.1 5.5 %copy-start.2 = (bf16[512,2048]{1,0:T(8,128)(2,1)S(1)}, bf16[512,2048]{1,0:T(8,128)(2,1)}, u32[]{:S(2)}) copy-start(bf16[512,2048]{1,0:T(8,128)(2,1)} %refs_5_.3) | copy-start | bytes 6291460
  24.1 6.6 %collective-permute-start.7 = (bf16[128,1024]{1,0:T(8,128)(2,1)S(1)}, bf16[128,1024]{1,0:T(8,128)(2,1)S(1)}, u32[]{:S(2)}, u32[]{:S(2)}) collective-permute-start(bf16[128,1024]{1,0:T(8,128)(2,1)S(1)} %get-tuple-element.59.refs_0_), channel_id=1, source_target_pairs={{0,2},{1,3},{2,0},{3,1},{4,6},{5,7},{6,4},{7,5},{8,10},{9,11},{10,... | collective-permute-start | bytes 786440 | tf_op jit(solution)/shard_map/ppermute | solution.py:476
  31.5 0.8 copy-start.8
  32.3 11.6 %all-to-all-start = ((bf16[8,16,1024]{2,1,0:T(8,128)(2,1)}), bf16[8,16,1024]{2,1,0:T(8,128)(2,1)S(1)}, u32[]{:S(2)}, u32[]{:S(2)}) async-start(bf16[8,16,1024]{2,1,0:T(8,128)(2,1)} %bitcast.4), calls=%async_computation | async-start | bytes 524288 | tf_op jit(solution)/shard_map/all_to_all | solution.py:549
  35.9 10.8 %collective-permute-start.10 = (bf16[256,1024]{1,0:T(8,128)(2,1)}, bf16[256,1024]{1,0:T(8,128)(2,1)}, u32[]{:S(2)}, u32[]{:S(2)}) collective-permute-start(bf16[256,1024]{1,0:T(8,128)(2,1)} %copy-done.8), channel_id=1, source_target_pairs={{0,1},{1,0},{2,3},{3,2},{4,5},{5,4},{6,7},{7,6},{8,9},{9,8},{10,11... | collective-permute-start | bytes 1572872 | tf_op jit(solution)/shard_map/ppermute | solution.py:476
  35.9 13.6 %collective-permute-start.8 = (bf16[128,3072]{1,0:T(8,128)(2,1)S(1)}, bf16[128,3072]{1,0:T(8,128)(2,1)}, u32[]{:S(2)}, u32[]{:S(2)}) collective-permute-start(bf16[128,3072]{1,0:T(8,128)(2,1)S(1)} %get-tuple-element.69.refs_0_), channel_id=1, source_target_pairs={{0,1},{1,0},{2,3},{3,2},{4,5},{5,4},{6,7},{7,6},{8,9},{9,8},{10,11... | collective-permute-start | bytes 2359304 | tf_op jit(solution)/shard_map/ppermute | solution.py:476
  43.9 2.7 %copy-start.7 = (bf16[512,512]{1,0:T(8,128)(2,1)S(1)}, bf16[512,512]{1,0:T(8,128)(2,1)}, u32[]{:S(2)}) copy-start(bf16[512,512]{1,0:T(8,128)(2,1)} %copy-done.6) | copy-start | bytes 1572868
  43.9 2.7 %copy-start.9 = (bf16[256,1024]{1,0:T(8,128)(2,1)S(1)}, bf16[256,1024]{1,0:T(8,128)(2,1)}, u32[]{:S(2)}) copy-start(bf16[256,1024]{1,0:T(8,128)(2,1)} %copy-done.8) | copy-start | bytes 1572868
  46.6 3.0 %collective-permute-start.9 = (bf16[128,2048]{1,0:T(8,128)(2,1)S(1)}, bf16[128,2048]{1,0:T(8,128)(2,1)S(1)}, u32[]{:S(2)}, u32[]{:S(2)}) collective-permute-start(bf16[128,2048]{1,0:T(8,128)(2,1)S(1)} %shard_map.141.refs_2_.refs_1_), channel_id=1, source_target_pairs={{0,1},{1,0},{2,3},{3,2},{4,5},{5,4},{6,7},{7,6},{8,9},{9,8},{10,11... | collective-permute-start | bytes 1572872 | tf_op jit(solution)/shard_map/ppermute | solution.py:476
  49.4 14.8 %collective-permute-start.20 = (bf16[4,64,1024]{2,1,0:T(8,128)(2,1)S(1)}, bf16[4,64,1024]{2,1,0:T(8,128)(2,1)S(1)}, u32[]{:S(2)}, u32[]{:S(2)}) collective-permute-start(bf16[4,64,1024]{2,1,0:T(8,128)(2,1)S(1)} %get-tuple-element.81), channel_id=1, source_target_pairs={{0,4},{1,5},{2,6},{3,7},{4,0},{5,1},{6,2},{7,3},{8,12},{9,13},{10,... | collective-permute-start | bytes 1572872 | tf_op jit(solution)/shard_map/ppermute | solution.py:476
  51.7 18.1 %collective-permute-start.11 = (bf16[4,256,128]{2,1,0:T(8,128)(2,1)S(1)}, bf16[4,256,128]{2,1,0:T(8,128)(2,1)S(1)}, u32[]{:S(2)}, u32[]{:S(2)}) collective-permute-start(bf16[4,256,128]{2,1,0:T(8,128)(2,1)S(1)} %get-tuple-element.74), channel_id=1, source_target_pairs={{0,4},{1,5},{2,6},{3,7},{4,0},{5,1},{6,2},{7,3},{8,12},{9,13},{10,... | collective-permute-start | bytes 786440 | tf_op jit(solution)/shard_map/ppermute | solution.py:476
  53.8 16.6 %collective-permute-start.12 = (bf16[4,256,128]{2,1,0:T(8,128)(2,1)S(1)}, bf16[4,256,128]{2,1,0:T(8,128)(2,1)S(1)}, u32[]{:S(2)}, u32[]{:S(2)}) collective-permute-start(bf16[4,256,128]{2,1,0:T(8,128)(2,1)S(1)} %get-tuple-element.75), channel_id=1, source_target_pairs={{0,2},{1,3},{2,0},{3,1},{4,6},{5,7},{6,4},{7,5},{8,10},{9,11},{10,... | collective-permute-start | bytes 786440 | tf_op jit(solution)/shard_map/ppermute | solution.py:476
  55.1 20.6 %collective-permute-start.13 = (bf16[4,256,128]{2,1,0:T(8,128)(2,1)S(1)}, bf16[4,256,128]{2,1,0:T(8,128)(2,1)S(1)}, u32[]{:S(2)}, u32[]{:S(2)}) collective-permute-start(bf16[4,256,128]{2,1,0:T(8,128)(2,1)S(1)} %get-tuple-element.76), channel_id=1, source_target_pairs={{0,6},{1,7},{2,4},{3,5},{4,2},{5,3},{6,0},{7,1},{8,14},{9,15},{10,... | collective-permute-start | bytes 786440 | tf_op jit(solution)/shard_map/ppermute | solution.py:476
  64.3 11.7 %collective-permute-start.21 = (bf16[1,64,1024]{2,1,0:T(8,128)(2,1)S(1)}, bf16[1,64,1024]{2,1,0:T(8,128)(2,1)S(1)}, u32[]{:S(2)}, u32[]{:S(2)}) collective-permute-start(bf16[1,64,1024]{2,1,0:T(8,128)(2,1)S(1)} %get-tuple-element.83), channel_id=1, source_target_pairs={{0,8},{1,9},{2,10},{3,11},{4,12},{5,13},{6,14},{7,15},{8,0},{9,1},... | collective-permute-start | bytes 393224 | tf_op jit(solution)/shard_map/ppermute | solution.py:476
  64.4 11.6 %collective-permute-start.22 = (bf16[1,64,1024]{2,1,0:T(8,128)(2,1)S(1)}, bf16[1,64,1024]{2,1,0:T(8,128)(2,1)S(1)}, u32[]{:S(2)}, u32[]{:S(2)}) collective-permute-start(bf16[1,64,1024]{2,1,0:T(8,128)(2,1)S(1)} %get-tuple-element.84), channel_id=1, source_target_pairs={{0,16},{1,17},{2,18},{3,19},{4,20},{5,21},{6,22},{7,23},{8,24},{9,... | collective-permute-start | bytes 393224 | tf_op jit(solution)/shard_map/ppermute | solution.py:476
  69.8 6.8 %collective-permute-start.23 = (bf16[1,64,1024]{2,1,0:T(8,128)(2,1)S(1)}, bf16[1,64,1024]{2,1,0:T(8,128)(2,1)S(1)}, u32[]{:S(2)}, u32[]{:S(2)}) collective-permute-start(bf16[1,64,1024]{2,1,0:T(8,128)(2,1)S(1)} %get-tuple-element.85), channel_id=1, source_target_pairs={{0,24},{1,25},{2,26},{3,27},{4,28},{5,29},{6,30},{7,31},{8,16},{9,... | collective-permute-start | bytes 393224 | tf_op jit(solution)/shard_map/ppermute | solution.py:476
  75.9 7.1 %collective-permute-start.14 = (bf16[1,256,128]{2,1,0:T(8,128)(2,1)S(1)}, bf16[1,256,128]{2,1,0:T(8,128)(2,1)S(1)}, u32[]{:S(2)}, u32[]{:S(2)}) collective-permute-start(bf16[1,256,128]{2,1,0:T(8,128)(2,1)S(1)} %get-tuple-element.78), channel_id=1, source_target_pairs={{0,8},{1,9},{2,10},{3,11},{4,12},{5,13},{6,14},{7,15},{8,0},{9,1},... | collective-permute-start | bytes 196616 | tf_op jit(solution)/shard_map/ppermute | solution.py:476
  76.7 11.1 %collective-permute-start.24 = (bf16[1,64,1024]{2,1,0:T(8,128)(2,1)S(1)}, bf16[1,64,1024]{2,1,0:T(8,128)(2,1)S(1)}, u32[]{:S(2)}, u32[]{:S(2)}) collective-permute-start(bf16[1,64,1024]{2,1,0:T(8,128)(2,1)S(1)} %shard_map.148.refs_0_), channel_id=1, source_target_pairs={{0,1},{1,0},{2,3},{3,2},{4,5},{5,4},{6,7},{7,6},{8,9},{9,8},{10,11... | collective-permute-start | bytes 393224 | tf_op jit(solution)/shard_map/ppermute | solution.py:476
  76.8 13.6 %collective-permute-start.25 = (bf16[1,64,1024]{2,1,0:T(8,128)(2,1)S(1)}, bf16[1,64,1024]{2,1,0:T(8,128)(2,1)S(1)}, u32[]{:S(2)}, u32[]{:S(2)}) collective-permute-start(bf16[1,64,1024]{2,1,0:T(8,128)(2,1)S(1)} %shard_map.148.refs_0_), channel_id=1, source_target_pairs={{0,2},{1,3},{2,0},{3,1},{4,6},{5,7},{6,4},{7,5},{8,10},{9,11},{10,... | collective-permute-start | bytes 393224 | tf_op jit(solution)/shard_map/ppermute | solution.py:476
  78.2 7.8 %collective-permute-start.15 = (bf16[1,256,128]{2,1,0:T(8,128)(2,1)S(1)}, bf16[1,256,128]{2,1,0:T(8,128)(2,1)S(1)}, u32[]{:S(2)}, u32[]{:S(2)}) collective-permute-start(bf16[1,256,128]{2,1,0:T(8,128)(2,1)S(1)} %get-tuple-element.79), channel_id=1, source_target_pairs={{0,16},{1,17},{2,18},{3,19},{4,20},{5,21},{6,22},{7,23},{8,24},{9,... | collective-permute-start | bytes 196616 | tf_op jit(solution)/shard_map/ppermute | solution.py:476
  80.7 6.1 %collective-permute-start.16 = (bf16[1,256,128]{2,1,0:T(8,128)(2,1)S(1)}, bf16[1,256,128]{2,1,0:T(8,128)(2,1)S(1)}, u32[]{:S(2)}, u32[]{:S(2)}) collective-permute-start(bf16[1,256,128]{2,1,0:T(8,128)(2,1)S(1)} %get-tuple-element.80), channel_id=1, source_target_pairs={{0,24},{1,25},{2,26},{3,27},{4,28},{5,29},{6,30},{7,31},{8,16},{9,... | collective-permute-start | bytes 196616 | tf_op jit(solution)/shard_map/ppermute | solution.py:476
  82.9 7.5 %collective-permute-start.26 = (bf16[1,64,1024]{2,1,0:T(8,128)(2,1)S(1)}, bf16[1,64,1024]{2,1,0:T(8,128)(2,1)S(1)}, u32[]{:S(2)}, u32[]{:S(2)}) collective-permute-start(bf16[1,64,1024]{2,1,0:T(8,128)(2,1)S(1)} %shard_map.148.refs_0_), channel_id=1, source_target_pairs={{0,3},{1,2},{2,1},{3,0},{4,7},{5,6},{6,5},{7,4},{8,11},{9,10},{10,... | collective-permute-start | bytes 393224 | tf_op jit(solution)/shard_map/ppermute | solution.py:476
  86.9 5.6 %collective-permute-start.17 = (bf16[1,256,128]{2,1,0:T(8,128)(2,1)S(1)}, bf16[1,256,128]{2,1,0:T(8,128)(2,1)S(1)}, u32[]{:S(2)}, u32[]{:S(2)}) collective-permute-start(bf16[1,256,128]{2,1,0:T(8,128)(2,1)S(1)} %shard_map.146.refs_0_), channel_id=1, source_target_pairs={{0,1},{1,0},{2,3},{3,2},{4,5},{5,4},{6,7},{7,6},{8,9},{9,8},{10,11... | collective-permute-start | bytes 196616 | tf_op jit(solution)/shard_map/ppermute | solution.py:476
  87.0 5.5 %collective-permute-start.18 = (bf16[1,256,128]{2,1,0:T(8,128)(2,1)S(1)}, bf16[1,256,128]{2,1,0:T(8,128)(2,1)S(1)}, u32[]{:S(2)}, u32[]{:S(2)}) collective-permute-start(bf16[1,256,128]{2,1,0:T(8,128)(2,1)S(1)} %shard_map.146.refs_0_), channel_id=1, source_target_pairs={{0,2},{1,3},{2,0},{3,1},{4,6},{5,7},{6,4},{7,5},{8,10},{9,11},{10,... | collective-permute-start | bytes 196616 | tf_op jit(solution)/shard_map/ppermute | solution.py:476
  87.8 4.7 %collective-permute-start.19 = (bf16[1,256,128]{2,1,0:T(8,128)(2,1)S(1)}, bf16[1,256,128]{2,1,0:T(8,128)(2,1)S(1)}, u32[]{:S(2)}, u32[]{:S(2)}) collective-permute-start(bf16[1,256,128]{2,1,0:T(8,128)(2,1)S(1)} %shard_map.146.refs_0_), channel_id=1, source_target_pairs={{0,3},{1,2},{2,1},{3,0},{4,7},{5,6},{6,5},{7,4},{8,11},{9,10},{10,... | collective-permute-start | bytes 196616 | tf_op jit(solution)/shard_map/ppermute | solution.py:476

commit v3 on v2

--- a/solution.py
+++ b/solution.py
@@ -294,11 +294,10 @@
     )
 
 
-def join_kernel(a_ref, b_ref, back_ref, out_ref, passed_ref):
+def join_kernel(a_ref, b_ref, out_ref):
     rows = a_ref.shape[0]
     out_ref[:rows, :] = a_ref[...]
     out_ref[rows:, :] = b_ref[...]
-    passed_ref[...] = back_ref[...]
 
 
 def plane_grads_kernel(sizes, parts, *refs):
@@ -312,7 +311,8 @@
 
 
 def plane_tokens_kernel(sizes, parts, *refs):
-    back_ref, pack_ref, x_ref, gain_ref, w_ref, grad_ref = refs
+    back_ref, pack_ref, x_ref, gain_ref, w_ref, grad_ref, flag_ref = refs
+    flag_ref[...] = jnp.zeros_like(flag_ref)
     width = w_ref.shape[0]
     normed, inverse = norm_stats(x_ref[...].astype(F32))
     grad_hidden = dot_nt(pack_ref[:, width:], w_ref[...])
@@ -539,15 +539,20 @@
         gain_one,
         w_qkv,
     )
-    around, back = call(
-        join_kernel,
-        [shape_of((2 * count, 2 * width), BF16), shape_of((count, 2 * width), BF16)],
-        shared,
-        shared_y,
-        back,
-    )
     back = lax.all_to_all(back, "slab", split_axis=0, concat_axis=0, tiled=True)
     pack_z_core = permute(pack_z, 0, 1)
+    (pack_p,) = call(
+        functools.partial(plane_grads_kernel, sizes, parts),
+        [shape_of((count, 4 * width), BF16)],
+        back,
+        hold_x,
+        gain_one,
+        w_qkv,
+        scratch=[pltpu.VMEM((count, 3 * width), BF16)],
+    )
+    (around,) = call(
+        join_kernel, [shape_of((2 * count, 2 * width), BF16)], shared, shared_y, after=[pack_p]
+    )
     big_keep, big_send = call(
         functools.partial(grads_mlp_kernel, factor),
         [shape_of((spans, rows, 2 * width), BF16)] * 2,
@@ -556,15 +561,6 @@
         w_up_mine,
         w_down_mine,
         scratch=[pltpu.VMEM((units // 4, width), F32), pltpu.VMEM((width, units // 4), F32)],
-    )
-    (pack_p,) = call(
-        functools.partial(plane_grads_kernel, sizes, parts),
-        [shape_of((count, 4 * width), BF16)],
-        back,
-        hold_x,
-        gain_one,
-        w_qkv,
-        scratch=[pltpu.VMEM((count, 3 * width), BF16)],
     )
     small = call(
         functools.partial(grads_qkv_kernel, factor, width, slabs),
@@ -578,9 +574,9 @@
     )
     ready = small[0]
     small = [small[0], permute(small[1], 1, 0), permute(small[2], 0, 2), permute(small[3], 1, 2)]
-    (grad_tokens,) = call(
+    grad_tokens, flag = call(
         functools.partial(plane_tokens_kernel, sizes, parts),
-        [rows_bf],
+        [rows_bf, shape_of((8, LANES), F32)],
         back,
         pack_p,
         hold_x,
@@ -603,7 +599,7 @@
         (last,) = fold(0, 1, pieces, after)
         return [last] + [permute(last, 0, j) for j in range(1, 4)]
 
-    big = reduce_z([big_keep, permute(big_send, 1, 0)], [ready])
+    big = reduce_z([big_keep, permute(big_send, 1, 0)], [flag])
     small = reduce_z(small)
     big = gather(big, [small[0]])
     full_up, full_down, full_two, w_rows = call(

time: 93.8 us -> 93.5 us (level)
  Pallas kernels: 23 us -> 21 us
  waiting for transfers between devices: 33.2 us -> 34.2 us
    pallas_call x16, Pallas kernels: 23 us -> 21 us  [call(): pl.pallas_call(run, out_shape=outs, in_specs=[vmem if one else far for on...]
    ppermute x27, waiting for transfers between devices: 25.8 us -> 27.5 us  [permute(): lax.ppermute(array, BOTH, swap_pairs(slabs, cases, flip_slab, flip_case))]
    unnamed x24 -> x22, local copies, waits for them, and re-layouts: 4.12 us -> 4.8 us
  transfers between devices with their start and end apart: 28 -> 28, of which waited for: 8 -> 10; matrix products, arithmetic and copies ran while one was open for 0% -> 0% of each run, Pallas kernels for 18% -> 11%
where the time goes in v3:
time: 93.5 us; the launch traced here: 93.1 us
  waiting for transfers between devices  34.2 us (37%)
  starting transfers between devices  32.3 us (35%)
  Pallas kernels  21 us (22%)
  local copies, waits for them, and re-layouts  4.8 us (5%)
    ppermute x27, starting transfers between devices, permute(): lax.ppermute(array, BOTH, swap_pairs(slabs, cases, flip_slab, flip_case))  27.9 us
    ppermute x27, waiting for transfers between devices, permute(): lax.ppermute(array, BOTH, swap_pairs(slabs, cases, flip_slab, flip_case))  27.5 us
    pallas_call x16, Pallas kernels, call(): pl.pallas_call(run, out_shape=outs, in_specs=[vmem if one else far for on...  21 us
    all_to_all x1, waiting for transfers between devices, body(): back = lax.all_to_all(back, 'slab', split_axis=0, concat_axis=0, tiled=True)  6.7 us
    unnamed x22, local copies, waits for them, and re-layouts  4.8 us
    all_to_all x1, starting transfers between devices, body(): back = lax.all_to_all(back, 'slab', split_axis=0, concat_axis=0, tiled=True)  4.32 us
  transfers between devices with their start and end apart: 28, of which 10 were waited for; matrix products, arithmetic and copies ran while one was open for 0% of the time, Pallas kernels for 11%

profile of v3, /device:TPU:0, one launch (start us, length us, event | category | flops | bytes accessed | tf_op | source)
XLA Modules:
  0.0 93.1 jit_solution(6152526084811324575)
XLA Ops:
  0.6 2.9 %shard_map.135 = (bf16[16,1536]{1,0:T(8,128)(2,1)S(1)}, bf16[16,1536]{1,0:T(8,128)(2,1)S(1)}, bf16[16,1536]{1,0:T(8,128)(2,1)S(1)}, bf16[16,1536]{1,0:T(8,128)(2...) custom-call(bf16[128,512]{1,0:T(8,128)(2,1)} %bitcast.21, ...), custom_call_target="tpu_custom_call" | custom-call | flops 10000000 | bytes 10000 | tf_op jit(solution)/shard_map/pallas_call | solution.py:50
  3.5 3.0 %collective-permute-start = (bf16[16,1536]{1,0:T(8,128)(2,1)S(1)}, bf16[16,1536]{1,0:T(8,128)(2,1)S(1)}, u32[]{:S(2)}, u32[]{:S(2)}) collective-permute-start(bf16[16,1536]{1,0:T(8,128)(2,1)S(1)} %get-tuple-element.51), channel_id=1, source_target_pairs={{0,4},{1,5},{2,6},{3,7},{4,0},{5,1},{6,2},{7,3},{8,12},{9,13},{10,... | collective-permute-start | bytes 147464 | tf_op jit(solution)/shard_map/ppermute | solution.py:476
  6.5 1.6 %collective-permute-start.1 = (bf16[16,1536]{1,0:T(8,128)(2,1)S(1)}, bf16[16,1536]{1,0:T(8,128)(2,1)S(1)}, u32[]{:S(2)}, u32[]{:S(2)}) collective-permute-start(bf16[16,1536]{1,0:T(8,128)(2,1)S(1)} %get-tuple-element.52), channel_id=1, source_target_pairs={{0,8},{1,9},{2,10},{3,11},{4,12},{5,13},{6,14},{7,15},{8,0},{9,1},... | collective-permute-start | bytes 147464 | tf_op jit(solution)/shard_map/ppermute | solution.py:476
  8.1 0.0 collective-permute-start.2
  8.1 3.0 %collective-permute-start.3 = (bf16[16,1536]{1,0:T(8,128)(2,1)S(1)}, bf16[16,1536]{1,0:T(8,128)(2,1)S(1)}, u32[]{:S(2)}, u32[]{:S(2)}) collective-permute-start(bf16[16,1536]{1,0:T(8,128)(2,1)S(1)} %get-tuple-element.54), channel_id=1, source_target_pairs={{0,16},{1,17},{2,18},{3,19},{4,20},{5,21},{6,22},{7,23},{8,24},{9,... | collective-permute-start | bytes 147464 | tf_op jit(solution)/shard_map/ppermute | solution.py:476
  11.1 1.3 %collective-permute-start.4 = (bf16[16,1536]{1,0:T(8,128)(2,1)S(1)}, bf16[16,1536]{1,0:T(8,128)(2,1)S(1)}, u32[]{:S(2)}, u32[]{:S(2)}) collective-permute-start(bf16[16,1536]{1,0:T(8,128)(2,1)S(1)} %get-tuple-element.55), channel_id=1, source_target_pairs={{0,20},{1,21},{2,22},{3,23},{4,16},{5,17},{6,18},{7,19},{8,28},{9,... | collective-permute-start | bytes 147464 | tf_op jit(solution)/shard_map/ppermute | solution.py:476
  12.4 0.0 collective-permute-done.refs_1_
  12.4 3.6 %collective-permute-start.5 = (bf16[16,1536]{1,0:T(8,128)(2,1)S(1)}, bf16[16,1536]{1,0:T(8,128)(2,1)S(1)}, u32[]{:S(2)}, u32[]{:S(2)}) collective-permute-start(bf16[16,1536]{1,0:T(8,128)(2,1)S(1)} %get-tuple-element.56), channel_id=1, source_target_pairs={{0,24},{1,25},{2,26},{3,27},{4,28},{5,29},{6,30},{7,31},{8,16},{9,... | collective-permute-start | bytes 147464 | tf_op jit(solution)/shard_map/ppermute | solution.py:476
  16.0 0.0 collective-permute-start.6
  16.1 1.7 %copy-done.1 = bf16[512,2048]{1,0:T(8,128)(2,1)S(1)} copy-done((bf16[512,2048]{1,0:T(8,128)(2,1)S(1)}, bf16[512,2048]{1,0:T(8,128)(2,1)}, u32[]{:S(2)}) %copy-start.1) | copy-done | bytes 2097176
  17.8 1.6 %copy-done.3 = bf16[2048,512]{1,0:T(8,128)(2,1)S(1)} copy-done((bf16[2048,512]{1,0:T(8,128)(2,1)S(1)}, bf16[2048,512]{1,0:T(8,128)(2,1)}, u32[]{:S(2)}) %copy-start.3) | copy-done | bytes 2097176
  19.4 0.7 shard_map.136
  20.1 0.0 copy-start.6
  20.1 0.8 copy-done.6
  20.9 0.0 collective-permute-done.3.refs_4_
  20.9 0.0 collective-permute-done.4.refs_5_
  20.9 0.0 collective-permute-done.5.refs_6_
  20.9 1.9 %collective-permute-done.6.refs_7_ = bf16[16,1536]{1,0:T(8,128)(2,1)S(1)} collective-permute-done((bf16[16,1536]{1,0:T(8,128)(2,1)S(1)}, bf16[16,1536]{1,0:T(8,128)(2,1)S(1)}, u32[]{:S(2)}, u32[]{:S(2)}) %collective-permute-start.6) | collective-permute-done | bytes 49184 | tf_op jit(solution)/shard_map/ppermute | solution.py:476
  22.8 1.2 %shard_map.137 = (bf16[128,1024]{1,0:T(8,128)(2,1)S(1)}, bf16[128,1536]{1,0:T(8,128)(2,1)S(1)}, bf16[128,512]{1,0:T(8,128)(2,1)S(1)}, bf16[128,512]{1,0:T(8,128)(2,1)S(1)}, bf16[128,512]{1,0:T(8,128)(2,1)S(1)}) custom-call(bf16[16,1536]{1,0:T(8,128)(2,1)S(1)} %get-tuple-element.50.refs_0_, bf16[16,1536]{1,0:T(8,128)(2,1)S(1)} %collective-permute-done.refs_1_, ...), custom_call_target="tpu_custom_call" | custom-call | flops 10000000 | bytes 10000 | tf_op jit(solution)/shard_map/pallas_call | solution.py:50
  24.1 2.4 %shard_map.138 = (bf16[128,512]{1,0:T(8,128)(2,1)S(1)}, f32[128,512]{1,0:T(8,128)S(1)}) custom-call(bf16[128,1024]{1,0:T(8,128)(2,1)S(1)} %get-tuple-element.60.refs_0_, bf16[128,512]{1,0:T(8,128)(2,1)S(1)} %get-tuple-element.61.refs_1_, f32[1,512]{1,0:T(1,128)S(1)} %bitcast.19, bf16[512,512]{1,0:T(8,128)(2,1)S(1)} %copy-done.5, ...), custom_call_target="tpu_custom_call" | custom-call | flops 10000000 | bytes 10000 | tf_op jit(solution)/shard_map/pallas_call | solution.py:50
  26.5 2.6 %shard_map.139 = (bf16[128,1024]{1,0:T(8,128)(2,1)S(1)}, bf16[128,3072]{1,0:T(8,128)(2,1)S(1)}) custom-call(bf16[128,1536]{1,0:T(8,128)(2,1)S(1)} %get-tuple-element.59.refs_0_, bf16[128,512]{1,0:T(8,128)(2,1)S(1)} %get-tuple-element.62.refs_1_, f32[128,512]{1,0:T(8,128)S(1)} %get-tuple-element.63.refs_2_, bf16[128,512]{1,0:T(8,128)(2,1)S(1)} %get-tuple-element.64.refs_3_, ...), custom_call_target="tpu_custom_call" | custom-call | flops 10000000 | bytes 10000 | tf_op jit(solution)/shard_map/pallas_call | solution.py:50
  29.1 0.0 copy-start.8
  29.1 0.7 copy-done.8
  29.8 4.3 %all-to-all-start = ((bf16[8,16,1024]{2,1,0:T(8,128)(2,1)}), bf16[8,16,1024]{2,1,0:T(8,128)(2,1)S(1)}, u32[]{:S(2)}, u32[]{:S(2)}) async-start(bf16[8,16,1024]{2,1,0:T(8,128)(2,1)} %bitcast.11), calls=%async_computation | async-start | bytes 524288 | tf_op jit(solution)/shard_map/all_to_all | solution.py:542
  34.2 1.5 %collective-permute-start.9 = (bf16[128,1024]{1,0:T(8,128)(2,1)S(1)}, bf16[128,1024]{1,0:T(8,128)(2,1)}, u32[]{:S(2)}, u32[]{:S(2)}) collective-permute-start(bf16[128,1024]{1,0:T(8,128)(2,1)S(1)} %get-tuple-element.60.refs_0_), channel_id=1, source_target_pairs={{0,2},{1,3},{2,0},{3,1},{4,6},{5,7},{6,4},{7,5},{8,10},{9,11},{10,... | collective-permute-start | bytes 786440 | tf_op jit(solution)/shard_map/ppermute | solution.py:476
  35.7 6.7 %all-to-all-done = bf16[8,16,1024]{2,1,0:T(8,128)(2,1)S(1)} async-done(((bf16[8,16,1024]{2,1,0:T(8,128)(2,1)}), bf16[8,16,1024]{2,1,0:T(8,128)(2,1)S(1)}, u32[]{:S(2)}, u32[]{:S(2)}) %all-to-all-start) | async-done | bytes 262176 | tf_op jit(solution)/shard_map/all_to_all | solution.py:542
  42.4 2.6 %shard_map.140.refs_2_.refs_1_ = bf16[128,2048]{1,0:T(8,128)(2,1)S(1)} custom-call(bf16[128,1024]{1,0:T(8,128)(2,1)S(1)} %bitcast.9, bf16[128,512]{1,0:T(8,128)(2,1)S(1)} %get-tuple-element.67.refs_1_.refs_2_, f32[1,512]{1,0:T(1,128)S(1)} %bitcast.15, bf16[512,1536]{1,0:T(8,128)(2,1)S(1)} %copy-done), custom_call_target="tpu_custom_call" | custom-call | flops 10000000 | bytes 10000 | tf_op jit(solution)/shard_map/pallas_call | solution.py:50
  45.0 0.0 collective-permute-done.9.refs_1_
  45.0 1.0 %shard_map.141.refs_0_ = bf16[256,1024]{1,0:T(8,128)(2,1)S(1)} custom-call(bf16[128,1024]{1,0:T(8,128)(2,1)S(1)} %get-tuple-element.60.refs_0_, bf16[128,1024]{1,0:T(8,128)(2,1)} %collective-permute-done.9.refs_1_, bf16[128,2048]{1,0:T(8,128)(2,1)S(1)} %shard_map.140.refs_2_.refs_1_), custom_call_target="tpu_custom_call" | custom-call | flops 10000000 | bytes 10000 | tf_op jit(solution)/shard_map/pallas_call | solution.py:50
  46.0 0.1 collective-permute-start.10
  46.1 0.5 collective-permute-start.7
  46.6 0.1 collective-permute-start.8
  46.7 1.3 %collective-permute-done.10.refs_1_ = bf16[256,1024]{1,0:T(8,128)(2,1)S(1)} collective-permute-done((bf16[256,1024]{1,0:T(8,128)(2,1)S(1)}, bf16[256,1024]{1,0:T(8,128)(2,1)S(1)}, u32[]{:S(2)}, u32[]{:S(2)}) %collective-permute-start.10) | collective-permute-done | bytes 524320 | tf_op jit(solution)/shard_map/ppermute | solution.py:476
  48.0 1.7 %shard_map.142 = (bf16[4,64,1024]{2,1,0:T(8,128)(2,1)S(1)}, bf16[4,64,1024]{2,1,0:T(8,128)(2,1)S(1)}) custom-call(bf16[256,1024]{1,0:T(8,128)(2,1)S(1)} %shard_map.141.refs_0_, bf16[256,1024]{1,0:T(8,128)(2,1)S(1)} %collective-permute-done.10.refs_1_, bf16[512,512]{1,0:T(8,128)(2,1)S(1)} %get-tuple-element.58.refs_12_.refs_2_, bf16[512,512]{1,0:T(8,128)(2,1)S(1)} %copy-done.7), custom_call_target="tpu_custom_call" | custom-call | flops 10000000 | bytes 10000 | tf_op jit(solution)/shard_map/pallas_call | solution.py:50
  49.7 0.2 collective-permute-start.20
  49.8 0.0 collective-permute-done.8.refs_3_
  49.9 1.0 %shard_map.143 = (bf16[4,256,128]{2,1,0:T(8,128)(2,1)S(1)}, bf16[4,256,128]{2,1,0:T(8,128)(2,1)S(1)}, bf16[4,256,128]{2,1,0:T(8,128)(2,1)S(1)}, bf16[4,256,128]{2,1,0:T(8,128)(2,1)S(1)}) custom-call(bf16[128,3072]{1,0:T(8,128)(2,1)S(1)} %get-tuple-element.68.refs_0_, bf16[128,3072]{1,0:T(8,128)(2,1)S(1)} %collective-permute-done.7.refs_1_, ...), custom_call_target="tpu_custom_call" | custom-call | flops 10000000 | bytes 10000 | tf_op jit(solution)/shard_map/pallas_call | solution.py:50
  50.9 2.0 %collective-permute-start.11 = (bf16[4,256,128]{2,1,0:T(8,128)(2,1)S(1)}, bf16[4,256,128]{2,1,0:T(8,128)(2,1)S(1)}, u32[]{:S(2)}, u32[]{:S(2)}) collective-permute-start(bf16[4,256,128]{2,1,0:T(8,128)(2,1)S(1)} %get-tuple-element.73), channel_id=1, source_target_pairs={{0,4},{1,5},{2,6},{3,7},{4,0},{5,1},{6,2},{7,3},{8,12},{9,13},{10,... | collective-permute-start | bytes 786440 | tf_op jit(solution)/shard_map/ppermute | solution.py:476
  52.9 1.5 %collective-permute-start.12 = (bf16[4,256,128]{2,1,0:T(8,128)(2,1)S(1)}, bf16[4,256,128]{2,1,0:T(8,128)(2,1)S(1)}, u32[]{:S(2)}, u32[]{:S(2)}) collective-permute-start(bf16[4,256,128]{2,1,0:T(8,128)(2,1)S(1)} %get-tuple-element.74), channel_id=1, source_target_pairs={{0,2},{1,3},{2,0},{3,1},{4,6},{5,7},{6,4},{7,5},{8,10},{9,11},{10,... | collective-permute-start | bytes 786440 | tf_op jit(solution)/shard_map/ppermute | solution.py:476
  54.4 0.0 collective-permute-start.13
  54.5 1.6 %shard_map.144 = (bf16[128,512]{1,0:T(8,128)(2,1)}, f32[8,128]{1,0:T(8,128)S(1)}) custom-call(bf16[128,1024]{1,0:T(8,128)(2,1)S(1)} %bitcast.10, bf16[128,2048]{1,0:T(8,128)(2,1)S(1)} %shard_map.140.refs_2_.refs_1_, bf16[128,512]{1,0:T(8,128)(2,1)S(1)} %get-tuple-element.67.refs_1_.refs_2_, f32[1,512]{1,0:T(1,128)S(1)} %bitcast.16, ...), custom_call_target="tpu_custom_call" | custom-call | flops 10000000 | bytes 10000 | tf_op jit(solution)/shard_map/pallas_call | solution.py:50
  56.0 8.5 %collective-permute-done.20.refs_1_ = bf16[4,64,1024]{2,1,0:T(8,128)(2,1)S(1)} collective-permute-done((bf16[4,64,1024]{2,1,0:T(8,128)(2,1)S(1)}, bf16[4,64,1024]{2,1,0:T(8,128)(2,1)S(1)}, u32[]{:S(2)}, u32[]{:S(2)}) %collective-permute-start.20) | collective-permute-done | bytes 524320 | tf_op jit(solution)/shard_map/ppermute | solution.py:476
  64.5 0.1 shard_map.147
  64.6 0.1 collective-permute-start.21
  64.7 1.1 %collective-permute-start.22 = (bf16[1,64,1024]{2,1,0:T(8,128)(2,1)S(1)}, bf16[1,64,1024]{2,1,0:T(8,128)(2,1)S(1)}, u32[]{:S(2)}, u32[]{:S(2)}) collective-permute-start(bf16[1,64,1024]{2,1,0:T(8,128)(2,1)S(1)} %get-tuple-element.84), channel_id=1, source_target_pairs={{0,16},{1,17},{2,18},{3,19},{4,20},{5,21},{6,22},{7,23},{8,24},{9,... | collective-permute-start | bytes 393224 | tf_op jit(solution)/shard_map/ppermute | solution.py:476
  65.8 4.3 %collective-permute-done.11.refs_1_ = bf16[4,256,128]{2,1,0:T(8,128)(2,1)S(1)} collective-permute-done((bf16[4,256,128]{2,1,0:T(8,128)(2,1)S(1)}, bf16[4,256,128]{2,1,0:T(8,128)(2,1)S(1)}, u32[]{:S(2)}, u32[]{:S(2)}) %collective-permute-start.11) | collective-permute-done | bytes 262176 | tf_op jit(solution)/shard_map/ppermute | solution.py:476
  70.1 0.6 collective-permute-start.23
  70.7 5.2 %collective-permute-done.13.refs_3_ = bf16[4,256,128]{2,1,0:T(8,128)(2,1)S(1)} collective-permute-done((bf16[4,256,128]{2,1,0:T(8,128)(2,1)S(1)}, bf16[4,256,128]{2,1,0:T(8,128)(2,1)S(1)}, u32[]{:S(2)}, u32[]{:S(2)}) %collective-permute-start.13) | collective-permute-done | bytes 262176 | tf_op jit(solution)/shard_map/ppermute | solution.py:476
  75.9 0.1 shard_map.145
  76.0 0.1 collective-permute-start.14
  76.1 0.9 collective-permute-done.23.refs_3_
  77.0 0.1 shard_map.148.refs_0_
  77.1 0.1 collective-permute-start.26
  77.1 2.6 %collective-permute-start.15 = (bf16[1,256,128]{2,1,0:T(8,128)(2,1)S(1)}, bf16[1,256,128]{2,1,0:T(8,128)(2,1)S(1)}, u32[]{:S(2)}, u32[]{:S(2)}) collective-permute-start(bf16[1,256,128]{2,1,0:T(8,128)(2,1)S(1)} %get-tuple-element.78), channel_id=1, source_target_pairs={{0,16},{1,17},{2,18},{3,19},{4,20},{5,21},{6,22},{7,23},{8,24},{9,... | collective-permute-start | bytes 196616 | tf_op jit(solution)/shard_map/ppermute | solution.py:476
  79.7 2.2 %collective-permute-start.16 = (bf16[1,256,128]{2,1,0:T(8,128)(2,1)S(1)}, bf16[1,256,128]{2,1,0:T(8,128)(2,1)S(1)}, u32[]{:S(2)}, u32[]{:S(2)}) collective-permute-start(bf16[1,256,128]{2,1,0:T(8,128)(2,1)S(1)} %get-tuple-element.79), channel_id=1, source_target_pairs={{0,24},{1,25},{2,26},{3,27},{4,28},{5,29},{6,30},{7,31},{8,16},{9,... | collective-permute-start | bytes 196616 | tf_op jit(solution)/shard_map/ppermute | solution.py:476
  81.9 0.9 %collective-permute-start.25 = (bf16[1,64,1024]{2,1,0:T(8,128)(2,1)S(1)}, bf16[1,64,1024]{2,1,0:T(8,128)(2,1)S(1)}, u32[]{:S(2)}, u32[]{:S(2)}) collective-permute-start(bf16[1,64,1024]{2,1,0:T(8,128)(2,1)S(1)} %shard_map.148.refs_0_), channel_id=1, source_target_pairs={{0,2},{1,3},{2,0},{3,1},{4,6},{5,7},{6,4},{7,5},{8,10},{9,11},{10,... | collective-permute-start | bytes 393224 | tf_op jit(solution)/shard_map/ppermute | solution.py:476
  82.9 3.5 %collective-permute-done.16.refs_3_ = bf16[1,256,128]{2,1,0:T(8,128)(2,1)S(1)} collective-permute-done((bf16[1,256,128]{2,1,0:T(8,128)(2,1)S(1)}, bf16[1,256,128]{2,1,0:T(8,128)(2,1)S(1)}, u32[]{:S(2)}, u32[]{:S(2)}) %collective-permute-start.16) | collective-permute-done | bytes 65568 | tf_op jit(solution)/shard_map/ppermute | solution.py:476
  86.4 0.1 collective-permute-start.19
  86.5 1.4 %collective-permute-start.18 = (bf16[1,256,128]{2,1,0:T(8,128)(2,1)S(1)}, bf16[1,256,128]{2,1,0:T(8,128)(2,1)S(1)}, u32[]{:S(2)}, u32[]{:S(2)}) collective-permute-start(bf16[1,256,128]{2,1,0:T(8,128)(2,1)S(1)} %shard_map.146.refs_0_), channel_id=1, source_target_pairs={{0,2},{1,3},{2,0},{3,1},{4,6},{5,7},{6,4},{7,5},{8,10},{9,11},{10,... | collective-permute-start | bytes 196616 | tf_op jit(solution)/shard_map/ppermute | solution.py:476
  87.9 0.4 collective-permute-start.17
  88.4 2.1 %shard_map.149 = (f32[64,2048]{1,0:T(8,128)}, f32[256,512]{1,0:T(8,128)}, f32[1,64]{1,0:T(1,128)}, bf16[64,1536]{1,0:T(8,128)(2,1)S(1)}) custom-call(bf16[1,64,1024]{2,1,0:T(8,128)(2,1)S(1)} %shard_map.148.refs_0_, bf16[1,64,1024]{2,1,0:T(8,128)(2,1)S(1)} %collective-permute-done.24.refs_1_, bf16[1,64,1024]{2,1,0:T(8,128)(2,1)S(1)} %collective-permute-done.25.refs_2_, ...), custom_call_target="tpu_custom_call" | custom-call | flops 10000000 | bytes 10000 | tf_op jit(solution)/shard_map/pallas_call | solution.py:50
  90.4 0.4 collective-permute-done.19.refs_3_
  90.9 1.4 %collective-permute-done.18.refs_2_ = bf16[1,256,128]{2,1,0:T(8,128)(2,1)S(1)} collective-permute-done((bf16[1,256,128]{2,1,0:T(8,128)(2,1)S(1)}, bf16[1,256,128]{2,1,0:T(8,128)(2,1)S(1)}, u32[]{:S(2)}, u32[]{:S(2)}) %collective-permute-start.18) | collective-permute-done | bytes 65568 | tf_op jit(solution)/shard_map/ppermute | solution.py:476
  92.3 0.8 shard_map.150
  (30 shorter events, 0.1 us)
Async XLA Ops:
  3.5 8.9 %collective-permute-start = (bf16[16,1536]{1,0:T(8,128)(2,1)S(1)}, bf16[16,1536]{1,0:T(8,128)(2,1)S(1)}, u32[]{:S(2)}, u32[]{:S(2)}) collective-permute-start(bf16[16,1536]{1,0:T(8,128)(2,1)S(1)} %get-tuple-element.51), channel_id=1, source_target_pairs={{0,4},{1,5},{2,6},{3,7},{4,0},{5,1},{6,2},{7,3},{8,12},{9,13},{10,... | collective-permute-start | bytes 147464 | tf_op jit(solution)/shard_map/ppermute | solution.py:476
  6.5 9.5 %collective-permute-start.1 = (bf16[16,1536]{1,0:T(8,128)(2,1)S(1)}, bf16[16,1536]{1,0:T(8,128)(2,1)S(1)}, u32[]{:S(2)}, u32[]{:S(2)}) collective-permute-start(bf16[16,1536]{1,0:T(8,128)(2,1)S(1)} %get-tuple-element.52), channel_id=1, source_target_pairs={{0,8},{1,9},{2,10},{3,11},{4,12},{5,13},{6,14},{7,15},{8,0},{9,1},... | collective-permute-start | bytes 147464 | tf_op jit(solution)/shard_map/ppermute | solution.py:476
  8.1 12.8 %collective-permute-start.2 = (bf16[16,1536]{1,0:T(8,128)(2,1)S(1)}, bf16[16,1536]{1,0:T(8,128)(2,1)S(1)}, u32[]{:S(2)}, u32[]{:S(2)}) collective-permute-start(bf16[16,1536]{1,0:T(8,128)(2,1)S(1)} %get-tuple-element.53), channel_id=1, source_target_pairs={{0,12},{1,13},{2,14},{3,15},{4,8},{5,9},{6,10},{7,11},{8,4},{9,5},... | collective-permute-start | bytes 147464 | tf_op jit(solution)/shard_map/ppermute | solution.py:476
  8.1 12.8 %collective-permute-start.3 = (bf16[16,1536]{1,0:T(8,128)(2,1)S(1)}, bf16[16,1536]{1,0:T(8,128)(2,1)S(1)}, u32[]{:S(2)}, u32[]{:S(2)}) collective-permute-start(bf16[16,1536]{1,0:T(8,128)(2,1)S(1)} %get-tuple-element.54), channel_id=1, source_target_pairs={{0,16},{1,17},{2,18},{3,19},{4,20},{5,21},{6,22},{7,23},{8,24},{9,... | collective-permute-start | bytes 147464 | tf_op jit(solution)/shard_map/ppermute | solution.py:476
  11.1 9.8 %collective-permute-start.4 = (bf16[16,1536]{1,0:T(8,128)(2,1)S(1)}, bf16[16,1536]{1,0:T(8,128)(2,1)S(1)}, u32[]{:S(2)}, u32[]{:S(2)}) collective-permute-start(bf16[16,1536]{1,0:T(8,128)(2,1)S(1)} %get-tuple-element.55), channel_id=1, source_target_pairs={{0,20},{1,21},{2,22},{3,23},{4,16},{5,17},{6,18},{7,19},{8,28},{9,... | collective-permute-start | bytes 147464 | tf_op jit(solution)/shard_map/ppermute | solution.py:476
  12.4 8.5 %collective-permute-start.5 = (bf16[16,1536]{1,0:T(8,128)(2,1)S(1)}, bf16[16,1536]{1,0:T(8,128)(2,1)S(1)}, u32[]{:S(2)}, u32[]{:S(2)}) collective-permute-start(bf16[16,1536]{1,0:T(8,128)(2,1)S(1)} %get-tuple-element.56), channel_id=1, source_target_pairs={{0,24},{1,25},{2,26},{3,27},{4,28},{5,29},{6,30},{7,31},{8,16},{9,... | collective-permute-start | bytes 147464 | tf_op jit(solution)/shard_map/ppermute | solution.py:476
  16.0 6.8 %copy-start = (bf16[512,1536]{1,0:T(8,128)(2,1)S(1)}, bf16[512,1536]{1,0:T(8,128)(2,1)}, u32[]{:S(2)}) copy-start(bf16[512,1536]{1,0:T(8,128)(2,1)} %refs_6_.3) | copy-start | bytes 4718596
  16.0 6.8 %collective-permute-start.6 = (bf16[16,1536]{1,0:T(8,128)(2,1)S(1)}, bf16[16,1536]{1,0:T(8,128)(2,1)S(1)}, u32[]{:S(2)}, u32[]{:S(2)}) collective-permute-start(bf16[16,1536]{1,0:T(8,128)(2,1)S(1)} %get-tuple-element.57), channel_id=1, source_target_pairs={{0,28},{1,29},{2,30},{3,31},{4,24},{5,25},{6,26},{7,27},{8,20},{9,... | collective-permute-start | bytes 147464 | tf_op jit(solution)/shard_map/ppermute | solution.py:476
  16.1 1.7 %copy-start.1 = (bf16[512,2048]{1,0:T(8,128)(2,1)S(1)}, bf16[512,2048]{1,0:T(8,128)(2,1)}, u32[]{:S(2)}) copy-start(bf16[512,2048]{1,0:T(8,128)(2,1)} %refs_5_.3) | copy-start | bytes 6291460
  17.8 1.6 %copy-start.3 = (bf16[2048,512]{1,0:T(8,128)(2,1)S(1)}, bf16[2048,512]{1,0:T(8,128)(2,1)}, u32[]{:S(2)}) copy-start(bf16[2048,512]{1,0:T(8,128)(2,1)} %refs_5_.2) | copy-start | bytes 6291460
  19.4 3.5 %copy-start.5 = (bf16[512,512]{1,0:T(8,128)(2,1)S(1)}, bf16[512,512]{1,0:T(8,128)(2,1)}, u32[]{:S(2)}) copy-start(bf16[512,512]{1,0:T(8,128)(2,1)} %refs_3_.4) | copy-start | bytes 1572868
  19.4 3.5 %copy-start.9 = (f32[512]{0:T(512)S(1)}, f32[512]{0:T(512)}, u32[]{:S(2)}) copy-start(f32[512]{0:T(512)} %param.14) | copy-start | bytes 6148
  19.4 3.5 %copy-start.10 = (f32[512]{0:T(512)S(1)}, f32[512]{0:T(512)}, u32[]{:S(2)}) copy-start(f32[512]{0:T(512)} %param.15) | copy-start | bytes 6148
  19.4 4.7 %copy-start.4 = (bf16[2048,512]{1,0:T(8,128)(2,1)S(1)}, bf16[2048,512]{1,0:T(8,128)(2,1)}, u32[]{:S(2)}) copy-start(bf16[2048,512]{1,0:T(8,128)(2,1)} %refs_5_.2) | copy-start | bytes 6291460
  20.1 0.8 copy-start.6
  20.9 3.2 %copy-start.2 = (bf16[512,2048]{1,0:T(8,128)(2,1)S(1)}, bf16[512,2048]{1,0:T(8,128)(2,1)}, u32[]{:S(2)}) copy-start(bf16[512,2048]{1,0:T(8,128)(2,1)} %refs_5_.3) | copy-start | bytes 6291460
  29.1 0.7 copy-start.8
  29.8 12.5 %all-to-all-start = ((bf16[8,16,1024]{2,1,0:T(8,128)(2,1)}), bf16[8,16,1024]{2,1,0:T(8,128)(2,1)S(1)}, u32[]{:S(2)}, u32[]{:S(2)}) async-start(bf16[8,16,1024]{2,1,0:T(8,128)(2,1)} %bitcast.11), calls=%async_computation | async-start | bytes 524288 | tf_op jit(solution)/shard_map/all_to_all | solution.py:542
  34.2 10.9 %collective-permute-start.9 = (bf16[128,1024]{1,0:T(8,128)(2,1)S(1)}, bf16[128,1024]{1,0:T(8,128)(2,1)}, u32[]{:S(2)}, u32[]{:S(2)}) collective-permute-start(bf16[128,1024]{1,0:T(8,128)(2,1)S(1)} %get-tuple-element.60.refs_0_), channel_id=1, source_target_pairs={{0,2},{1,3},{2,0},{3,1},{4,6},{5,7},{6,4},{7,5},{8,10},{9,11},{10,... | collective-permute-start | bytes 786440 | tf_op jit(solution)/shard_map/ppermute | solution.py:476
  42.4 5.6 %copy-start.7 = (bf16[512,512]{1,0:T(8,128)(2,1)S(1)}, bf16[512,512]{1,0:T(8,128)(2,1)}, u32[]{:S(2)}) copy-start(bf16[512,512]{1,0:T(8,128)(2,1)} %copy-done.6) | copy-start | bytes 1572868
  46.0 2.0 %collective-permute-start.10 = (bf16[256,1024]{1,0:T(8,128)(2,1)S(1)}, bf16[256,1024]{1,0:T(8,128)(2,1)S(1)}, u32[]{:S(2)}, u32[]{:S(2)}) collective-permute-start(bf16[256,1024]{1,0:T(8,128)(2,1)S(1)} %shard_map.141.refs_0_), channel_id=1, source_target_pairs={{0,1},{1,0},{2,3},{3,2},{4,5},{5,4},{6,7},{7,6},{8,9},{9,8},{10,11... | collective-permute-start | bytes 1572872 | tf_op jit(solution)/shard_map/ppermute | solution.py:476
  46.1 3.7 %collective-permute-start.7 = (bf16[128,3072]{1,0:T(8,128)(2,1)S(1)}, bf16[128,3072]{1,0:T(8,128)(2,1)S(1)}, u32[]{:S(2)}, u32[]{:S(2)}) collective-permute-start(bf16[128,3072]{1,0:T(8,128)(2,1)S(1)} %get-tuple-element.68.refs_0_), channel_id=1, source_target_pairs={{0,1},{1,0},{2,3},{3,2},{4,5},{5,4},{6,7},{7,6},{8,9},{9,8},{10,11... | collective-permute-start | bytes 2359304 | tf_op jit(solution)/shard_map/ppermute | solution.py:476
  46.6 3.3 %collective-permute-start.8 = (bf16[128,2048]{1,0:T(8,128)(2,1)S(1)}, bf16[128,2048]{1,0:T(8,128)(2,1)S(1)}, u32[]{:S(2)}, u32[]{:S(2)}) collective-permute-start(bf16[128,2048]{1,0:T(8,128)(2,1)S(1)} %shard_map.140.refs_2_.refs_1_), channel_id=1, source_target_pairs={{0,1},{1,0},{2,3},{3,2},{4,5},{5,4},{6,7},{7,6},{8,9},{9,8},{10,11... | collective-permute-start | bytes 1572872 | tf_op jit(solution)/shard_map/ppermute | solution.py:476
  49.7 14.8 %collective-permute-start.20 = (bf16[4,64,1024]{2,1,0:T(8,128)(2,1)S(1)}, bf16[4,64,1024]{2,1,0:T(8,128)(2,1)S(1)}, u32[]{:S(2)}, u32[]{:S(2)}) collective-permute-start(bf16[4,64,1024]{2,1,0:T(8,128)(2,1)S(1)} %get-tuple-element.80), channel_id=1, source_target_pairs={{0,4},{1,5},{2,6},{3,7},{4,0},{5,1},{6,2},{7,3},{8,12},{9,13},{10,... | collective-permute-start | bytes 1572872 | tf_op jit(solution)/shard_map/ppermute | solution.py:476
  50.9 19.2 %collective-permute-start.11 = (bf16[4,256,128]{2,1,0:T(8,128)(2,1)S(1)}, bf16[4,256,128]{2,1,0:T(8,128)(2,1)S(1)}, u32[]{:S(2)}, u32[]{:S(2)}) collective-permute-start(bf16[4,256,128]{2,1,0:T(8,128)(2,1)S(1)} %get-tuple-element.73), channel_id=1, source_target_pairs={{0,4},{1,5},{2,6},{3,7},{4,0},{5,1},{6,2},{7,3},{8,12},{9,13},{10,... | collective-permute-start | bytes 786440 | tf_op jit(solution)/shard_map/ppermute | solution.py:476
  52.9 17.8 %collective-permute-start.12 = (bf16[4,256,128]{2,1,0:T(8,128)(2,1)S(1)}, bf16[4,256,128]{2,1,0:T(8,128)(2,1)S(1)}, u32[]{:S(2)}, u32[]{:S(2)}) collective-permute-start(bf16[4,256,128]{2,1,0:T(8,128)(2,1)S(1)} %get-tuple-element.74), channel_id=1, source_target_pairs={{0,2},{1,3},{2,0},{3,1},{4,6},{5,7},{6,4},{7,5},{8,10},{9,11},{10,... | collective-permute-start | bytes 786440 | tf_op jit(solution)/shard_map/ppermute | solution.py:476
  54.4 21.4 %collective-permute-start.13 = (bf16[4,256,128]{2,1,0:T(8,128)(2,1)S(1)}, bf16[4,256,128]{2,1,0:T(8,128)(2,1)S(1)}, u32[]{:S(2)}, u32[]{:S(2)}) collective-permute-start(bf16[4,256,128]{2,1,0:T(8,128)(2,1)S(1)} %get-tuple-element.75), channel_id=1, source_target_pairs={{0,6},{1,7},{2,4},{3,5},{4,2},{5,3},{6,0},{7,1},{8,14},{9,15},{10,... | collective-permute-start | bytes 786440 | tf_op jit(solution)/shard_map/ppermute | solution.py:476
  64.6 11.5 %collective-permute-start.21 = (bf16[1,64,1024]{2,1,0:T(8,128)(2,1)S(1)}, bf16[1,64,1024]{2,1,0:T(8,128)(2,1)S(1)}, u32[]{:S(2)}, u32[]{:S(2)}) collective-permute-start(bf16[1,64,1024]{2,1,0:T(8,128)(2,1)S(1)} %get-tuple-element.83), channel_id=1, source_target_pairs={{0,8},{1,9},{2,10},{3,11},{4,12},{5,13},{6,14},{7,15},{8,0},{9,1},... | collective-permute-start | bytes 393224 | tf_op jit(solution)/shard_map/ppermute | solution.py:476
  64.7 11.4 %collective-permute-start.22 = (bf16[1,64,1024]{2,1,0:T(8,128)(2,1)S(1)}, bf16[1,64,1024]{2,1,0:T(8,128)(2,1)S(1)}, u32[]{:S(2)}, u32[]{:S(2)}) collective-permute-start(bf16[1,64,1024]{2,1,0:T(8,128)(2,1)S(1)} %get-tuple-element.84), channel_id=1, source_target_pairs={{0,16},{1,17},{2,18},{3,19},{4,20},{5,21},{6,22},{7,23},{8,24},{9,... | collective-permute-start | bytes 393224 | tf_op jit(solution)/shard_map/ppermute | solution.py:476
  70.1 6.9 %collective-permute-start.23 = (bf16[1,64,1024]{2,1,0:T(8,128)(2,1)S(1)}, bf16[1,64,1024]{2,1,0:T(8,128)(2,1)S(1)}, u32[]{:S(2)}, u32[]{:S(2)}) collective-permute-start(bf16[1,64,1024]{2,1,0:T(8,128)(2,1)S(1)} %get-tuple-element.85), channel_id=1, source_target_pairs={{0,24},{1,25},{2,26},{3,27},{4,28},{5,29},{6,30},{7,31},{8,16},{9,... | collective-permute-start | bytes 393224 | tf_op jit(solution)/shard_map/ppermute | solution.py:476
  76.0 6.9 %collective-permute-start.14 = (bf16[1,256,128]{2,1,0:T(8,128)(2,1)S(1)}, bf16[1,256,128]{2,1,0:T(8,128)(2,1)S(1)}, u32[]{:S(2)}, u32[]{:S(2)}) collective-permute-start(bf16[1,256,128]{2,1,0:T(8,128)(2,1)S(1)} %get-tuple-element.77), channel_id=1, source_target_pairs={{0,8},{1,9},{2,10},{3,11},{4,12},{5,13},{6,14},{7,15},{8,0},{9,1},... | collective-permute-start | bytes 196616 | tf_op jit(solution)/shard_map/ppermute | solution.py:476
  77.1 10.9 %collective-permute-start.26 = (bf16[1,64,1024]{2,1,0:T(8,128)(2,1)S(1)}, bf16[1,64,1024]{2,1,0:T(8,128)(2,1)S(1)}, u32[]{:S(2)}, u32[]{:S(2)}) collective-permute-start(bf16[1,64,1024]{2,1,0:T(8,128)(2,1)S(1)} %shard_map.148.refs_0_), channel_id=1, source_target_pairs={{0,3},{1,2},{2,1},{3,0},{4,7},{5,6},{6,5},{7,4},{8,11},{9,10},{10,... | collective-permute-start | bytes 393224 | tf_op jit(solution)/shard_map/ppermute | solution.py:476
  77.1 5.7 %collective-permute-start.15 = (bf16[1,256,128]{2,1,0:T(8,128)(2,1)S(1)}, bf16[1,256,128]{2,1,0:T(8,128)(2,1)S(1)}, u32[]{:S(2)}, u32[]{:S(2)}) collective-permute-start(bf16[1,256,128]{2,1,0:T(8,128)(2,1)S(1)} %get-tuple-element.78), channel_id=1, source_target_pairs={{0,16},{1,17},{2,18},{3,19},{4,20},{5,21},{6,22},{7,23},{8,24},{9,... | collective-permute-start | bytes 196616 | tf_op jit(solution)/shard_map/ppermute | solution.py:476
  79.7 6.7 %collective-permute-start.16 = (bf16[1,256,128]{2,1,0:T(8,128)(2,1)S(1)}, bf16[1,256,128]{2,1,0:T(8,128)(2,1)S(1)}, u32[]{:S(2)}, u32[]{:S(2)}) collective-permute-start(bf16[1,256,128]{2,1,0:T(8,128)(2,1)S(1)} %get-tuple-element.79), channel_id=1, source_target_pairs={{0,24},{1,25},{2,26},{3,27},{4,28},{5,29},{6,30},{7,31},{8,16},{9,... | collective-permute-start | bytes 196616 | tf_op jit(solution)/shard_map/ppermute | solution.py:476
  81.9 6.4 %collective-permute-start.25 = (bf16[1,64,1024]{2,1,0:T(8,128)(2,1)S(1)}, bf16[1,64,1024]{2,1,0:T(8,128)(2,1)S(1)}, u32[]{:S(2)}, u32[]{:S(2)}) collective-permute-start(bf16[1,64,1024]{2,1,0:T(8,128)(2,1)S(1)} %shard_map.148.refs_0_), channel_id=1, source_target_pairs={{0,2},{1,3},{2,0},{3,1},{4,6},{5,7},{6,4},{7,5},{8,10},{9,11},{10,... | collective-permute-start | bytes 393224 | tf_op jit(solution)/shard_map/ppermute | solution.py:476
  82.9 5.5 %collective-permute-start.24 = (bf16[1,64,1024]{2,1,0:T(8,128)(2,1)S(1)}, bf16[1,64,1024]{2,1,0:T(8,128)(2,1)S(1)}, u32[]{:S(2)}, u32[]{:S(2)}) collective-permute-start(bf16[1,64,1024]{2,1,0:T(8,128)(2,1)S(1)} %shard_map.148.refs_0_), channel_id=1, source_target_pairs={{0,1},{1,0},{2,3},{3,2},{4,5},{5,4},{6,7},{7,6},{8,9},{9,8},{10,11... | collective-permute-start | bytes 393224 | tf_op jit(solution)/shard_map/ppermute | solution.py:476
  86.4 4.5 %collective-permute-start.19 = (bf16[1,256,128]{2,1,0:T(8,128)(2,1)S(1)}, bf16[1,256,128]{2,1,0:T(8,128)(2,1)S(1)}, u32[]{:S(2)}, u32[]{:S(2)}) collective-permute-start(bf16[1,256,128]{2,1,0:T(8,128)(2,1)S(1)} %shard_map.146.refs_0_), channel_id=1, source_target_pairs={{0,3},{1,2},{2,1},{3,0},{4,7},{5,6},{6,5},{7,4},{8,11},{9,10},{10,... | collective-permute-start | bytes 196616 | tf_op jit(solution)/shard_map/ppermute | solution.py:476
  86.5 5.8 %collective-permute-start.18 = (bf16[1,256,128]{2,1,0:T(8,128)(2,1)S(1)}, bf16[1,256,128]{2,1,0:T(8,128)(2,1)S(1)}, u32[]{:S(2)}, u32[]{:S(2)}) collective-permute-start(bf16[1,256,128]{2,1,0:T(8,128)(2,1)S(1)} %shard_map.146.refs_0_), channel_id=1, source_target_pairs={{0,2},{1,3},{2,0},{3,1},{4,6},{5,7},{6,4},{7,5},{8,10},{9,11},{10,... | collective-permute-start | bytes 196616 | tf_op jit(solution)/shard_map/ppermute | solution.py:476
  87.9 4.3 %collective-permute-start.17 = (bf16[1,256,128]{2,1,0:T(8,128)(2,1)S(1)}, bf16[1,256,128]{2,1,0:T(8,128)(2,1)S(1)}, u32[]{:S(2)}, u32[]{:S(2)}) collective-permute-start(bf16[1,256,128]{2,1,0:T(8,128)(2,1)S(1)} %shard_map.146.refs_0_), channel_id=1, source_target_pairs={{0,1},{1,0},{2,3},{3,2},{4,5},{5,4},{6,7},{7,6},{8,9},{9,8},{10,11... | collective-permute-start | bytes 196616 | tf_op jit(solution)/shard_map/ppermute | solution.py:476

commit v4 on v3

--- a/solution.py
+++ b/solution.py
@@ -15,7 +15,7 @@
 F32 = jnp.float32
 BF16 = jnp.bfloat16
 BOTH = ("slab", "case")
-VMEM_BYTES = 16 * 1024 * 1024
+VMEM_BYTES = 24 * 1024 * 1024
 
 
 def dot(a, b):
@@ -203,18 +203,20 @@
     quarter = lax.axis_index("case")
     units = w_up_ref.shape[1]
     fine = units // slabs // 4
-    pack = LANES // fine
-    rows = lax.broadcasted_iota(jnp.int32, (4 * LANES, LANES), 0)
-    cols = lax.broadcasted_iota(jnp.int32, (4 * LANES, LANES), 1)
-    wanted = (cols // fine) * (4 * fine) + quarter * fine + (cols & (fine - 1))
-    pick = (rows == wanted).astype(F32).astype(BF16)
-    for group in range(slabs // pack):
-        up_ref[:, group * LANES : (group + 1) * LANES] = dot(
-            w_up_ref[:, group * 4 * LANES : (group + 1) * 4 * LANES], pick
-        ).astype(BF16)
-    for block in range(slabs):
-        start = pl.multiple_of((block * 4 + quarter) * fine, 8)
-        down_ref[block * fine : (block + 1) * fine, :] = w_down_ref[pl.ds(start, fine), :]
+    rows = lax.broadcasted_iota(jnp.int32, (8 * LANES, LANES), 0)
+    cols = lax.broadcasted_iota(jnp.int32, (8 * LANES, LANES), 1)
+    for flip in range(2):
+        x = (lax.axis_index("slab") & 1) ^ flip
+        wanted = ((cols // fine * 2 + x) * 4 + quarter) * fine + (cols & (fine - 1))
+        pick = (rows == wanted).astype(F32).astype(BF16)
+        start = flip * units // 8
+        for group in range(units // 8 // LANES):
+            up_ref[:, start + group * LANES : start + (group + 1) * LANES] = dot(
+                w_up_ref[:, group * 8 * LANES : (group + 1) * 8 * LANES], pick
+            ).astype(BF16)
+        for z in range(slabs // 2):
+            at = pl.multiple_of(((z * 2 + x) * 4 + quarter) * fine, 8)
+            down_ref[start + z * fine : start + (z + 1) * fine, :] = w_down_ref[pl.ds(at, fine), :]
 
 
 def lines_kernel(sizes, parts, *refs):
@@ -294,10 +296,15 @@
     )
 
 
-def join_kernel(a_ref, b_ref, out_ref):
-    rows = a_ref.shape[0]
-    out_ref[:rows, :] = a_ref[...]
-    out_ref[rows:, :] = b_ref[...]
+def copy_kernel(in_ref, out_ref):
+    out_ref[...] = in_ref[...]
+
+
+def join_kernel(*refs):
+    out_ref = refs[-1]
+    rows = refs[0].shape[0]
+    for j, ref in enumerate(refs[:-1]):
+        out_ref[j * rows : (j + 1) * rows, :] = ref[...]
 
 
 def plane_grads_kernel(sizes, parts, *refs):
@@ -338,21 +345,28 @@
             ]
 
 
-def grads_mlp_kernel(factor, here_ref, there_ref, w_up_ref, w_down_ref, keep_ref, send_ref, down, up):
+def grads_mlp_kernel(factor, shift, here_ref, there_ref, w_up_ref, w_down_ref, *refs):
+    outs, down, up = refs[:-2], refs[-2], refs[-1]
     width, units = w_up_ref.shape
-    x, _, _, _ = place()
+    slab = lax.axis_index("slab")
+    digit = (slab >> shift) & (len(outs) - 1)
     hidden = jnp.concatenate([ref[:, :width] for ref in (here_ref, there_ref)], axis=0)
     cot = jnp.concatenate([ref[:, width:] for ref in (here_ref, there_ref)], axis=0)
-    active, slope = gelu_parts(dot(hidden, w_up_ref[...]))
-    grad_upper = (dot_nt(cot, w_down_ref[...]) * slope).astype(BF16)
-    down[...] = dot_tn(active, cot) * factor
-    up[...] = dot_tn(hidden, grad_upper) * factor
-    spans, rows = keep_ref.shape[:2]
-    for flip, out in ((0, keep_ref), (1, send_ref)):
-        for z in range(spans):
-            at = pl.ds(pl.multiple_of((z * 2 + (x ^ flip)) * rows, 8), rows)
-            out[z, :, :width] = down[at, :].astype(BF16)
-            out[z, :, width:] = up[at, :].astype(BF16)
+    half = units // 2
+    for at in (0, half):
+        active, slope = gelu_parts(dot(hidden, w_up_ref[:, at : at + half]))
+        grad_upper = (dot_nt(cot, w_down_ref[at : at + half, :]) * slope).astype(BF16)
+        up[:, at : at + half] = dot_tn(hidden, grad_upper) * factor
+        if at == 0:
+            down[...] = dot_tn(active, cot) * factor
+    rest, rows = outs[0].shape[:2]
+    for j, out in enumerate(outs):
+        for k in range(rest):
+            z = (digit ^ j) * rest + k
+            at = pl.ds(pl.multiple_of(z * rows, 8), rows)
+            out[k, :, :width] = down[at, :].astype(BF16)
+            at = pl.ds(pl.multiple_of((z * 2 + (slab & 1)) * rows, 8), rows)
+            out[k, :, width:] = up[at, :].astype(BF16)
 
 
 def grads_qkv_kernel(factor, width, slabs, za_ref, zb_ref, pa_ref, pb_ref, *refs):
@@ -424,15 +438,24 @@
     ]
     for copy in copies:
         copy.start()
-    case = lax.axis_index("case")
+    case, x = lax.axis_index("case"), lax.axis_index("slab") & 1
+    eighth, fine = units // 8, units // 4 // slabs
     for j in range(4):
-        held[case ^ j] = pieces[j][0].astype(F32)
-    fine = units // 4 // slabs
+        piece = pieces[j][0].astype(F32)
+        held[case ^ j, :, :width] = piece[:, :width]
+        for flip in range(2):
+            at = pl.multiple_of(width + (x ^ flip) * eighth, LANES)
+            held[case ^ j, :, pl.ds(at, eighth)] = piece[
+                :, width + flip * eighth : width + (flip + 1) * eighth
+            ]
     for quarter in range(4):
         down[quarter * rows : (quarter + 1) * rows, :] = held[quarter, :, :width]
     for block in range(slabs):
         up[:, block * 4 * fine : (block + 1) * 4 * fine] = jnp.concatenate(
-            [held[quarter, :, width + block * fine : width + (block + 1) * fine] for quarter in range(4)],
+            [
+                held[quarter, :, pl.ds(width + block % 2 * eighth + block // 2 * fine, fine)]
+                for quarter in range(4)
+            ],
             axis=1,
         )
     for copy in copies:
@@ -517,7 +540,7 @@
         w_out,
         after=[w_up_mine],
     )
-    shared_y = permute(shared, 0, 2)
+    shared_x, shared_y = permute(shared, 1, 0), permute(shared, 0, 2)
     grad_mixed, grad_residual = call(
         mlp_kernel,
         [rows_bf, shape_of((count, width), F32)],
@@ -539,6 +562,9 @@
         gain_one,
         w_qkv,
     )
+    (back,) = call(
+        copy_kernel, [shape_of((count, 2 * width), BF16)], back, after=[shared_x, shared_y]
+    )
     back = lax.all_to_all(back, "slab", split_axis=0, concat_axis=0, tiled=True)
     pack_z_core = permute(pack_z, 0, 1)
     (pack_p,) = call(
@@ -551,17 +577,26 @@
         scratch=[pltpu.VMEM((count, 3 * width), BF16)],
     )
     (around,) = call(
-        join_kernel, [shape_of((2 * count, 2 * width), BF16)], shared, shared_y, after=[pack_p]
-    )
-    big_keep, big_send = call(
-        functools.partial(grads_mlp_kernel, factor),
-        [shape_of((spans, rows, 2 * width), BF16)] * 2,
+        join_kernel,
+        [shape_of((4 * count, 2 * width), BF16)],
+        shared,
+        shared_x,
+        shared_y,
+        permute(shared_x, 0, 2),
+        after=[pack_p],
+    )
+    radix = min(4, spans)
+    shift = (slabs // radix).bit_length() - 1
+    big = call(
+        functools.partial(grads_mlp_kernel, factor, shift),
+        [shape_of((spans // radix, rows, 2 * width), BF16)] * radix,
         around,
         permute(around, 0, 1),
         w_up_mine,
         w_down_mine,
-        scratch=[pltpu.VMEM((units // 4, width), F32), pltpu.VMEM((width, units // 4), F32)],
-    )
+        scratch=[pltpu.VMEM((units // 8, width), F32), pltpu.VMEM((width, units // 4), F32)],
+    )
+    early = big[0]
     small = call(
         functools.partial(grads_qkv_kernel, factor, width, slabs),
         [shape_of((spans, rows * (width // LANES), LANES), BF16)] * 4,
@@ -569,7 +604,6 @@
         pack_z_core,
         pack_p,
         permute(pack_p, 0, 1),
-        after=[big_keep],
         scratch=[pltpu.VMEM((width, width), F32)],
     )
     ready = small[0]
@@ -582,26 +616,27 @@
         hold_x,
         gain_one,
         w_qkv,
-        after=[ready],
-    )
-
-    def reduce_z(pieces, after=()):
+        after=[ready, early],
+    )
+
+    def reduce_z(split):
         left = spans
-        while left > 1:
-            radix = min(4, left)
+        while True:
+            radix = len(split)
             left //= radix
             shift = (left * 2).bit_length() - 1
-            split = fold(shift, radix, pieces, after)
             pieces = [split[0]] + [permute(split[j], j << shift, 0) for j in range(1, radix)]
-        return pieces
-
-    def gather(pieces, after=()):
-        (last,) = fold(0, 1, pieces, after)
+            if left == 1:
+                return pieces
+            radix = min(4, left)
+            split = fold((left // radix * 2).bit_length() - 1, radix, pieces)
+
+    def gather(last):
         return [last] + [permute(last, 0, j) for j in range(1, 4)]
 
-    big = reduce_z([big_keep, permute(big_send, 1, 0)], [flag])
-    small = reduce_z(small)
-    big = gather(big, [small[0]])
+    big = reduce_z(big)
+    small = reduce_z(fold(shift, radix, small, [flag]))
+    big = gather(fold(0, 1, big, [small[0]])[0])
     full_up, full_down, full_two, w_rows = call(
         functools.partial(place_mlp_kernel, slabs, width, units),
         [
@@ -621,7 +656,7 @@
             pltpu.SemaphoreType.DMA((2,)),
         ],
     )
-    small = gather(small)
+    small = gather(fold(0, 1, small)[0])
     full_qkv, full_out, full_one = call(
         functools.partial(place_qkv_kernel, slabs, width),
         [shape_of((rows, 3 * width), F32), shape_of((rows, width), F32), shape_of((1, rows), F32)],

time: 93.5 us -> 89.5 us (0.957)
  waiting for transfers between devices: 34.2 us -> 24.8 us
  starting transfers between devices: 32.3 us -> 35.9 us
  Pallas kernels: 21 us -> 22.7 us
    ppermute x27 -> x28, waiting for transfers between devices: 27.5 us -> 17.1 us  [permute(): lax.ppermute(array, BOTH, swap_pairs(slabs, cases, flip_slab, flip_case))]
    ppermute x27 -> x28, starting transfers between devices: 27.9 us -> 31.3 us  [permute(): lax.ppermute(array, BOTH, swap_pairs(slabs, cases, flip_slab, flip_case))]
    pallas_call x16, Pallas kernels: 21 us -> 22.7 us  [call(): pl.pallas_call(run, out_shape=outs, in_specs=[vmem if one else far for on...]
    all_to_all x1, waiting for transfers between devices: 6.7 us -> 7.71 us  [body(): back = lax.all_to_all(back, 'slab', split_axis=0, concat_axis=0, tiled=True)]
    unnamed x22 -> x24, local copies, waits for them, and re-layouts: 4.8 us -> 5 us
  transfers between devices with their start and end apart: 28 -> 29, of which waited for: 10 -> 12; matrix products, arithmetic and copies ran while one was open for 0% -> 0% of each run, Pallas kernels for 11% -> 19%
where the time goes in v4:
time: 89.5 us; the launch traced here: 89.2 us
  starting transfers between devices  35.9 us (40%)
  waiting for transfers between devices  24.8 us (28%)
  Pallas kernels  22.7 us (25%)
  local copies, waits for them, and re-layouts  5 us (6%)
    ppermute x28, starting transfers between devices, permute(): lax.ppermute(array, BOTH, swap_pairs(slabs, cases, flip_slab, flip_case))  31.3 us
    pallas_call x16, Pallas kernels, call(): pl.pallas_call(run, out_shape=outs, in_specs=[vmem if one else far for on...  22.7 us
    ppermute x28, waiting for transfers between devices, permute(): lax.ppermute(array, BOTH, swap_pairs(slabs, cases, flip_slab, flip_case))  17.1 us
    all_to_all x1, waiting for transfers between devices, body(): back = lax.all_to_all(back, 'slab', split_axis=0, concat_axis=0, tiled=True)  7.71 us
    unnamed x24, local copies, waits for them, and re-layouts  5 us
    all_to_all x1, starting transfers between devices, body(): back = lax.all_to_all(back, 'slab', split_axis=0, concat_axis=0, tiled=True)  4.59 us
  transfers between devices with their start and end apart: 29, of which 12 were waited for; matrix products, arithmetic and copies ran while one was open for 0% of the time, Pallas kernels for 19%

profile of v4, /device:TPU:0, one launch (start us, length us, event | category | flops | bytes accessed | tf_op | source)
XLA Modules:
  0.0 89.2 jit_solution(7594514561114711544)
XLA Ops:
  0.6 2.9 %shard_map.135 = (bf16[16,1536]{1,0:T(8,128)(2,1)S(1)}, bf16[16,1536]{1,0:T(8,128)(2,1)S(1)}, bf16[16,1536]{1,0:T(8,128)(2,1)S(1)}, bf16[16,1536]{1,0:T(8,128)(2...) custom-call(bf16[128,512]{1,0:T(8,128)(2,1)} %bitcast.20, ...), custom_call_target="tpu_custom_call" | custom-call | flops 10000000 | bytes 10000 | tf_op jit(solution)/shard_map/pallas_call | solution.py:50
  3.5 3.0 %collective-permute-start = (bf16[16,1536]{1,0:T(8,128)(2,1)S(1)}, bf16[16,1536]{1,0:T(8,128)(2,1)S(1)}, u32[]{:S(2)}, u32[]{:S(2)}) collective-permute-start(bf16[16,1536]{1,0:T(8,128)(2,1)S(1)} %get-tuple-element.49), channel_id=1, source_target_pairs={{0,4},{1,5},{2,6},{3,7},{4,0},{5,1},{6,2},{7,3},{8,12},{9,13},{10,... | collective-permute-start | bytes 147464 | tf_op jit(solution)/shard_map/ppermute | solution.py:499
  6.5 1.6 %collective-permute-start.1 = (bf16[16,1536]{1,0:T(8,128)(2,1)S(1)}, bf16[16,1536]{1,0:T(8,128)(2,1)S(1)}, u32[]{:S(2)}, u32[]{:S(2)}) collective-permute-start(bf16[16,1536]{1,0:T(8,128)(2,1)S(1)} %get-tuple-element.50), channel_id=1, source_target_pairs={{0,8},{1,9},{2,10},{3,11},{4,12},{5,13},{6,14},{7,15},{8,0},{9,1},... | collective-permute-start | bytes 147464 | tf_op jit(solution)/shard_map/ppermute | solution.py:499
  8.1 0.0 collective-permute-start.2
  8.1 3.0 %collective-permute-start.3 = (bf16[16,1536]{1,0:T(8,128)(2,1)S(1)}, bf16[16,1536]{1,0:T(8,128)(2,1)S(1)}, u32[]{:S(2)}, u32[]{:S(2)}) collective-permute-start(bf16[16,1536]{1,0:T(8,128)(2,1)S(1)} %get-tuple-element.52), channel_id=1, source_target_pairs={{0,16},{1,17},{2,18},{3,19},{4,20},{5,21},{6,22},{7,23},{8,24},{9,... | collective-permute-start | bytes 147464 | tf_op jit(solution)/shard_map/ppermute | solution.py:499
  11.1 1.3 %collective-permute-start.4 = (bf16[16,1536]{1,0:T(8,128)(2,1)S(1)}, bf16[16,1536]{1,0:T(8,128)(2,1)S(1)}, u32[]{:S(2)}, u32[]{:S(2)}) collective-permute-start(bf16[16,1536]{1,0:T(8,128)(2,1)S(1)} %get-tuple-element.53), channel_id=1, source_target_pairs={{0,20},{1,21},{2,22},{3,23},{4,16},{5,17},{6,18},{7,19},{8,28},{9,... | collective-permute-start | bytes 147464 | tf_op jit(solution)/shard_map/ppermute | solution.py:499
  12.4 3.6 %collective-permute-start.5 = (bf16[16,1536]{1,0:T(8,128)(2,1)S(1)}, bf16[16,1536]{1,0:T(8,128)(2,1)S(1)}, u32[]{:S(2)}, u32[]{:S(2)}) collective-permute-start(bf16[16,1536]{1,0:T(8,128)(2,1)S(1)} %get-tuple-element.54), channel_id=1, source_target_pairs={{0,24},{1,25},{2,26},{3,27},{4,28},{5,29},{6,30},{7,31},{8,16},{9,... | collective-permute-start | bytes 147464 | tf_op jit(solution)/shard_map/ppermute | solution.py:499
  16.0 0.0 collective-permute-start.6
  16.1 1.7 %copy-done.1 = bf16[512,2048]{1,0:T(8,128)(2,1)S(1)} copy-done((bf16[512,2048]{1,0:T(8,128)(2,1)S(1)}, bf16[512,2048]{1,0:T(8,128)(2,1)}, u32[]{:S(2)}) %copy-start.1) | copy-done | bytes 2097176
  17.8 1.6 %copy-done.3 = bf16[2048,512]{1,0:T(8,128)(2,1)S(1)} copy-done((bf16[2048,512]{1,0:T(8,128)(2,1)S(1)}, bf16[2048,512]{1,0:T(8,128)(2,1)}, u32[]{:S(2)}) %copy-start.3) | copy-done | bytes 2097176
  19.4 1.3 %shard_map.136 = (bf16[512,512]{1,0:T(8,128)(2,1)S(1)}, bf16[512,512]{1,0:T(8,128)(2,1)S(1)}) custom-call(bf16[512,2048]{1,0:T(8,128)(2,1)S(1)} %copy-done.1, bf16[2048,512]{1,0:T(8,128)(2,1)S(1)} %copy-done.3), custom_call_target="tpu_custom_call" | custom-call | flops 10000000 | bytes 10000 | tf_op jit(solution)/shard_map/pallas_call | solution.py:50
  20.7 0.0 copy-start.8
  20.7 0.8 copy-done.8
  21.5 0.0 collective-permute-done.3.refs_4_
  21.5 0.0 collective-permute-done.4.refs_5_
  21.5 1.3 %collective-permute-done.6.refs_7_ = bf16[16,1536]{1,0:T(8,128)(2,1)S(1)} collective-permute-done((bf16[16,1536]{1,0:T(8,128)(2,1)S(1)}, bf16[16,1536]{1,0:T(8,128)(2,1)S(1)}, u32[]{:S(2)}, u32[]{:S(2)}) %collective-permute-start.6) | collective-permute-done | bytes 49184 | tf_op jit(solution)/shard_map/ppermute | solution.py:499
  22.8 1.3 %shard_map.137 = (bf16[128,1024]{1,0:T(8,128)(2,1)S(1)}, bf16[128,1536]{1,0:T(8,128)(2,1)S(1)}, bf16[128,512]{1,0:T(8,128)(2,1)S(1)}, bf16[128,512]{1,0:T(8,128)(2,1)S(1)}, bf16[128,512]{1,0:T(8,128)(2,1)S(1)}) custom-call(bf16[16,1536]{1,0:T(8,128)(2,1)S(1)} %get-tuple-element.48.refs_0_, bf16[16,1536]{1,0:T(8,128)(2,1)S(1)} %collective-permute-done.refs_1_, ...), custom_call_target="tpu_custom_call" | custom-call | flops 10000000 | bytes 10000 | tf_op jit(solution)/shard_map/pallas_call | solution.py:50
  24.1 0.6 collective-permute-start.7
  24.7 1.5 %collective-permute-start.8 = (bf16[128,1024]{1,0:T(8,128)(2,1)S(1)}, bf16[128,1024]{1,0:T(8,128)(2,1)S(1)}, u32[]{:S(2)}, u32[]{:S(2)}) collective-permute-start(bf16[128,1024]{1,0:T(8,128)(2,1)S(1)} %get-tuple-element.58.refs_0_), channel_id=1, source_target_pairs={{0,2},{1,3},{2,0},{3,1},{4,6},{5,7},{6,4},{7,5},{8,10},{9,11},{10,... | collective-permute-start | bytes 786440 | tf_op jit(solution)/shard_map/ppermute | solution.py:499
  26.2 2.4 %shard_map.138 = (bf16[128,512]{1,0:T(8,128)(2,1)S(1)}, f32[128,512]{1,0:T(8,128)S(1)}) custom-call(bf16[128,1024]{1,0:T(8,128)(2,1)S(1)} %get-tuple-element.58.refs_0_, bf16[128,512]{1,0:T(8,128)(2,1)S(1)} %get-tuple-element.59.refs_1_, f32[1,512]{1,0:T(1,128)S(1)} %bitcast.18, bf16[512,512]{1,0:T(8,128)(2,1)S(1)} %copy-done.5, ...), custom_call_target="tpu_custom_call" | custom-call | flops 10000000 | bytes 10000 | tf_op jit(solution)/shard_map/pallas_call | solution.py:50
  28.6 2.7 %shard_map.139 = (bf16[128,1024]{1,0:T(8,128)(2,1)S(1)}, bf16[128,3072]{1,0:T(8,128)(2,1)S(1)}) custom-call(bf16[128,1536]{1,0:T(8,128)(2,1)S(1)} %get-tuple-element.57.refs_0_, bf16[128,512]{1,0:T(8,128)(2,1)S(1)} %get-tuple-element.60.refs_1_, f32[128,512]{1,0:T(8,128)S(1)} %get-tuple-element.61.refs_2_, bf16[128,512]{1,0:T(8,128)(2,1)S(1)} %get-tuple-element.62.refs_3_, ...), custom_call_target="tpu_custom_call" | custom-call | flops 10000000 | bytes 10000 | tf_op jit(solution)/shard_map/pallas_call | solution.py:50
  31.3 0.9 copy-done.6
  32.2 0.7 shard_map.140
  32.9 4.6 %all-to-all-start = ((bf16[8,16,1024]{2,1,0:T(8,128)(2,1)}), bf16[8,16,1024]{2,1,0:T(8,128)(2,1)S(1)}, u32[]{:S(2)}, u32[]{:S(2)}) async-start(bf16[8,16,1024]{2,1,0:T(8,128)(2,1)} %bitcast.4), calls=%async_computation | async-start | bytes 524288 | tf_op jit(solution)/shard_map/all_to_all | solution.py:568
  37.5 0.5 collective-permute-start.11
  38.0 7.7 %all-to-all-done = bf16[8,16,1024]{2,1,0:T(8,128)(2,1)S(1)} async-done(((bf16[8,16,1024]{2,1,0:T(8,128)(2,1)}), bf16[8,16,1024]{2,1,0:T(8,128)(2,1)S(1)}, u32[]{:S(2)}, u32[]{:S(2)}) %all-to-all-start) | async-done | bytes 262176 | tf_op jit(solution)/shard_map/all_to_all | solution.py:568
  45.7 2.6 %shard_map.141.refs_2_.refs_4_.refs_1_ = bf16[128,2048]{1,0:T(8,128)(2,1)S(1)} custom-call(bf16[128,1024]{1,0:T(8,128)(2,1)S(1)} %bitcast.9, bf16[128,512]{1,0:T(8,128)(2,1)S(1)} %get-tuple-element.65.refs_1_.refs_2_, f32[1,512]{1,0:T(1,128)S(1)} %bitcast.14, bf16[512,1536]{1,0:T(8,128)(2,1)S(1)} %copy-done), custom_call_target="tpu_custom_call" | custom-call | flops 10000000 | bytes 10000 | tf_op jit(solution)/shard_map/pallas_call | solution.py:50
  48.3 0.0 copy-start.9
  48.4 0.1 shard_map.143.refs_0_
  48.4 0.1 collective-permute-start.12
  48.5 0.5 collective-permute-start.9
  49.0 0.1 collective-permute-start.10
  49.1 3.2 %collective-permute-done.9.refs_1_ = bf16[128,3072]{1,0:T(8,128)(2,1)S(1)} collective-permute-done((bf16[128,3072]{1,0:T(8,128)(2,1)S(1)}, bf16[128,3072]{1,0:T(8,128)(2,1)S(1)}, u32[]{:S(2)}, u32[]{:S(2)}) %collective-permute-start.9) | collective-permute-done | bytes 786464 | tf_op jit(solution)/shard_map/ppermute | solution.py:499
  52.3 0.7 collective-permute-done.10.refs_3_
  53.0 1.0 %shard_map.142 = (bf16[4,256,128]{2,1,0:T(8,128)(2,1)S(1)}, bf16[4,256,128]{2,1,0:T(8,128)(2,1)S(1)}, bf16[4,256,128]{2,1,0:T(8,128)(2,1)S(1)}, bf16[4,256,128]{2,1,0:T(8,128)(2,1)S(1)}) custom-call(bf16[128,3072]{1,0:T(8,128)(2,1)S(1)} %copy-done.7, bf16[128,3072]{1,0:T(8,128)(2,1)S(1)} %collective-permute-done.9.refs_1_, ...), custom_call_target="tpu_custom_call" | custom-call | flops 10000000 | bytes 10000 | tf_op jit(solution)/shard_map/pallas_call | solution.py:50
  54.1 0.1 collective-permute-start.13
  54.2 0.5 collective-permute-start.14
  54.8 2.9 %collective-permute-start.15 = (bf16[4,256,128]{2,1,0:T(8,128)(2,1)S(1)}, bf16[4,256,128]{2,1,0:T(8,128)(2,1)S(1)}, u32[]{:S(2)}, u32[]{:S(2)}) collective-permute-start(bf16[4,256,128]{2,1,0:T(8,128)(2,1)S(1)} %get-tuple-element.73), channel_id=1, source_target_pairs={{0,6},{1,7},{2,4},{3,5},{4,2},{5,3},{6,0},{7,1},{8,14},{9,15},{10,... | collective-permute-start | bytes 786440 | tf_op jit(solution)/shard_map/ppermute | solution.py:499
  57.7 3.0 %shard_map.144 = (bf16[1,64,1024]{2,1,0:T(8,128)(2,1)S(1)}, bf16[1,64,1024]{2,1,0:T(8,128)(2,1)S(1)}, bf16[1,64,1024]{2,1,0:T(8,128)(2,1)S(1)}, bf16[1,64,1024]{2,1,0:T(8,128)(2,1)S(1)}) custom-call(bf16[512,1024]{1,0:T(8,128)(2,1)S(1)} %shard_map.143.refs_0_, bf16[512,1024]{1,0:T(8,128)(2,1)S(1)} %collective-permute-done.12.refs_1_, ...), custom_call_target="tpu_custom_call" | custom-call | flops 10000000 | bytes 10000 | tf_op jit(solution)/shard_map/pallas_call | solution.py:50
  60.7 0.1 collective-permute-start.22
  60.8 1.1 %collective-permute-start.23 = (bf16[1,64,1024]{2,1,0:T(8,128)(2,1)S(1)}, bf16[1,64,1024]{2,1,0:T(8,128)(2,1)S(1)}, u32[]{:S(2)}, u32[]{:S(2)}) collective-permute-start(bf16[1,64,1024]{2,1,0:T(8,128)(2,1)S(1)} %get-tuple-element.80), channel_id=1, source_target_pairs={{0,16},{1,17},{2,18},{3,19},{4,20},{5,21},{6,22},{7,23},{8,24},{9,... | collective-permute-start | bytes 393224 | tf_op jit(solution)/shard_map/ppermute | solution.py:499
  61.9 1.4 %collective-permute-done.13.refs_1_ = bf16[4,256,128]{2,1,0:T(8,128)(2,1)S(1)} collective-permute-done((bf16[4,256,128]{2,1,0:T(8,128)(2,1)S(1)}, bf16[4,256,128]{2,1,0:T(8,128)(2,1)S(1)}, u32[]{:S(2)}, u32[]{:S(2)}) %collective-permute-start.13) | collective-permute-done | bytes 262176 | tf_op jit(solution)/shard_map/ppermute | solution.py:499
  63.3 1.8 %collective-permute-start.24 = (bf16[1,64,1024]{2,1,0:T(8,128)(2,1)S(1)}, bf16[1,64,1024]{2,1,0:T(8,128)(2,1)S(1)}, u32[]{:S(2)}, u32[]{:S(2)}) collective-permute-start(bf16[1,64,1024]{2,1,0:T(8,128)(2,1)S(1)} %get-tuple-element.81), channel_id=1, source_target_pairs={{0,24},{1,25},{2,26},{3,27},{4,28},{5,29},{6,30},{7,31},{8,16},{9,... | collective-permute-start | bytes 393224 | tf_op jit(solution)/shard_map/ppermute | solution.py:499
  65.1 1.6 %shard_map.145 = (bf16[128,512]{1,0:T(8,128)(2,1)}, f32[8,128]{1,0:T(8,128)S(1)}) custom-call(bf16[128,1024]{1,0:T(8,128)(2,1)S(1)} %bitcast.10, bf16[128,2048]{1,0:T(8,128)(2,1)S(1)} %shard_map.141.refs_2_.refs_4_.refs_1_, bf16[128,512]{1,0:T(8,128)(2,1)S(1)} %get-tuple-element.65.refs_1_.refs_2_, f32[1,512]{1,0:T(1,128)S(1)} %bitcast.15, ...), custom_call_target="tpu_custom_call" | custom-call | flops 10000000 | bytes 10000 | tf_op jit(solution)/shard_map/pallas_call | solution.py:50
  66.7 1.5 %collective-permute-done.14.refs_2_ = bf16[4,256,128]{2,1,0:T(8,128)(2,1)S(1)} collective-permute-done((bf16[4,256,128]{2,1,0:T(8,128)(2,1)S(1)}, bf16[4,256,128]{2,1,0:T(8,128)(2,1)S(1)}, u32[]{:S(2)}, u32[]{:S(2)}) %collective-permute-start.14) | collective-permute-done | bytes 262176 | tf_op jit(solution)/shard_map/ppermute | solution.py:499
  68.2 0.1 shard_map.146
  68.4 1.2 %collective-permute-start.16 = (bf16[1,256,128]{2,1,0:T(8,128)(2,1)S(1)}, bf16[1,256,128]{2,1,0:T(8,128)(2,1)S(1)}, u32[]{:S(2)}, u32[]{:S(2)}) collective-permute-start(bf16[1,256,128]{2,1,0:T(8,128)(2,1)S(1)} %get-tuple-element.76), channel_id=1, source_target_pairs={{0,8},{1,9},{2,10},{3,11},{4,12},{5,13},{6,14},{7,15},{8,0},{9,1},... | collective-permute-start | bytes 196616 | tf_op jit(solution)/shard_map/ppermute | solution.py:499
  69.6 3.9 %collective-permute-done.23.refs_2_ = bf16[1,64,1024]{2,1,0:T(8,128)(2,1)S(1)} collective-permute-done((bf16[1,64,1024]{2,1,0:T(8,128)(2,1)S(1)}, bf16[1,64,1024]{2,1,0:T(8,128)(2,1)S(1)}, u32[]{:S(2)}, u32[]{:S(2)}) %collective-permute-start.23) | collective-permute-done | bytes 131104 | tf_op jit(solution)/shard_map/ppermute | solution.py:499
  73.5 0.1 shard_map.148.refs_0_
  73.5 0.1 collective-permute-start.25
  73.6 2.2 %collective-permute-start.17 = (bf16[1,256,128]{2,1,0:T(8,128)(2,1)S(1)}, bf16[1,256,128]{2,1,0:T(8,128)(2,1)S(1)}, u32[]{:S(2)}, u32[]{:S(2)}) collective-permute-start(bf16[1,256,128]{2,1,0:T(8,128)(2,1)S(1)} %get-tuple-element.77), channel_id=1, source_target_pairs={{0,16},{1,17},{2,18},{3,19},{4,20},{5,21},{6,22},{7,23},{8,24},{9,... | collective-permute-start | bytes 196616 | tf_op jit(solution)/shard_map/ppermute | solution.py:499
  75.8 2.2 %collective-permute-start.18 = (bf16[1,256,128]{2,1,0:T(8,128)(2,1)S(1)}, bf16[1,256,128]{2,1,0:T(8,128)(2,1)S(1)}, u32[]{:S(2)}, u32[]{:S(2)}) collective-permute-start(bf16[1,256,128]{2,1,0:T(8,128)(2,1)S(1)} %get-tuple-element.78), channel_id=1, source_target_pairs={{0,24},{1,25},{2,26},{3,27},{4,28},{5,29},{6,30},{7,31},{8,16},{9,... | collective-permute-start | bytes 196616 | tf_op jit(solution)/shard_map/ppermute | solution.py:499
  78.1 0.5 collective-permute-start.26
  78.5 0.7 collective-permute-start.27
  79.3 3.0 %collective-permute-done.17.refs_2_ = bf16[1,256,128]{2,1,0:T(8,128)(2,1)S(1)} collective-permute-done((bf16[1,256,128]{2,1,0:T(8,128)(2,1)S(1)}, bf16[1,256,128]{2,1,0:T(8,128)(2,1)S(1)}, u32[]{:S(2)}, u32[]{:S(2)}) %collective-permute-start.17) | collective-permute-done | bytes 65568 | tf_op jit(solution)/shard_map/ppermute | solution.py:499
  82.3 0.1 collective-permute-start.19
  82.4 0.6 collective-permute-start.20
  83.0 1.3 %collective-permute-start.21 = (bf16[1,256,128]{2,1,0:T(8,128)(2,1)S(1)}, bf16[1,256,128]{2,1,0:T(8,128)(2,1)S(1)}, u32[]{:S(2)}, u32[]{:S(2)}) collective-permute-start(bf16[1,256,128]{2,1,0:T(8,128)(2,1)S(1)} %shard_map.147.refs_0_), channel_id=1, source_target_pairs={{0,3},{1,2},{2,1},{3,0},{4,7},{5,6},{6,5},{7,4},{8,11},{9,10},{10,... | collective-permute-start | bytes 196616 | tf_op jit(solution)/shard_map/ppermute | solution.py:499
  84.3 0.2 collective-permute-done.26.refs_2_
  84.4 0.6 collective-permute-done.27.refs_3_
  85.1 2.1 %shard_map.149 = (f32[64,2048]{1,0:T(8,128)}, f32[256,512]{1,0:T(8,128)}, f32[1,64]{1,0:T(1,128)}, bf16[64,1536]{1,0:T(8,128)(2,1)S(1)}) custom-call(bf16[1,64,1024]{2,1,0:T(8,128)(2,1)S(1)} %shard_map.148.refs_0_, bf16[1,64,1024]{2,1,0:T(8,128)(2,1)S(1)} %collective-permute-done.25.refs_1_, bf16[1,64,1024]{2,1,0:T(8,128)(2,1)S(1)} %collective-permute-done.26.refs_2_, ...), custom_call_target="tpu_custom_call" | custom-call | flops 10000000 | bytes 10000 | tf_op jit(solution)/shard_map/pallas_call | solution.py:50
  87.1 1.0 %collective-permute-done.20.refs_2_ = bf16[1,256,128]{2,1,0:T(8,128)(2,1)S(1)} collective-permute-done((bf16[1,256,128]{2,1,0:T(8,128)(2,1)S(1)}, bf16[1,256,128]{2,1,0:T(8,128)(2,1)S(1)}, u32[]{:S(2)}, u32[]{:S(2)}) %collective-permute-start.20) | collective-permute-done | bytes 65568 | tf_op jit(solution)/shard_map/ppermute | solution.py:499
  88.1 0.2 collective-permute-done.21.refs_3_
  88.4 0.8 shard_map.150
  (34 shorter events, 0.1 us)
Async XLA Ops:
  3.5 8.9 %collective-permute-start = (bf16[16,1536]{1,0:T(8,128)(2,1)S(1)}, bf16[16,1536]{1,0:T(8,128)(2,1)S(1)}, u32[]{:S(2)}, u32[]{:S(2)}) collective-permute-start(bf16[16,1536]{1,0:T(8,128)(2,1)S(1)} %get-tuple-element.49), channel_id=1, source_target_pairs={{0,4},{1,5},{2,6},{3,7},{4,0},{5,1},{6,2},{7,3},{8,12},{9,13},{10,... | collective-permute-start | bytes 147464 | tf_op jit(solution)/shard_map/ppermute | solution.py:499
  6.5 9.5 %collective-permute-start.1 = (bf16[16,1536]{1,0:T(8,128)(2,1)S(1)}, bf16[16,1536]{1,0:T(8,128)(2,1)S(1)}, u32[]{:S(2)}, u32[]{:S(2)}) collective-permute-start(bf16[16,1536]{1,0:T(8,128)(2,1)S(1)} %get-tuple-element.50), channel_id=1, source_target_pairs={{0,8},{1,9},{2,10},{3,11},{4,12},{5,13},{6,14},{7,15},{8,0},{9,1},... | collective-permute-start | bytes 147464 | tf_op jit(solution)/shard_map/ppermute | solution.py:499
  8.1 13.4 %collective-permute-start.2 = (bf16[16,1536]{1,0:T(8,128)(2,1)S(1)}, bf16[16,1536]{1,0:T(8,128)(2,1)S(1)}, u32[]{:S(2)}, u32[]{:S(2)}) collective-permute-start(bf16[16,1536]{1,0:T(8,128)(2,1)S(1)} %get-tuple-element.51), channel_id=1, source_target_pairs={{0,12},{1,13},{2,14},{3,15},{4,8},{5,9},{6,10},{7,11},{8,4},{9,5},... | collective-permute-start | bytes 147464 | tf_op jit(solution)/shard_map/ppermute | solution.py:499
  8.1 13.4 %collective-permute-start.3 = (bf16[16,1536]{1,0:T(8,128)(2,1)S(1)}, bf16[16,1536]{1,0:T(8,128)(2,1)S(1)}, u32[]{:S(2)}, u32[]{:S(2)}) collective-permute-start(bf16[16,1536]{1,0:T(8,128)(2,1)S(1)} %get-tuple-element.52), channel_id=1, source_target_pairs={{0,16},{1,17},{2,18},{3,19},{4,20},{5,21},{6,22},{7,23},{8,24},{9,... | collective-permute-start | bytes 147464 | tf_op jit(solution)/shard_map/ppermute | solution.py:499
  11.1 10.3 %collective-permute-start.4 = (bf16[16,1536]{1,0:T(8,128)(2,1)S(1)}, bf16[16,1536]{1,0:T(8,128)(2,1)S(1)}, u32[]{:S(2)}, u32[]{:S(2)}) collective-permute-start(bf16[16,1536]{1,0:T(8,128)(2,1)S(1)} %get-tuple-element.53), channel_id=1, source_target_pairs={{0,20},{1,21},{2,22},{3,23},{4,16},{5,17},{6,18},{7,19},{8,28},{9,... | collective-permute-start | bytes 147464 | tf_op jit(solution)/shard_map/ppermute | solution.py:499
  12.4 9.1 %collective-permute-start.5 = (bf16[16,1536]{1,0:T(8,128)(2,1)S(1)}, bf16[16,1536]{1,0:T(8,128)(2,1)S(1)}, u32[]{:S(2)}, u32[]{:S(2)}) collective-permute-start(bf16[16,1536]{1,0:T(8,128)(2,1)S(1)} %get-tuple-element.54), channel_id=1, source_target_pairs={{0,24},{1,25},{2,26},{3,27},{4,28},{5,29},{6,30},{7,31},{8,16},{9,... | collective-permute-start | bytes 147464 | tf_op jit(solution)/shard_map/ppermute | solution.py:499
  16.0 6.8 %copy-start = (bf16[512,1536]{1,0:T(8,128)(2,1)S(1)}, bf16[512,1536]{1,0:T(8,128)(2,1)}, u32[]{:S(2)}) copy-start(bf16[512,1536]{1,0:T(8,128)(2,1)} %refs_6_.3) | copy-start | bytes 4718596
  16.0 6.8 %collective-permute-start.6 = (bf16[16,1536]{1,0:T(8,128)(2,1)S(1)}, bf16[16,1536]{1,0:T(8,128)(2,1)S(1)}, u32[]{:S(2)}, u32[]{:S(2)}) collective-permute-start(bf16[16,1536]{1,0:T(8,128)(2,1)S(1)} %get-tuple-element.55), channel_id=1, source_target_pairs={{0,28},{1,29},{2,30},{3,31},{4,24},{5,25},{6,26},{7,27},{8,20},{9,... | collective-permute-start | bytes 147464 | tf_op jit(solution)/shard_map/ppermute | solution.py:499
  16.1 1.7 %copy-start.1 = (bf16[512,2048]{1,0:T(8,128)(2,1)S(1)}, bf16[512,2048]{1,0:T(8,128)(2,1)}, u32[]{:S(2)}) copy-start(bf16[512,2048]{1,0:T(8,128)(2,1)} %refs_5_.3) | copy-start | bytes 6291460
  17.8 1.6 %copy-start.3 = (bf16[2048,512]{1,0:T(8,128)(2,1)S(1)}, bf16[2048,512]{1,0:T(8,128)(2,1)}, u32[]{:S(2)}) copy-start(bf16[2048,512]{1,0:T(8,128)(2,1)} %refs_5_.2) | copy-start | bytes 6291460
  19.4 3.5 %copy-start.5 = (bf16[512,512]{1,0:T(8,128)(2,1)S(1)}, bf16[512,512]{1,0:T(8,128)(2,1)}, u32[]{:S(2)}) copy-start(bf16[512,512]{1,0:T(8,128)(2,1)} %refs_3_.4) | copy-start | bytes 1572868
  19.4 3.5 %copy-start.10 = (f32[512]{0:T(512)S(1)}, f32[512]{0:T(512)}, u32[]{:S(2)}) copy-start(f32[512]{0:T(512)} %param.14) | copy-start | bytes 6148
  19.4 3.5 %copy-start.11 = (f32[512]{0:T(512)S(1)}, f32[512]{0:T(512)}, u32[]{:S(2)}) copy-start(f32[512]{0:T(512)} %param.15) | copy-start | bytes 6148
  19.4 6.8 %copy-start.4 = (bf16[2048,512]{1,0:T(8,128)(2,1)S(1)}, bf16[2048,512]{1,0:T(8,128)(2,1)}, u32[]{:S(2)}) copy-start(bf16[2048,512]{1,0:T(8,128)(2,1)} %refs_5_.2) | copy-start | bytes 6291460
  20.7 0.8 copy-start.8
  21.5 4.7 %copy-start.2 = (bf16[512,2048]{1,0:T(8,128)(2,1)S(1)}, bf16[512,2048]{1,0:T(8,128)(2,1)}, u32[]{:S(2)}) copy-start(bf16[512,2048]{1,0:T(8,128)(2,1)} %refs_5_.3) | copy-start | bytes 6291460
  24.1 8.1 %collective-permute-start.7 = (bf16[128,1024]{1,0:T(8,128)(2,1)S(1)}, bf16[128,1024]{1,0:T(8,128)(2,1)S(1)}, u32[]{:S(2)}, u32[]{:S(2)}) collective-permute-start(bf16[128,1024]{1,0:T(8,128)(2,1)S(1)} %get-tuple-element.58.refs_0_), channel_id=1, source_target_pairs={{0,4},{1,5},{2,6},{3,7},{4,0},{5,1},{6,2},{7,3},{8,12},{9,13},{10,... | collective-permute-start | bytes 786440 | tf_op jit(solution)/shard_map/ppermute | solution.py:499
  24.7 7.5 %collective-permute-start.8 = (bf16[128,1024]{1,0:T(8,128)(2,1)S(1)}, bf16[128,1024]{1,0:T(8,128)(2,1)S(1)}, u32[]{:S(2)}, u32[]{:S(2)}) collective-permute-start(bf16[128,1024]{1,0:T(8,128)(2,1)S(1)} %get-tuple-element.58.refs_0_), channel_id=1, source_target_pairs={{0,2},{1,3},{2,0},{3,1},{4,6},{5,7},{6,4},{7,5},{8,10},{9,11},{10,... | collective-permute-start | bytes 786440 | tf_op jit(solution)/shard_map/ppermute | solution.py:499
  31.3 0.9 %copy-start.6 = (bf16[128,3072]{1,0:T(8,128)(2,1)}, bf16[128,3072]{1,0:T(8,128)(2,1)S(1)}, u32[]{:S(2)}) copy-start(bf16[128,3072]{1,0:T(8,128)(2,1)S(1)} %get-tuple-element.66.refs_0_) | copy-start | bytes 2359300
  32.9 12.8 %all-to-all-start = ((bf16[8,16,1024]{2,1,0:T(8,128)(2,1)}), bf16[8,16,1024]{2,1,0:T(8,128)(2,1)S(1)}, u32[]{:S(2)}, u32[]{:S(2)}) async-start(bf16[8,16,1024]{2,1,0:T(8,128)(2,1)} %bitcast.4), calls=%async_computation | async-start | bytes 524288 | tf_op jit(solution)/shard_map/all_to_all | solution.py:568
  37.5 10.9 %collective-permute-start.11 = (bf16[128,1024]{1,0:T(8,128)(2,1)S(1)}, bf16[128,1024]{1,0:T(8,128)(2,1)S(1)}, u32[]{:S(2)}, u32[]{:S(2)}) collective-permute-start(bf16[128,1024]{1,0:T(8,128)(2,1)S(1)} %collective-permute-done.7.refs_1_), channel_id=1, source_target_pairs={{0,2},{1,3},{2,0},{3,1},{4,6},{5,7},{6,4},{7,5},{8,10},{9,11},{10,... | collective-permute-start | bytes 786440 | tf_op jit(solution)/shard_map/ppermute | solution.py:499
  45.7 2.8 %copy-start.7 = (bf16[128,3072]{1,0:T(8,128)(2,1)S(1)}, bf16[128,3072]{1,0:T(8,128)(2,1)}, u32[]{:S(2)}) copy-start(bf16[128,3072]{1,0:T(8,128)(2,1)} %copy-done.6) | copy-start | bytes 2359300
  48.3 9.3 %copy-start.9 = (bf16[512,512]{1,0:T(8,128)(2,1)S(1)}, bf16[512,512]{1,0:T(8,128)(2,1)}, u32[]{:S(2)}) copy-start(bf16[512,512]{1,0:T(8,128)(2,1)} %copy-done.8) | copy-start | bytes 1572868
  48.4 9.2 %collective-permute-start.12 = (bf16[512,1024]{1,0:T(8,128)(2,1)S(1)}, bf16[512,1024]{1,0:T(8,128)(2,1)S(1)}, u32[]{:S(2)}, u32[]{:S(2)}) collective-permute-start(bf16[512,1024]{1,0:T(8,128)(2,1)S(1)} %shard_map.143.refs_0_), channel_id=1, source_target_pairs={{0,1},{1,0},{2,3},{3,2},{4,5},{5,4},{6,7},{7,6},{8,9},{9,8},{10,11... | collective-permute-start | bytes 3145736 | tf_op jit(solution)/shard_map/ppermute | solution.py:499
  48.5 3.8 %collective-permute-start.9 = (bf16[128,3072]{1,0:T(8,128)(2,1)S(1)}, bf16[128,3072]{1,0:T(8,128)(2,1)S(1)}, u32[]{:S(2)}, u32[]{:S(2)}) collective-permute-start(bf16[128,3072]{1,0:T(8,128)(2,1)S(1)} %copy-done.7), channel_id=1, source_target_pairs={{0,1},{1,0},{2,3},{3,2},{4,5},{5,4},{6,7},{7,6},{8,9},{9,8},{10,11... | collective-permute-start | bytes 2359304 | tf_op jit(solution)/shard_map/ppermute | solution.py:499
  49.0 4.0 %collective-permute-start.10 = (bf16[128,2048]{1,0:T(8,128)(2,1)S(1)}, bf16[128,2048]{1,0:T(8,128)(2,1)S(1)}, u32[]{:S(2)}, u32[]{:S(2)}) collective-permute-start(bf16[128,2048]{1,0:T(8,128)(2,1)S(1)} %shard_map.141.refs_2_.refs_4_.refs_1_), channel_id=1, source_target_pairs={{0,1},{1,0},{2,3},{3,2},{4,5},{5,4},{6,7},{7,6},{8,9},{9,8},{10,11... | collective-permute-start | bytes 1572872 | tf_op jit(solution)/shard_map/ppermute | solution.py:499
  54.1 9.2 %collective-permute-start.13 = (bf16[4,256,128]{2,1,0:T(8,128)(2,1)S(1)}, bf16[4,256,128]{2,1,0:T(8,128)(2,1)S(1)}, u32[]{:S(2)}, u32[]{:S(2)}) collective-permute-start(bf16[4,256,128]{2,1,0:T(8,128)(2,1)S(1)} %get-tuple-element.71), channel_id=1, source_target_pairs={{0,4},{1,5},{2,6},{3,7},{4,0},{5,1},{6,2},{7,3},{8,12},{9,13},{10,... | collective-permute-start | bytes 786440 | tf_op jit(solution)/shard_map/ppermute | solution.py:499
  54.2 14.0 %collective-permute-start.14 = (bf16[4,256,128]{2,1,0:T(8,128)(2,1)S(1)}, bf16[4,256,128]{2,1,0:T(8,128)(2,1)S(1)}, u32[]{:S(2)}, u32[]{:S(2)}) collective-permute-start(bf16[4,256,128]{2,1,0:T(8,128)(2,1)S(1)} %get-tuple-element.72), channel_id=1, source_target_pairs={{0,2},{1,3},{2,0},{3,1},{4,6},{5,7},{6,4},{7,5},{8,10},{9,11},{10,... | collective-permute-start | bytes 786440 | tf_op jit(solution)/shard_map/ppermute | solution.py:499
  54.8 13.5 %collective-permute-start.15 = (bf16[4,256,128]{2,1,0:T(8,128)(2,1)S(1)}, bf16[4,256,128]{2,1,0:T(8,128)(2,1)S(1)}, u32[]{:S(2)}, u32[]{:S(2)}) collective-permute-start(bf16[4,256,128]{2,1,0:T(8,128)(2,1)S(1)} %get-tuple-element.73), channel_id=1, source_target_pairs={{0,6},{1,7},{2,4},{3,5},{4,2},{5,3},{6,0},{7,1},{8,14},{9,15},{10,... | collective-permute-start | bytes 786440 | tf_op jit(solution)/shard_map/ppermute | solution.py:499
  60.7 8.9 %collective-permute-start.22 = (bf16[1,64,1024]{2,1,0:T(8,128)(2,1)S(1)}, bf16[1,64,1024]{2,1,0:T(8,128)(2,1)S(1)}, u32[]{:S(2)}, u32[]{:S(2)}) collective-permute-start(bf16[1,64,1024]{2,1,0:T(8,128)(2,1)S(1)} %get-tuple-element.79), channel_id=1, source_target_pairs={{0,8},{1,9},{2,10},{3,11},{4,12},{5,13},{6,14},{7,15},{8,0},{9,1},... | collective-permute-start | bytes 393224 | tf_op jit(solution)/shard_map/ppermute | solution.py:499
  60.8 12.7 %collective-permute-start.23 = (bf16[1,64,1024]{2,1,0:T(8,128)(2,1)S(1)}, bf16[1,64,1024]{2,1,0:T(8,128)(2,1)S(1)}, u32[]{:S(2)}, u32[]{:S(2)}) collective-permute-start(bf16[1,64,1024]{2,1,0:T(8,128)(2,1)S(1)} %get-tuple-element.80), channel_id=1, source_target_pairs={{0,16},{1,17},{2,18},{3,19},{4,20},{5,21},{6,22},{7,23},{8,24},{9,... | collective-permute-start | bytes 393224 | tf_op jit(solution)/shard_map/ppermute | solution.py:499
  63.3 10.2 %collective-permute-start.24 = (bf16[1,64,1024]{2,1,0:T(8,128)(2,1)S(1)}, bf16[1,64,1024]{2,1,0:T(8,128)(2,1)S(1)}, u32[]{:S(2)}, u32[]{:S(2)}) collective-permute-start(bf16[1,64,1024]{2,1,0:T(8,128)(2,1)S(1)} %get-tuple-element.81), channel_id=1, source_target_pairs={{0,24},{1,25},{2,26},{3,27},{4,28},{5,29},{6,30},{7,31},{8,16},{9,... | collective-permute-start | bytes 393224 | tf_op jit(solution)/shard_map/ppermute | solution.py:499
  68.4 10.2 %collective-permute-start.16 = (bf16[1,256,128]{2,1,0:T(8,128)(2,1)S(1)}, bf16[1,256,128]{2,1,0:T(8,128)(2,1)S(1)}, u32[]{:S(2)}, u32[]{:S(2)}) collective-permute-start(bf16[1,256,128]{2,1,0:T(8,128)(2,1)S(1)} %get-tuple-element.76), channel_id=1, source_target_pairs={{0,8},{1,9},{2,10},{3,11},{4,12},{5,13},{6,14},{7,15},{8,0},{9,1},... | collective-permute-start | bytes 196616 | tf_op jit(solution)/shard_map/ppermute | solution.py:499
  73.5 9.4 %collective-permute-start.25 = (bf16[1,64,1024]{2,1,0:T(8,128)(2,1)S(1)}, bf16[1,64,1024]{2,1,0:T(8,128)(2,1)S(1)}, u32[]{:S(2)}, u32[]{:S(2)}) collective-permute-start(bf16[1,64,1024]{2,1,0:T(8,128)(2,1)S(1)} %shard_map.148.refs_0_), channel_id=1, source_target_pairs={{0,1},{1,0},{2,3},{3,2},{4,5},{5,4},{6,7},{7,6},{8,9},{9,8},{10,11... | collective-permute-start | bytes 393224 | tf_op jit(solution)/shard_map/ppermute | solution.py:499
  73.6 8.7 %collective-permute-start.17 = (bf16[1,256,128]{2,1,0:T(8,128)(2,1)S(1)}, bf16[1,256,128]{2,1,0:T(8,128)(2,1)S(1)}, u32[]{:S(2)}, u32[]{:S(2)}) collective-permute-start(bf16[1,256,128]{2,1,0:T(8,128)(2,1)S(1)} %get-tuple-element.77), channel_id=1, source_target_pairs={{0,16},{1,17},{2,18},{3,19},{4,20},{5,21},{6,22},{7,23},{8,24},{9,... | collective-permute-start | bytes 196616 | tf_op jit(solution)/shard_map/ppermute | solution.py:499
  75.8 6.4 %collective-permute-start.18 = (bf16[1,256,128]{2,1,0:T(8,128)(2,1)S(1)}, bf16[1,256,128]{2,1,0:T(8,128)(2,1)S(1)}, u32[]{:S(2)}, u32[]{:S(2)}) collective-permute-start(bf16[1,256,128]{2,1,0:T(8,128)(2,1)S(1)} %get-tuple-element.78), channel_id=1, source_target_pairs={{0,24},{1,25},{2,26},{3,27},{4,28},{5,29},{6,30},{7,31},{8,16},{9,... | collective-permute-start | bytes 196616 | tf_op jit(solution)/shard_map/ppermute | solution.py:499
  78.1 6.4 %collective-permute-start.26 = (bf16[1,64,1024]{2,1,0:T(8,128)(2,1)S(1)}, bf16[1,64,1024]{2,1,0:T(8,128)(2,1)S(1)}, u32[]{:S(2)}, u32[]{:S(2)}) collective-permute-start(bf16[1,64,1024]{2,1,0:T(8,128)(2,1)S(1)} %shard_map.148.refs_0_), channel_id=1, source_target_pairs={{0,2},{1,3},{2,0},{3,1},{4,6},{5,7},{6,4},{7,5},{8,10},{9,11},{10,... | collective-permute-start | bytes 393224 | tf_op jit(solution)/shard_map/ppermute | solution.py:499
  78.5 6.5 %collective-permute-start.27 = (bf16[1,64,1024]{2,1,0:T(8,128)(2,1)S(1)}, bf16[1,64,1024]{2,1,0:T(8,128)(2,1)S(1)}, u32[]{:S(2)}, u32[]{:S(2)}) collective-permute-start(bf16[1,64,1024]{2,1,0:T(8,128)(2,1)S(1)} %shard_map.148.refs_0_), channel_id=1, source_target_pairs={{0,3},{1,2},{2,1},{3,0},{4,7},{5,6},{6,5},{7,4},{8,11},{9,10},{10,... | collective-permute-start | bytes 393224 | tf_op jit(solution)/shard_map/ppermute | solution.py:499
  82.3 4.8 %collective-permute-start.19 = (bf16[1,256,128]{2,1,0:T(8,128)(2,1)S(1)}, bf16[1,256,128]{2,1,0:T(8,128)(2,1)S(1)}, u32[]{:S(2)}, u32[]{:S(2)}) collective-permute-start(bf16[1,256,128]{2,1,0:T(8,128)(2,1)S(1)} %shard_map.147.refs_0_), channel_id=1, source_target_pairs={{0,1},{1,0},{2,3},{3,2},{4,5},{5,4},{6,7},{7,6},{8,9},{9,8},{10,11... | collective-permute-start | bytes 196616 | tf_op jit(solution)/shard_map/ppermute | solution.py:499
  82.4 5.7 %collective-permute-start.20 = (bf16[1,256,128]{2,1,0:T(8,128)(2,1)S(1)}, bf16[1,256,128]{2,1,0:T(8,128)(2,1)S(1)}, u32[]{:S(2)}, u32[]{:S(2)}) collective-permute-start(bf16[1,256,128]{2,1,0:T(8,128)(2,1)S(1)} %shard_map.147.refs_0_), channel_id=1, source_target_pairs={{0,2},{1,3},{2,0},{3,1},{4,6},{5,7},{6,4},{7,5},{8,10},{9,11},{10,... | collective-permute-start | bytes 196616 | tf_op jit(solution)/shard_map/ppermute | solution.py:499
  83.0 5.4 %collective-permute-start.21 = (bf16[1,256,128]{2,1,0:T(8,128)(2,1)S(1)}, bf16[1,256,128]{2,1,0:T(8,128)(2,1)S(1)}, u32[]{:S(2)}, u32[]{:S(2)}) collective-permute-start(bf16[1,256,128]{2,1,0:T(8,128)(2,1)S(1)} %shard_map.147.refs_0_), channel_id=1, source_target_pairs={{0,3},{1,2},{2,1},{3,0},{4,7},{5,6},{6,5},{7,4},{8,11},{9,10},{10,... | collective-permute-start | bytes 196616 | tf_op jit(solution)/shard_map/ppermute | solution.py:499

commit v5 on v4

--- a/solution.py
+++ b/solution.py
@@ -565,6 +565,7 @@
     (back,) = call(
         copy_kernel, [shape_of((count, 2 * width), BF16)], back, after=[shared_x, shared_y]
     )
+    shared_xy = permute(shared_x, 0, 2)
     back = lax.all_to_all(back, "slab", split_axis=0, concat_axis=0, tiled=True)
     pack_z_core = permute(pack_z, 0, 1)
     (pack_p,) = call(
@@ -574,16 +575,18 @@
         hold_x,
         gain_one,
         w_qkv,
+        after=[shared_xy],
         scratch=[pltpu.VMEM((count, 3 * width), BF16)],
     )
+    pack_p_core = permute(pack_p, 0, 1)
     (around,) = call(
         join_kernel,
         [shape_of((4 * count, 2 * width), BF16)],
         shared,
         shared_x,
         shared_y,
-        permute(shared_x, 0, 2),
-        after=[pack_p],
+        shared_xy,
+        after=[pack_p_core, pack_z_core],
     )
     radix = min(4, spans)
     shift = (slabs // radix).bit_length() - 1
@@ -603,7 +606,7 @@
         pack_z,
         pack_z_core,
         pack_p,
-        permute(pack_p, 0, 1),
+        pack_p_core,
         scratch=[pltpu.VMEM((width, width), F32)],
     )
     ready = small[0]

time: 89.5 us -> 90.4 us (1.010)
  waiting for transfers between devices: 24.8 us -> 20 us
  local copies, waits for them, and re-layouts: 5 us -> 7.38 us
  starting transfers between devices: 35.9 us -> 38.2 us
    all_to_all x1, waiting for transfers between devices: 7.71 us -> 0.94 us  [body(): back = lax.all_to_all(back, 'slab', split_axis=0, concat_axis=0, tiled=True)]
    unnamed x24 -> x34, local copies, waits for them, and re-layouts: 5 us -> 7.38 us
    ppermute x28, starting transfers between devices: 31.3 us -> 33.6 us  [permute(): lax.ppermute(array, BOTH, swap_pairs(slabs, cases, flip_slab, flip_case))]
    ppermute x28, waiting for transfers between devices: 17.1 us -> 19 us  [permute(): lax.ppermute(array, BOTH, swap_pairs(slabs, cases, flip_slab, flip_case))]
    pallas_call x16, Pallas kernels: 22.7 us -> 23.6 us  [call(): pl.pallas_call(run, out_shape=outs, in_specs=[vmem if one else far for on...]
  transfers between devices with their start and end apart: 29 -> 29, of which waited for: 12 -> 9; matrix products, arithmetic and copies ran while one was open for 0% -> 0% of each run, Pallas kernels for 19% -> 19%
where the time goes in v5:
time: 90.4 us; the launch traced here: 90 us
  starting transfers between devices  38.2 us (42%)
  Pallas kernels  23.6 us (26%)
  waiting for transfers between devices  20 us (22%)
  local copies, waits for them, and re-layouts  7.38 us (8%)
    ppermute x28, starting transfers between devices, permute(): lax.ppermute(array, BOTH, swap_pairs(slabs, cases, flip_slab, flip_case))  33.6 us
    pallas_call x16, Pallas kernels, call(): pl.pallas_call(run, out_shape=outs, in_specs=[vmem if one else far for on...  23.6 us
    ppermute x28, waiting for transfers between devices, permute(): lax.ppermute(array, BOTH, swap_pairs(slabs, cases, flip_slab, flip_case))  19 us
    unnamed x34, local copies, waits for them, and re-layouts  7.38 us
    all_to_all x1, starting transfers between devices, body(): back = lax.all_to_all(back, 'slab', split_axis=0, concat_axis=0, tiled=True)  4.59 us
  transfers between devices with their start and end apart: 29, of which 9 were waited for; matrix products, arithmetic and copies ran while one was open for 0% of the time, Pallas kernels for 19%

profile of v5, /device:TPU:0, one launch (start us, length us, event | category | flops | bytes accessed | tf_op | source)
XLA Modules:
  0.0 90.0 jit_solution(7224447928360217625)
XLA Ops:
  0.6 2.9 %shard_map.135 = (bf16[16,1536]{1,0:T(8,128)(2,1)S(1)}, bf16[16,1536]{1,0:T(8,128)(2,1)S(1)}, bf16[16,1536]{1,0:T(8,128)(2,1)S(1)}, bf16[16,1536]{1,0:T(8,128)(2...) custom-call(bf16[128,512]{1,0:T(8,128)(2,1)} %bitcast.20, ...), custom_call_target="tpu_custom_call" | custom-call | flops 10000000 | bytes 10000 | tf_op jit(solution)/shard_map/pallas_call | solution.py:50
  3.5 3.0 %collective-permute-start = (bf16[16,1536]{1,0:T(8,128)(2,1)S(1)}, bf16[16,1536]{1,0:T(8,128)(2,1)S(1)}, u32[]{:S(2)}, u32[]{:S(2)}) collective-permute-start(bf16[16,1536]{1,0:T(8,128)(2,1)S(1)} %get-tuple-element.49), channel_id=1, source_target_pairs={{0,4},{1,5},{2,6},{3,7},{4,0},{5,1},{6,2},{7,3},{8,12},{9,13},{10,... | collective-permute-start | bytes 147464 | tf_op jit(solution)/shard_map/ppermute | solution.py:499
  6.5 1.6 %collective-permute-start.1 = (bf16[16,1536]{1,0:T(8,128)(2,1)S(1)}, bf16[16,1536]{1,0:T(8,128)(2,1)S(1)}, u32[]{:S(2)}, u32[]{:S(2)}) collective-permute-start(bf16[16,1536]{1,0:T(8,128)(2,1)S(1)} %get-tuple-element.50), channel_id=1, source_target_pairs={{0,8},{1,9},{2,10},{3,11},{4,12},{5,13},{6,14},{7,15},{8,0},{9,1},... | collective-permute-start | bytes 147464 | tf_op jit(solution)/shard_map/ppermute | solution.py:499
  8.1 3.0 %collective-permute-start.3 = (bf16[16,1536]{1,0:T(8,128)(2,1)S(1)}, bf16[16,1536]{1,0:T(8,128)(2,1)S(1)}, u32[]{:S(2)}, u32[]{:S(2)}) collective-permute-start(bf16[16,1536]{1,0:T(8,128)(2,1)S(1)} %get-tuple-element.52), channel_id=1, source_target_pairs={{0,16},{1,17},{2,18},{3,19},{4,20},{5,21},{6,22},{7,23},{8,24},{9,... | collective-permute-start | bytes 147464 | tf_op jit(solution)/shard_map/ppermute | solution.py:499
  11.1 1.3 %collective-permute-start.4 = (bf16[16,1536]{1,0:T(8,128)(2,1)S(1)}, bf16[16,1536]{1,0:T(8,128)(2,1)S(1)}, u32[]{:S(2)}, u32[]{:S(2)}) collective-permute-start(bf16[16,1536]{1,0:T(8,128)(2,1)S(1)} %get-tuple-element.53), channel_id=1, source_target_pairs={{0,20},{1,21},{2,22},{3,23},{4,16},{5,17},{6,18},{7,19},{8,28},{9,... | collective-permute-start | bytes 147464 | tf_op jit(solution)/shard_map/ppermute | solution.py:499
  12.4 0.0 collective-permute-done.refs_1_
  12.4 3.6 %collective-permute-start.5 = (bf16[16,1536]{1,0:T(8,128)(2,1)S(1)}, bf16[16,1536]{1,0:T(8,128)(2,1)S(1)}, u32[]{:S(2)}, u32[]{:S(2)}) collective-permute-start(bf16[16,1536]{1,0:T(8,128)(2,1)S(1)} %get-tuple-element.54), channel_id=1, source_target_pairs={{0,24},{1,25},{2,26},{3,27},{4,28},{5,29},{6,30},{7,31},{8,16},{9,... | collective-permute-start | bytes 147464 | tf_op jit(solution)/shard_map/ppermute | solution.py:499
  16.0 0.0 collective-permute-start.6
  16.1 1.7 %copy-done.1 = bf16[512,2048]{1,0:T(8,128)(2,1)S(1)} copy-done((bf16[512,2048]{1,0:T(8,128)(2,1)S(1)}, bf16[512,2048]{1,0:T(8,128)(2,1)}, u32[]{:S(2)}) %copy-start.1) | copy-done | bytes 2097176
  17.8 1.6 %copy-done.3 = bf16[2048,512]{1,0:T(8,128)(2,1)S(1)} copy-done((bf16[2048,512]{1,0:T(8,128)(2,1)S(1)}, bf16[2048,512]{1,0:T(8,128)(2,1)}, u32[]{:S(2)}) %copy-start.3) | copy-done | bytes 2097176
  19.4 1.3 %shard_map.136 = (bf16[512,512]{1,0:T(8,128)(2,1)S(1)}, bf16[512,512]{1,0:T(8,128)(2,1)S(1)}) custom-call(bf16[512,2048]{1,0:T(8,128)(2,1)S(1)} %copy-done.1, bf16[2048,512]{1,0:T(8,128)(2,1)S(1)} %copy-done.3), custom_call_target="tpu_custom_call" | custom-call | flops 10000000 | bytes 10000 | tf_op jit(solution)/shard_map/pallas_call | solution.py:50
  20.7 0.0 copy-start.13
  20.7 0.8 copy-done.13
  21.5 0.0 collective-permute-done.4.refs_5_
  21.5 1.3 %collective-permute-done.6.refs_7_ = bf16[16,1536]{1,0:T(8,128)(2,1)S(1)} collective-permute-done((bf16[16,1536]{1,0:T(8,128)(2,1)S(1)}, bf16[16,1536]{1,0:T(8,128)(2,1)S(1)}, u32[]{:S(2)}, u32[]{:S(2)}) %collective-permute-start.6) | collective-permute-done | bytes 49184 | tf_op jit(solution)/shard_map/ppermute | solution.py:499
  22.8 1.3 %shard_map.137 = (bf16[128,1024]{1,0:T(8,128)(2,1)S(1)}, bf16[128,1536]{1,0:T(8,128)(2,1)S(1)}, bf16[128,512]{1,0:T(8,128)(2,1)S(1)}, bf16[128,512]{1,0:T(8,128)(2,1)S(1)}, bf16[128,512]{1,0:T(8,128)(2,1)S(1)}) custom-call(bf16[16,1536]{1,0:T(8,128)(2,1)S(1)} %get-tuple-element.48.refs_0_, bf16[16,1536]{1,0:T(8,128)(2,1)S(1)} %collective-permute-done.refs_1_, ...), custom_call_target="tpu_custom_call" | custom-call | flops 10000000 | bytes 10000 | tf_op jit(solution)/shard_map/pallas_call | solution.py:50
  24.1 1.6 %collective-permute-start.8 = (bf16[128,1024]{1,0:T(8,128)(2,1)S(1)}, bf16[128,1024]{1,0:T(8,128)(2,1)S(1)}, u32[]{:S(2)}, u32[]{:S(2)}) collective-permute-start(bf16[128,1024]{1,0:T(8,128)(2,1)S(1)} %get-tuple-element.58.refs_0_), channel_id=1, source_target_pairs={{0,2},{1,3},{2,0},{3,1},{4,6},{5,7},{6,4},{7,5},{8,10},{9,11},{10,... | collective-permute-start | bytes 786440 | tf_op jit(solution)/shard_map/ppermute | solution.py:499
  25.7 0.5 collective-permute-start.7
  26.2 2.4 %shard_map.138 = (bf16[128,512]{1,0:T(8,128)(2,1)S(1)}, f32[128,512]{1,0:T(8,128)S(1)}) custom-call(bf16[128,1024]{1,0:T(8,128)(2,1)S(1)} %get-tuple-element.58.refs_0_, bf16[128,512]{1,0:T(8,128)(2,1)S(1)} %get-tuple-element.59.refs_1_, f32[1,512]{1,0:T(1,128)S(1)} %bitcast.18, bf16[512,512]{1,0:T(8,128)(2,1)S(1)} %copy-done.5, ...), custom_call_target="tpu_custom_call" | custom-call | flops 10000000 | bytes 10000 | tf_op jit(solution)/shard_map/pallas_call | solution.py:50
  28.6 2.6 %shard_map.139 = (bf16[128,1024]{1,0:T(8,128)(2,1)S(1)}, bf16[128,3072]{1,0:T(8,128)(2,1)S(1)}) custom-call(bf16[128,1536]{1,0:T(8,128)(2,1)S(1)} %get-tuple-element.57.refs_0_, bf16[128,512]{1,0:T(8,128)(2,1)S(1)} %get-tuple-element.60.refs_1_, f32[128,512]{1,0:T(8,128)S(1)} %get-tuple-element.61.refs_2_, bf16[128,512]{1,0:T(8,128)(2,1)S(1)} %get-tuple-element.62.refs_3_, ...), custom_call_target="tpu_custom_call" | custom-call | flops 10000000 | bytes 10000 | tf_op jit(solution)/shard_map/pallas_call | solution.py:50
  31.2 0.9 %copy-done.11 = bf16[128,3072]{1,0:T(8,128)(2,1)} copy-done((bf16[128,3072]{1,0:T(8,128)(2,1)}, bf16[128,3072]{1,0:T(8,128)(2,1)S(1)}, u32[]{:S(2)}) %copy-start.11) | copy-done | bytes 786456
  32.1 0.0 collective-permute-done.7.refs_1_
  32.1 0.7 shard_map.140
  32.9 0.7 copy-done.9
  33.6 4.6 %all-to-all-start = ((bf16[8,16,1024]{2,1,0:T(8,128)(2,1)}), bf16[8,16,1024]{2,1,0:T(8,128)(2,1)S(1)}, u32[]{:S(2)}, u32[]{:S(2)}) async-start(bf16[8,16,1024]{2,1,0:T(8,128)(2,1)} %bitcast.4), calls=%async_computation | async-start | bytes 524288 | tf_op jit(solution)/shard_map/all_to_all | solution.py:569
  38.2 0.5 collective-permute-start.9
  38.7 6.1 %collective-permute-done.9.refs_4_.refs_3_ = bf16[128,1024]{1,0:T(8,128)(2,1)S(1)} collective-permute-done((bf16[128,1024]{1,0:T(8,128)(2,1)}, bf16[128,1024]{1,0:T(8,128)(2,1)S(1)}, u32[]{:S(2)}, u32[]{:S(2)}) %collective-permute-start.9) | collective-permute-done | bytes 262176 | tf_op jit(solution)/shard_map/ppermute | solution.py:499
  44.7 0.7 copy-done.6
  45.4 0.9 %all-to-all-done = bf16[8,16,1024]{2,1,0:T(8,128)(2,1)S(1)} async-done(((bf16[8,16,1024]{2,1,0:T(8,128)(2,1)}), bf16[8,16,1024]{2,1,0:T(8,128)(2,1)S(1)}, u32[]{:S(2)}, u32[]{:S(2)}) %all-to-all-start) | async-done | bytes 262176 | tf_op jit(solution)/shard_map/all_to_all | solution.py:569
  46.4 0.9 %copy-done.7 = bf16[128,1024]{1,0:T(8,128)(2,1)S(1)} copy-done((bf16[128,1024]{1,0:T(8,128)(2,1)S(1)}, bf16[128,1024]{1,0:T(8,128)(2,1)}, u32[]{:S(2)}) %copy-start.7) | copy-done | bytes 262168
  47.3 2.6 %shard_map.141.refs_2_.refs_1_ = bf16[128,2048]{1,0:T(8,128)(2,1)S(1)} custom-call(bf16[128,1024]{1,0:T(8,128)(2,1)S(1)} %bitcast.9, bf16[128,512]{1,0:T(8,128)(2,1)S(1)} %get-tuple-element.65.refs_1_.refs_2_, f32[1,512]{1,0:T(1,128)S(1)} %bitcast.14, bf16[512,1536]{1,0:T(8,128)(2,1)S(1)} %copy-done, bf16[128,1024]{1,0:T(8,128)(2,1)S(1)} %copy-done.7), custom_call_target="tpu_custom_call" | custom-call | flops 10000000 | bytes 10000 | tf_op jit(solution)/shard_map/pallas_call | solution.py:50
  50.0 0.1 collective-permute-start.11
  50.1 1.9 %collective-permute-done.11.refs_3_.refs_4_ = bf16[128,2048]{1,0:T(8,128)(2,1)S(1)} collective-permute-done((bf16[128,2048]{1,0:T(8,128)(2,1)S(1)}, bf16[128,2048]{1,0:T(8,128)(2,1)S(1)}, u32[]{:S(2)}, u32[]{:S(2)}) %collective-permute-start.11) | collective-permute-done | bytes 524320 | tf_op jit(solution)/shard_map/ppermute | solution.py:499
  52.0 1.0 %shard_map.143.refs_0_ = bf16[512,1024]{1,0:T(8,128)(2,1)S(1)} custom-call(bf16[128,1024]{1,0:T(8,128)(2,1)S(1)} %get-tuple-element.58.refs_0_, bf16[128,1024]{1,0:T(8,128)(2,1)} %collective-permute-done.7.refs_1_, bf16[128,1024]{1,0:T(8,128)(2,1)S(1)} %copy-done.10, bf16[128,1024]{1,0:T(8,128)(2,1)S(1)} %copy-done.8, ...), custom_call_target="tpu_custom_call" | custom-call | flops 10000000 | bytes 10000 | tf_op jit(solution)/shard_map/pallas_call | solution.py:50
  53.0 0.0 copy-start.14
  53.0 0.2 collective-permute-start.12
  53.2 1.0 %shard_map.142 = (bf16[4,256,128]{2,1,0:T(8,128)(2,1)S(1)}, bf16[4,256,128]{2,1,0:T(8,128)(2,1)S(1)}, bf16[4,256,128]{2,1,0:T(8,128)(2,1)S(1)}, bf16[4,256,128]{2,1,0:T(8,128)(2,1)S(1)}) custom-call(bf16[128,3072]{1,0:T(8,128)(2,1)S(1)} %copy-done.12, bf16[128,3072]{1,0:T(8,128)(2,1)S(1)} %collective-permute-done.10.refs_1_.refs_5_, ...), custom_call_target="tpu_custom_call" | custom-call | flops 10000000 | bytes 10000 | tf_op jit(solution)/shard_map/pallas_call | solution.py:50
  54.3 1.2 %collective-permute-start.13 = (bf16[4,256,128]{2,1,0:T(8,128)(2,1)S(1)}, bf16[4,256,128]{2,1,0:T(8,128)(2,1)S(1)}, u32[]{:S(2)}, u32[]{:S(2)}) collective-permute-start(bf16[4,256,128]{2,1,0:T(8,128)(2,1)S(1)} %get-tuple-element.71), channel_id=1, source_target_pairs={{0,4},{1,5},{2,6},{3,7},{4,0},{5,1},{6,2},{7,3},{8,12},{9,13},{10,... | collective-permute-start | bytes 786440 | tf_op jit(solution)/shard_map/ppermute | solution.py:499
  55.5 0.5 collective-permute-start.14
  56.0 1.9 %collective-permute-start.15 = (bf16[4,256,128]{2,1,0:T(8,128)(2,1)S(1)}, bf16[4,256,128]{2,1,0:T(8,128)(2,1)S(1)}, u32[]{:S(2)}, u32[]{:S(2)}) collective-permute-start(bf16[4,256,128]{2,1,0:T(8,128)(2,1)S(1)} %get-tuple-element.73), channel_id=1, source_target_pairs={{0,6},{1,7},{2,4},{3,5},{4,2},{5,3},{6,0},{7,1},{8,14},{9,15},{10,... | collective-permute-start | bytes 786440 | tf_op jit(solution)/shard_map/ppermute | solution.py:499
  57.8 0.0 collective-permute-done.12.refs_1_
  57.9 3.0 %shard_map.144 = (bf16[1,64,1024]{2,1,0:T(8,128)(2,1)S(1)}, bf16[1,64,1024]{2,1,0:T(8,128)(2,1)S(1)}, bf16[1,64,1024]{2,1,0:T(8,128)(2,1)S(1)}, bf16[1,64,1024]{2,1,0:T(8,128)(2,1)S(1)}) custom-call(bf16[512,1024]{1,0:T(8,128)(2,1)S(1)} %shard_map.143.refs_0_, bf16[512,1024]{1,0:T(8,128)(2,1)S(1)} %collective-permute-done.12.refs_1_, ...), custom_call_target="tpu_custom_call" | custom-call | flops 10000000 | bytes 10000 | tf_op jit(solution)/shard_map/pallas_call | solution.py:50
  60.9 1.1 %collective-permute-start.22 = (bf16[1,64,1024]{2,1,0:T(8,128)(2,1)S(1)}, bf16[1,64,1024]{2,1,0:T(8,128)(2,1)S(1)}, u32[]{:S(2)}, u32[]{:S(2)}) collective-permute-start(bf16[1,64,1024]{2,1,0:T(8,128)(2,1)S(1)} %get-tuple-element.79), channel_id=1, source_target_pairs={{0,8},{1,9},{2,10},{3,11},{4,12},{5,13},{6,14},{7,15},{8,0},{9,1},... | collective-permute-start | bytes 393224 | tf_op jit(solution)/shard_map/ppermute | solution.py:499
  62.0 2.4 %collective-permute-start.23 = (bf16[1,64,1024]{2,1,0:T(8,128)(2,1)S(1)}, bf16[1,64,1024]{2,1,0:T(8,128)(2,1)S(1)}, u32[]{:S(2)}, u32[]{:S(2)}) collective-permute-start(bf16[1,64,1024]{2,1,0:T(8,128)(2,1)S(1)} %get-tuple-element.80), channel_id=1, source_target_pairs={{0,16},{1,17},{2,18},{3,19},{4,20},{5,21},{6,22},{7,23},{8,24},{9,... | collective-permute-start | bytes 393224 | tf_op jit(solution)/shard_map/ppermute | solution.py:499
  64.4 2.0 %collective-permute-start.24 = (bf16[1,64,1024]{2,1,0:T(8,128)(2,1)S(1)}, bf16[1,64,1024]{2,1,0:T(8,128)(2,1)S(1)}, u32[]{:S(2)}, u32[]{:S(2)}) collective-permute-start(bf16[1,64,1024]{2,1,0:T(8,128)(2,1)S(1)} %get-tuple-element.81), channel_id=1, source_target_pairs={{0,24},{1,25},{2,26},{3,27},{4,28},{5,29},{6,30},{7,31},{8,16},{9,... | collective-permute-start | bytes 393224 | tf_op jit(solution)/shard_map/ppermute | solution.py:499
  66.4 1.6 %shard_map.145 = (bf16[128,512]{1,0:T(8,128)(2,1)}, f32[8,128]{1,0:T(8,128)S(1)}) custom-call(bf16[128,1024]{1,0:T(8,128)(2,1)S(1)} %bitcast.10, bf16[128,2048]{1,0:T(8,128)(2,1)S(1)} %shard_map.141.refs_2_.refs_1_, bf16[128,512]{1,0:T(8,128)(2,1)S(1)} %get-tuple-element.65.refs_1_.refs_2_, f32[1,512]{1,0:T(1,128)S(1)} %bitcast.15, ...), custom_call_target="tpu_custom_call" | custom-call | flops 10000000 | bytes 10000 | tf_op jit(solution)/shard_map/pallas_call | solution.py:50
  67.9 1.5 %collective-permute-done.14.refs_2_ = bf16[4,256,128]{2,1,0:T(8,128)(2,1)S(1)} collective-permute-done((bf16[4,256,128]{2,1,0:T(8,128)(2,1)S(1)}, bf16[4,256,128]{2,1,0:T(8,128)(2,1)S(1)}, u32[]{:S(2)}, u32[]{:S(2)}) %collective-permute-start.14) | collective-permute-done | bytes 262176 | tf_op jit(solution)/shard_map/ppermute | solution.py:499
  69.4 0.1 shard_map.146
  69.5 1.5 %collective-permute-start.16 = (bf16[1,256,128]{2,1,0:T(8,128)(2,1)S(1)}, bf16[1,256,128]{2,1,0:T(8,128)(2,1)S(1)}, u32[]{:S(2)}, u32[]{:S(2)}) collective-permute-start(bf16[1,256,128]{2,1,0:T(8,128)(2,1)S(1)} %get-tuple-element.76), channel_id=1, source_target_pairs={{0,8},{1,9},{2,10},{3,11},{4,12},{5,13},{6,14},{7,15},{8,0},{9,1},... | collective-permute-start | bytes 196616 | tf_op jit(solution)/shard_map/ppermute | solution.py:499
  71.1 3.6 %collective-permute-done.23.refs_2_ = bf16[1,64,1024]{2,1,0:T(8,128)(2,1)S(1)} collective-permute-done((bf16[1,64,1024]{2,1,0:T(8,128)(2,1)S(1)}, bf16[1,64,1024]{2,1,0:T(8,128)(2,1)S(1)}, u32[]{:S(2)}, u32[]{:S(2)}) %collective-permute-start.23) | collective-permute-done | bytes 131104 | tf_op jit(solution)/shard_map/ppermute | solution.py:499
  74.6 0.1 shard_map.148.refs_0_
  74.7 0.1 collective-permute-start.27
  74.8 2.9 %collective-permute-start.17 = (bf16[1,256,128]{2,1,0:T(8,128)(2,1)S(1)}, bf16[1,256,128]{2,1,0:T(8,128)(2,1)S(1)}, u32[]{:S(2)}, u32[]{:S(2)}) collective-permute-start(bf16[1,256,128]{2,1,0:T(8,128)(2,1)S(1)} %get-tuple-element.77), channel_id=1, source_target_pairs={{0,16},{1,17},{2,18},{3,19},{4,20},{5,21},{6,22},{7,23},{8,24},{9,... | collective-permute-start | bytes 196616 | tf_op jit(solution)/shard_map/ppermute | solution.py:499
  77.7 1.5 %collective-permute-start.18 = (bf16[1,256,128]{2,1,0:T(8,128)(2,1)S(1)}, bf16[1,256,128]{2,1,0:T(8,128)(2,1)S(1)}, u32[]{:S(2)}, u32[]{:S(2)}) collective-permute-start(bf16[1,256,128]{2,1,0:T(8,128)(2,1)S(1)} %get-tuple-element.78), channel_id=1, source_target_pairs={{0,24},{1,25},{2,26},{3,27},{4,28},{5,29},{6,30},{7,31},{8,16},{9,... | collective-permute-start | bytes 196616 | tf_op jit(solution)/shard_map/ppermute | solution.py:499
  79.2 0.5 collective-permute-start.26
  79.7 0.7 collective-permute-start.25
  80.4 1.7 %collective-permute-done.17.refs_2_ = bf16[1,256,128]{2,1,0:T(8,128)(2,1)S(1)} collective-permute-done((bf16[1,256,128]{2,1,0:T(8,128)(2,1)S(1)}, bf16[1,256,128]{2,1,0:T(8,128)(2,1)S(1)}, u32[]{:S(2)}, u32[]{:S(2)}) %collective-permute-start.17) | collective-permute-done | bytes 65568 | tf_op jit(solution)/shard_map/ppermute | solution.py:499
  82.1 1.7 %collective-permute-done.18.refs_3_ = bf16[1,256,128]{2,1,0:T(8,128)(2,1)S(1)} collective-permute-done((bf16[1,256,128]{2,1,0:T(8,128)(2,1)S(1)}, bf16[1,256,128]{2,1,0:T(8,128)(2,1)S(1)}, u32[]{:S(2)}, u32[]{:S(2)}) %collective-permute-start.18) | collective-permute-done | bytes 65568 | tf_op jit(solution)/shard_map/ppermute | solution.py:499
  83.8 0.7 collective-permute-start.21
  84.6 0.3 collective-permute-start.20
  84.9 0.9 %collective-permute-start.19 = (bf16[1,256,128]{2,1,0:T(8,128)(2,1)S(1)}, bf16[1,256,128]{2,1,0:T(8,128)(2,1)S(1)}, u32[]{:S(2)}, u32[]{:S(2)}) collective-permute-start(bf16[1,256,128]{2,1,0:T(8,128)(2,1)S(1)} %shard_map.147.refs_0_), channel_id=1, source_target_pairs={{0,1},{1,0},{2,3},{3,2},{4,5},{5,4},{6,7},{7,6},{8,9},{9,8},{10,11... | collective-permute-start | bytes 196616 | tf_op jit(solution)/shard_map/ppermute | solution.py:499
  85.8 2.1 %shard_map.149 = (f32[64,2048]{1,0:T(8,128)}, f32[256,512]{1,0:T(8,128)}, f32[1,64]{1,0:T(1,128)}, bf16[64,1536]{1,0:T(8,128)(2,1)S(1)}) custom-call(bf16[1,64,1024]{2,1,0:T(8,128)(2,1)S(1)} %shard_map.148.refs_0_, bf16[1,64,1024]{2,1,0:T(8,128)(2,1)S(1)} %collective-permute-done.25.refs_1_, bf16[1,64,1024]{2,1,0:T(8,128)(2,1)S(1)} %collective-permute-done.26.refs_2_, ...), custom_call_target="tpu_custom_call" | custom-call | flops 10000000 | bytes 10000 | tf_op jit(solution)/shard_map/pallas_call | solution.py:50
  87.9 1.3 %collective-permute-done.20.refs_2_ = bf16[1,256,128]{2,1,0:T(8,128)(2,1)S(1)} collective-permute-done((bf16[1,256,128]{2,1,0:T(8,128)(2,1)S(1)}, bf16[1,256,128]{2,1,0:T(8,128)(2,1)S(1)}, u32[]{:S(2)}, u32[]{:S(2)}) %collective-permute-start.20) | collective-permute-done | bytes 65568 | tf_op jit(solution)/shard_map/ppermute | solution.py:499
  89.1 0.8 shard_map.150
  (44 shorter events, 0.1 us)
Async XLA Ops:
  3.5 8.9 %collective-permute-start = (bf16[16,1536]{1,0:T(8,128)(2,1)S(1)}, bf16[16,1536]{1,0:T(8,128)(2,1)S(1)}, u32[]{:S(2)}, u32[]{:S(2)}) collective-permute-start(bf16[16,1536]{1,0:T(8,128)(2,1)S(1)} %get-tuple-element.49), channel_id=1, source_target_pairs={{0,4},{1,5},{2,6},{3,7},{4,0},{5,1},{6,2},{7,3},{8,12},{9,13},{10,... | collective-permute-start | bytes 147464 | tf_op jit(solution)/shard_map/ppermute | solution.py:499
  6.5 9.5 %collective-permute-start.1 = (bf16[16,1536]{1,0:T(8,128)(2,1)S(1)}, bf16[16,1536]{1,0:T(8,128)(2,1)S(1)}, u32[]{:S(2)}, u32[]{:S(2)}) collective-permute-start(bf16[16,1536]{1,0:T(8,128)(2,1)S(1)} %get-tuple-element.50), channel_id=1, source_target_pairs={{0,8},{1,9},{2,10},{3,11},{4,12},{5,13},{6,14},{7,15},{8,0},{9,1},... | collective-permute-start | bytes 147464 | tf_op jit(solution)/shard_map/ppermute | solution.py:499
  8.1 13.4 %collective-permute-start.2 = (bf16[16,1536]{1,0:T(8,128)(2,1)S(1)}, bf16[16,1536]{1,0:T(8,128)(2,1)S(1)}, u32[]{:S(2)}, u32[]{:S(2)}) collective-permute-start(bf16[16,1536]{1,0:T(8,128)(2,1)S(1)} %get-tuple-element.51), channel_id=1, source_target_pairs={{0,12},{1,13},{2,14},{3,15},{4,8},{5,9},{6,10},{7,11},{8,4},{9,5},... | collective-permute-start | bytes 147464 | tf_op jit(solution)/shard_map/ppermute | solution.py:499
  8.1 13.4 %collective-permute-start.3 = (bf16[16,1536]{1,0:T(8,128)(2,1)S(1)}, bf16[16,1536]{1,0:T(8,128)(2,1)S(1)}, u32[]{:S(2)}, u32[]{:S(2)}) collective-permute-start(bf16[16,1536]{1,0:T(8,128)(2,1)S(1)} %get-tuple-element.52), channel_id=1, source_target_pairs={{0,16},{1,17},{2,18},{3,19},{4,20},{5,21},{6,22},{7,23},{8,24},{9,... | collective-permute-start | bytes 147464 | tf_op jit(solution)/shard_map/ppermute | solution.py:499
  11.1 10.3 %collective-permute-start.4 = (bf16[16,1536]{1,0:T(8,128)(2,1)S(1)}, bf16[16,1536]{1,0:T(8,128)(2,1)S(1)}, u32[]{:S(2)}, u32[]{:S(2)}) collective-permute-start(bf16[16,1536]{1,0:T(8,128)(2,1)S(1)} %get-tuple-element.53), channel_id=1, source_target_pairs={{0,20},{1,21},{2,22},{3,23},{4,16},{5,17},{6,18},{7,19},{8,28},{9,... | collective-permute-start | bytes 147464 | tf_op jit(solution)/shard_map/ppermute | solution.py:499
  12.4 9.1 %collective-permute-start.5 = (bf16[16,1536]{1,0:T(8,128)(2,1)S(1)}, bf16[16,1536]{1,0:T(8,128)(2,1)S(1)}, u32[]{:S(2)}, u32[]{:S(2)}) collective-permute-start(bf16[16,1536]{1,0:T(8,128)(2,1)S(1)} %get-tuple-element.54), channel_id=1, source_target_pairs={{0,24},{1,25},{2,26},{3,27},{4,28},{5,29},{6,30},{7,31},{8,16},{9,... | collective-permute-start | bytes 147464 | tf_op jit(solution)/shard_map/ppermute | solution.py:499
  16.0 6.8 %copy-start = (bf16[512,1536]{1,0:T(8,128)(2,1)S(1)}, bf16[512,1536]{1,0:T(8,128)(2,1)}, u32[]{:S(2)}) copy-start(bf16[512,1536]{1,0:T(8,128)(2,1)} %refs_6_.3) | copy-start | bytes 4718596
  16.0 6.8 %collective-permute-start.6 = (bf16[16,1536]{1,0:T(8,128)(2,1)S(1)}, bf16[16,1536]{1,0:T(8,128)(2,1)S(1)}, u32[]{:S(2)}, u32[]{:S(2)}) collective-permute-start(bf16[16,1536]{1,0:T(8,128)(2,1)S(1)} %get-tuple-element.55), channel_id=1, source_target_pairs={{0,28},{1,29},{2,30},{3,31},{4,24},{5,25},{6,26},{7,27},{8,20},{9,... | collective-permute-start | bytes 147464 | tf_op jit(solution)/shard_map/ppermute | solution.py:499
  16.1 1.7 %copy-start.1 = (bf16[512,2048]{1,0:T(8,128)(2,1)S(1)}, bf16[512,2048]{1,0:T(8,128)(2,1)}, u32[]{:S(2)}) copy-start(bf16[512,2048]{1,0:T(8,128)(2,1)} %refs_5_.3) | copy-start | bytes 6291460
  17.8 1.6 %copy-start.3 = (bf16[2048,512]{1,0:T(8,128)(2,1)S(1)}, bf16[2048,512]{1,0:T(8,128)(2,1)}, u32[]{:S(2)}) copy-start(bf16[2048,512]{1,0:T(8,128)(2,1)} %refs_5_.2) | copy-start | bytes 6291460
  19.4 3.5 %copy-start.5 = (bf16[512,512]{1,0:T(8,128)(2,1)S(1)}, bf16[512,512]{1,0:T(8,128)(2,1)}, u32[]{:S(2)}) copy-start(bf16[512,512]{1,0:T(8,128)(2,1)} %refs_3_.4) | copy-start | bytes 1572868
  19.4 3.5 %copy-start.15 = (f32[512]{0:T(512)S(1)}, f32[512]{0:T(512)}, u32[]{:S(2)}) copy-start(f32[512]{0:T(512)} %param.14) | copy-start | bytes 6148
  19.4 3.5 %copy-start.16 = (f32[512]{0:T(512)S(1)}, f32[512]{0:T(512)}, u32[]{:S(2)}) copy-start(f32[512]{0:T(512)} %param.15) | copy-start | bytes 6148
  19.4 6.8 %copy-start.4 = (bf16[2048,512]{1,0:T(8,128)(2,1)S(1)}, bf16[2048,512]{1,0:T(8,128)(2,1)}, u32[]{:S(2)}) copy-start(bf16[2048,512]{1,0:T(8,128)(2,1)} %refs_5_.2) | copy-start | bytes 6291460
  20.7 0.8 copy-start.13
  21.5 4.7 %copy-start.2 = (bf16[512,2048]{1,0:T(8,128)(2,1)S(1)}, bf16[512,2048]{1,0:T(8,128)(2,1)}, u32[]{:S(2)}) copy-start(bf16[512,2048]{1,0:T(8,128)(2,1)} %refs_5_.3) | copy-start | bytes 6291460
  24.1 8.1 %collective-permute-start.8 = (bf16[128,1024]{1,0:T(8,128)(2,1)S(1)}, bf16[128,1024]{1,0:T(8,128)(2,1)S(1)}, u32[]{:S(2)}, u32[]{:S(2)}) collective-permute-start(bf16[128,1024]{1,0:T(8,128)(2,1)S(1)} %get-tuple-element.58.refs_0_), channel_id=1, source_target_pairs={{0,2},{1,3},{2,0},{3,1},{4,6},{5,7},{6,4},{7,5},{8,10},{9,11},{10,... | collective-permute-start | bytes 786440 | tf_op jit(solution)/shard_map/ppermute | solution.py:499
  25.7 6.5 %collective-permute-start.7 = (bf16[128,1024]{1,0:T(8,128)(2,1)S(1)}, bf16[128,1024]{1,0:T(8,128)(2,1)}, u32[]{:S(2)}, u32[]{:S(2)}) collective-permute-start(bf16[128,1024]{1,0:T(8,128)(2,1)S(1)} %get-tuple-element.58.refs_0_), channel_id=1, source_target_pairs={{0,4},{1,5},{2,6},{3,7},{4,0},{5,1},{6,2},{7,3},{8,12},{9,13},{10,... | collective-permute-start | bytes 786440 | tf_op jit(solution)/shard_map/ppermute | solution.py:499
  31.2 0.9 %copy-start.11 = (bf16[128,3072]{1,0:T(8,128)(2,1)}, bf16[128,3072]{1,0:T(8,128)(2,1)S(1)}, u32[]{:S(2)}) copy-start(bf16[128,3072]{1,0:T(8,128)(2,1)S(1)} %get-tuple-element.66.refs_0_) | copy-start | bytes 2359300
  32.9 0.7 copy-start.9
  33.6 12.8 %all-to-all-start = ((bf16[8,16,1024]{2,1,0:T(8,128)(2,1)}), bf16[8,16,1024]{2,1,0:T(8,128)(2,1)S(1)}, u32[]{:S(2)}, u32[]{:S(2)}) async-start(bf16[8,16,1024]{2,1,0:T(8,128)(2,1)} %bitcast.4), calls=%async_computation | async-start | bytes 524288 | tf_op jit(solution)/shard_map/all_to_all | solution.py:569
  38.2 6.6 %collective-permute-start.9 = (bf16[128,1024]{1,0:T(8,128)(2,1)}, bf16[128,1024]{1,0:T(8,128)(2,1)S(1)}, u32[]{:S(2)}, u32[]{:S(2)}) collective-permute-start(bf16[128,1024]{1,0:T(8,128)(2,1)} %collective-permute-done.7.refs_1_), channel_id=1, source_target_pairs={{0,2},{1,3},{2,0},{3,1},{4,6},{5,7},{6,4},{7,5},{8,10},{9,11},{10,... | collective-permute-start | bytes 786440 | tf_op jit(solution)/shard_map/ppermute | solution.py:499
  38.7 11.4 %collective-permute-start.10 = (bf16[128,3072]{1,0:T(8,128)(2,1)}, bf16[128,3072]{1,0:T(8,128)(2,1)S(1)}, u32[]{:S(2)}, u32[]{:S(2)}) collective-permute-start(bf16[128,3072]{1,0:T(8,128)(2,1)} %copy-done.11), channel_id=1, source_target_pairs={{0,1},{1,0},{2,3},{3,2},{4,5},{5,4},{6,7},{7,6},{8,9},{9,8},{10,11... | collective-permute-start | bytes 2359304 | tf_op jit(solution)/shard_map/ppermute | solution.py:499
  44.7 0.7 copy-start.6
  46.4 1.0 %copy-start.7 = (bf16[128,1024]{1,0:T(8,128)(2,1)S(1)}, bf16[128,1024]{1,0:T(8,128)(2,1)}, u32[]{:S(2)}) copy-start(bf16[128,1024]{1,0:T(8,128)(2,1)} %copy-done.6) | copy-start | bytes 786436
  47.3 4.6 %copy-start.8 = (bf16[128,1024]{1,0:T(8,128)(2,1)S(1)}, bf16[128,1024]{1,0:T(8,128)(2,1)}, u32[]{:S(2)}) copy-start(bf16[128,1024]{1,0:T(8,128)(2,1)} %copy-done.6) | copy-start | bytes 786436
  47.3 4.6 %copy-start.10 = (bf16[128,1024]{1,0:T(8,128)(2,1)S(1)}, bf16[128,1024]{1,0:T(8,128)(2,1)}, u32[]{:S(2)}) copy-start(bf16[128,1024]{1,0:T(8,128)(2,1)} %copy-done.9) | copy-start | bytes 786436
  50.0 3.2 %copy-start.12 = (bf16[128,3072]{1,0:T(8,128)(2,1)S(1)}, bf16[128,3072]{1,0:T(8,128)(2,1)}, u32[]{:S(2)}) copy-start(bf16[128,3072]{1,0:T(8,128)(2,1)} %copy-done.11) | copy-start | bytes 2359300
  50.0 2.0 %collective-permute-start.11 = (bf16[128,2048]{1,0:T(8,128)(2,1)S(1)}, bf16[128,2048]{1,0:T(8,128)(2,1)S(1)}, u32[]{:S(2)}, u32[]{:S(2)}) collective-permute-start(bf16[128,2048]{1,0:T(8,128)(2,1)S(1)} %shard_map.141.refs_2_.refs_1_), channel_id=1, source_target_pairs={{0,1},{1,0},{2,3},{3,2},{4,5},{5,4},{6,7},{7,6},{8,9},{9,8},{10,11... | collective-permute-start | bytes 1572872 | tf_op jit(solution)/shard_map/ppermute | solution.py:499
  53.0 4.8 %copy-start.14 = (bf16[512,512]{1,0:T(8,128)(2,1)S(1)}, bf16[512,512]{1,0:T(8,128)(2,1)}, u32[]{:S(2)}) copy-start(bf16[512,512]{1,0:T(8,128)(2,1)} %copy-done.13) | copy-start | bytes 1572868
  53.0 4.8 %collective-permute-start.12 = (bf16[512,1024]{1,0:T(8,128)(2,1)S(1)}, bf16[512,1024]{1,0:T(8,128)(2,1)S(1)}, u32[]{:S(2)}, u32[]{:S(2)}) collective-permute-start(bf16[512,1024]{1,0:T(8,128)(2,1)S(1)} %shard_map.143.refs_0_), channel_id=1, source_target_pairs={{0,1},{1,0},{2,3},{3,2},{4,5},{5,4},{6,7},{7,6},{8,9},{9,8},{10,11... | collective-permute-start | bytes 3145736 | tf_op jit(solution)/shard_map/ppermute | solution.py:499
  54.3 10.1 %collective-permute-start.13 = (bf16[4,256,128]{2,1,0:T(8,128)(2,1)S(1)}, bf16[4,256,128]{2,1,0:T(8,128)(2,1)S(1)}, u32[]{:S(2)}, u32[]{:S(2)}) collective-permute-start(bf16[4,256,128]{2,1,0:T(8,128)(2,1)S(1)} %get-tuple-element.71), channel_id=1, source_target_pairs={{0,4},{1,5},{2,6},{3,7},{4,0},{5,1},{6,2},{7,3},{8,12},{9,13},{10,... | collective-permute-start | bytes 786440 | tf_op jit(solution)/shard_map/ppermute | solution.py:499
  55.5 13.9 %collective-permute-start.14 = (bf16[4,256,128]{2,1,0:T(8,128)(2,1)S(1)}, bf16[4,256,128]{2,1,0:T(8,128)(2,1)S(1)}, u32[]{:S(2)}, u32[]{:S(2)}) collective-permute-start(bf16[4,256,128]{2,1,0:T(8,128)(2,1)S(1)} %get-tuple-element.72), channel_id=1, source_target_pairs={{0,2},{1,3},{2,0},{3,1},{4,6},{5,7},{6,4},{7,5},{8,10},{9,11},{10,... | collective-permute-start | bytes 786440 | tf_op jit(solution)/shard_map/ppermute | solution.py:499
  56.0 13.4 %collective-permute-start.15 = (bf16[4,256,128]{2,1,0:T(8,128)(2,1)S(1)}, bf16[4,256,128]{2,1,0:T(8,128)(2,1)S(1)}, u32[]{:S(2)}, u32[]{:S(2)}) collective-permute-start(bf16[4,256,128]{2,1,0:T(8,128)(2,1)S(1)} %get-tuple-element.73), channel_id=1, source_target_pairs={{0,6},{1,7},{2,4},{3,5},{4,2},{5,3},{6,0},{7,1},{8,14},{9,15},{10,... | collective-permute-start | bytes 786440 | tf_op jit(solution)/shard_map/ppermute | solution.py:499
  60.9 10.2 %collective-permute-start.22 = (bf16[1,64,1024]{2,1,0:T(8,128)(2,1)S(1)}, bf16[1,64,1024]{2,1,0:T(8,128)(2,1)S(1)}, u32[]{:S(2)}, u32[]{:S(2)}) collective-permute-start(bf16[1,64,1024]{2,1,0:T(8,128)(2,1)S(1)} %get-tuple-element.79), channel_id=1, source_target_pairs={{0,8},{1,9},{2,10},{3,11},{4,12},{5,13},{6,14},{7,15},{8,0},{9,1},... | collective-permute-start | bytes 393224 | tf_op jit(solution)/shard_map/ppermute | solution.py:499
  62.0 12.6 %collective-permute-start.23 = (bf16[1,64,1024]{2,1,0:T(8,128)(2,1)S(1)}, bf16[1,64,1024]{2,1,0:T(8,128)(2,1)S(1)}, u32[]{:S(2)}, u32[]{:S(2)}) collective-permute-start(bf16[1,64,1024]{2,1,0:T(8,128)(2,1)S(1)} %get-tuple-element.80), channel_id=1, source_target_pairs={{0,16},{1,17},{2,18},{3,19},{4,20},{5,21},{6,22},{7,23},{8,24},{9,... | collective-permute-start | bytes 393224 | tf_op jit(solution)/shard_map/ppermute | solution.py:499
  64.4 10.2 %collective-permute-start.24 = (bf16[1,64,1024]{2,1,0:T(8,128)(2,1)S(1)}, bf16[1,64,1024]{2,1,0:T(8,128)(2,1)S(1)}, u32[]{:S(2)}, u32[]{:S(2)}) collective-permute-start(bf16[1,64,1024]{2,1,0:T(8,128)(2,1)S(1)} %get-tuple-element.81), channel_id=1, source_target_pairs={{0,24},{1,25},{2,26},{3,27},{4,28},{5,29},{6,30},{7,31},{8,16},{9,... | collective-permute-start | bytes 393224 | tf_op jit(solution)/shard_map/ppermute | solution.py:499
  69.5 10.1 %collective-permute-start.16 = (bf16[1,256,128]{2,1,0:T(8,128)(2,1)S(1)}, bf16[1,256,128]{2,1,0:T(8,128)(2,1)S(1)}, u32[]{:S(2)}, u32[]{:S(2)}) collective-permute-start(bf16[1,256,128]{2,1,0:T(8,128)(2,1)S(1)} %get-tuple-element.76), channel_id=1, source_target_pairs={{0,8},{1,9},{2,10},{3,11},{4,12},{5,13},{6,14},{7,15},{8,0},{9,1},... | collective-permute-start | bytes 196616 | tf_op jit(solution)/shard_map/ppermute | solution.py:499
  74.7 10.2 %collective-permute-start.27 = (bf16[1,64,1024]{2,1,0:T(8,128)(2,1)S(1)}, bf16[1,64,1024]{2,1,0:T(8,128)(2,1)S(1)}, u32[]{:S(2)}, u32[]{:S(2)}) collective-permute-start(bf16[1,64,1024]{2,1,0:T(8,128)(2,1)S(1)} %shard_map.148.refs_0_), channel_id=1, source_target_pairs={{0,3},{1,2},{2,1},{3,0},{4,7},{5,6},{6,5},{7,4},{8,11},{9,10},{10,... | collective-permute-start | bytes 393224 | tf_op jit(solution)/shard_map/ppermute | solution.py:499
  74.8 7.3 %collective-permute-start.17 = (bf16[1,256,128]{2,1,0:T(8,128)(2,1)S(1)}, bf16[1,256,128]{2,1,0:T(8,128)(2,1)S(1)}, u32[]{:S(2)}, u32[]{:S(2)}) collective-permute-start(bf16[1,256,128]{2,1,0:T(8,128)(2,1)S(1)} %get-tuple-element.77), channel_id=1, source_target_pairs={{0,16},{1,17},{2,18},{3,19},{4,20},{5,21},{6,22},{7,23},{8,24},{9,... | collective-permute-start | bytes 196616 | tf_op jit(solution)/shard_map/ppermute | solution.py:499
  77.7 6.1 %collective-permute-start.18 = (bf16[1,256,128]{2,1,0:T(8,128)(2,1)S(1)}, bf16[1,256,128]{2,1,0:T(8,128)(2,1)S(1)}, u32[]{:S(2)}, u32[]{:S(2)}) collective-permute-start(bf16[1,256,128]{2,1,0:T(8,128)(2,1)S(1)} %get-tuple-element.78), channel_id=1, source_target_pairs={{0,24},{1,25},{2,26},{3,27},{4,28},{5,29},{6,30},{7,31},{8,16},{9,... | collective-permute-start | bytes 196616 | tf_op jit(solution)/shard_map/ppermute | solution.py:499
  79.2 6.6 %collective-permute-start.26 = (bf16[1,64,1024]{2,1,0:T(8,128)(2,1)S(1)}, bf16[1,64,1024]{2,1,0:T(8,128)(2,1)S(1)}, u32[]{:S(2)}, u32[]{:S(2)}) collective-permute-start(bf16[1,64,1024]{2,1,0:T(8,128)(2,1)S(1)} %shard_map.148.refs_0_), channel_id=1, source_target_pairs={{0,2},{1,3},{2,0},{3,1},{4,6},{5,7},{6,4},{7,5},{8,10},{9,11},{10,... | collective-permute-start | bytes 393224 | tf_op jit(solution)/shard_map/ppermute | solution.py:499
  79.7 6.1 %collective-permute-start.25 = (bf16[1,64,1024]{2,1,0:T(8,128)(2,1)S(1)}, bf16[1,64,1024]{2,1,0:T(8,128)(2,1)S(1)}, u32[]{:S(2)}, u32[]{:S(2)}) collective-permute-start(bf16[1,64,1024]{2,1,0:T(8,128)(2,1)S(1)} %shard_map.148.refs_0_), channel_id=1, source_target_pairs={{0,1},{1,0},{2,3},{3,2},{4,5},{5,4},{6,7},{7,6},{8,9},{9,8},{10,11... | collective-permute-start | bytes 393224 | tf_op jit(solution)/shard_map/ppermute | solution.py:499
  83.8 4.0 %collective-permute-start.21 = (bf16[1,256,128]{2,1,0:T(8,128)(2,1)S(1)}, bf16[1,256,128]{2,1,0:T(8,128)(2,1)S(1)}, u32[]{:S(2)}, u32[]{:S(2)}) collective-permute-start(bf16[1,256,128]{2,1,0:T(8,128)(2,1)S(1)} %shard_map.147.refs_0_), channel_id=1, source_target_pairs={{0,3},{1,2},{2,1},{3,0},{4,7},{5,6},{6,5},{7,4},{8,11},{9,10},{10,... | collective-permute-start | bytes 196616 | tf_op jit(solution)/shard_map/ppermute | solution.py:499
  84.6 4.6 %collective-permute-start.20 = (bf16[1,256,128]{2,1,0:T(8,128)(2,1)S(1)}, bf16[1,256,128]{2,1,0:T(8,128)(2,1)S(1)}, u32[]{:S(2)}, u32[]{:S(2)}) collective-permute-start(bf16[1,256,128]{2,1,0:T(8,128)(2,1)S(1)} %shard_map.147.refs_0_), channel_id=1, source_target_pairs={{0,2},{1,3},{2,0},{3,1},{4,6},{5,7},{6,4},{7,5},{8,10},{9,11},{10,... | collective-permute-start | bytes 196616 | tf_op jit(solution)/shard_map/ppermute | solution.py:499
  84.9 4.3 %collective-permute-start.19 = (bf16[1,256,128]{2,1,0:T(8,128)(2,1)S(1)}, bf16[1,256,128]{2,1,0:T(8,128)(2,1)S(1)}, u32[]{:S(2)}, u32[]{:S(2)}) collective-permute-start(bf16[1,256,128]{2,1,0:T(8,128)(2,1)S(1)} %shard_map.147.refs_0_), channel_id=1, source_target_pairs={{0,1},{1,0},{2,3},{3,2},{4,5},{5,4},{6,7},{7,6},{8,9},{9,8},{10,11... | collective-permute-start | bytes 196616 | tf_op jit(solution)/shard_map/ppermute | solution.py:499

commit v6 on v4

--- a/solution.py
+++ b/solution.py
@@ -631,12 +631,14 @@
             radix = min(4, left)
             split = fold((left // radix * 2).bit_length() - 1, radix, pieces)
 
-    def gather(last):
-        return [last] + [permute(last, 0, j) for j in range(1, 4)]
+    def gather(last, relay=False):
+        other = permute(last, 0, 2)
+        both = permute(other, 0, 1) if relay else permute(last, 0, 3)
+        return [last, permute(last, 0, 1), other, both]
 
     big = reduce_z(big)
     small = reduce_z(fold(shift, radix, small, [flag]))
-    big = gather(fold(0, 1, big, [small[0]])[0])
+    big = gather(fold(0, 1, big, [small[0]])[0], True)
     full_up, full_down, full_two, w_rows = call(
         functools.partial(place_mlp_kernel, slabs, width, units),
         [

time: 89.5 us -> 89.4 us (level)
  starting transfers between devices: 35.9 us -> 34.3 us
  waiting for transfers between devices: 24.8 us -> 26.3 us
    ppermute x28, starting transfers between devices: 31.3 us -> 29.7 us  [permute(): lax.ppermute(array, BOTH, swap_pairs(slabs, cases, flip_slab, flip_case))]
    ppermute x28, waiting for transfers between devices: 17.1 us -> 18.6 us  [permute(): lax.ppermute(array, BOTH, swap_pairs(slabs, cases, flip_slab, flip_case))]
  transfers between devices with their start and end apart: 29 -> 29, of which waited for: 12 -> 13; matrix products, arithmetic and copies ran while one was open for 0% -> 0% of each run, Pallas kernels for 19% -> 19%
where the time goes in v6:
time: 89.4 us; the launch traced here: 89.1 us
  starting transfers between devices  34.3 us (38%)
  waiting for transfers between devices  26.3 us (29%)
  Pallas kernels  22.7 us (25%)
  local copies, waits for them, and re-layouts  5 us (6%)
    ppermute x28, starting transfers between devices, permute(): lax.ppermute(array, BOTH, swap_pairs(slabs, cases, flip_slab, flip_case))  29.7 us
    pallas_call x16, Pallas kernels, call(): pl.pallas_call(run, out_shape=outs, in_specs=[vmem if one else far for on...  22.7 us
    ppermute x28, waiting for transfers between devices, permute(): lax.ppermute(array, BOTH, swap_pairs(slabs, cases, flip_slab, flip_case))  18.6 us
    all_to_all x1, waiting for transfers between devices, body(): back = lax.all_to_all(back, 'slab', split_axis=0, concat_axis=0, tiled=True)  7.71 us
    unnamed x24, local copies, waits for them, and re-layouts  5 us
    all_to_all x1, starting transfers between devices, body(): back = lax.all_to_all(back, 'slab', split_axis=0, concat_axis=0, tiled=True)  4.59 us
  transfers between devices with their start and end apart: 29, of which 13 were waited for; matrix products, arithmetic and copies ran while one was open for 0% of the time, Pallas kernels for 19%

profile of v6, /device:TPU:0, one launch (start us, length us, event | category | flops | bytes accessed | tf_op | source)
XLA Modules:
  0.0 89.1 jit_solution(8390245861516301395)
XLA Ops:
  0.6 2.9 %shard_map.135 = (bf16[16,1536]{1,0:T(8,128)(2,1)S(1)}, bf16[16,1536]{1,0:T(8,128)(2,1)S(1)}, bf16[16,1536]{1,0:T(8,128)(2,1)S(1)}, bf16[16,1536]{1,0:T(8,128)(2...) custom-call(bf16[128,512]{1,0:T(8,128)(2,1)} %bitcast.20, ...), custom_call_target="tpu_custom_call" | custom-call | flops 10000000 | bytes 10000 | tf_op jit(solution)/shard_map/pallas_call | solution.py:50
  3.5 3.0 %collective-permute-start = (bf16[16,1536]{1,0:T(8,128)(2,1)S(1)}, bf16[16,1536]{1,0:T(8,128)(2,1)S(1)}, u32[]{:S(2)}, u32[]{:S(2)}) collective-permute-start(bf16[16,1536]{1,0:T(8,128)(2,1)S(1)} %get-tuple-element.49), channel_id=1, source_target_pairs={{0,4},{1,5},{2,6},{3,7},{4,0},{5,1},{6,2},{7,3},{8,12},{9,13},{10,... | collective-permute-start | bytes 147464 | tf_op jit(solution)/shard_map/ppermute | solution.py:499
  6.5 1.6 %collective-permute-start.1 = (bf16[16,1536]{1,0:T(8,128)(2,1)S(1)}, bf16[16,1536]{1,0:T(8,128)(2,1)S(1)}, u32[]{:S(2)}, u32[]{:S(2)}) collective-permute-start(bf16[16,1536]{1,0:T(8,128)(2,1)S(1)} %get-tuple-element.50), channel_id=1, source_target_pairs={{0,8},{1,9},{2,10},{3,11},{4,12},{5,13},{6,14},{7,15},{8,0},{9,1},... | collective-permute-start | bytes 147464 | tf_op jit(solution)/shard_map/ppermute | solution.py:499
  8.1 3.0 %collective-permute-start.3 = (bf16[16,1536]{1,0:T(8,128)(2,1)S(1)}, bf16[16,1536]{1,0:T(8,128)(2,1)S(1)}, u32[]{:S(2)}, u32[]{:S(2)}) collective-permute-start(bf16[16,1536]{1,0:T(8,128)(2,1)S(1)} %get-tuple-element.52), channel_id=1, source_target_pairs={{0,16},{1,17},{2,18},{3,19},{4,20},{5,21},{6,22},{7,23},{8,24},{9,... | collective-permute-start | bytes 147464 | tf_op jit(solution)/shard_map/ppermute | solution.py:499
  11.1 1.3 %collective-permute-start.4 = (bf16[16,1536]{1,0:T(8,128)(2,1)S(1)}, bf16[16,1536]{1,0:T(8,128)(2,1)S(1)}, u32[]{:S(2)}, u32[]{:S(2)}) collective-permute-start(bf16[16,1536]{1,0:T(8,128)(2,1)S(1)} %get-tuple-element.53), channel_id=1, source_target_pairs={{0,20},{1,21},{2,22},{3,23},{4,16},{5,17},{6,18},{7,19},{8,28},{9,... | collective-permute-start | bytes 147464 | tf_op jit(solution)/shard_map/ppermute | solution.py:499
  12.4 0.0 collective-permute-done.refs_1_
  12.4 3.6 %collective-permute-start.5 = (bf16[16,1536]{1,0:T(8,128)(2,1)S(1)}, bf16[16,1536]{1,0:T(8,128)(2,1)S(1)}, u32[]{:S(2)}, u32[]{:S(2)}) collective-permute-start(bf16[16,1536]{1,0:T(8,128)(2,1)S(1)} %get-tuple-element.54), channel_id=1, source_target_pairs={{0,24},{1,25},{2,26},{3,27},{4,28},{5,29},{6,30},{7,31},{8,16},{9,... | collective-permute-start | bytes 147464 | tf_op jit(solution)/shard_map/ppermute | solution.py:499
  16.0 0.0 collective-permute-start.6
  16.1 1.7 %copy-done.1 = bf16[512,2048]{1,0:T(8,128)(2,1)S(1)} copy-done((bf16[512,2048]{1,0:T(8,128)(2,1)S(1)}, bf16[512,2048]{1,0:T(8,128)(2,1)}, u32[]{:S(2)}) %copy-start.1) | copy-done | bytes 2097176
  17.8 1.6 %copy-done.3 = bf16[2048,512]{1,0:T(8,128)(2,1)S(1)} copy-done((bf16[2048,512]{1,0:T(8,128)(2,1)S(1)}, bf16[2048,512]{1,0:T(8,128)(2,1)}, u32[]{:S(2)}) %copy-start.3) | copy-done | bytes 2097176
  19.4 1.3 %shard_map.136 = (bf16[512,512]{1,0:T(8,128)(2,1)S(1)}, bf16[512,512]{1,0:T(8,128)(2,1)S(1)}) custom-call(bf16[512,2048]{1,0:T(8,128)(2,1)S(1)} %copy-done.1, bf16[2048,512]{1,0:T(8,128)(2,1)S(1)} %copy-done.3), custom_call_target="tpu_custom_call" | custom-call | flops 10000000 | bytes 10000 | tf_op jit(solution)/shard_map/pallas_call | solution.py:50
  20.7 0.0 copy-start.8
  20.7 0.8 copy-done.8
  21.5 0.0 collective-permute-done.2.refs_3_
  21.5 0.0 collective-permute-done.4.refs_5_
  21.5 1.3 %collective-permute-done.6.refs_7_ = bf16[16,1536]{1,0:T(8,128)(2,1)S(1)} collective-permute-done((bf16[16,1536]{1,0:T(8,128)(2,1)S(1)}, bf16[16,1536]{1,0:T(8,128)(2,1)S(1)}, u32[]{:S(2)}, u32[]{:S(2)}) %collective-permute-start.6) | collective-permute-done | bytes 49184 | tf_op jit(solution)/shard_map/ppermute | solution.py:499
  22.8 1.3 %shard_map.137 = (bf16[128,1024]{1,0:T(8,128)(2,1)S(1)}, bf16[128,1536]{1,0:T(8,128)(2,1)S(1)}, bf16[128,512]{1,0:T(8,128)(2,1)S(1)}, bf16[128,512]{1,0:T(8,128)(2,1)S(1)}, bf16[128,512]{1,0:T(8,128)(2,1)S(1)}) custom-call(bf16[16,1536]{1,0:T(8,128)(2,1)S(1)} %get-tuple-element.48.refs_0_, bf16[16,1536]{1,0:T(8,128)(2,1)S(1)} %collective-permute-done.refs_1_, ...), custom_call_target="tpu_custom_call" | custom-call | flops 10000000 | bytes 10000 | tf_op jit(solution)/shard_map/pallas_call | solution.py:50
  24.1 0.6 collective-permute-start.7
  24.7 1.5 %collective-permute-start.8 = (bf16[128,1024]{1,0:T(8,128)(2,1)S(1)}, bf16[128,1024]{1,0:T(8,128)(2,1)S(1)}, u32[]{:S(2)}, u32[]{:S(2)}) collective-permute-start(bf16[128,1024]{1,0:T(8,128)(2,1)S(1)} %get-tuple-element.58.refs_0_), channel_id=1, source_target_pairs={{0,2},{1,3},{2,0},{3,1},{4,6},{5,7},{6,4},{7,5},{8,10},{9,11},{10,... | collective-permute-start | bytes 786440 | tf_op jit(solution)/shard_map/ppermute | solution.py:499
  26.2 2.4 %shard_map.138 = (bf16[128,512]{1,0:T(8,128)(2,1)S(1)}, f32[128,512]{1,0:T(8,128)S(1)}) custom-call(bf16[128,1024]{1,0:T(8,128)(2,1)S(1)} %get-tuple-element.58.refs_0_, bf16[128,512]{1,0:T(8,128)(2,1)S(1)} %get-tuple-element.59.refs_1_, f32[1,512]{1,0:T(1,128)S(1)} %bitcast.18, bf16[512,512]{1,0:T(8,128)(2,1)S(1)} %copy-done.5, ...), custom_call_target="tpu_custom_call" | custom-call | flops 10000000 | bytes 10000 | tf_op jit(solution)/shard_map/pallas_call | solution.py:50
  28.6 2.7 %shard_map.139 = (bf16[128,1024]{1,0:T(8,128)(2,1)S(1)}, bf16[128,3072]{1,0:T(8,128)(2,1)S(1)}) custom-call(bf16[128,1536]{1,0:T(8,128)(2,1)S(1)} %get-tuple-element.57.refs_0_, bf16[128,512]{1,0:T(8,128)(2,1)S(1)} %get-tuple-element.60.refs_1_, f32[128,512]{1,0:T(8,128)S(1)} %get-tuple-element.61.refs_2_, bf16[128,512]{1,0:T(8,128)(2,1)S(1)} %get-tuple-element.62.refs_3_, ...), custom_call_target="tpu_custom_call" | custom-call | flops 10000000 | bytes 10000 | tf_op jit(solution)/shard_map/pallas_call | solution.py:50
  31.3 0.9 copy-done.6
  32.2 0.7 shard_map.140
  32.9 4.6 %all-to-all-start = ((bf16[8,16,1024]{2,1,0:T(8,128)(2,1)}), bf16[8,16,1024]{2,1,0:T(8,128)(2,1)S(1)}, u32[]{:S(2)}, u32[]{:S(2)}) async-start(bf16[8,16,1024]{2,1,0:T(8,128)(2,1)} %bitcast.4), calls=%async_computation | async-start | bytes 524288 | tf_op jit(solution)/shard_map/all_to_all | solution.py:568
  37.5 0.5 collective-permute-start.11
  38.0 7.7 %all-to-all-done = bf16[8,16,1024]{2,1,0:T(8,128)(2,1)S(1)} async-done(((bf16[8,16,1024]{2,1,0:T(8,128)(2,1)}), bf16[8,16,1024]{2,1,0:T(8,128)(2,1)S(1)}, u32[]{:S(2)}, u32[]{:S(2)}) %all-to-all-start) | async-done | bytes 262176 | tf_op jit(solution)/shard_map/all_to_all | solution.py:568
  45.7 2.6 %shard_map.141.refs_2_.refs_4_.refs_1_ = bf16[128,2048]{1,0:T(8,128)(2,1)S(1)} custom-call(bf16[128,1024]{1,0:T(8,128)(2,1)S(1)} %bitcast.9, bf16[128,512]{1,0:T(8,128)(2,1)S(1)} %get-tuple-element.65.refs_1_.refs_2_, f32[1,512]{1,0:T(1,128)S(1)} %bitcast.14, bf16[512,1536]{1,0:T(8,128)(2,1)S(1)} %copy-done), custom_call_target="tpu_custom_call" | custom-call | flops 10000000 | bytes 10000 | tf_op jit(solution)/shard_map/pallas_call | solution.py:50
  48.3 0.0 copy-start.9
  48.4 0.1 shard_map.143.refs_0_
  48.4 0.1 collective-permute-start.12
  48.5 0.5 collective-permute-start.9
  49.0 0.1 collective-permute-start.10
  49.1 3.2 %collective-permute-done.9.refs_1_ = bf16[128,3072]{1,0:T(8,128)(2,1)S(1)} collective-permute-done((bf16[128,3072]{1,0:T(8,128)(2,1)S(1)}, bf16[128,3072]{1,0:T(8,128)(2,1)S(1)}, u32[]{:S(2)}, u32[]{:S(2)}) %collective-permute-start.9) | collective-permute-done | bytes 786464 | tf_op jit(solution)/shard_map/ppermute | solution.py:499
  52.3 0.7 collective-permute-done.10.refs_3_
  53.0 1.0 %shard_map.142 = (bf16[4,256,128]{2,1,0:T(8,128)(2,1)S(1)}, bf16[4,256,128]{2,1,0:T(8,128)(2,1)S(1)}, bf16[4,256,128]{2,1,0:T(8,128)(2,1)S(1)}, bf16[4,256,128]{2,1,0:T(8,128)(2,1)S(1)}) custom-call(bf16[128,3072]{1,0:T(8,128)(2,1)S(1)} %copy-done.7, bf16[128,3072]{1,0:T(8,128)(2,1)S(1)} %collective-permute-done.9.refs_1_, ...), custom_call_target="tpu_custom_call" | custom-call | flops 10000000 | bytes 10000 | tf_op jit(solution)/shard_map/pallas_call | solution.py:50
  54.1 0.1 collective-permute-start.13
  54.2 0.5 collective-permute-start.14
  54.8 2.9 %collective-permute-start.15 = (bf16[4,256,128]{2,1,0:T(8,128)(2,1)S(1)}, bf16[4,256,128]{2,1,0:T(8,128)(2,1)S(1)}, u32[]{:S(2)}, u32[]{:S(2)}) collective-permute-start(bf16[4,256,128]{2,1,0:T(8,128)(2,1)S(1)} %get-tuple-element.73), channel_id=1, source_target_pairs={{0,6},{1,7},{2,4},{3,5},{4,2},{5,3},{6,0},{7,1},{8,14},{9,15},{10,... | collective-permute-start | bytes 786440 | tf_op jit(solution)/shard_map/ppermute | solution.py:499
  57.7 3.0 %shard_map.144 = (bf16[1,64,1024]{2,1,0:T(8,128)(2,1)S(1)}, bf16[1,64,1024]{2,1,0:T(8,128)(2,1)S(1)}, bf16[1,64,1024]{2,1,0:T(8,128)(2,1)S(1)}, bf16[1,64,1024]{2,1,0:T(8,128)(2,1)S(1)}) custom-call(bf16[512,1024]{1,0:T(8,128)(2,1)S(1)} %shard_map.143.refs_0_, bf16[512,1024]{1,0:T(8,128)(2,1)S(1)} %collective-permute-done.12.refs_1_, ...), custom_call_target="tpu_custom_call" | custom-call | flops 10000000 | bytes 10000 | tf_op jit(solution)/shard_map/pallas_call | solution.py:50
  60.7 0.1 collective-permute-start.22
  60.8 1.1 %collective-permute-start.23 = (bf16[1,64,1024]{2,1,0:T(8,128)(2,1)S(1)}, bf16[1,64,1024]{2,1,0:T(8,128)(2,1)S(1)}, u32[]{:S(2)}, u32[]{:S(2)}) collective-permute-start(bf16[1,64,1024]{2,1,0:T(8,128)(2,1)S(1)} %get-tuple-element.80), channel_id=1, source_target_pairs={{0,16},{1,17},{2,18},{3,19},{4,20},{5,21},{6,22},{7,23},{8,24},{9,... | collective-permute-start | bytes 393224 | tf_op jit(solution)/shard_map/ppermute | solution.py:499
  61.9 1.4 %collective-permute-done.13.refs_1_ = bf16[4,256,128]{2,1,0:T(8,128)(2,1)S(1)} collective-permute-done((bf16[4,256,128]{2,1,0:T(8,128)(2,1)S(1)}, bf16[4,256,128]{2,1,0:T(8,128)(2,1)S(1)}, u32[]{:S(2)}, u32[]{:S(2)}) %collective-permute-start.13) | collective-permute-done | bytes 262176 | tf_op jit(solution)/shard_map/ppermute | solution.py:499
  63.3 1.8 %collective-permute-start.24 = (bf16[1,64,1024]{2,1,0:T(8,128)(2,1)S(1)}, bf16[1,64,1024]{2,1,0:T(8,128)(2,1)S(1)}, u32[]{:S(2)}, u32[]{:S(2)}) collective-permute-start(bf16[1,64,1024]{2,1,0:T(8,128)(2,1)S(1)} %get-tuple-element.81), channel_id=1, source_target_pairs={{0,24},{1,25},{2,26},{3,27},{4,28},{5,29},{6,30},{7,31},{8,16},{9,... | collective-permute-start | bytes 393224 | tf_op jit(solution)/shard_map/ppermute | solution.py:499
  65.1 1.6 %shard_map.145 = (bf16[128,512]{1,0:T(8,128)(2,1)}, f32[8,128]{1,0:T(8,128)S(1)}) custom-call(bf16[128,1024]{1,0:T(8,128)(2,1)S(1)} %bitcast.10, bf16[128,2048]{1,0:T(8,128)(2,1)S(1)} %shard_map.141.refs_2_.refs_4_.refs_1_, bf16[128,512]{1,0:T(8,128)(2,1)S(1)} %get-tuple-element.65.refs_1_.refs_2_, f32[1,512]{1,0:T(1,128)S(1)} %bitcast.15, ...), custom_call_target="tpu_custom_call" | custom-call | flops 10000000 | bytes 10000 | tf_op jit(solution)/shard_map/pallas_call | solution.py:50
  66.7 1.5 %collective-permute-done.14.refs_2_ = bf16[4,256,128]{2,1,0:T(8,128)(2,1)S(1)} collective-permute-done((bf16[4,256,128]{2,1,0:T(8,128)(2,1)S(1)}, bf16[4,256,128]{2,1,0:T(8,128)(2,1)S(1)}, u32[]{:S(2)}, u32[]{:S(2)}) %collective-permute-start.14) | collective-permute-done | bytes 262176 | tf_op jit(solution)/shard_map/ppermute | solution.py:499
  68.2 0.1 shard_map.146
  68.4 5.1 %collective-permute-done.23.refs_2_ = bf16[1,64,1024]{2,1,0:T(8,128)(2,1)S(1)} collective-permute-done((bf16[1,64,1024]{2,1,0:T(8,128)(2,1)S(1)}, bf16[1,64,1024]{2,1,0:T(8,128)(2,1)S(1)}, u32[]{:S(2)}, u32[]{:S(2)}) %collective-permute-start.23) | collective-permute-done | bytes 131104 | tf_op jit(solution)/shard_map/ppermute | solution.py:499
  73.5 0.1 shard_map.148.refs_0_
  73.5 0.6 collective-permute-start.26
  74.1 2.0 %collective-permute-start.16 = (bf16[1,256,128]{2,1,0:T(8,128)(2,1)S(1)}, bf16[1,256,128]{2,1,0:T(8,128)(2,1)S(1)}, u32[]{:S(2)}, u32[]{:S(2)}) collective-permute-start(bf16[1,256,128]{2,1,0:T(8,128)(2,1)S(1)} %get-tuple-element.76), channel_id=1, source_target_pairs={{0,8},{1,9},{2,10},{3,11},{4,12},{5,13},{6,14},{7,15},{8,0},{9,1},... | collective-permute-start | bytes 196616 | tf_op jit(solution)/shard_map/ppermute | solution.py:499
  76.1 0.2 collective-permute-start.17
  76.3 2.2 %collective-permute-start.18 = (bf16[1,256,128]{2,1,0:T(8,128)(2,1)S(1)}, bf16[1,256,128]{2,1,0:T(8,128)(2,1)S(1)}, u32[]{:S(2)}, u32[]{:S(2)}) collective-permute-start(bf16[1,256,128]{2,1,0:T(8,128)(2,1)S(1)} %get-tuple-element.78), channel_id=1, source_target_pairs={{0,24},{1,25},{2,26},{3,27},{4,28},{5,29},{6,30},{7,31},{8,16},{9,... | collective-permute-start | bytes 196616 | tf_op jit(solution)/shard_map/ppermute | solution.py:499
  78.5 0.1 collective-permute-done.26.refs_2_
  78.6 0.4 collective-permute-start.27
  79.0 0.8 collective-permute-done.16.refs_1_
  79.8 2.0 %collective-permute-done.17.refs_2_ = bf16[1,256,128]{2,1,0:T(8,128)(2,1)S(1)} collective-permute-done((bf16[1,256,128]{2,1,0:T(8,128)(2,1)S(1)}, bf16[1,256,128]{2,1,0:T(8,128)(2,1)S(1)}, u32[]{:S(2)}, u32[]{:S(2)}) %collective-permute-start.17) | collective-permute-done | bytes 65568 | tf_op jit(solution)/shard_map/ppermute | solution.py:499
  81.8 0.7 collective-permute-done.18.refs_3_
  82.5 0.1 collective-permute-start.19
  82.6 1.6 %collective-permute-start.20 = (bf16[1,256,128]{2,1,0:T(8,128)(2,1)S(1)}, bf16[1,256,128]{2,1,0:T(8,128)(2,1)S(1)}, u32[]{:S(2)}, u32[]{:S(2)}) collective-permute-start(bf16[1,256,128]{2,1,0:T(8,128)(2,1)S(1)} %shard_map.147.refs_0_), channel_id=1, source_target_pairs={{0,2},{1,3},{2,0},{3,1},{4,6},{5,7},{6,4},{7,5},{8,10},{9,11},{10,... | collective-permute-start | bytes 196616 | tf_op jit(solution)/shard_map/ppermute | solution.py:499
  84.2 0.3 collective-permute-start.21
  84.5 2.1 %shard_map.149 = (f32[64,2048]{1,0:T(8,128)}, f32[256,512]{1,0:T(8,128)}, f32[1,64]{1,0:T(1,128)}, bf16[64,1536]{1,0:T(8,128)(2,1)S(1)}) custom-call(bf16[1,64,1024]{2,1,0:T(8,128)(2,1)S(1)} %shard_map.148.refs_0_, bf16[1,64,1024]{2,1,0:T(8,128)(2,1)S(1)} %collective-permute-done.25.refs_1_, bf16[1,64,1024]{2,1,0:T(8,128)(2,1)S(1)} %collective-permute-done.26.refs_2_, ...), custom_call_target="tpu_custom_call" | custom-call | flops 10000000 | bytes 10000 | tf_op jit(solution)/shard_map/pallas_call | solution.py:50
  86.6 0.6 collective-permute-done.20.refs_2_
  87.1 1.1 %collective-permute-done.21.refs_3_ = bf16[1,256,128]{2,1,0:T(8,128)(2,1)S(1)} collective-permute-done((bf16[1,256,128]{2,1,0:T(8,128)(2,1)S(1)}, bf16[1,256,128]{2,1,0:T(8,128)(2,1)S(1)}, u32[]{:S(2)}, u32[]{:S(2)}) %collective-permute-start.21) | collective-permute-done | bytes 65568 | tf_op jit(solution)/shard_map/ppermute | solution.py:499
  88.3 0.8 shard_map.150
  (34 shorter events, 0.1 us)
Async XLA Ops:
  3.5 8.9 %collective-permute-start = (bf16[16,1536]{1,0:T(8,128)(2,1)S(1)}, bf16[16,1536]{1,0:T(8,128)(2,1)S(1)}, u32[]{:S(2)}, u32[]{:S(2)}) collective-permute-start(bf16[16,1536]{1,0:T(8,128)(2,1)S(1)} %get-tuple-element.49), channel_id=1, source_target_pairs={{0,4},{1,5},{2,6},{3,7},{4,0},{5,1},{6,2},{7,3},{8,12},{9,13},{10,... | collective-permute-start | bytes 147464 | tf_op jit(solution)/shard_map/ppermute | solution.py:499
  6.5 9.5 %collective-permute-start.1 = (bf16[16,1536]{1,0:T(8,128)(2,1)S(1)}, bf16[16,1536]{1,0:T(8,128)(2,1)S(1)}, u32[]{:S(2)}, u32[]{:S(2)}) collective-permute-start(bf16[16,1536]{1,0:T(8,128)(2,1)S(1)} %get-tuple-element.50), channel_id=1, source_target_pairs={{0,8},{1,9},{2,10},{3,11},{4,12},{5,13},{6,14},{7,15},{8,0},{9,1},... | collective-permute-start | bytes 147464 | tf_op jit(solution)/shard_map/ppermute | solution.py:499
  8.1 13.4 %collective-permute-start.2 = (bf16[16,1536]{1,0:T(8,128)(2,1)S(1)}, bf16[16,1536]{1,0:T(8,128)(2,1)S(1)}, u32[]{:S(2)}, u32[]{:S(2)}) collective-permute-start(bf16[16,1536]{1,0:T(8,128)(2,1)S(1)} %get-tuple-element.51), channel_id=1, source_target_pairs={{0,12},{1,13},{2,14},{3,15},{4,8},{5,9},{6,10},{7,11},{8,4},{9,5},... | collective-permute-start | bytes 147464 | tf_op jit(solution)/shard_map/ppermute | solution.py:499
  8.1 13.4 %collective-permute-start.3 = (bf16[16,1536]{1,0:T(8,128)(2,1)S(1)}, bf16[16,1536]{1,0:T(8,128)(2,1)S(1)}, u32[]{:S(2)}, u32[]{:S(2)}) collective-permute-start(bf16[16,1536]{1,0:T(8,128)(2,1)S(1)} %get-tuple-element.52), channel_id=1, source_target_pairs={{0,16},{1,17},{2,18},{3,19},{4,20},{5,21},{6,22},{7,23},{8,24},{9,... | collective-permute-start | bytes 147464 | tf_op jit(solution)/shard_map/ppermute | solution.py:499
  11.1 10.3 %collective-permute-start.4 = (bf16[16,1536]{1,0:T(8,128)(2,1)S(1)}, bf16[16,1536]{1,0:T(8,128)(2,1)S(1)}, u32[]{:S(2)}, u32[]{:S(2)}) collective-permute-start(bf16[16,1536]{1,0:T(8,128)(2,1)S(1)} %get-tuple-element.53), channel_id=1, source_target_pairs={{0,20},{1,21},{2,22},{3,23},{4,16},{5,17},{6,18},{7,19},{8,28},{9,... | collective-permute-start | bytes 147464 | tf_op jit(solution)/shard_map/ppermute | solution.py:499
  12.4 9.1 %collective-permute-start.5 = (bf16[16,1536]{1,0:T(8,128)(2,1)S(1)}, bf16[16,1536]{1,0:T(8,128)(2,1)S(1)}, u32[]{:S(2)}, u32[]{:S(2)}) collective-permute-start(bf16[16,1536]{1,0:T(8,128)(2,1)S(1)} %get-tuple-element.54), channel_id=1, source_target_pairs={{0,24},{1,25},{2,26},{3,27},{4,28},{5,29},{6,30},{7,31},{8,16},{9,... | collective-permute-start | bytes 147464 | tf_op jit(solution)/shard_map/ppermute | solution.py:499
  16.0 6.8 %copy-start = (bf16[512,1536]{1,0:T(8,128)(2,1)S(1)}, bf16[512,1536]{1,0:T(8,128)(2,1)}, u32[]{:S(2)}) copy-start(bf16[512,1536]{1,0:T(8,128)(2,1)} %refs_6_.3) | copy-start | bytes 4718596
  16.0 6.8 %collective-permute-start.6 = (bf16[16,1536]{1,0:T(8,128)(2,1)S(1)}, bf16[16,1536]{1,0:T(8,128)(2,1)S(1)}, u32[]{:S(2)}, u32[]{:S(2)}) collective-permute-start(bf16[16,1536]{1,0:T(8,128)(2,1)S(1)} %get-tuple-element.55), channel_id=1, source_target_pairs={{0,28},{1,29},{2,30},{3,31},{4,24},{5,25},{6,26},{7,27},{8,20},{9,... | collective-permute-start | bytes 147464 | tf_op jit(solution)/shard_map/ppermute | solution.py:499
  16.1 1.7 %copy-start.1 = (bf16[512,2048]{1,0:T(8,128)(2,1)S(1)}, bf16[512,2048]{1,0:T(8,128)(2,1)}, u32[]{:S(2)}) copy-start(bf16[512,2048]{1,0:T(8,128)(2,1)} %refs_5_.3) | copy-start | bytes 6291460
  17.8 1.6 %copy-start.3 = (bf16[2048,512]{1,0:T(8,128)(2,1)S(1)}, bf16[2048,512]{1,0:T(8,128)(2,1)}, u32[]{:S(2)}) copy-start(bf16[2048,512]{1,0:T(8,128)(2,1)} %refs_5_.2) | copy-start | bytes 6291460
  19.4 3.5 %copy-start.5 = (bf16[512,512]{1,0:T(8,128)(2,1)S(1)}, bf16[512,512]{1,0:T(8,128)(2,1)}, u32[]{:S(2)}) copy-start(bf16[512,512]{1,0:T(8,128)(2,1)} %refs_3_.4) | copy-start | bytes 1572868
  19.4 3.5 %copy-start.10 = (f32[512]{0:T(512)S(1)}, f32[512]{0:T(512)}, u32[]{:S(2)}) copy-start(f32[512]{0:T(512)} %param.14) | copy-start | bytes 6148
  19.4 3.5 %copy-start.11 = (f32[512]{0:T(512)S(1)}, f32[512]{0:T(512)}, u32[]{:S(2)}) copy-start(f32[512]{0:T(512)} %param.15) | copy-start | bytes 6148
  19.4 6.8 %copy-start.4 = (bf16[2048,512]{1,0:T(8,128)(2,1)S(1)}, bf16[2048,512]{1,0:T(8,128)(2,1)}, u32[]{:S(2)}) copy-start(bf16[2048,512]{1,0:T(8,128)(2,1)} %refs_5_.2) | copy-start | bytes 6291460
  20.7 0.8 copy-start.8
  21.5 4.7 %copy-start.2 = (bf16[512,2048]{1,0:T(8,128)(2,1)S(1)}, bf16[512,2048]{1,0:T(8,128)(2,1)}, u32[]{:S(2)}) copy-start(bf16[512,2048]{1,0:T(8,128)(2,1)} %refs_5_.3) | copy-start | bytes 6291460
  24.1 8.1 %collective-permute-start.7 = (bf16[128,1024]{1,0:T(8,128)(2,1)S(1)}, bf16[128,1024]{1,0:T(8,128)(2,1)S(1)}, u32[]{:S(2)}, u32[]{:S(2)}) collective-permute-start(bf16[128,1024]{1,0:T(8,128)(2,1)S(1)} %get-tuple-element.58.refs_0_), channel_id=1, source_target_pairs={{0,4},{1,5},{2,6},{3,7},{4,0},{5,1},{6,2},{7,3},{8,12},{9,13},{10,... | collective-permute-start | bytes 786440 | tf_op jit(solution)/shard_map/ppermute | solution.py:499
  24.7 7.5 %collective-permute-start.8 = (bf16[128,1024]{1,0:T(8,128)(2,1)S(1)}, bf16[128,1024]{1,0:T(8,128)(2,1)S(1)}, u32[]{:S(2)}, u32[]{:S(2)}) collective-permute-start(bf16[128,1024]{1,0:T(8,128)(2,1)S(1)} %get-tuple-element.58.refs_0_), channel_id=1, source_target_pairs={{0,2},{1,3},{2,0},{3,1},{4,6},{5,7},{6,4},{7,5},{8,10},{9,11},{10,... | collective-permute-start | bytes 786440 | tf_op jit(solution)/shard_map/ppermute | solution.py:499
  31.3 0.9 %copy-start.6 = (bf16[128,3072]{1,0:T(8,128)(2,1)}, bf16[128,3072]{1,0:T(8,128)(2,1)S(1)}, u32[]{:S(2)}) copy-start(bf16[128,3072]{1,0:T(8,128)(2,1)S(1)} %get-tuple-element.66.refs_0_) | copy-start | bytes 2359300
  32.9 12.8 %all-to-all-start = ((bf16[8,16,1024]{2,1,0:T(8,128)(2,1)}), bf16[8,16,1024]{2,1,0:T(8,128)(2,1)S(1)}, u32[]{:S(2)}, u32[]{:S(2)}) async-start(bf16[8,16,1024]{2,1,0:T(8,128)(2,1)} %bitcast.4), calls=%async_computation | async-start | bytes 524288 | tf_op jit(solution)/shard_map/all_to_all | solution.py:568
  37.5 10.9 %collective-permute-start.11 = (bf16[128,1024]{1,0:T(8,128)(2,1)S(1)}, bf16[128,1024]{1,0:T(8,128)(2,1)S(1)}, u32[]{:S(2)}, u32[]{:S(2)}) collective-permute-start(bf16[128,1024]{1,0:T(8,128)(2,1)S(1)} %collective-permute-done.7.refs_1_), channel_id=1, source_target_pairs={{0,2},{1,3},{2,0},{3,1},{4,6},{5,7},{6,4},{7,5},{8,10},{9,11},{10,... | collective-permute-start | bytes 786440 | tf_op jit(solution)/shard_map/ppermute | solution.py:499
  45.7 2.8 %copy-start.7 = (bf16[128,3072]{1,0:T(8,128)(2,1)S(1)}, bf16[128,3072]{1,0:T(8,128)(2,1)}, u32[]{:S(2)}) copy-start(bf16[128,3072]{1,0:T(8,128)(2,1)} %copy-done.6) | copy-start | bytes 2359300
  48.3 9.3 %copy-start.9 = (bf16[512,512]{1,0:T(8,128)(2,1)S(1)}, bf16[512,512]{1,0:T(8,128)(2,1)}, u32[]{:S(2)}) copy-start(bf16[512,512]{1,0:T(8,128)(2,1)} %copy-done.8) | copy-start | bytes 1572868
  48.4 9.2 %collective-permute-start.12 = (bf16[512,1024]{1,0:T(8,128)(2,1)S(1)}, bf16[512,1024]{1,0:T(8,128)(2,1)S(1)}, u32[]{:S(2)}, u32[]{:S(2)}) collective-permute-start(bf16[512,1024]{1,0:T(8,128)(2,1)S(1)} %shard_map.143.refs_0_), channel_id=1, source_target_pairs={{0,1},{1,0},{2,3},{3,2},{4,5},{5,4},{6,7},{7,6},{8,9},{9,8},{10,11... | collective-permute-start | bytes 3145736 | tf_op jit(solution)/shard_map/ppermute | solution.py:499
  48.5 3.8 %collective-permute-start.9 = (bf16[128,3072]{1,0:T(8,128)(2,1)S(1)}, bf16[128,3072]{1,0:T(8,128)(2,1)S(1)}, u32[]{:S(2)}, u32[]{:S(2)}) collective-permute-start(bf16[128,3072]{1,0:T(8,128)(2,1)S(1)} %copy-done.7), channel_id=1, source_target_pairs={{0,1},{1,0},{2,3},{3,2},{4,5},{5,4},{6,7},{7,6},{8,9},{9,8},{10,11... | collective-permute-start | bytes 2359304 | tf_op jit(solution)/shard_map/ppermute | solution.py:499
  49.0 4.0 %collective-permute-start.10 = (bf16[128,2048]{1,0:T(8,128)(2,1)S(1)}, bf16[128,2048]{1,0:T(8,128)(2,1)S(1)}, u32[]{:S(2)}, u32[]{:S(2)}) collective-permute-start(bf16[128,2048]{1,0:T(8,128)(2,1)S(1)} %shard_map.141.refs_2_.refs_4_.refs_1_), channel_id=1, source_target_pairs={{0,1},{1,0},{2,3},{3,2},{4,5},{5,4},{6,7},{7,6},{8,9},{9,8},{10,11... | collective-permute-start | bytes 1572872 | tf_op jit(solution)/shard_map/ppermute | solution.py:499
  54.1 9.2 %collective-permute-start.13 = (bf16[4,256,128]{2,1,0:T(8,128)(2,1)S(1)}, bf16[4,256,128]{2,1,0:T(8,128)(2,1)S(1)}, u32[]{:S(2)}, u32[]{:S(2)}) collective-permute-start(bf16[4,256,128]{2,1,0:T(8,128)(2,1)S(1)} %get-tuple-element.71), channel_id=1, source_target_pairs={{0,4},{1,5},{2,6},{3,7},{4,0},{5,1},{6,2},{7,3},{8,12},{9,13},{10,... | collective-permute-start | bytes 786440 | tf_op jit(solution)/shard_map/ppermute | solution.py:499
  54.2 14.0 %collective-permute-start.14 = (bf16[4,256,128]{2,1,0:T(8,128)(2,1)S(1)}, bf16[4,256,128]{2,1,0:T(8,128)(2,1)S(1)}, u32[]{:S(2)}, u32[]{:S(2)}) collective-permute-start(bf16[4,256,128]{2,1,0:T(8,128)(2,1)S(1)} %get-tuple-element.72), channel_id=1, source_target_pairs={{0,2},{1,3},{2,0},{3,1},{4,6},{5,7},{6,4},{7,5},{8,10},{9,11},{10,... | collective-permute-start | bytes 786440 | tf_op jit(solution)/shard_map/ppermute | solution.py:499
  54.8 13.5 %collective-permute-start.15 = (bf16[4,256,128]{2,1,0:T(8,128)(2,1)S(1)}, bf16[4,256,128]{2,1,0:T(8,128)(2,1)S(1)}, u32[]{:S(2)}, u32[]{:S(2)}) collective-permute-start(bf16[4,256,128]{2,1,0:T(8,128)(2,1)S(1)} %get-tuple-element.73), channel_id=1, source_target_pairs={{0,6},{1,7},{2,4},{3,5},{4,2},{5,3},{6,0},{7,1},{8,14},{9,15},{10,... | collective-permute-start | bytes 786440 | tf_op jit(solution)/shard_map/ppermute | solution.py:499
  60.7 7.7 %collective-permute-start.22 = (bf16[1,64,1024]{2,1,0:T(8,128)(2,1)S(1)}, bf16[1,64,1024]{2,1,0:T(8,128)(2,1)S(1)}, u32[]{:S(2)}, u32[]{:S(2)}) collective-permute-start(bf16[1,64,1024]{2,1,0:T(8,128)(2,1)S(1)} %get-tuple-element.79), channel_id=1, source_target_pairs={{0,8},{1,9},{2,10},{3,11},{4,12},{5,13},{6,14},{7,15},{8,0},{9,1},... | collective-permute-start | bytes 393224 | tf_op jit(solution)/shard_map/ppermute | solution.py:499
  60.8 12.7 %collective-permute-start.23 = (bf16[1,64,1024]{2,1,0:T(8,128)(2,1)S(1)}, bf16[1,64,1024]{2,1,0:T(8,128)(2,1)S(1)}, u32[]{:S(2)}, u32[]{:S(2)}) collective-permute-start(bf16[1,64,1024]{2,1,0:T(8,128)(2,1)S(1)} %get-tuple-element.80), channel_id=1, source_target_pairs={{0,16},{1,17},{2,18},{3,19},{4,20},{5,21},{6,22},{7,23},{8,24},{9,... | collective-permute-start | bytes 393224 | tf_op jit(solution)/shard_map/ppermute | solution.py:499
  63.3 10.2 %collective-permute-start.24 = (bf16[1,64,1024]{2,1,0:T(8,128)(2,1)S(1)}, bf16[1,64,1024]{2,1,0:T(8,128)(2,1)S(1)}, u32[]{:S(2)}, u32[]{:S(2)}) collective-permute-start(bf16[1,64,1024]{2,1,0:T(8,128)(2,1)S(1)} %get-tuple-element.81), channel_id=1, source_target_pairs={{0,24},{1,25},{2,26},{3,27},{4,28},{5,29},{6,30},{7,31},{8,16},{9,... | collective-permute-start | bytes 393224 | tf_op jit(solution)/shard_map/ppermute | solution.py:499
  73.5 5.0 %collective-permute-start.26 = (bf16[1,64,1024]{2,1,0:T(8,128)(2,1)S(1)}, bf16[1,64,1024]{2,1,0:T(8,128)(2,1)S(1)}, u32[]{:S(2)}, u32[]{:S(2)}) collective-permute-start(bf16[1,64,1024]{2,1,0:T(8,128)(2,1)S(1)} %shard_map.148.refs_0_), channel_id=1, source_target_pairs={{0,2},{1,3},{2,0},{3,1},{4,6},{5,7},{6,4},{7,5},{8,10},{9,11},{10,... | collective-permute-start | bytes 393224 | tf_op jit(solution)/shard_map/ppermute | solution.py:499
  74.1 5.7 %collective-permute-start.16 = (bf16[1,256,128]{2,1,0:T(8,128)(2,1)S(1)}, bf16[1,256,128]{2,1,0:T(8,128)(2,1)S(1)}, u32[]{:S(2)}, u32[]{:S(2)}) collective-permute-start(bf16[1,256,128]{2,1,0:T(8,128)(2,1)S(1)} %get-tuple-element.76), channel_id=1, source_target_pairs={{0,8},{1,9},{2,10},{3,11},{4,12},{5,13},{6,14},{7,15},{8,0},{9,1},... | collective-permute-start | bytes 196616 | tf_op jit(solution)/shard_map/ppermute | solution.py:499
  76.1 5.7 %collective-permute-start.17 = (bf16[1,256,128]{2,1,0:T(8,128)(2,1)S(1)}, bf16[1,256,128]{2,1,0:T(8,128)(2,1)S(1)}, u32[]{:S(2)}, u32[]{:S(2)}) collective-permute-start(bf16[1,256,128]{2,1,0:T(8,128)(2,1)S(1)} %get-tuple-element.77), channel_id=1, source_target_pairs={{0,16},{1,17},{2,18},{3,19},{4,20},{5,21},{6,22},{7,23},{8,24},{9,... | collective-permute-start | bytes 196616 | tf_op jit(solution)/shard_map/ppermute | solution.py:499
  76.3 6.2 %collective-permute-start.18 = (bf16[1,256,128]{2,1,0:T(8,128)(2,1)S(1)}, bf16[1,256,128]{2,1,0:T(8,128)(2,1)S(1)}, u32[]{:S(2)}, u32[]{:S(2)}) collective-permute-start(bf16[1,256,128]{2,1,0:T(8,128)(2,1)S(1)} %get-tuple-element.78), channel_id=1, source_target_pairs={{0,24},{1,25},{2,26},{3,27},{4,28},{5,29},{6,30},{7,31},{8,16},{9,... | collective-permute-start | bytes 196616 | tf_op jit(solution)/shard_map/ppermute | solution.py:499
  78.5 6.0 %collective-permute-start.25 = (bf16[1,64,1024]{2,1,0:T(8,128)(2,1)S(1)}, bf16[1,64,1024]{2,1,0:T(8,128)(2,1)S(1)}, u32[]{:S(2)}, u32[]{:S(2)}) collective-permute-start(bf16[1,64,1024]{2,1,0:T(8,128)(2,1)S(1)} %shard_map.148.refs_0_), channel_id=1, source_target_pairs={{0,1},{1,0},{2,3},{3,2},{4,5},{5,4},{6,7},{7,6},{8,9},{9,8},{10,11... | collective-permute-start | bytes 393224 | tf_op jit(solution)/shard_map/ppermute | solution.py:499
  78.6 5.9 %collective-permute-start.27 = (bf16[1,64,1024]{2,1,0:T(8,128)(2,1)S(1)}, bf16[1,64,1024]{2,1,0:T(8,128)(2,1)S(1)}, u32[]{:S(2)}, u32[]{:S(2)}) collective-permute-start(bf16[1,64,1024]{2,1,0:T(8,128)(2,1)S(1)} %collective-permute-done.26.refs_2_), channel_id=1, source_target_pairs={{0,1},{1,0},{2,3},{3,2},{4,5},{5,4},{6,7},{7,6},{8,9},{9,8},{10,11... | collective-permute-start | bytes 393224 | tf_op jit(solution)/shard_map/ppermute | solution.py:499
  82.5 4.0 %collective-permute-start.19 = (bf16[1,256,128]{2,1,0:T(8,128)(2,1)S(1)}, bf16[1,256,128]{2,1,0:T(8,128)(2,1)S(1)}, u32[]{:S(2)}, u32[]{:S(2)}) collective-permute-start(bf16[1,256,128]{2,1,0:T(8,128)(2,1)S(1)} %shard_map.147.refs_0_), channel_id=1, source_target_pairs={{0,1},{1,0},{2,3},{3,2},{4,5},{5,4},{6,7},{7,6},{8,9},{9,8},{10,11... | collective-permute-start | bytes 196616 | tf_op jit(solution)/shard_map/ppermute | solution.py:499
  82.6 4.5 %collective-permute-start.20 = (bf16[1,256,128]{2,1,0:T(8,128)(2,1)S(1)}, bf16[1,256,128]{2,1,0:T(8,128)(2,1)S(1)}, u32[]{:S(2)}, u32[]{:S(2)}) collective-permute-start(bf16[1,256,128]{2,1,0:T(8,128)(2,1)S(1)} %shard_map.147.refs_0_), channel_id=1, source_target_pairs={{0,2},{1,3},{2,0},{3,1},{4,6},{5,7},{6,4},{7,5},{8,10},{9,11},{10,... | collective-permute-start | bytes 196616 | tf_op jit(solution)/shard_map/ppermute | solution.py:499
  84.2 4.0 %collective-permute-start.21 = (bf16[1,256,128]{2,1,0:T(8,128)(2,1)S(1)}, bf16[1,256,128]{2,1,0:T(8,128)(2,1)S(1)}, u32[]{:S(2)}, u32[]{:S(2)}) collective-permute-start(bf16[1,256,128]{2,1,0:T(8,128)(2,1)S(1)} %shard_map.147.refs_0_), channel_id=1, source_target_pairs={{0,3},{1,2},{2,1},{3,0},{4,7},{5,6},{6,5},{7,4},{8,11},{9,10},{10,... | collective-permute-start | bytes 196616 | tf_op jit(solution)/shard_map/ppermute | solution.py:499

commit v7 on v4

--- a/solution.py
+++ b/solution.py
@@ -625,7 +625,8 @@
             radix = len(split)
             left //= radix
             shift = (left * 2).bit_length() - 1
-            pieces = [split[0]] + [permute(split[j], j << shift, 0) for j in range(1, radix)]
+            got = [permute(split[j], j << shift, 0) for j in range(radix - 1, 0, -1)]
+            pieces = [split[0]] + got[::-1]
             if left == 1:
                 return pieces
             radix = min(4, left)

time: 89.5 us -> 89.5 us (level)
  no operation moved by 1% of the time
where the time goes in v7:
time: 89.5 us; the launch traced here: 89.2 us
  starting transfers between devices  35.9 us (40%)
  waiting for transfers between devices  24.8 us (28%)
  Pallas kernels  22.7 us (25%)
  local copies, waits for them, and re-layouts  5 us (6%)
    ppermute x28, starting transfers between devices, permute(): lax.ppermute(array, BOTH, swap_pairs(slabs, cases, flip_slab, flip_case))  31.3 us
    pallas_call x16, Pallas kernels, call(): pl.pallas_call(run, out_shape=outs, in_specs=[vmem if one else far for on...  22.7 us
    ppermute x28, waiting for transfers between devices, permute(): lax.ppermute(array, BOTH, swap_pairs(slabs, cases, flip_slab, flip_case))  17.1 us
    all_to_all x1, waiting for transfers between devices, body(): back = lax.all_to_all(back, 'slab', split_axis=0, concat_axis=0, tiled=True)  7.71 us
    unnamed x24, local copies, waits for them, and re-layouts  5 us
    all_to_all x1, starting transfers between devices, body(): back = lax.all_to_all(back, 'slab', split_axis=0, concat_axis=0, tiled=True)  4.59 us
  transfers between devices with their start and end apart: 29, of which 12 were waited for; matrix products, arithmetic and copies ran while one was open for 0% of the time, Pallas kernels for 19%

profile of v7, /device:TPU:0, one launch (start us, length us, event | category | flops | bytes accessed | tf_op | source)
XLA Modules:
  0.0 89.2 jit_solution(7594514561114711544)
XLA Ops:
  0.6 2.9 %shard_map.135 = (bf16[16,1536]{1,0:T(8,128)(2,1)S(1)}, bf16[16,1536]{1,0:T(8,128)(2,1)S(1)}, bf16[16,1536]{1,0:T(8,128)(2,1)S(1)}, bf16[16,1536]{1,0:T(8,128)(2...) custom-call(bf16[128,512]{1,0:T(8,128)(2,1)} %bitcast.20, ...), custom_call_target="tpu_custom_call" | custom-call | flops 10000000 | bytes 10000 | tf_op jit(solution)/shard_map/pallas_call | solution.py:50
  3.5 3.0 %collective-permute-start = (bf16[16,1536]{1,0:T(8,128)(2,1)S(1)}, bf16[16,1536]{1,0:T(8,128)(2,1)S(1)}, u32[]{:S(2)}, u32[]{:S(2)}) collective-permute-start(bf16[16,1536]{1,0:T(8,128)(2,1)S(1)} %get-tuple-element.49), channel_id=1, source_target_pairs={{0,4},{1,5},{2,6},{3,7},{4,0},{5,1},{6,2},{7,3},{8,12},{9,13},{10,... | collective-permute-start | bytes 147464 | tf_op jit(solution)/shard_map/ppermute | solution.py:499
  6.5 1.6 %collective-permute-start.1 = (bf16[16,1536]{1,0:T(8,128)(2,1)S(1)}, bf16[16,1536]{1,0:T(8,128)(2,1)S(1)}, u32[]{:S(2)}, u32[]{:S(2)}) collective-permute-start(bf16[16,1536]{1,0:T(8,128)(2,1)S(1)} %get-tuple-element.50), channel_id=1, source_target_pairs={{0,8},{1,9},{2,10},{3,11},{4,12},{5,13},{6,14},{7,15},{8,0},{9,1},... | collective-permute-start | bytes 147464 | tf_op jit(solution)/shard_map/ppermute | solution.py:499
  8.1 0.0 collective-permute-start.2
  8.1 3.0 %collective-permute-start.3 = (bf16[16,1536]{1,0:T(8,128)(2,1)S(1)}, bf16[16,1536]{1,0:T(8,128)(2,1)S(1)}, u32[]{:S(2)}, u32[]{:S(2)}) collective-permute-start(bf16[16,1536]{1,0:T(8,128)(2,1)S(1)} %get-tuple-element.52), channel_id=1, source_target_pairs={{0,16},{1,17},{2,18},{3,19},{4,20},{5,21},{6,22},{7,23},{8,24},{9,... | collective-permute-start | bytes 147464 | tf_op jit(solution)/shard_map/ppermute | solution.py:499
  11.1 1.3 %collective-permute-start.4 = (bf16[16,1536]{1,0:T(8,128)(2,1)S(1)}, bf16[16,1536]{1,0:T(8,128)(2,1)S(1)}, u32[]{:S(2)}, u32[]{:S(2)}) collective-permute-start(bf16[16,1536]{1,0:T(8,128)(2,1)S(1)} %get-tuple-element.53), channel_id=1, source_target_pairs={{0,20},{1,21},{2,22},{3,23},{4,16},{5,17},{6,18},{7,19},{8,28},{9,... | collective-permute-start | bytes 147464 | tf_op jit(solution)/shard_map/ppermute | solution.py:499
  12.4 3.6 %collective-permute-start.5 = (bf16[16,1536]{1,0:T(8,128)(2,1)S(1)}, bf16[16,1536]{1,0:T(8,128)(2,1)S(1)}, u32[]{:S(2)}, u32[]{:S(2)}) collective-permute-start(bf16[16,1536]{1,0:T(8,128)(2,1)S(1)} %get-tuple-element.54), channel_id=1, source_target_pairs={{0,24},{1,25},{2,26},{3,27},{4,28},{5,29},{6,30},{7,31},{8,16},{9,... | collective-permute-start | bytes 147464 | tf_op jit(solution)/shard_map/ppermute | solution.py:499
  16.0 0.0 collective-permute-start.6
  16.1 1.7 %copy-done.1 = bf16[512,2048]{1,0:T(8,128)(2,1)S(1)} copy-done((bf16[512,2048]{1,0:T(8,128)(2,1)S(1)}, bf16[512,2048]{1,0:T(8,128)(2,1)}, u32[]{:S(2)}) %copy-start.1) | copy-done | bytes 2097176
  17.8 1.6 %copy-done.3 = bf16[2048,512]{1,0:T(8,128)(2,1)S(1)} copy-done((bf16[2048,512]{1,0:T(8,128)(2,1)S(1)}, bf16[2048,512]{1,0:T(8,128)(2,1)}, u32[]{:S(2)}) %copy-start.3) | copy-done | bytes 2097176
  19.4 1.3 %shard_map.136 = (bf16[512,512]{1,0:T(8,128)(2,1)S(1)}, bf16[512,512]{1,0:T(8,128)(2,1)S(1)}) custom-call(bf16[512,2048]{1,0:T(8,128)(2,1)S(1)} %copy-done.1, bf16[2048,512]{1,0:T(8,128)(2,1)S(1)} %copy-done.3), custom_call_target="tpu_custom_call" | custom-call | flops 10000000 | bytes 10000 | tf_op jit(solution)/shard_map/pallas_call | solution.py:50
  20.7 0.0 copy-start.8
  20.7 0.8 copy-done.8
  21.5 0.0 collective-permute-done.3.refs_4_
  21.5 0.0 collective-permute-done.4.refs_5_
  21.5 1.3 %collective-permute-done.6.refs_7_ = bf16[16,1536]{1,0:T(8,128)(2,1)S(1)} collective-permute-done((bf16[16,1536]{1,0:T(8,128)(2,1)S(1)}, bf16[16,1536]{1,0:T(8,128)(2,1)S(1)}, u32[]{:S(2)}, u32[]{:S(2)}) %collective-permute-start.6) | collective-permute-done | bytes 49184 | tf_op jit(solution)/shard_map/ppermute | solution.py:499
  22.8 1.3 %shard_map.137 = (bf16[128,1024]{1,0:T(8,128)(2,1)S(1)}, bf16[128,1536]{1,0:T(8,128)(2,1)S(1)}, bf16[128,512]{1,0:T(8,128)(2,1)S(1)}, bf16[128,512]{1,0:T(8,128)(2,1)S(1)}, bf16[128,512]{1,0:T(8,128)(2,1)S(1)}) custom-call(bf16[16,1536]{1,0:T(8,128)(2,1)S(1)} %get-tuple-element.48.refs_0_, bf16[16,1536]{1,0:T(8,128)(2,1)S(1)} %collective-permute-done.refs_1_, ...), custom_call_target="tpu_custom_call" | custom-call | flops 10000000 | bytes 10000 | tf_op jit(solution)/shard_map/pallas_call | solution.py:50
  24.1 0.6 collective-permute-start.7
  24.7 1.5 %collective-permute-start.8 = (bf16[128,1024]{1,0:T(8,128)(2,1)S(1)}, bf16[128,1024]{1,0:T(8,128)(2,1)S(1)}, u32[]{:S(2)}, u32[]{:S(2)}) collective-permute-start(bf16[128,1024]{1,0:T(8,128)(2,1)S(1)} %get-tuple-element.58.refs_0_), channel_id=1, source_target_pairs={{0,2},{1,3},{2,0},{3,1},{4,6},{5,7},{6,4},{7,5},{8,10},{9,11},{10,... | collective-permute-start | bytes 786440 | tf_op jit(solution)/shard_map/ppermute | solution.py:499
  26.2 2.4 %shard_map.138 = (bf16[128,512]{1,0:T(8,128)(2,1)S(1)}, f32[128,512]{1,0:T(8,128)S(1)}) custom-call(bf16[128,1024]{1,0:T(8,128)(2,1)S(1)} %get-tuple-element.58.refs_0_, bf16[128,512]{1,0:T(8,128)(2,1)S(1)} %get-tuple-element.59.refs_1_, f32[1,512]{1,0:T(1,128)S(1)} %bitcast.18, bf16[512,512]{1,0:T(8,128)(2,1)S(1)} %copy-done.5, ...), custom_call_target="tpu_custom_call" | custom-call | flops 10000000 | bytes 10000 | tf_op jit(solution)/shard_map/pallas_call | solution.py:50
  28.6 2.7 %shard_map.139 = (bf16[128,1024]{1,0:T(8,128)(2,1)S(1)}, bf16[128,3072]{1,0:T(8,128)(2,1)S(1)}) custom-call(bf16[128,1536]{1,0:T(8,128)(2,1)S(1)} %get-tuple-element.57.refs_0_, bf16[128,512]{1,0:T(8,128)(2,1)S(1)} %get-tuple-element.60.refs_1_, f32[128,512]{1,0:T(8,128)S(1)} %get-tuple-element.61.refs_2_, bf16[128,512]{1,0:T(8,128)(2,1)S(1)} %get-tuple-element.62.refs_3_, ...), custom_call_target="tpu_custom_call" | custom-call | flops 10000000 | bytes 10000 | tf_op jit(solution)/shard_map/pallas_call | solution.py:50
  31.3 0.9 copy-done.6
  32.2 0.7 shard_map.140
  32.9 4.6 %all-to-all-start = ((bf16[8,16,1024]{2,1,0:T(8,128)(2,1)}), bf16[8,16,1024]{2,1,0:T(8,128)(2,1)S(1)}, u32[]{:S(2)}, u32[]{:S(2)}) async-start(bf16[8,16,1024]{2,1,0:T(8,128)(2,1)} %bitcast.4), calls=%async_computation | async-start | bytes 524288 | tf_op jit(solution)/shard_map/all_to_all | solution.py:568
  37.5 0.5 collective-permute-start.11
  38.0 7.7 %all-to-all-done = bf16[8,16,1024]{2,1,0:T(8,128)(2,1)S(1)} async-done(((bf16[8,16,1024]{2,1,0:T(8,128)(2,1)}), bf16[8,16,1024]{2,1,0:T(8,128)(2,1)S(1)}, u32[]{:S(2)}, u32[]{:S(2)}) %all-to-all-start) | async-done | bytes 262176 | tf_op jit(solution)/shard_map/all_to_all | solution.py:568
  45.7 2.6 %shard_map.141.refs_2_.refs_4_.refs_1_ = bf16[128,2048]{1,0:T(8,128)(2,1)S(1)} custom-call(bf16[128,1024]{1,0:T(8,128)(2,1)S(1)} %bitcast.9, bf16[128,512]{1,0:T(8,128)(2,1)S(1)} %get-tuple-element.65.refs_1_.refs_2_, f32[1,512]{1,0:T(1,128)S(1)} %bitcast.14, bf16[512,1536]{1,0:T(8,128)(2,1)S(1)} %copy-done), custom_call_target="tpu_custom_call" | custom-call | flops 10000000 | bytes 10000 | tf_op jit(solution)/shard_map/pallas_call | solution.py:50
  48.3 0.0 copy-start.9
  48.4 0.1 shard_map.143.refs_0_
  48.4 0.1 collective-permute-start.12
  48.5 0.5 collective-permute-start.9
  49.0 0.1 collective-permute-start.10
  49.1 3.2 %collective-permute-done.9.refs_1_ = bf16[128,3072]{1,0:T(8,128)(2,1)S(1)} collective-permute-done((bf16[128,3072]{1,0:T(8,128)(2,1)S(1)}, bf16[128,3072]{1,0:T(8,128)(2,1)S(1)}, u32[]{:S(2)}, u32[]{:S(2)}) %collective-permute-start.9) | collective-permute-done | bytes 786464 | tf_op jit(solution)/shard_map/ppermute | solution.py:499
  52.3 0.7 collective-permute-done.10.refs_3_
  53.0 1.0 %shard_map.142 = (bf16[4,256,128]{2,1,0:T(8,128)(2,1)S(1)}, bf16[4,256,128]{2,1,0:T(8,128)(2,1)S(1)}, bf16[4,256,128]{2,1,0:T(8,128)(2,1)S(1)}, bf16[4,256,128]{2,1,0:T(8,128)(2,1)S(1)}) custom-call(bf16[128,3072]{1,0:T(8,128)(2,1)S(1)} %copy-done.7, bf16[128,3072]{1,0:T(8,128)(2,1)S(1)} %collective-permute-done.9.refs_1_, ...), custom_call_target="tpu_custom_call" | custom-call | flops 10000000 | bytes 10000 | tf_op jit(solution)/shard_map/pallas_call | solution.py:50
  54.1 0.1 collective-permute-start.13
  54.2 0.5 collective-permute-start.14
  54.8 2.9 %collective-permute-start.15 = (bf16[4,256,128]{2,1,0:T(8,128)(2,1)S(1)}, bf16[4,256,128]{2,1,0:T(8,128)(2,1)S(1)}, u32[]{:S(2)}, u32[]{:S(2)}) collective-permute-start(bf16[4,256,128]{2,1,0:T(8,128)(2,1)S(1)} %get-tuple-element.73), channel_id=1, source_target_pairs={{0,6},{1,7},{2,4},{3,5},{4,2},{5,3},{6,0},{7,1},{8,14},{9,15},{10,... | collective-permute-start | bytes 786440 | tf_op jit(solution)/shard_map/ppermute | solution.py:499
  57.7 3.0 %shard_map.144 = (bf16[1,64,1024]{2,1,0:T(8,128)(2,1)S(1)}, bf16[1,64,1024]{2,1,0:T(8,128)(2,1)S(1)}, bf16[1,64,1024]{2,1,0:T(8,128)(2,1)S(1)}, bf16[1,64,1024]{2,1,0:T(8,128)(2,1)S(1)}) custom-call(bf16[512,1024]{1,0:T(8,128)(2,1)S(1)} %shard_map.143.refs_0_, bf16[512,1024]{1,0:T(8,128)(2,1)S(1)} %collective-permute-done.12.refs_1_, ...), custom_call_target="tpu_custom_call" | custom-call | flops 10000000 | bytes 10000 | tf_op jit(solution)/shard_map/pallas_call | solution.py:50
  60.7 0.1 collective-permute-start.22
  60.8 1.1 %collective-permute-start.23 = (bf16[1,64,1024]{2,1,0:T(8,128)(2,1)S(1)}, bf16[1,64,1024]{2,1,0:T(8,128)(2,1)S(1)}, u32[]{:S(2)}, u32[]{:S(2)}) collective-permute-start(bf16[1,64,1024]{2,1,0:T(8,128)(2,1)S(1)} %get-tuple-element.80), channel_id=1, source_target_pairs={{0,16},{1,17},{2,18},{3,19},{4,20},{5,21},{6,22},{7,23},{8,24},{9,... | collective-permute-start | bytes 393224 | tf_op jit(solution)/shard_map/ppermute | solution.py:499
  61.9 1.4 %collective-permute-done.13.refs_1_ = bf16[4,256,128]{2,1,0:T(8,128)(2,1)S(1)} collective-permute-done((bf16[4,256,128]{2,1,0:T(8,128)(2,1)S(1)}, bf16[4,256,128]{2,1,0:T(8,128)(2,1)S(1)}, u32[]{:S(2)}, u32[]{:S(2)}) %collective-permute-start.13) | collective-permute-done | bytes 262176 | tf_op jit(solution)/shard_map/ppermute | solution.py:499
  63.3 1.8 %collective-permute-start.24 = (bf16[1,64,1024]{2,1,0:T(8,128)(2,1)S(1)}, bf16[1,64,1024]{2,1,0:T(8,128)(2,1)S(1)}, u32[]{:S(2)}, u32[]{:S(2)}) collective-permute-start(bf16[1,64,1024]{2,1,0:T(8,128)(2,1)S(1)} %get-tuple-element.81), channel_id=1, source_target_pairs={{0,24},{1,25},{2,26},{3,27},{4,28},{5,29},{6,30},{7,31},{8,16},{9,... | collective-permute-start | bytes 393224 | tf_op jit(solution)/shard_map/ppermute | solution.py:499
  65.1 1.6 %shard_map.145 = (bf16[128,512]{1,0:T(8,128)(2,1)}, f32[8,128]{1,0:T(8,128)S(1)}) custom-call(bf16[128,1024]{1,0:T(8,128)(2,1)S(1)} %bitcast.10, bf16[128,2048]{1,0:T(8,128)(2,1)S(1)} %shard_map.141.refs_2_.refs_4_.refs_1_, bf16[128,512]{1,0:T(8,128)(2,1)S(1)} %get-tuple-element.65.refs_1_.refs_2_, f32[1,512]{1,0:T(1,128)S(1)} %bitcast.15, ...), custom_call_target="tpu_custom_call" | custom-call | flops 10000000 | bytes 10000 | tf_op jit(solution)/shard_map/pallas_call | solution.py:50
  66.7 1.5 %collective-permute-done.14.refs_2_ = bf16[4,256,128]{2,1,0:T(8,128)(2,1)S(1)} collective-permute-done((bf16[4,256,128]{2,1,0:T(8,128)(2,1)S(1)}, bf16[4,256,128]{2,1,0:T(8,128)(2,1)S(1)}, u32[]{:S(2)}, u32[]{:S(2)}) %collective-permute-start.14) | collective-permute-done | bytes 262176 | tf_op jit(solution)/shard_map/ppermute | solution.py:499
  68.2 0.1 shard_map.146
  68.4 1.2 %collective-permute-start.16 = (bf16[1,256,128]{2,1,0:T(8,128)(2,1)S(1)}, bf16[1,256,128]{2,1,0:T(8,128)(2,1)S(1)}, u32[]{:S(2)}, u32[]{:S(2)}) collective-permute-start(bf16[1,256,128]{2,1,0:T(8,128)(2,1)S(1)} %get-tuple-element.76), channel_id=1, source_target_pairs={{0,8},{1,9},{2,10},{3,11},{4,12},{5,13},{6,14},{7,15},{8,0},{9,1},... | collective-permute-start | bytes 196616 | tf_op jit(solution)/shard_map/ppermute | solution.py:499
  69.6 3.9 %collective-permute-done.23.refs_2_ = bf16[1,64,1024]{2,1,0:T(8,128)(2,1)S(1)} collective-permute-done((bf16[1,64,1024]{2,1,0:T(8,128)(2,1)S(1)}, bf16[1,64,1024]{2,1,0:T(8,128)(2,1)S(1)}, u32[]{:S(2)}, u32[]{:S(2)}) %collective-permute-start.23) | collective-permute-done | bytes 131104 | tf_op jit(solution)/shard_map/ppermute | solution.py:499
  73.5 0.1 shard_map.148.refs_0_
  73.5 0.1 collective-permute-start.25
  73.6 2.2 %collective-permute-start.17 = (bf16[1,256,128]{2,1,0:T(8,128)(2,1)S(1)}, bf16[1,256,128]{2,1,0:T(8,128)(2,1)S(1)}, u32[]{:S(2)}, u32[]{:S(2)}) collective-permute-start(bf16[1,256,128]{2,1,0:T(8,128)(2,1)S(1)} %get-tuple-element.77), channel_id=1, source_target_pairs={{0,16},{1,17},{2,18},{3,19},{4,20},{5,21},{6,22},{7,23},{8,24},{9,... | collective-permute-start | bytes 196616 | tf_op jit(solution)/shard_map/ppermute | solution.py:499
  75.8 2.2 %collective-permute-start.18 = (bf16[1,256,128]{2,1,0:T(8,128)(2,1)S(1)}, bf16[1,256,128]{2,1,0:T(8,128)(2,1)S(1)}, u32[]{:S(2)}, u32[]{:S(2)}) collective-permute-start(bf16[1,256,128]{2,1,0:T(8,128)(2,1)S(1)} %get-tuple-element.78), channel_id=1, source_target_pairs={{0,24},{1,25},{2,26},{3,27},{4,28},{5,29},{6,30},{7,31},{8,16},{9,... | collective-permute-start | bytes 196616 | tf_op jit(solution)/shard_map/ppermute | solution.py:499
  78.1 0.5 collective-permute-start.26
  78.5 0.7 collective-permute-start.27
  79.3 3.0 %collective-permute-done.17.refs_2_ = bf16[1,256,128]{2,1,0:T(8,128)(2,1)S(1)} collective-permute-done((bf16[1,256,128]{2,1,0:T(8,128)(2,1)S(1)}, bf16[1,256,128]{2,1,0:T(8,128)(2,1)S(1)}, u32[]{:S(2)}, u32[]{:S(2)}) %collective-permute-start.17) | collective-permute-done | bytes 65568 | tf_op jit(solution)/shard_map/ppermute | solution.py:499
  82.3 0.1 collective-permute-start.19
  82.4 0.6 collective-permute-start.20
  83.0 1.3 %collective-permute-start.21 = (bf16[1,256,128]{2,1,0:T(8,128)(2,1)S(1)}, bf16[1,256,128]{2,1,0:T(8,128)(2,1)S(1)}, u32[]{:S(2)}, u32[]{:S(2)}) collective-permute-start(bf16[1,256,128]{2,1,0:T(8,128)(2,1)S(1)} %shard_map.147.refs_0_), channel_id=1, source_target_pairs={{0,3},{1,2},{2,1},{3,0},{4,7},{5,6},{6,5},{7,4},{8,11},{9,10},{10,... | collective-permute-start | bytes 196616 | tf_op jit(solution)/shard_map/ppermute | solution.py:499
  84.3 0.2 collective-permute-done.26.refs_2_
  84.4 0.6 collective-permute-done.27.refs_3_
  85.1 2.1 %shard_map.149 = (f32[64,2048]{1,0:T(8,128)}, f32[256,512]{1,0:T(8,128)}, f32[1,64]{1,0:T(1,128)}, bf16[64,1536]{1,0:T(8,128)(2,1)S(1)}) custom-call(bf16[1,64,1024]{2,1,0:T(8,128)(2,1)S(1)} %shard_map.148.refs_0_, bf16[1,64,1024]{2,1,0:T(8,128)(2,1)S(1)} %collective-permute-done.25.refs_1_, bf16[1,64,1024]{2,1,0:T(8,128)(2,1)S(1)} %collective-permute-done.26.refs_2_, ...), custom_call_target="tpu_custom_call" | custom-call | flops 10000000 | bytes 10000 | tf_op jit(solution)/shard_map/pallas_call | solution.py:50
  87.1 1.0 %collective-permute-done.20.refs_2_ = bf16[1,256,128]{2,1,0:T(8,128)(2,1)S(1)} collective-permute-done((bf16[1,256,128]{2,1,0:T(8,128)(2,1)S(1)}, bf16[1,256,128]{2,1,0:T(8,128)(2,1)S(1)}, u32[]{:S(2)}, u32[]{:S(2)}) %collective-permute-start.20) | collective-permute-done | bytes 65568 | tf_op jit(solution)/shard_map/ppermute | solution.py:499
  88.1 0.2 collective-permute-done.21.refs_3_
  88.4 0.8 shard_map.150
  (34 shorter events, 0.1 us)
Async XLA Ops:
  3.5 8.9 %collective-permute-start = (bf16[16,1536]{1,0:T(8,128)(2,1)S(1)}, bf16[16,1536]{1,0:T(8,128)(2,1)S(1)}, u32[]{:S(2)}, u32[]{:S(2)}) collective-permute-start(bf16[16,1536]{1,0:T(8,128)(2,1)S(1)} %get-tuple-element.49), channel_id=1, source_target_pairs={{0,4},{1,5},{2,6},{3,7},{4,0},{5,1},{6,2},{7,3},{8,12},{9,13},{10,... | collective-permute-start | bytes 147464 | tf_op jit(solution)/shard_map/ppermute | solution.py:499
  6.5 9.5 %collective-permute-start.1 = (bf16[16,1536]{1,0:T(8,128)(2,1)S(1)}, bf16[16,1536]{1,0:T(8,128)(2,1)S(1)}, u32[]{:S(2)}, u32[]{:S(2)}) collective-permute-start(bf16[16,1536]{1,0:T(8,128)(2,1)S(1)} %get-tuple-element.50), channel_id=1, source_target_pairs={{0,8},{1,9},{2,10},{3,11},{4,12},{5,13},{6,14},{7,15},{8,0},{9,1},... | collective-permute-start | bytes 147464 | tf_op jit(solution)/shard_map/ppermute | solution.py:499
  8.1 13.4 %collective-permute-start.2 = (bf16[16,1536]{1,0:T(8,128)(2,1)S(1)}, bf16[16,1536]{1,0:T(8,128)(2,1)S(1)}, u32[]{:S(2)}, u32[]{:S(2)}) collective-permute-start(bf16[16,1536]{1,0:T(8,128)(2,1)S(1)} %get-tuple-element.51), channel_id=1, source_target_pairs={{0,12},{1,13},{2,14},{3,15},{4,8},{5,9},{6,10},{7,11},{8,4},{9,5},... | collective-permute-start | bytes 147464 | tf_op jit(solution)/shard_map/ppermute | solution.py:499
  8.1 13.4 %collective-permute-start.3 = (bf16[16,1536]{1,0:T(8,128)(2,1)S(1)}, bf16[16,1536]{1,0:T(8,128)(2,1)S(1)}, u32[]{:S(2)}, u32[]{:S(2)}) collective-permute-start(bf16[16,1536]{1,0:T(8,128)(2,1)S(1)} %get-tuple-element.52), channel_id=1, source_target_pairs={{0,16},{1,17},{2,18},{3,19},{4,20},{5,21},{6,22},{7,23},{8,24},{9,... | collective-permute-start | bytes 147464 | tf_op jit(solution)/shard_map/ppermute | solution.py:499
  11.1 10.3 %collective-permute-start.4 = (bf16[16,1536]{1,0:T(8,128)(2,1)S(1)}, bf16[16,1536]{1,0:T(8,128)(2,1)S(1)}, u32[]{:S(2)}, u32[]{:S(2)}) collective-permute-start(bf16[16,1536]{1,0:T(8,128)(2,1)S(1)} %get-tuple-element.53), channel_id=1, source_target_pairs={{0,20},{1,21},{2,22},{3,23},{4,16},{5,17},{6,18},{7,19},{8,28},{9,... | collective-permute-start | bytes 147464 | tf_op jit(solution)/shard_map/ppermute | solution.py:499
  12.4 9.1 %collective-permute-start.5 = (bf16[16,1536]{1,0:T(8,128)(2,1)S(1)}, bf16[16,1536]{1,0:T(8,128)(2,1)S(1)}, u32[]{:S(2)}, u32[]{:S(2)}) collective-permute-start(bf16[16,1536]{1,0:T(8,128)(2,1)S(1)} %get-tuple-element.54), channel_id=1, source_target_pairs={{0,24},{1,25},{2,26},{3,27},{4,28},{5,29},{6,30},{7,31},{8,16},{9,... | collective-permute-start | bytes 147464 | tf_op jit(solution)/shard_map/ppermute | solution.py:499
  16.0 6.8 %copy-start = (bf16[512,1536]{1,0:T(8,128)(2,1)S(1)}, bf16[512,1536]{1,0:T(8,128)(2,1)}, u32[]{:S(2)}) copy-start(bf16[512,1536]{1,0:T(8,128)(2,1)} %refs_6_.3) | copy-start | bytes 4718596
  16.0 6.8 %collective-permute-start.6 = (bf16[16,1536]{1,0:T(8,128)(2,1)S(1)}, bf16[16,1536]{1,0:T(8,128)(2,1)S(1)}, u32[]{:S(2)}, u32[]{:S(2)}) collective-permute-start(bf16[16,1536]{1,0:T(8,128)(2,1)S(1)} %get-tuple-element.55), channel_id=1, source_target_pairs={{0,28},{1,29},{2,30},{3,31},{4,24},{5,25},{6,26},{7,27},{8,20},{9,... | collective-permute-start | bytes 147464 | tf_op jit(solution)/shard_map/ppermute | solution.py:499
  16.1 1.7 %copy-start.1 = (bf16[512,2048]{1,0:T(8,128)(2,1)S(1)}, bf16[512,2048]{1,0:T(8,128)(2,1)}, u32[]{:S(2)}) copy-start(bf16[512,2048]{1,0:T(8,128)(2,1)} %refs_5_.3) | copy-start | bytes 6291460
  17.8 1.6 %copy-start.3 = (bf16[2048,512]{1,0:T(8,128)(2,1)S(1)}, bf16[2048,512]{1,0:T(8,128)(2,1)}, u32[]{:S(2)}) copy-start(bf16[2048,512]{1,0:T(8,128)(2,1)} %refs_5_.2) | copy-start | bytes 6291460
  19.4 3.5 %copy-start.5 = (bf16[512,512]{1,0:T(8,128)(2,1)S(1)}, bf16[512,512]{1,0:T(8,128)(2,1)}, u32[]{:S(2)}) copy-start(bf16[512,512]{1,0:T(8,128)(2,1)} %refs_3_.4) | copy-start | bytes 1572868
  19.4 3.5 %copy-start.10 = (f32[512]{0:T(512)S(1)}, f32[512]{0:T(512)}, u32[]{:S(2)}) copy-start(f32[512]{0:T(512)} %param.14) | copy-start | bytes 6148
  19.4 3.5 %copy-start.11 = (f32[512]{0:T(512)S(1)}, f32[512]{0:T(512)}, u32[]{:S(2)}) copy-start(f32[512]{0:T(512)} %param.15) | copy-start | bytes 6148
  19.4 6.8 %copy-start.4 = (bf16[2048,512]{1,0:T(8,128)(2,1)S(1)}, bf16[2048,512]{1,0:T(8,128)(2,1)}, u32[]{:S(2)}) copy-start(bf16[2048,512]{1,0:T(8,128)(2,1)} %refs_5_.2) | copy-start | bytes 6291460
  20.7 0.8 copy-start.8
  21.5 4.7 %copy-start.2 = (bf16[512,2048]{1,0:T(8,128)(2,1)S(1)}, bf16[512,2048]{1,0:T(8,128)(2,1)}, u32[]{:S(2)}) copy-start(bf16[512,2048]{1,0:T(8,128)(2,1)} %refs_5_.3) | copy-start | bytes 6291460
  24.1 8.1 %collective-permute-start.7 = (bf16[128,1024]{1,0:T(8,128)(2,1)S(1)}, bf16[128,1024]{1,0:T(8,128)(2,1)S(1)}, u32[]{:S(2)}, u32[]{:S(2)}) collective-permute-start(bf16[128,1024]{1,0:T(8,128)(2,1)S(1)} %get-tuple-element.58.refs_0_), channel_id=1, source_target_pairs={{0,4},{1,5},{2,6},{3,7},{4,0},{5,1},{6,2},{7,3},{8,12},{9,13},{10,... | collective-permute-start | bytes 786440 | tf_op jit(solution)/shard_map/ppermute | solution.py:499
  24.7 7.5 %collective-permute-start.8 = (bf16[128,1024]{1,0:T(8,128)(2,1)S(1)}, bf16[128,1024]{1,0:T(8,128)(2,1)S(1)}, u32[]{:S(2)}, u32[]{:S(2)}) collective-permute-start(bf16[128,1024]{1,0:T(8,128)(2,1)S(1)} %get-tuple-element.58.refs_0_), channel_id=1, source_target_pairs={{0,2},{1,3},{2,0},{3,1},{4,6},{5,7},{6,4},{7,5},{8,10},{9,11},{10,... | collective-permute-start | bytes 786440 | tf_op jit(solution)/shard_map/ppermute | solution.py:499
  31.3 0.9 %copy-start.6 = (bf16[128,3072]{1,0:T(8,128)(2,1)}, bf16[128,3072]{1,0:T(8,128)(2,1)S(1)}, u32[]{:S(2)}) copy-start(bf16[128,3072]{1,0:T(8,128)(2,1)S(1)} %get-tuple-element.66.refs_0_) | copy-start | bytes 2359300
  32.9 12.8 %all-to-all-start = ((bf16[8,16,1024]{2,1,0:T(8,128)(2,1)}), bf16[8,16,1024]{2,1,0:T(8,128)(2,1)S(1)}, u32[]{:S(2)}, u32[]{:S(2)}) async-start(bf16[8,16,1024]{2,1,0:T(8,128)(2,1)} %bitcast.4), calls=%async_computation | async-start | bytes 524288 | tf_op jit(solution)/shard_map/all_to_all | solution.py:568
  37.5 10.9 %collective-permute-start.11 = (bf16[128,1024]{1,0:T(8,128)(2,1)S(1)}, bf16[128,1024]{1,0:T(8,128)(2,1)S(1)}, u32[]{:S(2)}, u32[]{:S(2)}) collective-permute-start(bf16[128,1024]{1,0:T(8,128)(2,1)S(1)} %collective-permute-done.7.refs_1_), channel_id=1, source_target_pairs={{0,2},{1,3},{2,0},{3,1},{4,6},{5,7},{6,4},{7,5},{8,10},{9,11},{10,... | collective-permute-start | bytes 786440 | tf_op jit(solution)/shard_map/ppermute | solution.py:499
  45.7 2.8 %copy-start.7 = (bf16[128,3072]{1,0:T(8,128)(2,1)S(1)}, bf16[128,3072]{1,0:T(8,128)(2,1)}, u32[]{:S(2)}) copy-start(bf16[128,3072]{1,0:T(8,128)(2,1)} %copy-done.6) | copy-start | bytes 2359300
  48.3 9.3 %copy-start.9 = (bf16[512,512]{1,0:T(8,128)(2,1)S(1)}, bf16[512,512]{1,0:T(8,128)(2,1)}, u32[]{:S(2)}) copy-start(bf16[512,512]{1,0:T(8,128)(2,1)} %copy-done.8) | copy-start | bytes 1572868
  48.4 9.2 %collective-permute-start.12 = (bf16[512,1024]{1,0:T(8,128)(2,1)S(1)}, bf16[512,1024]{1,0:T(8,128)(2,1)S(1)}, u32[]{:S(2)}, u32[]{:S(2)}) collective-permute-start(bf16[512,1024]{1,0:T(8,128)(2,1)S(1)} %shard_map.143.refs_0_), channel_id=1, source_target_pairs={{0,1},{1,0},{2,3},{3,2},{4,5},{5,4},{6,7},{7,6},{8,9},{9,8},{10,11... | collective-permute-start | bytes 3145736 | tf_op jit(solution)/shard_map/ppermute | solution.py:499
  48.5 3.8 %collective-permute-start.9 = (bf16[128,3072]{1,0:T(8,128)(2,1)S(1)}, bf16[128,3072]{1,0:T(8,128)(2,1)S(1)}, u32[]{:S(2)}, u32[]{:S(2)}) collective-permute-start(bf16[128,3072]{1,0:T(8,128)(2,1)S(1)} %copy-done.7), channel_id=1, source_target_pairs={{0,1},{1,0},{2,3},{3,2},{4,5},{5,4},{6,7},{7,6},{8,9},{9,8},{10,11... | collective-permute-start | bytes 2359304 | tf_op jit(solution)/shard_map/ppermute | solution.py:499
  49.0 4.0 %collective-permute-start.10 = (bf16[128,2048]{1,0:T(8,128)(2,1)S(1)}, bf16[128,2048]{1,0:T(8,128)(2,1)S(1)}, u32[]{:S(2)}, u32[]{:S(2)}) collective-permute-start(bf16[128,2048]{1,0:T(8,128)(2,1)S(1)} %shard_map.141.refs_2_.refs_4_.refs_1_), channel_id=1, source_target_pairs={{0,1},{1,0},{2,3},{3,2},{4,5},{5,4},{6,7},{7,6},{8,9},{9,8},{10,11... | collective-permute-start | bytes 1572872 | tf_op jit(solution)/shard_map/ppermute | solution.py:499
  54.1 9.2 %collective-permute-start.13 = (bf16[4,256,128]{2,1,0:T(8,128)(2,1)S(1)}, bf16[4,256,128]{2,1,0:T(8,128)(2,1)S(1)}, u32[]{:S(2)}, u32[]{:S(2)}) collective-permute-start(bf16[4,256,128]{2,1,0:T(8,128)(2,1)S(1)} %get-tuple-element.71), channel_id=1, source_target_pairs={{0,4},{1,5},{2,6},{3,7},{4,0},{5,1},{6,2},{7,3},{8,12},{9,13},{10,... | collective-permute-start | bytes 786440 | tf_op jit(solution)/shard_map/ppermute | solution.py:499
  54.2 14.0 %collective-permute-start.14 = (bf16[4,256,128]{2,1,0:T(8,128)(2,1)S(1)}, bf16[4,256,128]{2,1,0:T(8,128)(2,1)S(1)}, u32[]{:S(2)}, u32[]{:S(2)}) collective-permute-start(bf16[4,256,128]{2,1,0:T(8,128)(2,1)S(1)} %get-tuple-element.72), channel_id=1, source_target_pairs={{0,2},{1,3},{2,0},{3,1},{4,6},{5,7},{6,4},{7,5},{8,10},{9,11},{10,... | collective-permute-start | bytes 786440 | tf_op jit(solution)/shard_map/ppermute | solution.py:499
  54.8 13.5 %collective-permute-start.15 = (bf16[4,256,128]{2,1,0:T(8,128)(2,1)S(1)}, bf16[4,256,128]{2,1,0:T(8,128)(2,1)S(1)}, u32[]{:S(2)}, u32[]{:S(2)}) collective-permute-start(bf16[4,256,128]{2,1,0:T(8,128)(2,1)S(1)} %get-tuple-element.73), channel_id=1, source_target_pairs={{0,6},{1,7},{2,4},{3,5},{4,2},{5,3},{6,0},{7,1},{8,14},{9,15},{10,... | collective-permute-start | bytes 786440 | tf_op jit(solution)/shard_map/ppermute | solution.py:499
  60.7 8.9 %collective-permute-start.22 = (bf16[1,64,1024]{2,1,0:T(8,128)(2,1)S(1)}, bf16[1,64,1024]{2,1,0:T(8,128)(2,1)S(1)}, u32[]{:S(2)}, u32[]{:S(2)}) collective-permute-start(bf16[1,64,1024]{2,1,0:T(8,128)(2,1)S(1)} %get-tuple-element.79), channel_id=1, source_target_pairs={{0,8},{1,9},{2,10},{3,11},{4,12},{5,13},{6,14},{7,15},{8,0},{9,1},... | collective-permute-start | bytes 393224 | tf_op jit(solution)/shard_map/ppermute | solution.py:499
  60.8 12.7 %collective-permute-start.23 = (bf16[1,64,1024]{2,1,0:T(8,128)(2,1)S(1)}, bf16[1,64,1024]{2,1,0:T(8,128)(2,1)S(1)}, u32[]{:S(2)}, u32[]{:S(2)}) collective-permute-start(bf16[1,64,1024]{2,1,0:T(8,128)(2,1)S(1)} %get-tuple-element.80), channel_id=1, source_target_pairs={{0,16},{1,17},{2,18},{3,19},{4,20},{5,21},{6,22},{7,23},{8,24},{9,... | collective-permute-start | bytes 393224 | tf_op jit(solution)/shard_map/ppermute | solution.py:499
  63.3 10.2 %collective-permute-start.24 = (bf16[1,64,1024]{2,1,0:T(8,128)(2,1)S(1)}, bf16[1,64,1024]{2,1,0:T(8,128)(2,1)S(1)}, u32[]{:S(2)}, u32[]{:S(2)}) collective-permute-start(bf16[1,64,1024]{2,1,0:T(8,128)(2,1)S(1)} %get-tuple-element.81), channel_id=1, source_target_pairs={{0,24},{1,25},{2,26},{3,27},{4,28},{5,29},{6,30},{7,31},{8,16},{9,... | collective-permute-start | bytes 393224 | tf_op jit(solution)/shard_map/ppermute | solution.py:499
  68.4 10.2 %collective-permute-start.16 = (bf16[1,256,128]{2,1,0:T(8,128)(2,1)S(1)}, bf16[1,256,128]{2,1,0:T(8,128)(2,1)S(1)}, u32[]{:S(2)}, u32[]{:S(2)}) collective-permute-start(bf16[1,256,128]{2,1,0:T(8,128)(2,1)S(1)} %get-tuple-element.76), channel_id=1, source_target_pairs={{0,8},{1,9},{2,10},{3,11},{4,12},{5,13},{6,14},{7,15},{8,0},{9,1},... | collective-permute-start | bytes 196616 | tf_op jit(solution)/shard_map/ppermute | solution.py:499
  73.5 9.4 %collective-permute-start.25 = (bf16[1,64,1024]{2,1,0:T(8,128)(2,1)S(1)}, bf16[1,64,1024]{2,1,0:T(8,128)(2,1)S(1)}, u32[]{:S(2)}, u32[]{:S(2)}) collective-permute-start(bf16[1,64,1024]{2,1,0:T(8,128)(2,1)S(1)} %shard_map.148.refs_0_), channel_id=1, source_target_pairs={{0,1},{1,0},{2,3},{3,2},{4,5},{5,4},{6,7},{7,6},{8,9},{9,8},{10,11... | collective-permute-start | bytes 393224 | tf_op jit(solution)/shard_map/ppermute | solution.py:499
  73.6 8.7 %collective-permute-start.17 = (bf16[1,256,128]{2,1,0:T(8,128)(2,1)S(1)}, bf16[1,256,128]{2,1,0:T(8,128)(2,1)S(1)}, u32[]{:S(2)}, u32[]{:S(2)}) collective-permute-start(bf16[1,256,128]{2,1,0:T(8,128)(2,1)S(1)} %get-tuple-element.77), channel_id=1, source_target_pairs={{0,16},{1,17},{2,18},{3,19},{4,20},{5,21},{6,22},{7,23},{8,24},{9,... | collective-permute-start | bytes 196616 | tf_op jit(solution)/shard_map/ppermute | solution.py:499
  75.8 6.4 %collective-permute-start.18 = (bf16[1,256,128]{2,1,0:T(8,128)(2,1)S(1)}, bf16[1,256,128]{2,1,0:T(8,128)(2,1)S(1)}, u32[]{:S(2)}, u32[]{:S(2)}) collective-permute-start(bf16[1,256,128]{2,1,0:T(8,128)(2,1)S(1)} %get-tuple-element.78), channel_id=1, source_target_pairs={{0,24},{1,25},{2,26},{3,27},{4,28},{5,29},{6,30},{7,31},{8,16},{9,... | collective-permute-start | bytes 196616 | tf_op jit(solution)/shard_map/ppermute | solution.py:499
  78.1 6.4 %collective-permute-start.26 = (bf16[1,64,1024]{2,1,0:T(8,128)(2,1)S(1)}, bf16[1,64,1024]{2,1,0:T(8,128)(2,1)S(1)}, u32[]{:S(2)}, u32[]{:S(2)}) collective-permute-start(bf16[1,64,1024]{2,1,0:T(8,128)(2,1)S(1)} %shard_map.148.refs_0_), channel_id=1, source_target_pairs={{0,2},{1,3},{2,0},{3,1},{4,6},{5,7},{6,4},{7,5},{8,10},{9,11},{10,... | collective-permute-start | bytes 393224 | tf_op jit(solution)/shard_map/ppermute | solution.py:499
  78.5 6.5 %collective-permute-start.27 = (bf16[1,64,1024]{2,1,0:T(8,128)(2,1)S(1)}, bf16[1,64,1024]{2,1,0:T(8,128)(2,1)S(1)}, u32[]{:S(2)}, u32[]{:S(2)}) collective-permute-start(bf16[1,64,1024]{2,1,0:T(8,128)(2,1)S(1)} %shard_map.148.refs_0_), channel_id=1, source_target_pairs={{0,3},{1,2},{2,1},{3,0},{4,7},{5,6},{6,5},{7,4},{8,11},{9,10},{10,... | collective-permute-start | bytes 393224 | tf_op jit(solution)/shard_map/ppermute | solution.py:499
  82.3 4.8 %collective-permute-start.19 = (bf16[1,256,128]{2,1,0:T(8,128)(2,1)S(1)}, bf16[1,256,128]{2,1,0:T(8,128)(2,1)S(1)}, u32[]{:S(2)}, u32[]{:S(2)}) collective-permute-start(bf16[1,256,128]{2,1,0:T(8,128)(2,1)S(1)} %shard_map.147.refs_0_), channel_id=1, source_target_pairs={{0,1},{1,0},{2,3},{3,2},{4,5},{5,4},{6,7},{7,6},{8,9},{9,8},{10,11... | collective-permute-start | bytes 196616 | tf_op jit(solution)/shard_map/ppermute | solution.py:499
  82.4 5.7 %collective-permute-start.20 = (bf16[1,256,128]{2,1,0:T(8,128)(2,1)S(1)}, bf16[1,256,128]{2,1,0:T(8,128)(2,1)S(1)}, u32[]{:S(2)}, u32[]{:S(2)}) collective-permute-start(bf16[1,256,128]{2,1,0:T(8,128)(2,1)S(1)} %shard_map.147.refs_0_), channel_id=1, source_target_pairs={{0,2},{1,3},{2,0},{3,1},{4,6},{5,7},{6,4},{7,5},{8,10},{9,11},{10,... | collective-permute-start | bytes 196616 | tf_op jit(solution)/shard_map/ppermute | solution.py:499
  83.0 5.4 %collective-permute-start.21 = (bf16[1,256,128]{2,1,0:T(8,128)(2,1)S(1)}, bf16[1,256,128]{2,1,0:T(8,128)(2,1)S(1)}, u32[]{:S(2)}, u32[]{:S(2)}) collective-permute-start(bf16[1,256,128]{2,1,0:T(8,128)(2,1)S(1)} %shard_map.147.refs_0_), channel_id=1, source_target_pairs={{0,3},{1,2},{2,1},{3,0},{4,7},{5,6},{6,5},{7,4},{8,11},{9,10},{10,... | collective-permute-start | bytes 196616 | tf_op jit(solution)/shard_map/ppermute | solution.py:499

commit v8 on v4

--- a/solution.py
+++ b/solution.py
@@ -576,6 +576,16 @@
         w_qkv,
         scratch=[pltpu.VMEM((count, 3 * width), BF16)],
     )
+    small = call(
+        functools.partial(grads_qkv_kernel, factor, width, slabs),
+        [shape_of((spans, rows * (width // LANES), LANES), BF16)] * 4,
+        pack_z,
+        pack_z_core,
+        pack_p,
+        permute(pack_p, 0, 1),
+        scratch=[pltpu.VMEM((width, width), F32)],
+    )
+    ready = small[0]
     (around,) = call(
         join_kernel,
         [shape_of((4 * count, 2 * width), BF16)],
@@ -583,7 +593,7 @@
         shared_x,
         shared_y,
         permute(shared_x, 0, 2),
-        after=[pack_p],
+        after=[ready],
     )
     radix = min(4, spans)
     shift = (slabs // radix).bit_length() - 1
@@ -597,16 +607,6 @@
         scratch=[pltpu.VMEM((units // 8, width), F32), pltpu.VMEM((width, units // 4), F32)],
     )
     early = big[0]
-    small = call(
-        functools.partial(grads_qkv_kernel, factor, width, slabs),
-        [shape_of((spans, rows * (width // LANES), LANES), BF16)] * 4,
-        pack_z,
-        pack_z_core,
-        pack_p,
-        permute(pack_p, 0, 1),
-        scratch=[pltpu.VMEM((width, width), F32)],
-    )
-    ready = small[0]
     small = [small[0], permute(small[1], 1, 0), permute(small[2], 0, 2), permute(small[3], 1, 2)]
     grad_tokens, flag = call(
         functools.partial(plane_tokens_kernel, sizes, parts),

time: 89.5 us -> 93.3 us (1.042)
  waiting for transfers between devices: 24.8 us -> 27.3 us
  Pallas kernels: 22.7 us -> 23.8 us
    ppermute x28, waiting for transfers between devices: 17.1 us -> 19.1 us  [permute(): lax.ppermute(array, BOTH, swap_pairs(slabs, cases, flip_slab, flip_case))]
    pallas_call x16, Pallas kernels: 22.7 us -> 23.8 us  [call(): pl.pallas_call(run, out_shape=outs, in_specs=[vmem if one else far for on...]
  transfers between devices with their start and end apart: 29 -> 29, of which waited for: 12 -> 11; matrix products, arithmetic and copies ran while one was open for 0% -> 0% of each run, Pallas kernels for 19% -> 19%
where the time goes in v8:
time: 93.3 us; the launch traced here: 92.6 us
  starting transfers between devices  35.6 us (38%)
  waiting for transfers between devices  27.3 us (29%)
  Pallas kernels  23.8 us (26%)
  local copies, waits for them, and re-layouts  5 us (5%)
    ppermute x28, starting transfers between devices, permute(): lax.ppermute(array, BOTH, swap_pairs(slabs, cases, flip_slab, flip_case))  31 us
    pallas_call x16, Pallas kernels, call(): pl.pallas_call(run, out_shape=outs, in_specs=[vmem if one else far for on...  23.8 us
    ppermute x28, waiting for transfers between devices, permute(): lax.ppermute(array, BOTH, swap_pairs(slabs, cases, flip_slab, flip_case))  19.1 us
    all_to_all x1, waiting for transfers between devices, body(): back = lax.all_to_all(back, 'slab', split_axis=0, concat_axis=0, tiled=True)  8.21 us
    unnamed x24, local copies, waits for them, and re-layouts  5 us
    all_to_all x1, starting transfers between devices, body(): back = lax.all_to_all(back, 'slab', split_axis=0, concat_axis=0, tiled=True)  4.59 us
  transfers between devices with their start and end apart: 29, of which 11 were waited for; matrix products, arithmetic and copies ran while one was open for 0% of the time, Pallas kernels for 19%

profile of v8, /device:TPU:0, one launch (start us, length us, event | category | flops | bytes accessed | tf_op | source)
XLA Modules:
  0.0 92.6 jit_solution(1375767882705800385)
XLA Ops:
  0.6 2.9 %shard_map.135 = (bf16[16,1536]{1,0:T(8,128)(2,1)S(1)}, bf16[16,1536]{1,0:T(8,128)(2,1)S(1)}, bf16[16,1536]{1,0:T(8,128)(2,1)S(1)}, bf16[16,1536]{1,0:T(8,128)(2...) custom-call(bf16[128,512]{1,0:T(8,128)(2,1)} %bitcast.20, ...), custom_call_target="tpu_custom_call" | custom-call | flops 10000000 | bytes 10000 | tf_op jit(solution)/shard_map/pallas_call | solution.py:50
  3.5 3.0 %collective-permute-start = (bf16[16,1536]{1,0:T(8,128)(2,1)S(1)}, bf16[16,1536]{1,0:T(8,128)(2,1)S(1)}, u32[]{:S(2)}, u32[]{:S(2)}) collective-permute-start(bf16[16,1536]{1,0:T(8,128)(2,1)S(1)} %get-tuple-element.49), channel_id=1, source_target_pairs={{0,4},{1,5},{2,6},{3,7},{4,0},{5,1},{6,2},{7,3},{8,12},{9,13},{10,... | collective-permute-start | bytes 147464 | tf_op jit(solution)/shard_map/ppermute | solution.py:499
  6.5 1.6 %collective-permute-start.1 = (bf16[16,1536]{1,0:T(8,128)(2,1)S(1)}, bf16[16,1536]{1,0:T(8,128)(2,1)S(1)}, u32[]{:S(2)}, u32[]{:S(2)}) collective-permute-start(bf16[16,1536]{1,0:T(8,128)(2,1)S(1)} %get-tuple-element.50), channel_id=1, source_target_pairs={{0,8},{1,9},{2,10},{3,11},{4,12},{5,13},{6,14},{7,15},{8,0},{9,1},... | collective-permute-start | bytes 147464 | tf_op jit(solution)/shard_map/ppermute | solution.py:499
  8.1 3.0 %collective-permute-start.3 = (bf16[16,1536]{1,0:T(8,128)(2,1)S(1)}, bf16[16,1536]{1,0:T(8,128)(2,1)S(1)}, u32[]{:S(2)}, u32[]{:S(2)}) collective-permute-start(bf16[16,1536]{1,0:T(8,128)(2,1)S(1)} %get-tuple-element.52), channel_id=1, source_target_pairs={{0,16},{1,17},{2,18},{3,19},{4,20},{5,21},{6,22},{7,23},{8,24},{9,... | collective-permute-start | bytes 147464 | tf_op jit(solution)/shard_map/ppermute | solution.py:499
  11.1 1.3 %collective-permute-start.4 = (bf16[16,1536]{1,0:T(8,128)(2,1)S(1)}, bf16[16,1536]{1,0:T(8,128)(2,1)S(1)}, u32[]{:S(2)}, u32[]{:S(2)}) collective-permute-start(bf16[16,1536]{1,0:T(8,128)(2,1)S(1)} %get-tuple-element.53), channel_id=1, source_target_pairs={{0,20},{1,21},{2,22},{3,23},{4,16},{5,17},{6,18},{7,19},{8,28},{9,... | collective-permute-start | bytes 147464 | tf_op jit(solution)/shard_map/ppermute | solution.py:499
  12.4 0.0 collective-permute-done.refs_1_
  12.4 3.6 %collective-permute-start.5 = (bf16[16,1536]{1,0:T(8,128)(2,1)S(1)}, bf16[16,1536]{1,0:T(8,128)(2,1)S(1)}, u32[]{:S(2)}, u32[]{:S(2)}) collective-permute-start(bf16[16,1536]{1,0:T(8,128)(2,1)S(1)} %get-tuple-element.54), channel_id=1, source_target_pairs={{0,24},{1,25},{2,26},{3,27},{4,28},{5,29},{6,30},{7,31},{8,16},{9,... | collective-permute-start | bytes 147464 | tf_op jit(solution)/shard_map/ppermute | solution.py:499
  16.0 0.0 collective-permute-start.6
  16.1 1.7 %copy-done.1 = bf16[512,2048]{1,0:T(8,128)(2,1)S(1)} copy-done((bf16[512,2048]{1,0:T(8,128)(2,1)S(1)}, bf16[512,2048]{1,0:T(8,128)(2,1)}, u32[]{:S(2)}) %copy-start.1) | copy-done | bytes 2097176
  17.8 1.6 %copy-done.3 = bf16[2048,512]{1,0:T(8,128)(2,1)S(1)} copy-done((bf16[2048,512]{1,0:T(8,128)(2,1)S(1)}, bf16[2048,512]{1,0:T(8,128)(2,1)}, u32[]{:S(2)}) %copy-start.3) | copy-done | bytes 2097176
  19.4 1.3 %shard_map.136 = (bf16[512,512]{1,0:T(8,128)(2,1)S(1)}, bf16[512,512]{1,0:T(8,128)(2,1)S(1)}) custom-call(bf16[512,2048]{1,0:T(8,128)(2,1)S(1)} %copy-done.1, bf16[2048,512]{1,0:T(8,128)(2,1)S(1)} %copy-done.3), custom_call_target="tpu_custom_call" | custom-call | flops 10000000 | bytes 10000 | tf_op jit(solution)/shard_map/pallas_call | solution.py:50
  20.7 0.0 copy-start.8
  20.7 0.8 copy-done.8
  21.5 0.0 collective-permute-done.2.refs_3_
  21.5 0.0 collective-permute-done.4.refs_5_
  21.5 1.3 %collective-permute-done.6.refs_7_ = bf16[16,1536]{1,0:T(8,128)(2,1)S(1)} collective-permute-done((bf16[16,1536]{1,0:T(8,128)(2,1)S(1)}, bf16[16,1536]{1,0:T(8,128)(2,1)S(1)}, u32[]{:S(2)}, u32[]{:S(2)}) %collective-permute-start.6) | collective-permute-done | bytes 49184 | tf_op jit(solution)/shard_map/ppermute | solution.py:499
  22.8 1.3 %shard_map.137 = (bf16[128,1024]{1,0:T(8,128)(2,1)S(1)}, bf16[128,1536]{1,0:T(8,128)(2,1)S(1)}, bf16[128,512]{1,0:T(8,128)(2,1)S(1)}, bf16[128,512]{1,0:T(8,128)(2,1)S(1)}, bf16[128,512]{1,0:T(8,128)(2,1)S(1)}) custom-call(bf16[16,1536]{1,0:T(8,128)(2,1)S(1)} %get-tuple-element.48.refs_0_, bf16[16,1536]{1,0:T(8,128)(2,1)S(1)} %collective-permute-done.refs_1_, ...), custom_call_target="tpu_custom_call" | custom-call | flops 10000000 | bytes 10000 | tf_op jit(solution)/shard_map/pallas_call | solution.py:50
  24.1 0.6 collective-permute-start.7
  24.7 1.5 %collective-permute-start.8 = (bf16[128,1024]{1,0:T(8,128)(2,1)S(1)}, bf16[128,1024]{1,0:T(8,128)(2,1)S(1)}, u32[]{:S(2)}, u32[]{:S(2)}) collective-permute-start(bf16[128,1024]{1,0:T(8,128)(2,1)S(1)} %get-tuple-element.58.refs_0_), channel_id=1, source_target_pairs={{0,2},{1,3},{2,0},{3,1},{4,6},{5,7},{6,4},{7,5},{8,10},{9,11},{10,... | collective-permute-start | bytes 786440 | tf_op jit(solution)/shard_map/ppermute | solution.py:499
  26.2 2.4 %shard_map.138 = (bf16[128,512]{1,0:T(8,128)(2,1)S(1)}, f32[128,512]{1,0:T(8,128)S(1)}) custom-call(bf16[128,1024]{1,0:T(8,128)(2,1)S(1)} %get-tuple-element.58.refs_0_, bf16[128,512]{1,0:T(8,128)(2,1)S(1)} %get-tuple-element.59.refs_1_, f32[1,512]{1,0:T(1,128)S(1)} %bitcast.18, bf16[512,512]{1,0:T(8,128)(2,1)S(1)} %copy-done.5, ...), custom_call_target="tpu_custom_call" | custom-call | flops 10000000 | bytes 10000 | tf_op jit(solution)/shard_map/pallas_call | solution.py:50
  28.6 2.6 %shard_map.139 = (bf16[128,1024]{1,0:T(8,128)(2,1)S(1)}, bf16[128,3072]{1,0:T(8,128)(2,1)S(1)}) custom-call(bf16[128,1536]{1,0:T(8,128)(2,1)S(1)} %get-tuple-element.57.refs_0_, bf16[128,512]{1,0:T(8,128)(2,1)S(1)} %get-tuple-element.60.refs_1_, f32[128,512]{1,0:T(8,128)S(1)} %get-tuple-element.61.refs_2_, bf16[128,512]{1,0:T(8,128)(2,1)S(1)} %get-tuple-element.62.refs_3_, ...), custom_call_target="tpu_custom_call" | custom-call | flops 10000000 | bytes 10000 | tf_op jit(solution)/shard_map/pallas_call | solution.py:50
  31.2 0.9 copy-done.6
  32.1 0.0 collective-permute-done.7.refs_1_
  32.1 0.0 collective-permute-done.8.refs_2_
  32.1 0.7 shard_map.140
  32.9 4.6 %all-to-all-start = ((bf16[8,16,1024]{2,1,0:T(8,128)(2,1)}), bf16[8,16,1024]{2,1,0:T(8,128)(2,1)S(1)}, u32[]{:S(2)}, u32[]{:S(2)}) async-start(bf16[8,16,1024]{2,1,0:T(8,128)(2,1)} %bitcast.4), calls=%async_computation | async-start | bytes 524288 | tf_op jit(solution)/shard_map/all_to_all | solution.py:568
  37.5 8.2 %all-to-all-done = bf16[8,16,1024]{2,1,0:T(8,128)(2,1)S(1)} async-done(((bf16[8,16,1024]{2,1,0:T(8,128)(2,1)}), bf16[8,16,1024]{2,1,0:T(8,128)(2,1)S(1)}, u32[]{:S(2)}, u32[]{:S(2)}) %all-to-all-start) | async-done | bytes 262176 | tf_op jit(solution)/shard_map/all_to_all | solution.py:568
  45.7 2.6 %shard_map.141.refs_2_.refs_1_ = bf16[128,2048]{1,0:T(8,128)(2,1)S(1)} custom-call(bf16[128,1024]{1,0:T(8,128)(2,1)S(1)} %bitcast.9, bf16[128,512]{1,0:T(8,128)(2,1)S(1)} %get-tuple-element.65.refs_1_.refs_2_, f32[1,512]{1,0:T(1,128)S(1)} %bitcast.14, bf16[512,1536]{1,0:T(8,128)(2,1)S(1)} %copy-done), custom_call_target="tpu_custom_call" | custom-call | flops 10000000 | bytes 10000 | tf_op jit(solution)/shard_map/pallas_call | solution.py:50
  48.3 0.0 copy-start.9
  48.3 0.1 collective-permute-start.10
  48.4 0.6 collective-permute-start.11
  49.0 1.3 %collective-permute-done.10.refs_3_ = bf16[128,2048]{1,0:T(8,128)(2,1)S(1)} collective-permute-done((bf16[128,2048]{1,0:T(8,128)(2,1)S(1)}, bf16[128,2048]{1,0:T(8,128)(2,1)S(1)}, u32[]{:S(2)}, u32[]{:S(2)}) %collective-permute-start.10) | collective-permute-done | bytes 524320 | tf_op jit(solution)/shard_map/ppermute | solution.py:499
  50.3 2.2 %shard_map.142 = (bf16[4,256,128]{2,1,0:T(8,128)(2,1)S(1)}, bf16[4,256,128]{2,1,0:T(8,128)(2,1)S(1)}, bf16[4,256,128]{2,1,0:T(8,128)(2,1)S(1)}, bf16[4,256,128]{2,1,0:T(8,128)(2,1)S(1)}) custom-call(bf16[128,3072]{1,0:T(8,128)(2,1)S(1)} %copy-done.7, bf16[128,3072]{1,0:T(8,128)(2,1)} %collective-permute-done.9.refs_1_, ...), custom_call_target="tpu_custom_call" | custom-call | flops 10000000 | bytes 10000 | tf_op jit(solution)/shard_map/pallas_call | solution.py:50
  52.5 4.6 %collective-permute-done.11.refs_3_ = bf16[128,1024]{1,0:T(8,128)(2,1)S(1)} collective-permute-done((bf16[128,1024]{1,0:T(8,128)(2,1)S(1)}, bf16[128,1024]{1,0:T(8,128)(2,1)S(1)}, u32[]{:S(2)}, u32[]{:S(2)}) %collective-permute-start.11) | collective-permute-done | bytes 262176 | tf_op jit(solution)/shard_map/ppermute | solution.py:499
  57.1 0.1 shard_map.143.refs_0_
  57.2 0.1 collective-permute-start.12
  57.3 0.1 collective-permute-start.13
  57.4 0.6 collective-permute-start.14
  57.9 2.9 %collective-permute-start.15 = (bf16[4,256,128]{2,1,0:T(8,128)(2,1)S(1)}, bf16[4,256,128]{2,1,0:T(8,128)(2,1)S(1)}, u32[]{:S(2)}, u32[]{:S(2)}) collective-permute-start(bf16[4,256,128]{2,1,0:T(8,128)(2,1)S(1)} %get-tuple-element.73), channel_id=1, source_target_pairs={{0,6},{1,7},{2,4},{3,5},{4,2},{5,3},{6,0},{7,1},{8,14},{9,15},{10,... | collective-permute-start | bytes 786440 | tf_op jit(solution)/shard_map/ppermute | solution.py:499
  60.8 3.0 %shard_map.144 = (bf16[1,64,1024]{2,1,0:T(8,128)(2,1)S(1)}, bf16[1,64,1024]{2,1,0:T(8,128)(2,1)S(1)}, bf16[1,64,1024]{2,1,0:T(8,128)(2,1)S(1)}, bf16[1,64,1024]{2,1,0:T(8,128)(2,1)S(1)}) custom-call(bf16[512,1024]{1,0:T(8,128)(2,1)S(1)} %shard_map.143.refs_0_, bf16[512,1024]{1,0:T(8,128)(2,1)S(1)} %collective-permute-done.12.refs_1_, ...), custom_call_target="tpu_custom_call" | custom-call | flops 10000000 | bytes 10000 | tf_op jit(solution)/shard_map/pallas_call | solution.py:50
  63.9 0.1 collective-permute-start.22
  63.9 1.1 %collective-permute-start.23 = (bf16[1,64,1024]{2,1,0:T(8,128)(2,1)S(1)}, bf16[1,64,1024]{2,1,0:T(8,128)(2,1)S(1)}, u32[]{:S(2)}, u32[]{:S(2)}) collective-permute-start(bf16[1,64,1024]{2,1,0:T(8,128)(2,1)S(1)} %get-tuple-element.80), channel_id=1, source_target_pairs={{0,16},{1,17},{2,18},{3,19},{4,20},{5,21},{6,22},{7,23},{8,24},{9,... | collective-permute-start | bytes 393224 | tf_op jit(solution)/shard_map/ppermute | solution.py:499
  65.1 1.4 %collective-permute-done.13.refs_1_ = bf16[4,256,128]{2,1,0:T(8,128)(2,1)S(1)} collective-permute-done((bf16[4,256,128]{2,1,0:T(8,128)(2,1)S(1)}, bf16[4,256,128]{2,1,0:T(8,128)(2,1)S(1)}, u32[]{:S(2)}, u32[]{:S(2)}) %collective-permute-start.13) | collective-permute-done | bytes 262176 | tf_op jit(solution)/shard_map/ppermute | solution.py:499
  66.5 1.9 %collective-permute-start.24 = (bf16[1,64,1024]{2,1,0:T(8,128)(2,1)S(1)}, bf16[1,64,1024]{2,1,0:T(8,128)(2,1)S(1)}, u32[]{:S(2)}, u32[]{:S(2)}) collective-permute-start(bf16[1,64,1024]{2,1,0:T(8,128)(2,1)S(1)} %get-tuple-element.81), channel_id=1, source_target_pairs={{0,24},{1,25},{2,26},{3,27},{4,28},{5,29},{6,30},{7,31},{8,16},{9,... | collective-permute-start | bytes 393224 | tf_op jit(solution)/shard_map/ppermute | solution.py:499
  68.3 1.6 %shard_map.145 = (bf16[128,512]{1,0:T(8,128)(2,1)}, f32[8,128]{1,0:T(8,128)S(1)}) custom-call(bf16[128,1024]{1,0:T(8,128)(2,1)S(1)} %bitcast.10, bf16[128,2048]{1,0:T(8,128)(2,1)S(1)} %shard_map.141.refs_2_.refs_1_, bf16[128,512]{1,0:T(8,128)(2,1)S(1)} %get-tuple-element.65.refs_1_.refs_2_, f32[1,512]{1,0:T(1,128)S(1)} %bitcast.15, ...), custom_call_target="tpu_custom_call" | custom-call | flops 10000000 | bytes 10000 | tf_op jit(solution)/shard_map/pallas_call | solution.py:50
  69.9 1.7 %collective-permute-done.15.refs_3_ = bf16[4,256,128]{2,1,0:T(8,128)(2,1)S(1)} collective-permute-done((bf16[4,256,128]{2,1,0:T(8,128)(2,1)S(1)}, bf16[4,256,128]{2,1,0:T(8,128)(2,1)S(1)}, u32[]{:S(2)}, u32[]{:S(2)}) %collective-permute-start.15) | collective-permute-done | bytes 262176 | tf_op jit(solution)/shard_map/ppermute | solution.py:499
  71.6 0.1 shard_map.146
  71.7 1.3 %collective-permute-start.16 = (bf16[1,256,128]{2,1,0:T(8,128)(2,1)S(1)}, bf16[1,256,128]{2,1,0:T(8,128)(2,1)S(1)}, u32[]{:S(2)}, u32[]{:S(2)}) collective-permute-start(bf16[1,256,128]{2,1,0:T(8,128)(2,1)S(1)} %get-tuple-element.76), channel_id=1, source_target_pairs={{0,8},{1,9},{2,10},{3,11},{4,12},{5,13},{6,14},{7,15},{8,0},{9,1},... | collective-permute-start | bytes 196616 | tf_op jit(solution)/shard_map/ppermute | solution.py:499
  73.0 3.8 %collective-permute-done.23.refs_2_ = bf16[1,64,1024]{2,1,0:T(8,128)(2,1)S(1)} collective-permute-done((bf16[1,64,1024]{2,1,0:T(8,128)(2,1)S(1)}, bf16[1,64,1024]{2,1,0:T(8,128)(2,1)S(1)}, u32[]{:S(2)}, u32[]{:S(2)}) %collective-permute-start.23) | collective-permute-done | bytes 131104 | tf_op jit(solution)/shard_map/ppermute | solution.py:499
  76.8 0.1 shard_map.148.refs_0_
  76.9 0.1 collective-permute-start.25
  77.0 2.4 %collective-permute-start.17 = (bf16[1,256,128]{2,1,0:T(8,128)(2,1)S(1)}, bf16[1,256,128]{2,1,0:T(8,128)(2,1)S(1)}, u32[]{:S(2)}, u32[]{:S(2)}) collective-permute-start(bf16[1,256,128]{2,1,0:T(8,128)(2,1)S(1)} %get-tuple-element.77), channel_id=1, source_target_pairs={{0,16},{1,17},{2,18},{3,19},{4,20},{5,21},{6,22},{7,23},{8,24},{9,... | collective-permute-start | bytes 196616 | tf_op jit(solution)/shard_map/ppermute | solution.py:499
  79.4 2.2 %collective-permute-start.18 = (bf16[1,256,128]{2,1,0:T(8,128)(2,1)S(1)}, bf16[1,256,128]{2,1,0:T(8,128)(2,1)S(1)}, u32[]{:S(2)}, u32[]{:S(2)}) collective-permute-start(bf16[1,256,128]{2,1,0:T(8,128)(2,1)S(1)} %get-tuple-element.78), channel_id=1, source_target_pairs={{0,24},{1,25},{2,26},{3,27},{4,28},{5,29},{6,30},{7,31},{8,16},{9,... | collective-permute-start | bytes 196616 | tf_op jit(solution)/shard_map/ppermute | solution.py:499
  81.5 0.5 collective-permute-start.26
  82.0 0.7 collective-permute-start.27
  82.8 2.8 %collective-permute-done.17.refs_2_ = bf16[1,256,128]{2,1,0:T(8,128)(2,1)S(1)} collective-permute-done((bf16[1,256,128]{2,1,0:T(8,128)(2,1)S(1)}, bf16[1,256,128]{2,1,0:T(8,128)(2,1)S(1)}, u32[]{:S(2)}, u32[]{:S(2)}) %collective-permute-start.17) | collective-permute-done | bytes 65568 | tf_op jit(solution)/shard_map/ppermute | solution.py:499
  85.7 0.1 collective-permute-start.19
  85.7 0.6 collective-permute-start.20
  86.3 1.3 %collective-permute-start.21 = (bf16[1,256,128]{2,1,0:T(8,128)(2,1)S(1)}, bf16[1,256,128]{2,1,0:T(8,128)(2,1)S(1)}, u32[]{:S(2)}, u32[]{:S(2)}) collective-permute-start(bf16[1,256,128]{2,1,0:T(8,128)(2,1)S(1)} %shard_map.147.refs_0_), channel_id=1, source_target_pairs={{0,3},{1,2},{2,1},{3,0},{4,7},{5,6},{6,5},{7,4},{8,11},{9,10},{10,... | collective-permute-start | bytes 196616 | tf_op jit(solution)/shard_map/ppermute | solution.py:499
  87.6 0.3 collective-permute-done.26.refs_2_
  87.9 0.6 collective-permute-done.27.refs_3_
  88.5 2.1 %shard_map.149 = (f32[64,2048]{1,0:T(8,128)}, f32[256,512]{1,0:T(8,128)}, f32[1,64]{1,0:T(1,128)}, bf16[64,1536]{1,0:T(8,128)(2,1)S(1)}) custom-call(bf16[1,64,1024]{2,1,0:T(8,128)(2,1)S(1)} %shard_map.148.refs_0_, bf16[1,64,1024]{2,1,0:T(8,128)(2,1)S(1)} %collective-permute-done.25.refs_1_, bf16[1,64,1024]{2,1,0:T(8,128)(2,1)S(1)} %collective-permute-done.26.refs_2_, ...), custom_call_target="tpu_custom_call" | custom-call | flops 10000000 | bytes 10000 | tf_op jit(solution)/shard_map/pallas_call | solution.py:50
  90.6 1.1 %collective-permute-done.20.refs_2_ = bf16[1,256,128]{2,1,0:T(8,128)(2,1)S(1)} collective-permute-done((bf16[1,256,128]{2,1,0:T(8,128)(2,1)S(1)}, bf16[1,256,128]{2,1,0:T(8,128)(2,1)S(1)}, u32[]{:S(2)}, u32[]{:S(2)}) %collective-permute-start.20) | collective-permute-done | bytes 65568 | tf_op jit(solution)/shard_map/ppermute | solution.py:499
  91.7 0.8 shard_map.150
  (34 shorter events, 0.1 us)
Async XLA Ops:
  3.5 8.9 %collective-permute-start = (bf16[16,1536]{1,0:T(8,128)(2,1)S(1)}, bf16[16,1536]{1,0:T(8,128)(2,1)S(1)}, u32[]{:S(2)}, u32[]{:S(2)}) collective-permute-start(bf16[16,1536]{1,0:T(8,128)(2,1)S(1)} %get-tuple-element.49), channel_id=1, source_target_pairs={{0,4},{1,5},{2,6},{3,7},{4,0},{5,1},{6,2},{7,3},{8,12},{9,13},{10,... | collective-permute-start | bytes 147464 | tf_op jit(solution)/shard_map/ppermute | solution.py:499
  6.5 9.5 %collective-permute-start.1 = (bf16[16,1536]{1,0:T(8,128)(2,1)S(1)}, bf16[16,1536]{1,0:T(8,128)(2,1)S(1)}, u32[]{:S(2)}, u32[]{:S(2)}) collective-permute-start(bf16[16,1536]{1,0:T(8,128)(2,1)S(1)} %get-tuple-element.50), channel_id=1, source_target_pairs={{0,8},{1,9},{2,10},{3,11},{4,12},{5,13},{6,14},{7,15},{8,0},{9,1},... | collective-permute-start | bytes 147464 | tf_op jit(solution)/shard_map/ppermute | solution.py:499
  8.1 13.4 %collective-permute-start.2 = (bf16[16,1536]{1,0:T(8,128)(2,1)S(1)}, bf16[16,1536]{1,0:T(8,128)(2,1)S(1)}, u32[]{:S(2)}, u32[]{:S(2)}) collective-permute-start(bf16[16,1536]{1,0:T(8,128)(2,1)S(1)} %get-tuple-element.51), channel_id=1, source_target_pairs={{0,12},{1,13},{2,14},{3,15},{4,8},{5,9},{6,10},{7,11},{8,4},{9,5},... | collective-permute-start | bytes 147464 | tf_op jit(solution)/shard_map/ppermute | solution.py:499
  8.1 13.4 %collective-permute-start.3 = (bf16[16,1536]{1,0:T(8,128)(2,1)S(1)}, bf16[16,1536]{1,0:T(8,128)(2,1)S(1)}, u32[]{:S(2)}, u32[]{:S(2)}) collective-permute-start(bf16[16,1536]{1,0:T(8,128)(2,1)S(1)} %get-tuple-element.52), channel_id=1, source_target_pairs={{0,16},{1,17},{2,18},{3,19},{4,20},{5,21},{6,22},{7,23},{8,24},{9,... | collective-permute-start | bytes 147464 | tf_op jit(solution)/shard_map/ppermute | solution.py:499
  11.1 10.3 %collective-permute-start.4 = (bf16[16,1536]{1,0:T(8,128)(2,1)S(1)}, bf16[16,1536]{1,0:T(8,128)(2,1)S(1)}, u32[]{:S(2)}, u32[]{:S(2)}) collective-permute-start(bf16[16,1536]{1,0:T(8,128)(2,1)S(1)} %get-tuple-element.53), channel_id=1, source_target_pairs={{0,20},{1,21},{2,22},{3,23},{4,16},{5,17},{6,18},{7,19},{8,28},{9,... | collective-permute-start | bytes 147464 | tf_op jit(solution)/shard_map/ppermute | solution.py:499
  12.4 9.1 %collective-permute-start.5 = (bf16[16,1536]{1,0:T(8,128)(2,1)S(1)}, bf16[16,1536]{1,0:T(8,128)(2,1)S(1)}, u32[]{:S(2)}, u32[]{:S(2)}) collective-permute-start(bf16[16,1536]{1,0:T(8,128)(2,1)S(1)} %get-tuple-element.54), channel_id=1, source_target_pairs={{0,24},{1,25},{2,26},{3,27},{4,28},{5,29},{6,30},{7,31},{8,16},{9,... | collective-permute-start | bytes 147464 | tf_op jit(solution)/shard_map/ppermute | solution.py:499
  16.0 6.8 %copy-start = (bf16[512,1536]{1,0:T(8,128)(2,1)S(1)}, bf16[512,1536]{1,0:T(8,128)(2,1)}, u32[]{:S(2)}) copy-start(bf16[512,1536]{1,0:T(8,128)(2,1)} %refs_6_.3) | copy-start | bytes 4718596
  16.0 6.8 %collective-permute-start.6 = (bf16[16,1536]{1,0:T(8,128)(2,1)S(1)}, bf16[16,1536]{1,0:T(8,128)(2,1)S(1)}, u32[]{:S(2)}, u32[]{:S(2)}) collective-permute-start(bf16[16,1536]{1,0:T(8,128)(2,1)S(1)} %get-tuple-element.55), channel_id=1, source_target_pairs={{0,28},{1,29},{2,30},{3,31},{4,24},{5,25},{6,26},{7,27},{8,20},{9,... | collective-permute-start | bytes 147464 | tf_op jit(solution)/shard_map/ppermute | solution.py:499
  16.1 1.7 %copy-start.1 = (bf16[512,2048]{1,0:T(8,128)(2,1)S(1)}, bf16[512,2048]{1,0:T(8,128)(2,1)}, u32[]{:S(2)}) copy-start(bf16[512,2048]{1,0:T(8,128)(2,1)} %refs_5_.3) | copy-start | bytes 6291460
  17.8 1.6 %copy-start.3 = (bf16[2048,512]{1,0:T(8,128)(2,1)S(1)}, bf16[2048,512]{1,0:T(8,128)(2,1)}, u32[]{:S(2)}) copy-start(bf16[2048,512]{1,0:T(8,128)(2,1)} %refs_5_.2) | copy-start | bytes 6291460
  19.4 3.5 %copy-start.5 = (bf16[512,512]{1,0:T(8,128)(2,1)S(1)}, bf16[512,512]{1,0:T(8,128)(2,1)}, u32[]{:S(2)}) copy-start(bf16[512,512]{1,0:T(8,128)(2,1)} %refs_3_.4) | copy-start | bytes 1572868
  19.4 3.5 %copy-start.10 = (f32[512]{0:T(512)S(1)}, f32[512]{0:T(512)}, u32[]{:S(2)}) copy-start(f32[512]{0:T(512)} %param.14) | copy-start | bytes 6148
  19.4 3.5 %copy-start.11 = (f32[512]{0:T(512)S(1)}, f32[512]{0:T(512)}, u32[]{:S(2)}) copy-start(f32[512]{0:T(512)} %param.15) | copy-start | bytes 6148
  19.4 6.8 %copy-start.4 = (bf16[2048,512]{1,0:T(8,128)(2,1)S(1)}, bf16[2048,512]{1,0:T(8,128)(2,1)}, u32[]{:S(2)}) copy-start(bf16[2048,512]{1,0:T(8,128)(2,1)} %refs_5_.2) | copy-start | bytes 6291460
  20.7 0.8 copy-start.8
  21.5 4.7 %copy-start.2 = (bf16[512,2048]{1,0:T(8,128)(2,1)S(1)}, bf16[512,2048]{1,0:T(8,128)(2,1)}, u32[]{:S(2)}) copy-start(bf16[512,2048]{1,0:T(8,128)(2,1)} %refs_5_.3) | copy-start | bytes 6291460
  24.1 8.1 %collective-permute-start.7 = (bf16[128,1024]{1,0:T(8,128)(2,1)S(1)}, bf16[128,1024]{1,0:T(8,128)(2,1)S(1)}, u32[]{:S(2)}, u32[]{:S(2)}) collective-permute-start(bf16[128,1024]{1,0:T(8,128)(2,1)S(1)} %get-tuple-element.58.refs_0_), channel_id=1, source_target_pairs={{0,4},{1,5},{2,6},{3,7},{4,0},{5,1},{6,2},{7,3},{8,12},{9,13},{10,... | collective-permute-start | bytes 786440 | tf_op jit(solution)/shard_map/ppermute | solution.py:499
  24.7 7.5 %collective-permute-start.8 = (bf16[128,1024]{1,0:T(8,128)(2,1)S(1)}, bf16[128,1024]{1,0:T(8,128)(2,1)S(1)}, u32[]{:S(2)}, u32[]{:S(2)}) collective-permute-start(bf16[128,1024]{1,0:T(8,128)(2,1)S(1)} %get-tuple-element.58.refs_0_), channel_id=1, source_target_pairs={{0,2},{1,3},{2,0},{3,1},{4,6},{5,7},{6,4},{7,5},{8,10},{9,11},{10,... | collective-permute-start | bytes 786440 | tf_op jit(solution)/shard_map/ppermute | solution.py:499
  31.2 0.9 copy-start.6
  32.9 12.8 %all-to-all-start = ((bf16[8,16,1024]{2,1,0:T(8,128)(2,1)}), bf16[8,16,1024]{2,1,0:T(8,128)(2,1)S(1)}, u32[]{:S(2)}, u32[]{:S(2)}) async-start(bf16[8,16,1024]{2,1,0:T(8,128)(2,1)} %bitcast.4), calls=%async_computation | async-start | bytes 524288 | tf_op jit(solution)/shard_map/all_to_all | solution.py:568
  37.4 11.5 %collective-permute-start.9 = (bf16[128,3072]{1,0:T(8,128)(2,1)}, bf16[128,3072]{1,0:T(8,128)(2,1)}, u32[]{:S(2)}, u32[]{:S(2)}) collective-permute-start(bf16[128,3072]{1,0:T(8,128)(2,1)} %copy-done.6), channel_id=1, source_target_pairs={{0,1},{1,0},{2,3},{3,2},{4,5},{5,4},{6,7},{7,6},{8,9},{9,8},{10,11... | collective-permute-start | bytes 2359304 | tf_op jit(solution)/shard_map/ppermute | solution.py:499
  45.7 4.6 %copy-start.7 = (bf16[128,3072]{1,0:T(8,128)(2,1)S(1)}, bf16[128,3072]{1,0:T(8,128)(2,1)}, u32[]{:S(2)}) copy-start(bf16[128,3072]{1,0:T(8,128)(2,1)} %copy-done.6) | copy-start | bytes 2359300
  48.3 12.5 %copy-start.9 = (bf16[512,512]{1,0:T(8,128)(2,1)S(1)}, bf16[512,512]{1,0:T(8,128)(2,1)}, u32[]{:S(2)}) copy-start(bf16[512,512]{1,0:T(8,128)(2,1)} %copy-done.8) | copy-start | bytes 1572868
  48.3 2.0 %collective-permute-start.10 = (bf16[128,2048]{1,0:T(8,128)(2,1)S(1)}, bf16[128,2048]{1,0:T(8,128)(2,1)S(1)}, u32[]{:S(2)}, u32[]{:S(2)}) collective-permute-start(bf16[128,2048]{1,0:T(8,128)(2,1)S(1)} %shard_map.141.refs_2_.refs_1_), channel_id=1, source_target_pairs={{0,1},{1,0},{2,3},{3,2},{4,5},{5,4},{6,7},{7,6},{8,9},{9,8},{10,11... | collective-permute-start | bytes 1572872 | tf_op jit(solution)/shard_map/ppermute | solution.py:499
  48.4 8.7 %collective-permute-start.11 = (bf16[128,1024]{1,0:T(8,128)(2,1)S(1)}, bf16[128,1024]{1,0:T(8,128)(2,1)S(1)}, u32[]{:S(2)}, u32[]{:S(2)}) collective-permute-start(bf16[128,1024]{1,0:T(8,128)(2,1)S(1)} %collective-permute-done.7.refs_1_), channel_id=1, source_target_pairs={{0,2},{1,3},{2,0},{3,1},{4,6},{5,7},{6,4},{7,5},{8,10},{9,11},{10,... | collective-permute-start | bytes 786440 | tf_op jit(solution)/shard_map/ppermute | solution.py:499
  57.2 3.6 %collective-permute-start.12 = (bf16[512,1024]{1,0:T(8,128)(2,1)S(1)}, bf16[512,1024]{1,0:T(8,128)(2,1)S(1)}, u32[]{:S(2)}, u32[]{:S(2)}) collective-permute-start(bf16[512,1024]{1,0:T(8,128)(2,1)S(1)} %shard_map.143.refs_0_), channel_id=1, source_target_pairs={{0,1},{1,0},{2,3},{3,2},{4,5},{5,4},{6,7},{7,6},{8,9},{9,8},{10,11... | collective-permute-start | bytes 3145736 | tf_op jit(solution)/shard_map/ppermute | solution.py:499
  57.3 9.2 %collective-permute-start.13 = (bf16[4,256,128]{2,1,0:T(8,128)(2,1)S(1)}, bf16[4,256,128]{2,1,0:T(8,128)(2,1)S(1)}, u32[]{:S(2)}, u32[]{:S(2)}) collective-permute-start(bf16[4,256,128]{2,1,0:T(8,128)(2,1)S(1)} %get-tuple-element.71), channel_id=1, source_target_pairs={{0,4},{1,5},{2,6},{3,7},{4,0},{5,1},{6,2},{7,3},{8,12},{9,13},{10,... | collective-permute-start | bytes 786440 | tf_op jit(solution)/shard_map/ppermute | solution.py:499
  57.4 12.5 %collective-permute-start.14 = (bf16[4,256,128]{2,1,0:T(8,128)(2,1)S(1)}, bf16[4,256,128]{2,1,0:T(8,128)(2,1)S(1)}, u32[]{:S(2)}, u32[]{:S(2)}) collective-permute-start(bf16[4,256,128]{2,1,0:T(8,128)(2,1)S(1)} %get-tuple-element.72), channel_id=1, source_target_pairs={{0,2},{1,3},{2,0},{3,1},{4,6},{5,7},{6,4},{7,5},{8,10},{9,11},{10,... | collective-permute-start | bytes 786440 | tf_op jit(solution)/shard_map/ppermute | solution.py:499
  57.9 13.7 %collective-permute-start.15 = (bf16[4,256,128]{2,1,0:T(8,128)(2,1)S(1)}, bf16[4,256,128]{2,1,0:T(8,128)(2,1)S(1)}, u32[]{:S(2)}, u32[]{:S(2)}) collective-permute-start(bf16[4,256,128]{2,1,0:T(8,128)(2,1)S(1)} %get-tuple-element.73), channel_id=1, source_target_pairs={{0,6},{1,7},{2,4},{3,5},{4,2},{5,3},{6,0},{7,1},{8,14},{9,15},{10,... | collective-permute-start | bytes 786440 | tf_op jit(solution)/shard_map/ppermute | solution.py:499
  63.9 9.1 %collective-permute-start.22 = (bf16[1,64,1024]{2,1,0:T(8,128)(2,1)S(1)}, bf16[1,64,1024]{2,1,0:T(8,128)(2,1)S(1)}, u32[]{:S(2)}, u32[]{:S(2)}) collective-permute-start(bf16[1,64,1024]{2,1,0:T(8,128)(2,1)S(1)} %get-tuple-element.79), channel_id=1, source_target_pairs={{0,8},{1,9},{2,10},{3,11},{4,12},{5,13},{6,14},{7,15},{8,0},{9,1},... | collective-permute-start | bytes 393224 | tf_op jit(solution)/shard_map/ppermute | solution.py:499
  63.9 12.9 %collective-permute-start.23 = (bf16[1,64,1024]{2,1,0:T(8,128)(2,1)S(1)}, bf16[1,64,1024]{2,1,0:T(8,128)(2,1)S(1)}, u32[]{:S(2)}, u32[]{:S(2)}) collective-permute-start(bf16[1,64,1024]{2,1,0:T(8,128)(2,1)S(1)} %get-tuple-element.80), channel_id=1, source_target_pairs={{0,16},{1,17},{2,18},{3,19},{4,20},{5,21},{6,22},{7,23},{8,24},{9,... | collective-permute-start | bytes 393224 | tf_op jit(solution)/shard_map/ppermute | solution.py:499
  66.5 10.3 %collective-permute-start.24 = (bf16[1,64,1024]{2,1,0:T(8,128)(2,1)S(1)}, bf16[1,64,1024]{2,1,0:T(8,128)(2,1)S(1)}, u32[]{:S(2)}, u32[]{:S(2)}) collective-permute-start(bf16[1,64,1024]{2,1,0:T(8,128)(2,1)S(1)} %get-tuple-element.81), channel_id=1, source_target_pairs={{0,24},{1,25},{2,26},{3,27},{4,28},{5,29},{6,30},{7,31},{8,16},{9,... | collective-permute-start | bytes 393224 | tf_op jit(solution)/shard_map/ppermute | solution.py:499
  71.7 10.3 %collective-permute-start.16 = (bf16[1,256,128]{2,1,0:T(8,128)(2,1)S(1)}, bf16[1,256,128]{2,1,0:T(8,128)(2,1)S(1)}, u32[]{:S(2)}, u32[]{:S(2)}) collective-permute-start(bf16[1,256,128]{2,1,0:T(8,128)(2,1)S(1)} %get-tuple-element.76), channel_id=1, source_target_pairs={{0,8},{1,9},{2,10},{3,11},{4,12},{5,13},{6,14},{7,15},{8,0},{9,1},... | collective-permute-start | bytes 196616 | tf_op jit(solution)/shard_map/ppermute | solution.py:499
  76.9 9.4 %collective-permute-start.25 = (bf16[1,64,1024]{2,1,0:T(8,128)(2,1)S(1)}, bf16[1,64,1024]{2,1,0:T(8,128)(2,1)S(1)}, u32[]{:S(2)}, u32[]{:S(2)}) collective-permute-start(bf16[1,64,1024]{2,1,0:T(8,128)(2,1)S(1)} %shard_map.148.refs_0_), channel_id=1, source_target_pairs={{0,1},{1,0},{2,3},{3,2},{4,5},{5,4},{6,7},{7,6},{8,9},{9,8},{10,11... | collective-permute-start | bytes 393224 | tf_op jit(solution)/shard_map/ppermute | solution.py:499
  77.0 8.7 %collective-permute-start.17 = (bf16[1,256,128]{2,1,0:T(8,128)(2,1)S(1)}, bf16[1,256,128]{2,1,0:T(8,128)(2,1)S(1)}, u32[]{:S(2)}, u32[]{:S(2)}) collective-permute-start(bf16[1,256,128]{2,1,0:T(8,128)(2,1)S(1)} %get-tuple-element.77), channel_id=1, source_target_pairs={{0,16},{1,17},{2,18},{3,19},{4,20},{5,21},{6,22},{7,23},{8,24},{9,... | collective-permute-start | bytes 196616 | tf_op jit(solution)/shard_map/ppermute | solution.py:499
  79.4 6.3 %collective-permute-start.18 = (bf16[1,256,128]{2,1,0:T(8,128)(2,1)S(1)}, bf16[1,256,128]{2,1,0:T(8,128)(2,1)S(1)}, u32[]{:S(2)}, u32[]{:S(2)}) collective-permute-start(bf16[1,256,128]{2,1,0:T(8,128)(2,1)S(1)} %get-tuple-element.78), channel_id=1, source_target_pairs={{0,24},{1,25},{2,26},{3,27},{4,28},{5,29},{6,30},{7,31},{8,16},{9,... | collective-permute-start | bytes 196616 | tf_op jit(solution)/shard_map/ppermute | solution.py:499
  81.5 6.4 %collective-permute-start.26 = (bf16[1,64,1024]{2,1,0:T(8,128)(2,1)S(1)}, bf16[1,64,1024]{2,1,0:T(8,128)(2,1)S(1)}, u32[]{:S(2)}, u32[]{:S(2)}) collective-permute-start(bf16[1,64,1024]{2,1,0:T(8,128)(2,1)S(1)} %shard_map.148.refs_0_), channel_id=1, source_target_pairs={{0,2},{1,3},{2,0},{3,1},{4,6},{5,7},{6,4},{7,5},{8,10},{9,11},{10,... | collective-permute-start | bytes 393224 | tf_op jit(solution)/shard_map/ppermute | solution.py:499
  82.0 6.5 %collective-permute-start.27 = (bf16[1,64,1024]{2,1,0:T(8,128)(2,1)S(1)}, bf16[1,64,1024]{2,1,0:T(8,128)(2,1)S(1)}, u32[]{:S(2)}, u32[]{:S(2)}) collective-permute-start(bf16[1,64,1024]{2,1,0:T(8,128)(2,1)S(1)} %shard_map.148.refs_0_), channel_id=1, source_target_pairs={{0,3},{1,2},{2,1},{3,0},{4,7},{5,6},{6,5},{7,4},{8,11},{9,10},{10,... | collective-permute-start | bytes 393224 | tf_op jit(solution)/shard_map/ppermute | solution.py:499
  85.7 4.9 %collective-permute-start.19 = (bf16[1,256,128]{2,1,0:T(8,128)(2,1)S(1)}, bf16[1,256,128]{2,1,0:T(8,128)(2,1)S(1)}, u32[]{:S(2)}, u32[]{:S(2)}) collective-permute-start(bf16[1,256,128]{2,1,0:T(8,128)(2,1)S(1)} %shard_map.147.refs_0_), channel_id=1, source_target_pairs={{0,1},{1,0},{2,3},{3,2},{4,5},{5,4},{6,7},{7,6},{8,9},{9,8},{10,11... | collective-permute-start | bytes 196616 | tf_op jit(solution)/shard_map/ppermute | solution.py:499
  85.7 6.0 %collective-permute-start.20 = (bf16[1,256,128]{2,1,0:T(8,128)(2,1)S(1)}, bf16[1,256,128]{2,1,0:T(8,128)(2,1)S(1)}, u32[]{:S(2)}, u32[]{:S(2)}) collective-permute-start(bf16[1,256,128]{2,1,0:T(8,128)(2,1)S(1)} %shard_map.147.refs_0_), channel_id=1, source_target_pairs={{0,2},{1,3},{2,0},{3,1},{4,6},{5,7},{6,4},{7,5},{8,10},{9,11},{10,... | collective-permute-start | bytes 196616 | tf_op jit(solution)/shard_map/ppermute | solution.py:499
  86.3 5.4 %collective-permute-start.21 = (bf16[1,256,128]{2,1,0:T(8,128)(2,1)S(1)}, bf16[1,256,128]{2,1,0:T(8,128)(2,1)S(1)}, u32[]{:S(2)}, u32[]{:S(2)}) collective-permute-start(bf16[1,256,128]{2,1,0:T(8,128)(2,1)S(1)} %shard_map.147.refs_0_), channel_id=1, source_target_pairs={{0,3},{1,2},{2,1},{3,0},{4,7},{5,6},{6,5},{7,4},{8,11},{9,10},{10,... | collective-permute-start | bytes 196616 | tf_op jit(solution)/shard_map/ppermute | solution.py:499
